TPU v7x, 32 devices: a whole 2x2x4 slice. The times are simulated.
32 devices in a mesh: dp: 8 (over z, y), mp: 4 (over x, core).
Axes of the slice: x: 2, y: 2, z: 4, core: 2. Of those that a mesh axis runs over, the one named last changes fastest.
Arguments:
- inputs: bfloat16 [16, 1024, 768], P('dp', 'mp'), may hold values from -6 to 6
- cotangent: bfloat16 [16, 1024, 768], P('dp', 'mp'), may hold values from -6 to 6
- lengths: int32 [16], P('dp'), may hold values from 64 to 1024, as said below
- attn_weights: float32 [4, 768, 768], P(None, 'dp', 'mp'), may hold values from -0.57735027 to 0.57735027
- attn_first: float32 [4, 768, 768], P(None, 'dp', 'mp'), may hold values from -0.00024414062 to 0.00024414062
- attn_second: float32 [4, 768, 768], P(None, 'dp', 'mp'), may hold values from 1.4124676e-10 to 5.6498706e-10
- ffn_weights: float32 [2, 768, 3072], P(None, 'dp', 'mp'), may hold values from -0.5412659 to 0.5412659
- ffn_first: float32 [2, 768, 3072], P(None, 'dp', 'mp'), may hold values from -0.00024414062 to 0.00024414062
- ffn_second: float32 [2, 768, 3072], P(None, 'dp', 'mp'), may hold values from 1.4124676e-10 to 5.6498706e-10
- norm_gains: float32 [2, 768], P(None, 'dp'), may hold values from 0.38 to 2.6
- gain_first: float32 [2, 768], P(None, 'dp'), may hold values from -0.0007324219 to 0.0007324219
- gain_second: float32 [2, 768], P(None, 'dp'), may hold values from 1.2712209e-09 to 5.0848836e-09
- bias_table: float32 [12, 32], replicated, may hold values from -4 to 4
- table_first: float32 [12, 32], replicated, may hold values from -0.0007324219 to 0.0007324219
- table_second: float32 [12, 32], replicated, may hold values from 1.2712209e-10 to 5.0848836e-10
Outputs:
- block_out: bfloat16 [16, 1024, 768], P('dp', 'mp')
- input_grad: bfloat16 [16, 1024, 768], P('dp', 'mp')
- attn_grads: float32 [4, 768, 768], P(None, 'dp', 'mp')
- ffn_grads: float32 [2, 768, 3072], P(None, 'dp', 'mp')
- gain_grads: float32 [2, 768], P(None, 'dp')
- table_grads: float32 [12, 32], replicated
- grad_norm: float32 [], replicated
- attn_new: float32 [4, 768, 768], P(None, 'dp', 'mp')
- attn_first_new: float32 [4, 768, 768], P(None, 'dp', 'mp')
- attn_second_new: float32 [4, 768, 768], P(None, 'dp', 'mp')
- ffn_new: float32 [2, 768, 3072], P(None, 'dp', 'mp')
- ffn_first_new: float32 [2, 768, 3072], P(None, 'dp', 'mp')
- ffn_second_new: float32 [2, 768, 3072], P(None, 'dp', 'mp')
- gain_new: float32 [2, 768], P(None, 'dp')
- gain_first_new: float32 [2, 768], P(None, 'dp')
- gain_second_new: float32 [2, 768], P(None, 'dp')
- table_new: float32 [12, 32], replicated
- table_first_new: float32 [12, 32], replicated
- table_second_new: float32 [12, 32], replicated
Inputs may be any that keep to these rules, and one draw needn't show every extreme that they name: In each group of 2 sequences held by one index of dp, one has exactly 1024 real tokens; a sequence's first lengths positions are real and the rest is padding.
All inputs are finite; a program needn't handle non-finite values.
Results may differ from a plain program's by a relative error of at most 0.014.
The roundings to bfloat16 on the way count: a program that leaves them out, or rounds other values in their place, can miss the bound.
Values may be sent and summed in bfloat16 or wider, within the bound.
No kernel may reach another device: no remote copies, remote signals or barrier semaphores. Data moves between devices by JAX's collectives and lax.ppermute only.
A program may use at most 192 MiB of HBM per device.

v0:
```python
import functools

import jax
import jax.numpy as jnp
from jax import lax
from jax.experimental import pallas as pl
from jax.experimental.pallas import tpu as pltpu
from jax.sharding import PartitionSpec as P

H = 12
DH = 64
NB = 32
STEP = 10
D = 768

norm_eps = 1e-06
beta_one = 0.9
beta_two = 0.999
adam_eps = 1e-08
matrix_decay = 0.01
rate_matrix = 0.05
rate_small = 0.4
clip_level = 1.0

BF = jnp.bfloat16
F32 = jnp.float32
TILE = 128
GROUP = 3
WIDTH = GROUP * DH
NN = (((1,), (0,)), ((), ()))
NT = (((1,), (1,)), ((), ()))

shape_of = jax.ShapeDtypeStruct
in_smem = pl.BlockSpec(memory_space=pltpu.SMEM)
in_any = pl.BlockSpec(memory_space=pl.ANY)
in_vmem = pl.BlockSpec(memory_space=pltpu.VMEM)


def dot(left, right, dims):
    return lax.dot_general(left, right, dims, preferred_element_type=F32)


def params(mib):
    return pltpu.CompilerParams(vmem_limit_bytes=mib << 20)


def cost(flops, bytes_accessed, transcendentals=0):
    return pl.CostEstimate(
        flops=int(flops), bytes_accessed=int(bytes_accessed), transcendentals=int(transcendentals)
    )


def bucket_of(offset):
    distance = jnp.abs(offset)
    coarse = jnp.full(offset.shape, 8, jnp.int32)
    for level_bit in range(1, 8):
        coarse = coarse + (distance * distance >= 64 * 2**level_bit).astype(jnp.int32)
    inside = jnp.where(distance < 8, distance, coarse)
    return inside + jnp.where(offset > 0, 16, 0).astype(jnp.int32)


def adam_step(weight, first_old, second_old, gradient, step_rate, weight_decay):
    first_new = beta_one * first_old + (1.0 - beta_one) * gradient
    second_new = beta_two * second_old + (1.0 - beta_two) * gradient * gradient
    first_hat = first_new / (1.0 - beta_one**STEP)
    second_hat = second_new / (1.0 - beta_two**STEP)
    weight_new = weight - step_rate * (
        first_hat / (jnp.sqrt(second_hat) + adam_eps) + weight_decay * weight
    )
    return (weight_new, first_new, second_new)


def swap_core(v):
    return lax.ppermute(v, "mp", [(i, i ^ 1) for i in range(4)])


def swap_x(v):
    return lax.ppermute(v, "mp", [(i, i ^ 2) for i in range(4)])


def swap_y(v):
    n = lax.axis_size("dp")
    return lax.ppermute(v, "dp", [(i, i ^ 1) for i in range(n)])


def shift_z(v, step):
    n = lax.axis_size("dp")
    return lax.ppermute(v, "dp", [(i, (i + 2 * step) % n) for i in range(n)])


swap = {"x": swap_x, "y": swap_y}


def add_low(a, b):
    return (a.astype(F32) + b.astype(F32)).astype(BF)


def gather_weights(shard, order):
    depth = lax.axis_size("dp") // 2
    blocks = [shard]
    for _ in range(depth - 1):
        blocks.append(shift_z(blocks[-1], 1))
    ring = jnp.stack(blocks)
    second = swap[order[0]](ring)
    third, fourth = swap[order[1]](ring), swap[order[1]](second)
    if order == "xy":
        held = {(0, 0): ring, (1, 0): second, (0, 1): third, (1, 1): fourth}
    else:
        held = {(0, 0): ring, (0, 1): second, (1, 0): third, (1, 1): fourth}
    out = {}
    for (x, y), v in held.items():
        out[0, x, y] = v
        out[1, x, y] = swap_core(v)
    return out


def scatter_sums(held, order):
    depth = lax.axis_size("dp") // 2
    merged = {
        (x, y): add_low(held[0, x, y], swap_core(held[1, x, y])) for x in range(2) for y in range(2)
    }
    if order == "xy":
        half = [add_low(merged[x, 0], swap_y(merged[x, 1])) for x in range(2)]
        ring = add_low(half[0], swap_x(half[1]))
    else:
        half = [add_low(merged[0, y], swap_x(merged[1, y])) for y in range(2)]
        ring = add_low(half[0], swap_y(half[1]))
    total = ring[depth - 1]
    for s in range(depth - 2, 0, -1):
        total = add_low(ring[s], shift_z(total, -1))
    return ring[0].astype(F32) + shift_z(total, -1).astype(F32)


def sum_all(v):
    diagonal = lax.ppermute(v, "mp", [(i, i ^ 3) for i in range(4)])
    v = (v + swap_core(v)) + (swap_x(v) + diagonal)
    n = lax.axis_size("dp")
    if n != 8:
        return lax.psum(v, "dp")
    v = v + swap_y(v)
    far = [lax.ppermute(v, "dp", [(i, i ^ k) for i in range(n)]) for k in (2, 4, 6)]
    return (v + far[0]) + (far[1] + far[2])


def block_views(held, core, x):
    parts = [held[core, x, y] for y in range(2)]
    depth, rows, cols = parts[0].shape
    if rows % 16 == 0:
        return parts
    dp = lax.axis_index("dp")
    both = jnp.stack(parts)
    sides = jnp.take(both, jnp.arange(2) ^ (dp % 2), axis=0)
    lined = jnp.take(sides, (dp // 2 - jnp.arange(depth)) % depth, axis=1)
    return [jnp.transpose(lined, (1, 0, 2, 3)).reshape(1, D, cols)]


def block_shapes(depth, rows, cols):
    if rows % 16 == 0:
        return [shape_of((depth, rows, cols), BF)] * 2
    return [shape_of((1, D, cols), BF)]


def block_parts(outs, depth, rows):
    if rows % 16 == 0:
        return outs
    dp = lax.axis_index("dp")
    lined = jnp.transpose(outs[0].reshape(depth, 2, rows, -1), (1, 0, 2, 3))
    sides = jnp.take(lined, jnp.arange(2) ^ (dp % 2), axis=0)
    turned = jnp.take(sides, (dp // 2 - jnp.arange(depth)) % depth, axis=1)
    return [turned[0], turned[1]]


def piece_copies(refs, whole, place_ref, sems, first_sem, outward=False, cols=None):
    copies = []
    for i, ref in enumerate(refs):
        pieces, rows = ref.shape[0], ref.shape[1]
        for j in range(pieces):
            count = len(copies)
            start = pl.multiple_of(place_ref[4 + count], 16)
            there = whole.at[pl.ds(start, rows), :]
            here = ref.at[j] if cols is None else ref.at[j, :, pl.ds(cols[0], cols[1])]
            pair = (there, here) if outward else (here, there)
            copies.append(pltpu.make_async_copy(*pair, sems.at[first_sem + count]))
    return copies


def bias_kernel(place_ref, table_ref, out_ref):
    block = pl.program_id(0)
    head_base = (place_ref[3] ^ block) * GROUP
    row = lax.broadcasted_iota(jnp.int32, (TILE, TILE), 0)
    col = lax.broadcasted_iota(jnp.int32, (TILE, TILE), 1)
    for h in range(GROUP):
        out_ref[0, h, 0] = jnp.full((TILE, TILE), table_ref[head_base + h, 15], F32)
        out_ref[0, h, 4] = jnp.full((TILE, TILE), table_ref[head_base + h, 31], F32)
    for t in range(1, 4):
        bucket = bucket_of(col - row + (t - 2) * TILE)
        which = {1: range(16), 2: range(32), 3: range(16, 32)}[t]
        for h in range(GROUP):
            tile = jnp.zeros((TILE, TILE), F32)
            for b in which:
                tile = jnp.where(bucket == b, table_ref[head_base + h, b], tile)
            out_ref[0, h, t] = tile


def make_bias(place, table):
    return pl.pallas_call(
        bias_kernel,
        grid=(4,),
        in_specs=[in_smem, in_smem],
        out_specs=pl.BlockSpec((1, GROUP, 5, TILE, TILE), lambda i: (i, 0, 0, 0, 0)),
        out_shape=shape_of((4, GROUP, 5, TILE, TILE), F32),
        compiler_params=params(16),
        cost_estimate=cost(10e6, 4e6),
        name="bias_tiles",
    )(place, table)


def rms_of(v, gain):
    inverse = lax.rsqrt(jnp.mean(v * v, axis=-1, keepdims=True) + norm_eps)
    return v * inverse * gain


def rms_back(v, gain, t):
    inverse = lax.rsqrt(jnp.mean(v * v, axis=-1, keepdims=True) + norm_eps)
    along = jnp.mean(v * gain * t, axis=-1, keepdims=True)
    grad = inverse * gain * t - v * (inverse * inverse * inverse) * along
    return grad, jnp.sum(t * v * inverse, axis=0, keepdims=True)


def project_kernel(n_parts, place_ref, x_ref, gain_ref, *refs):
    w_refs, (q_ref, k_ref, v_ref, whole, sems) = refs[: 2 * n_parts], refs[2 * n_parts :]
    count = sems.shape[0] // 2
    copies = [
        piece_copies(w_refs[b * n_parts : (b + 1) * n_parts], whole.at[b], place_ref, sems, b * count)
        for b in range(2)
    ]
    for group in copies:
        for c in group:
            c.start()
    normed = rms_of(x_ref[...].astype(F32), gain_ref[0:1].astype(F32)).astype(BF)
    for b in range(2):
        for c in copies[b]:
            c.wait()
        out = dot(normed, whole[b, :, 0:640], NN).astype(BF)
        q_ref[b] = out[:, 0:WIDTH]
        k_ref[b] = out[:, WIDTH : 2 * WIDTH]
        v_ref[b] = out[:, 2 * WIDTH : 3 * WIDTH]


def project(place, rows_in, gain_low, blocks):
    rows = rows_in.shape[0]
    n_parts = len(blocks[0])
    pieces = sum(p.shape[0] for p in blocks[0])
    return pl.pallas_call(
        functools.partial(project_kernel, n_parts),
        in_specs=[in_smem, in_vmem, in_vmem] + [in_any] * (2 * n_parts),
        out_specs=[in_vmem] * 3,
        out_shape=[shape_of((2, rows, WIDTH), BF)] * 3,
        scratch_shapes=[pltpu.VMEM((2, D, D), BF), pltpu.SemaphoreType.DMA((2 * pieces,))],
        compiler_params=params(32),
        cost_estimate=cost(2 * 2 * rows * D * 576, 5e6),
        name="project",
    )(place, rows_in, gain_low, *blocks[0], *blocks[1])


def tile_places(place_ref):
    x, core = place_ref[0], place_ref[1]
    mine = [4 * (x if t < 2 else 1 - x) + 2 * core + t % 2 for t in range(4)]
    theirs = [4 * (x if t < 2 else 1 - x) + 2 * (1 - core) + t % 2 for t in range(4)]
    return mine, mine + theirs


def attend_kernel(place_ref, q_ref, ko_ref, vo_ref, kp_ref, vp_ref, bias_ref, ctx_ref, p_ref):
    rows = q_ref.shape[1]
    step = 256
    lane = lax.broadcasted_iota(jnp.int32, (1, 256), 1)
    key = lax.broadcasted_iota(jnp.int32, (1, TILE), 1)
    sub = lax.broadcasted_iota(jnp.int32, (64, 1), 0)
    row_tiles, key_tiles = tile_places(place_ref)
    length = place_ref[2]
    hide = jnp.concatenate([jnp.where(key + TILE * g < length, 0.0, -1e30) for g in key_tiles], 1)
    extra = jnp.where(sub == 0, hide, 0.0).astype(BF)
    keys_t = jnp.concatenate([jnp.concatenate([ko_ref[0].T, kp_ref[0].T], 1), extra], 0)
    values = jnp.concatenate([vo_ref[0], vp_ref[0]], 0)
    queries = jnp.concatenate([q_ref[0], jnp.ones((rows, 64), BF)], 1)
    total = [jnp.zeros((step, WIDTH), F32) for _ in range(rows // step)]
    for h in range(GROUP):
        inside = (lane >= h * DH) & (lane < (h + 1) * DH)
        used = inside | (lane == WIDTH)
        for r in range(rows // step):
            here = jnp.where(used, queries[r * step : (r + 1) * step], jnp.zeros((), BF))
            scores = dot(here, keys_t, NN)
            tiles = []
            for c in range(8):
                bias = []
                for u in range(step // TILE):
                    which = jnp.clip(key_tiles[c] - row_tiles[r * (step // TILE) + u] + 2, 0, 4)
                    bias.append(bias_ref[0, h, which])
                tiles.append(scores[:, c * TILE : (c + 1) * TILE] + jnp.concatenate(bias, 0))
            top = jnp.max(functools.reduce(jnp.maximum, tiles), axis=-1, keepdims=True)
            exps = [jnp.exp(t - top) for t in tiles]
            norm = jnp.sum(functools.reduce(jnp.add, exps), axis=-1, keepdims=True)
            scale = 1.0 / norm
            prob = jnp.concatenate([(e * scale).astype(BF) for e in exps], 1)
            p_ref[0, h, pl.ds(r * step, step), :] = prob
            total[r] = jnp.where(inside[:, :WIDTH], dot(prob, values, NN), total[r])
    for r in range(rows // step):
        ctx_ref[0, pl.ds(r * step, step), :] = total[r].astype(BF)


def attend(place, q, k_own, v_own, k_other, v_other, bias, blocks):
    n, rows = q.shape[0], q.shape[1]
    a, s = blocks
    spec = pl.BlockSpec((1, rows, WIDTH), lambda i: (i, 0, 0))
    return pl.pallas_call(
        attend_kernel,
        grid=(n,),
        in_specs=[in_smem]
        + [spec] * 5
        + [pl.BlockSpec((1, GROUP, 5, TILE, TILE), lambda i: (a + s * i, 0, 0, 0, 0))],
        out_specs=[spec, pl.BlockSpec((1, GROUP, rows, 2 * rows), lambda i: (i, 0, 0, 0))],
        out_shape=[
            shape_of((n, rows, WIDTH), BF),
            shape_of((n, GROUP, rows, 2 * rows), BF),
        ],
        compiler_params=params(40),
        cost_estimate=cost(n * GROUP * rows * 2 * rows * 256 * 4, 10e6, n * GROUP * rows * 2 * rows),
        name="attend",
    )(place, q, k_own, v_own, k_other, v_other, bias)


def middle_kernel(n_parts, place_ref, x_ref, gain_ref, back_ref, ctx_a_ref, ctx_b_ref, *refs):
    w_refs = refs[: 4 * n_parts]
    mid_ref, normed_ref, normed_t_ref, back_t_ref, whole, sems = refs[4 * n_parts :]
    count = sems.shape[0] // 4
    copies = [
        piece_copies(
            w_refs[b * n_parts : (b + 1) * n_parts],
            whole.at[b],
            place_ref,
            sems,
            b * count,
            cols=(512, 256),
        )
        for b in range(4)
    ]
    for group in copies:
        for c in group:
            c.start()
    rows = x_ref.shape[0]
    total = x_ref[...].astype(F32)
    back_t_ref[...] = back_ref[...].T
    blank = jnp.zeros((rows, 64), BF)
    for b in range(4):
        for c in copies[b]:
            c.wait()
        ctx = (ctx_a_ref if b % 2 == 0 else ctx_b_ref)[b // 2]
        total = total + dot(jnp.concatenate([blank, ctx], 1), whole[b], NT)
    mid_ref[...] = total
    normed = rms_of(total, gain_ref[1:2].astype(F32)).astype(BF)
    normed_ref[...] = normed
    normed_t_ref[...] = normed.T


def middle(place, rows_in, gain_low, back, ctx_a, ctx_b, blocks):
    rows = rows_in.shape[0]
    n_parts = len(blocks[0])
    pieces = sum(p.shape[0] for p in blocks[0])
    return pl.pallas_call(
        functools.partial(middle_kernel, n_parts),
        in_specs=[in_smem] + [in_vmem] * 5 + [in_any] * (4 * n_parts),
        out_specs=[in_vmem] * 4,
        out_shape=[
            shape_of((rows, D), F32),
            shape_of((rows, D), BF),
            shape_of((D, rows), BF),
            shape_of((D, rows), BF),
        ],
        scratch_shapes=[pltpu.VMEM((4, D, 256), BF), pltpu.SemaphoreType.DMA((4 * pieces,))],
        compiler_params=params(32),
        cost_estimate=cost(2 * rows * D * D, 8e6),
        name="middle",
    )(place, rows_in, gain_low, back, ctx_a, ctx_b, *[p for b in blocks for p in b])


def feed_kernel(n_parts, place_ref, n_ref, nt_ref, g_ref, gt_ref, acc_in, t_in, *refs):
    wi_refs, wf_refs = refs[: 2 * n_parts], refs[2 * n_parts : 4 * n_parts]
    rest = refs[4 * n_parts :]
    acc_ref, t_ref = rest[:2]
    gi_refs, gf_refs = rest[2 : 2 + 2 * n_parts], rest[2 + 2 * n_parts : 2 + 4 * n_parts]
    wi, wf, gi, gf, sems, out_sems = rest[2 + 4 * n_parts :]
    count = sems.shape[0] // 4
    loads = []
    for b in range(2):
        part = slice(b * n_parts, (b + 1) * n_parts)
        loads.append(
            piece_copies(wi_refs[part], wi.at[b], place_ref, sems, 2 * b * count)
            + piece_copies(wf_refs[part], wf.at[b], place_ref, sems, (2 * b + 1) * count)
        )
    for group in loads:
        for c in group:
            c.start()
    acc_ref[...] = acc_in[...]
    t_ref[...] = t_in[...]
    stores = []
    for b in range(2):
        for c in loads[b]:
            c.wait()

        def hidden(j, _):
            cols = pl.ds(pl.multiple_of(j * 256, 256), 256)
            wi_here, wf_here = wi[b, :, cols], wf[b, :, cols]
            pre = dot(n_ref[...], wi_here, NN)
            grad = dot(g_ref[...], wf_here, NN)
            cdf = 0.5 * (1.0 + lax.erf(pre * 0.7071067811865476))
            active = (pre * cdf).astype(BF)
            density = jnp.exp(pre * pre * -0.5) * 0.3989422804014327
            pre_grad = (grad * (cdf + pre * density)).astype(BF)
            acc_ref[...] += dot(active, wf_here, NT)
            t_ref[...] += dot(pre_grad, wi_here, NT)
            gi[b, :, cols] = dot(nt_ref[...], pre_grad, NN).astype(BF)
            gf[b, :, cols] = dot(gt_ref[...], active, NN).astype(BF)
            return 0

        lax.fori_loop(0, D // 256, hidden, 0)
        part = slice(b * n_parts, (b + 1) * n_parts)
        group = piece_copies(
            gi_refs[part], gi.at[b], place_ref, out_sems, 2 * b * count, outward=True
        ) + piece_copies(
            gf_refs[part], gf.at[b], place_ref, out_sems, (2 * b + 1) * count, outward=True
        )
        for c in group:
            c.start()
        stores.append(group)
    for group in stores:
        for c in group:
            c.wait()


def feed(place, normed, normed_t, back, back_t, acc, t_acc, wi_blocks, wf_blocks, out_shapes):
    rows = normed.shape[0]
    n_parts = len(wi_blocks[0])
    pieces = sum(p.shape[0] for p in wi_blocks[0])
    outs = pl.pallas_call(
        functools.partial(feed_kernel, n_parts),
        in_specs=[in_smem] + [in_vmem] * 6 + [in_any] * (4 * n_parts),
        out_specs=[in_vmem] * 2 + [in_any] * (4 * n_parts),
        out_shape=[shape_of((rows, D), F32)] * 2 + out_shapes * 4,
        scratch_shapes=[pltpu.VMEM((2, D, D), BF)] * 4
        + [pltpu.SemaphoreType.DMA((4 * pieces,))] * 2,
        compiler_params=params(48),
        cost_estimate=cost(2 * 6 * 2 * rows * D * D, 15e6, 4 * rows * D),
        name="feed",
    )(
        place,
        normed,
        normed_t,
        back,
        back_t,
        acc,
        t_acc,
        *[p for b in wi_blocks for p in b],
        *[p for b in wf_blocks for p in b],
    )
    n = n_parts
    groups = [outs[2 + i * n : 2 + (i + 1) * n] for i in range(4)]
    return outs[0], outs[1], groups[0:2], groups[2:4]


def turn_kernel(n_parts, place_ref, mid_ref, acc_ref, t_ref, back_ref, gain_ref, *refs):
    w_refs = refs[: 4 * n_parts]
    out_ref, grad_ref, low_ref, low_t_ref, gain_grad_ref, cg_a_ref, cg_b_ref, whole, sems = refs[
        4 * n_parts :
    ]
    count = sems.shape[0] // 4
    copies = [
        piece_copies(
            w_refs[b * n_parts : (b + 1) * n_parts],
            whole.at[b],
            place_ref,
            sems,
            b * count,
            cols=(512, 256),
        )
        for b in range(4)
    ]
    for group in copies:
        for c in group:
            c.start()
    mid = mid_ref[...]
    out_ref[...] = (mid + acc_ref[...]).astype(BF)
    grad, gain_grad = rms_back(mid, gain_ref[1:2].astype(F32), t_ref[...])
    gain_grad_ref[...] = gain_grad
    grad = back_ref[...].astype(F32) + grad
    grad_ref[...] = grad
    low = grad.astype(BF)
    low_ref[...] = low
    low_t_ref[...] = low.T
    for b in range(4):
        for c in copies[b]:
            c.wait()
        (cg_a_ref if b % 2 == 0 else cg_b_ref)[b // 2] = dot(low, whole[b], NN).astype(BF)[:, 64:]


def turn(place, mid, acc, t_acc, back, gain_low, blocks):
    rows = mid.shape[0]
    n_parts = len(blocks[0])
    pieces = sum(p.shape[0] for p in blocks[0])
    return pl.pallas_call(
        functools.partial(turn_kernel, n_parts),
        in_specs=[in_smem] + [in_vmem] * 5 + [in_any] * (4 * n_parts),
        out_specs=[in_vmem] * 7,
        out_shape=[
            shape_of((rows, D), BF),
            shape_of((rows, D), F32),
            shape_of((rows, D), BF),
            shape_of((D, rows), BF),
            shape_of((1, D), F32),
            shape_of((2, rows, WIDTH), BF),
            shape_of((2, rows, WIDTH), BF),
        ],
        scratch_shapes=[pltpu.VMEM((4, D, 256), BF), pltpu.SemaphoreType.DMA((4 * pieces,))],
        compiler_params=params(40),
        cost_estimate=cost(2 * rows * D * D, 10e6),
        name="turn",
    )(place, mid, acc, t_acc, back, gain_low, *[p for b in blocks for p in b])


def attend_back_kernel(
    place_ref,
    q_ref,
    ko_ref,
    vo_ref,
    kp_ref,
    vp_ref,
    g_ref,
    ctx_ref,
    p_ref,
    dq_ref,
    dko_ref,
    dvo_ref,
    dkp_ref,
    dvp_ref,
    sums_ref,
    ds_ref,
):
    rows = q_ref.shape[1]
    step = 128
    lane = lax.broadcasted_iota(jnp.int32, (1, WIDTH), 1)
    row_tiles, key_tiles = tile_places(place_ref)
    queries, grads = q_ref[0], g_ref[0]
    keys = jnp.concatenate([ko_ref[0], kp_ref[0]], 0)
    values_t = jnp.concatenate([vo_ref[0].T, vp_ref[0].T], 1)
    queries_t, grads_t = queries.T, grads.T
    product = grads.astype(F32) * ctx_ref[0].astype(F32)
    sums_ref[...] = jnp.zeros_like(sums_ref)
    total = [jnp.zeros((step, WIDTH), F32) for _ in range(rows // step)]
    key_grads, value_grads = [], []
    for h in range(GROUP):
        inside = (lane >= h * DH) & (lane < (h + 1) * DH)
        for r in range(rows // step):
            span = slice(r * step, (r + 1) * step)
            here = jnp.where(inside, grads[span], jnp.zeros((), BF))
            prob_grad = dot(here, values_t, NN)
            row_dot = jnp.sum(jnp.where(inside, product[span], 0.0), axis=-1, keepdims=True)
            lows = []
            for c in range(8):
                prob = p_ref[0, h, pl.ds(r * step, step), pl.ds(c * TILE, TILE)].astype(F32)
                dscore = prob * (prob_grad[:, c * TILE : (c + 1) * TILE] - row_dot)
                which = jnp.clip(key_tiles[c] - row_tiles[r] + 2, 0, 4)
                sums_ref[0, h, which] += dscore
                lows.append(dscore.astype(BF))
            low = jnp.concatenate(lows, 1)
            ds_ref[pl.ds(r * step, step), :] = low
            total[r] = jnp.where(inside, dot(low, keys, NN), total[r])
        key_grads.append(dot(queries_t[h * DH : (h + 1) * DH], ds_ref[...], NN))
        value_grads.append(dot(grads_t[h * DH : (h + 1) * DH], p_ref[0, h], NN))
    for r in range(rows // step):
        dq_ref[0, pl.ds(r * step, step), :] = total[r].astype(BF)
    key_grad = jnp.concatenate(key_grads, 0).T
    value_grad = jnp.concatenate(value_grads, 0).T
    dko_ref[0], dkp_ref[0] = key_grad[:rows], key_grad[rows:].astype(BF)
    dvo_ref[0], dvp_ref[0] = value_grad[:rows], value_grad[rows:].astype(BF)


def attend_back(place, q, k_own, v_own, k_other, v_other, grads, ctx, prob):
    n, rows = q.shape[0], q.shape[1]
    spec = pl.BlockSpec((1, rows, WIDTH), lambda i: (i, 0, 0))
    return pl.pallas_call(
        attend_back_kernel,
        grid=(n,),
        in_specs=[in_smem]
        + [spec] * 7
        + [pl.BlockSpec((1, GROUP, rows, 2 * rows), lambda i: (i, 0, 0, 0))],
        out_specs=[spec] * 5 + [pl.BlockSpec((1, GROUP, 5, TILE, TILE), lambda i: (i, 0, 0, 0, 0))],
        out_shape=[
            shape_of((n, rows, WIDTH), BF),
            shape_of((n, rows, WIDTH), F32),
            shape_of((n, rows, WIDTH), F32),
            shape_of((n, rows, WIDTH), BF),
            shape_of((n, rows, WIDTH), BF),
            shape_of((n, GROUP, 5, TILE, TILE), F32),
        ],
        scratch_shapes=[pltpu.VMEM((rows, 2 * rows), BF)],
        compiler_params=params(44),
        cost_estimate=cost(n * GROUP * rows * 2 * rows * 256 * 8, 12e6),
        name="attend_back",
    )(place, q, k_own, v_own, k_other, v_other, grads, ctx, prob)


def bucket_kernel(sums_ref, out_ref):
    row = lax.broadcasted_iota(jnp.int32, (TILE, TILE), 0)
    col = lax.broadcasted_iota(jnp.int32, (TILE, TILE), 1)
    buckets = {t: bucket_of(col - row + (t - 2) * TILE) for t in range(1, 4)}
    for h in range(GROUP):
        for b in range(NB):
            total = jnp.zeros((TILE, TILE), F32)
            if b == 15:
                total = sums_ref[0, h, 0]
            if b == 31:
                total = sums_ref[0, h, 4]
            for t in (1, 2) if b < 16 else (2, 3):
                total = total + jnp.where(buckets[t] == b, sums_ref[0, h, t], 0.0)
            out_ref[0, h, pl.ds(b, 1), :] = jnp.sum(total, axis=0, keepdims=True)


def bucket_sums(sums):
    n = sums.shape[0]
    return pl.pallas_call(
        bucket_kernel,
        grid=(n,),
        in_specs=[pl.BlockSpec((1, GROUP, 5, TILE, TILE), lambda i: (i, 0, 0, 0, 0))],
        out_specs=pl.BlockSpec((1, GROUP, NB, TILE), lambda i: (i, 0, 0, 0)),
        out_shape=shape_of((n, GROUP, NB, TILE), F32),
        compiler_params=params(16),
        cost_estimate=cost(n * 8e6, n * 1e6),
        name="bucket_sums",
    )(sums)


def project_back_kernel(n_parts, place_ref, x_ref, gain_ref, low_t_ref, acc_in, ctx_ref, dq_ref, *refs):
    dko_ref, dkp_ref, dvo_ref, dvp_ref = refs[:4]
    w_refs = refs[4 : 4 + 2 * n_parts]
    rest = refs[4 + 2 * n_parts :]
    acc_ref, g_refs = rest[0], rest[1 : 1 + 2 * n_parts]
    whole, grad, sems, out_sems = rest[1 + 2 * n_parts :]
    count = sems.shape[0] // 2
    copies = [
        piece_copies(w_refs[b * n_parts : (b + 1) * n_parts], whole.at[b], place_ref, sems, b * count)
        for b in range(2)
    ]
    for group in copies:
        for c in group:
            c.start()
    normed = rms_of(x_ref[...].astype(F32), gain_ref[0:1].astype(F32)).astype(BF)
    normed_t = normed.T
    low_t = low_t_ref[...]
    total = acc_in[...]
    stores = []
    for b in range(2):
        dk = (dko_ref[b] + dkp_ref[b].astype(F32)).astype(BF)
        dv = (dvo_ref[b] + dvp_ref[b].astype(F32)).astype(BF)
        heads = jnp.concatenate([dq_ref[b], dk, dv], 1)
        out = dot(normed_t, heads, NN).astype(BF)
        last = dot(low_t, ctx_ref[b], NN).astype(BF)
        grad[b] = jnp.concatenate([out, last], 1)
        group = piece_copies(
            g_refs[b * n_parts : (b + 1) * n_parts],
            grad.at[b],
            place_ref,
            out_sems,
            b * count,
            outward=True,
        )
        for c in group:
            c.start()
        stores.append(group)
        for c in copies[b]:
            c.wait()
        total = total + dot(heads, whole[b, :, 0:576], NT)
    acc_ref[...] = total
    for group in stores:
        for c in group:
            c.wait()


def project_back(place, rows_in, gain_low, low_t, acc, ctx, dq, dk, dv, blocks, out_shapes):
    rows = rows_in.shape[0]
    n_parts = len(blocks[0])
    pieces = sum(p.shape[0] for p in blocks[0])
    outs = pl.pallas_call(
        functools.partial(project_back_kernel, n_parts),
        in_specs=[in_smem] + [in_vmem] * 10 + [in_any] * (2 * n_parts),
        out_specs=[in_vmem] + [in_any] * (2 * n_parts),
        out_shape=[shape_of((rows, D), F32)] + out_shapes * 2,
        scratch_shapes=[pltpu.VMEM((2, D, D), BF)] * 2
        + [pltpu.SemaphoreType.DMA((2 * pieces,))] * 2,
        compiler_params=params(40),
        cost_estimate=cost(2 * 2 * 2 * rows * D * D, 10e6),
        name="project_back",
    )(place, rows_in, gain_low, low_t, acc, ctx, dq, *dk, *dv, *blocks[0], *blocks[1])
    return outs[0], [outs[1 : 1 + n_parts], outs[1 + n_parts :]]


def finish_kernel(x_ref, gain_ref, t_ref, mid_grad_ref, out_ref, gain_grad_ref):
    grad, gain_grad = rms_back(x_ref[...].astype(F32), gain_ref[0:1].astype(F32), t_ref[...])
    out_ref[...] = (mid_grad_ref[...] + grad).astype(BF)
    gain_grad_ref[...] = gain_grad


def finish(rows_in, gain_low, t_acc, mid_grad):
    rows = rows_in.shape[0]
    return pl.pallas_call(
        finish_kernel,
        in_specs=[in_vmem] * 4,
        out_specs=[in_vmem] * 2,
        out_shape=[shape_of((rows, D), BF), shape_of((1, D), F32)],
        compiler_params=params(24),
        cost_estimate=cost(rows * D * 12, 6e6),
        name="finish",
    )(rows_in, gain_low, t_acc, mid_grad)


def per_device(
    inputs,
    cotangent,
    lengths,
    attn_weights,
    attn_first,
    attn_second,
    ffn_weights,
    ffn_first,
    ffn_second,
    norm_gains,
    gain_first,
    gain_second,
    bias_table,
    table_first,
    table_second,
):
    assert lax.axis_size("mp") == 4 and inputs.shape[0] == 2
    depth = lax.axis_size("dp") // 2
    shard_rows = ffn_weights.shape[1]
    mp, dp = lax.axis_index("mp"), lax.axis_index("dp")
    x, core = mp // 2, mp % 2
    part = inputs.shape[1]

    def regroup(v):
        mine = lax.dynamic_index_in_dim(v, x, 0, keepdims=False)
        other = lax.dynamic_index_in_dim(v, 1 - x, 0, keepdims=False)
        return jnp.concatenate([mine, swap_x(other)], 0)

    def ungroup(v):
        mine, other = v[:part], swap_x(v[part:])
        low, high = jnp.where(x == 0, mine, other), jnp.where(x == 0, other, mine)
        return jnp.stack([low, high])

    length = lax.dynamic_index_in_dim(lengths, x, 0, keepdims=False)
    starts = [
        shard_rows * (((dp // 2 - s) % depth) * 2 + ((dp % 2) ^ y))
        for y in range(2)
        for s in range(depth)
    ]
    if shard_rows % 16:
        starts = [jnp.zeros((), jnp.int32)]
    place = jnp.stack([v.astype(jnp.int32) for v in [x, core, length, mp] + starts])

    gain_low = lax.all_gather(norm_gains.astype(BF), "dp", axis=1, tiled=True)
    rows_in = regroup(inputs)
    attn_low = jnp.transpose(attn_weights.astype(BF), (1, 0, 2)).reshape(shard_rows, D)
    ffn_low = ffn_weights.astype(BF)
    attn_held = gather_weights(attn_low, "xy")
    wi_held = gather_weights(ffn_low[0], "yx")
    wf_held = gather_weights(ffn_low[1], "xy")
    back = regroup(cotangent)
    bias = make_bias(place, bias_table)

    attn_blocks = {(c, xx): block_views(attn_held, c, xx) for c in range(2) for xx in range(2)}
    wi_blocks = {(c, xx): block_views(wi_held, c, xx) for c in range(2) for xx in range(2)}
    wf_blocks = {(c, xx): block_views(wf_held, c, xx) for c in range(2) for xx in range(2)}
    by_core = [[(c, 0), (c, 1)] for c in range(2)]
    every = [(0, 0), (1, 0), (0, 1), (1, 1)]
    out_shapes = block_shapes(depth, shard_rows, D)

    q, k, v = {}, {}, {}
    for c in range(2):
        q[c], k[c], v[c] = project(place, rows_in, gain_low, [attn_blocks[b] for b in by_core[c]])
    k_other = {1 - c: swap_core(k[c]) for c in range(2)}
    v_other = {1 - c: swap_core(v[c]) for c in range(2)}
    ctx, prob = {}, {}
    for c in (1, 0):
        ctx[c], prob[c] = attend(place, q[c], k[c], v[c], k_other[c], v_other[c], bias, (c, 2))
    mid, normed_two, normed_two_t, back_t = middle(
        place, rows_in, gain_low, back, ctx[0], ctx[1], [attn_blocks[b] for b in every]
    )
    acc = jnp.zeros(mid.shape, F32)
    t_acc = jnp.zeros(mid.shape, F32)
    wi_grads, wf_grads = {}, {}
    for c in range(2):
        acc, t_acc, gi, gf = feed(
            place,
            normed_two,
            normed_two_t,
            back,
            back_t,
            acc,
            t_acc,
            [wi_blocks[b] for b in by_core[c]],
            [wf_blocks[b] for b in by_core[c]],
            out_shapes,
        )
        for xx in range(2):
            for held, outs in ((wi_grads, gi), (wf_grads, gf)):
                held[c, xx, 0], held[c, xx, 1] = block_parts(outs[xx], depth, shard_rows)
    out_rows, mid_grad, mid_low, mid_low_t, gain_two_grad, cg_a, cg_b = turn(
        place, mid, acc, t_acc, back, gain_low, [attn_blocks[b] for b in every]
    )
    block_out = ungroup(out_rows)
    wi_total = scatter_sums(wi_grads, "yx")
    wf_total = scatter_sums(wf_grads, "xy")
    cg = {0: cg_a, 1: cg_b}
    dq, dko, dvo, dkp, dvp, sums = {}, {}, {}, {}, {}, {}
    for c in (1, 0):
        dq[c], dko[c], dvo[c], dkp[c], dvp[c], sums[c] = attend_back(
            place, q[c], k[c], v[c], k_other[c], v_other[c], cg[c], ctx[c], prob[c]
        )
    t_one = jnp.zeros(mid.shape, F32)
    attn_grads = {}
    for c in (1, 0):
        t_one, outs = project_back(
            place,
            rows_in,
            gain_low,
            mid_low_t,
            t_one,
            ctx[c],
            dq[c],
            (dko[c], swap_core(dkp[1 - c])),
            (dvo[c], swap_core(dvp[1 - c])),
            [attn_blocks[b] for b in by_core[c]],
            out_shapes,
        )
        for xx in range(2):
            attn_grads[c, xx, 0], attn_grads[c, xx, 1] = block_parts(outs[xx], depth, shard_rows)
    attn_total = scatter_sums(attn_grads, "xy")
    in_rows, gain_one_grad = finish(rows_in, gain_low, t_one, mid_grad)
    input_grad = ungroup(in_rows)

    lines = [bucket_sums(sums[c]) for c in range(2)]
    by_block = jnp.stack([lines[0][0], lines[1][0], lines[0][1], lines[1][1]])
    table_part = jnp.take(jnp.sum(by_block, -1), jnp.arange(4) ^ mp, axis=0).reshape(H * NB)
    small = jnp.concatenate([gain_one_grad[0], gain_two_grad[0], table_part])
    small = sum_all(small.reshape(-1, TILE)).reshape(-1)
    gain_total = small[: 2 * D].reshape(2, D)
    table_grads = small[2 * D :].reshape(H, NB)
    gain_cols = norm_gains.shape[1]
    gain_grads = lax.dynamic_slice_in_dim(gain_total, dp * gain_cols, gain_cols, 1)

    attn_reduced = jnp.transpose(attn_total.reshape(shard_rows, 4, WIDTH), (1, 0, 2))
    ffn_reduced = jnp.stack([wi_total, wf_total])
    squares = jnp.sum(attn_reduced * attn_reduced) + jnp.sum(ffn_reduced * ffn_reduced)
    squares = sum_all(jnp.full((8, TILE), squares))[0, 0]
    grad_norm = jnp.sqrt(squares + jnp.sum(small * small))
    clip_factor = jnp.minimum(1.0, clip_level / (grad_norm + 1e-06))
    attn_new, attn_first_new, attn_second_new = adam_step(
        attn_weights, attn_first, attn_second, attn_reduced * clip_factor, rate_matrix, matrix_decay
    )
    ffn_new, ffn_first_new, ffn_second_new = adam_step(
        ffn_weights, ffn_first, ffn_second, ffn_reduced * clip_factor, rate_matrix, matrix_decay
    )
    gain_new, gain_first_new, gain_second_new = adam_step(
        norm_gains, gain_first, gain_second, gain_grads * clip_factor, rate_small, 0.0
    )
    table_new, table_first_new, table_second_new = adam_step(
        bias_table, table_first, table_second, table_grads * clip_factor, rate_small, 0.0
    )
    return (
        block_out,
        input_grad,
        attn_reduced,
        ffn_reduced,
        gain_grads,
        table_grads,
        grad_norm,
        attn_new,
        attn_first_new,
        attn_second_new,
        ffn_new,
        ffn_first_new,
        ffn_second_new,
        gain_new,
        gain_first_new,
        gain_second_new,
        table_new,
        table_first_new,
        table_second_new,
    )


def solution(mesh):
    placed = (
        P("dp", "mp", None),
        P("dp", "mp", None),
        P("dp"),
        P(None, "dp", "mp"),
        P(None, "dp", "mp"),
        P(None, "dp", "mp"),
        P(None, "dp", "mp"),
        P(None, "dp", "mp"),
        P(None, "dp", "mp"),
        P(None, "dp"),
        P(None, "dp"),
        P(None, "dp"),
        P(),
        P(),
        P(),
    )
    return jax.shard_map(
        per_device,
        mesh=mesh,
        in_specs=placed,
        out_specs=(
            P("dp", "mp", None),
            P("dp", "mp", None),
            P(None, "dp", "mp"),
            P(None, "dp", "mp"),
            P(None, "dp"),
            P(),
            P(),
            P(None, "dp", "mp"),
            P(None, "dp", "mp"),
            P(None, "dp", "mp"),
            P(None, "dp", "mp"),
            P(None, "dp", "mp"),
            P(None, "dp", "mp"),
            P(None, "dp"),
            P(None, "dp"),
            P(None, "dp"),
            P(),
            P(),
            P(),
        ),
        check_vma=False,
    )
```

profile of v0, /device:TPU:0, one launch (start us, length us, event | category | flops | bytes accessed | tf_op | source)
XLA Modules:
  0.0 457.2 jit_solution(1031695378623328787)
XLA Ops:
  2.0 3.1 collective-permute-start.2
  5.1 5.9 %collective-permute-done.2 = bf16[96,768]{1,0:T(8,128)(2,1)S(1)} collective-permute-done((bf16[96,768]{1,0:T(8,128)(2,1)S(1)}, bf16[96,768]{1,0:T(8,128)(2,1)S(1)}, u32[]{:S(2)}, u32[]{:S(2)}) %collective-permute-start.2) | collective-permute-done | bytes 147488 | tf_op jit(solution)/shard_map/ppermute | solution.py:88
  11.0 6.9 %collective-permute-done.3 = bf16[96,768]{1,0:T(8,128)(2,1)S(1)} collective-permute-done((bf16[96,768]{1,0:T(8,128)(2,1)S(1)}, bf16[96,768]{1,0:T(8,128)(2,1)S(1)}, u32[]{:S(2)}, u32[]{:S(2)}) %collective-permute-start.3) | collective-permute-done | bytes 147488 | tf_op jit(solution)/shard_map/ppermute | solution.py:88
  18.1 6.7 %collective-permute-done.4 = bf16[96,768]{1,0:T(8,128)(2,1)S(1)} collective-permute-done((bf16[96,768]{1,0:T(8,128)(2,1)S(1)}, bf16[96,768]{1,0:T(8,128)(2,1)S(1)}, u32[]{:S(2)}, u32[]{:S(2)}) %collective-permute-start.4) | collective-permute-done | bytes 147488 | tf_op jit(solution)/shard_map/ppermute | solution.py:88
  28.3 7.4 %collective-permute-done.16 = bf16[96,768]{1,0:T(8,128)(2,1)S(1)} collective-permute-done((bf16[96,768]{1,0:T(8,128)(2,1)S(1)}, bf16[96,768]{1,0:T(8,128)(2,1)S(1)}, u32[]{:S(2)}, u32[]{:S(2)}) %collective-permute-start.16) | collective-permute-done | bytes 147488 | tf_op jit(solution)/shard_map/ppermute | solution.py:88
  38.5 4.5 collective-permute-done.17
  43.5 2.5 collective-permute-done.23
  46.0 5.7 %collective-permute-done.18 = bf16[96,768]{1,0:T(8,128)(2,1)} collective-permute-done((bf16[96,768]{1,0:T(8,128)(2,1)}, bf16[96,768]{1,0:T(8,128)(2,1)}, u32[]{:S(2)}, u32[]{:S(2)}) %collective-permute-start.18) | collective-permute-done | bytes 147488 | tf_op jit(solution)/shard_map/ppermute | solution.py:88
  54.3 1.9 pad_maximum_fusion.5.refs_0_
  56.4 2.1 pad_maximum_fusion.6.refs_4_
  58.4 6.8 %collective-permute-done = bf16[256,768]{1,0:T(8,128)(2,1)S(1)} collective-permute-done((bf16[256,768]{1,0:T(8,128)(2,1)S(1)}, bf16[256,768]{1,0:T(8,128)(2,1)S(1)}, u32[]{:S(2)}, u32[]{:S(2)}) %collective-permute-start) | collective-permute-done | bytes 393248 | tf_op jit(solution)/shard_map/ppermute | solution.py:78
  70.9 32.0 %all-gather = bf16[8,96,2]{1,2,0:T(2,128)(2,1)S(1)} all-gather(bf16[1,96,2]{1,2,0:T(2,128)(2,1)S(1)} %convert_bitcast_fusion.1), channel_id=1, replica_groups=mesh['dp'=8,'mp'=4] {'dp'}, dimensions={0}, use_global_device_ids=true | all-gather | bytes 3456 | tf_op jit(solution)/shard_map/all_gather | solution.py:768
  105.7 6.5 %project.2 = (bf16[2,512,192]{2,1,0:T(8,128)(2,1)S(1)}, bf16[2,512,192]{2,1,0:T(8,128)(2,1)S(1)}, bf16[2,512,192]{2,1,0:T(8,128)(2,1)S(1)}) custom-call(s32[12]{0:T(128)S(1)} %stack.114.place_ref, bf16[512,768]{1,0:T(8,128)(2,1)S(1)} %pad_maximum_fusion.x_ref, bf16[2,768]{1,0:T(2,128)(2,1)S(1)} %bitcast.115, ...), custom_call_target="tpu_custom_call" | custom-call | flops 905969664 | bytes 5000000 | tf_op jit(solution)/shard_map/project/pallas_call | solution.py:254
  112.3 4.6 project.3
  118.0 5.2 %bias_tiles.1.bias_ref = f32[4,3,5,128,128]{4,3,2,1,0:T(8,128)S(1)} custom-call(s32[12]{0:T(128)S(1)} %stack.114.place_ref, f32[12,32]{1,0:T(8,128)S(1)} %copy-done.62), custom_call_target="tpu_custom_call" | custom-call | flops 10000000 | bytes 4000000 | tf_op jit(solution)/shard_map/bias_tiles/pallas_call | solution.py:206
  129.5 7.7 %attend.3 = (bf16[2,512,192]{2,1,0:T(8,128)(2,1)S(1)}, bf16[2,3,512,1024]{3,2,1,0:T(8,128)(2,1)S(1)}) custom-call(s32[12]{0:T(128)S(1)} %stack.114.place_ref, bf16[2,512,192]{2,1,0:T(8,128)(2,1)S(1)} %get-tuple-element.89.q_ref, bf16[2,512,192]{2,1,0:T(8,128)(2,1)S(1)} %get-tuple-element.86.ko_ref, bf16[2,512,192]{2,1,0:T(8,128)(2,1)S(1)} %get-tuple-element.87.vo_ref, ...), custom_call_target="tpu_custom_call" | custom-call | flops 3221225472 | bytes 10000000 | tf_op jit(solution)/shard_map/attend/pallas_call | solution.py:315
  137.3 2.6 copy-done.112
  139.9 7.8 %attend.2 = (bf16[2,512,192]{2,1,0:T(8,128)(2,1)S(1)}, bf16[2,3,512,1024]{3,2,1,0:T(8,128)(2,1)S(1)}) custom-call(s32[12]{0:T(128)S(1)} %stack.114.place_ref, bf16[2,512,192]{2,1,0:T(8,128)(2,1)S(1)} %get-tuple-element.83.q_ref, bf16[2,512,192]{2,1,0:T(8,128)(2,1)S(1)} %get-tuple-element.84.ko_ref, bf16[2,512,192]{2,1,0:T(8,128)(2,1)S(1)} %get-tuple-element.85.vo_ref, ...), custom_call_target="tpu_custom_call" | custom-call | flops 3221225472 | bytes 10000000 | tf_op jit(solution)/shard_map/attend/pallas_call | solution.py:315
  147.7 3.7 middle.1
  156.9 22.8 %feed.2 = (f32[512,768]{1,0:T(8,128)}, f32[512,768]{1,0:T(8,128)}, bf16[4,96,768]{2,1,0:T(8,128)(2,1)S(1)}, bf16[4,96,768]{2,1,0:T(8,128)(2,1)S(1)}, bf16[4,96,7...) custom-call(s32[12]{0:T(128)S(1)} %stack.114.place_ref, ...), custom_call_target="tpu_custom_call" | custom-call | flops 7247757312 | bytes 15000000 | tf_op jit(solution)/shard_map/feed/pallas_call | solution.py:444
  188.3 25.0 %feed.3 = (f32[512,768]{1,0:T(8,128)}, f32[512,768]{1,0:T(8,128)}, bf16[4,96,768]{2,1,0:T(8,128)(2,1)S(1)}, bf16[4,96,768]{2,1,0:T(8,128)(2,1)S(1)}, bf16[4,96,7...) custom-call(s32[12]{0:T(128)S(1)} %stack.114.place_ref, ...), custom_call_target="tpu_custom_call" | custom-call | flops 7247757312 | bytes 15000000 | tf_op jit(solution)/shard_map/feed/pallas_call | solution.py:444
  220.0 6.0 %turn.1 = (bf16[512,768]{1,0:T(8,128)(2,1)S(1)}, f32[512,768]{1,0:T(8,128)S(1)}, bf16[512,768]{1,0:T(8,128)(2,1)}, bf16[768,512]{1,0:T(8,128)(2,1)S(1)}, f32[1,7...) custom-call(s32[12]{0:T(128)S(1)} %stack.114.place_ref, ...), custom_call_target="tpu_custom_call" | custom-call | flops 603979776 | bytes 10000000 | tf_op jit(solution)/shard_map/turn/pallas_call | solution.py:509
  228.9 10.9 %attend_back.3 = (bf16[2,512,192]{2,1,0:T(8,128)(2,1)S(1)}, f32[2,512,192]{2,1,0:T(8,128)S(1)}, f32[2,512,192]{2,1,0:T(8,128)S(1)}, bf16[2,512,192]{2,1,0:T(8,12...) custom-call(s32[12]{0:T(128)S(1)} %stack.114.place_ref, bf16[2,512,192]{2,1,0:T(8,128)(2,1)S(1)} %copy-done.111, ...), custom_call_target="tpu_custom_call" | custom-call | flops 6442450944 | bytes 12000000 | tf_op jit(solution)/shard_map/attend_back/pallas_call | solution.py:589
  242.3 9.9 %attend_back.2 = (bf16[2,512,192]{2,1,0:T(8,128)(2,1)S(1)}, f32[2,512,192]{2,1,0:T(8,128)S(1)}, f32[2,512,192]{2,1,0:T(8,128)S(1)}, bf16[2,512,192]{2,1,0:T(8,12...) custom-call(s32[12]{0:T(128)S(1)} %stack.114.place_ref, bf16[2,512,192]{2,1,0:T(8,128)(2,1)S(1)} %copy-done.109, ...), custom_call_target="tpu_custom_call" | custom-call | flops 6442450944 | bytes 12000000 | tf_op jit(solution)/shard_map/attend_back/pallas_call | solution.py:589
  253.2 3.2 bucket_sums.2
  256.4 3.2 bucket_sums.3
  260.5 2.0 gather_fusion
  274.3 12.0 %project_back.2 = (f32[512,768]{1,0:T(8,128)S(1)}, bf16[4,96,768]{2,1,0:T(8,128)(2,1)S(1)}, bf16[4,96,768]{2,1,0:T(8,128)(2,1)S(1)}, bf16[4,96,768]{2,1,0:T(8,128)(2,1)S(1)}, bf16[4,96,768]{2,1,0:T(8,128)(2,1)S(1)}) custom-call(s32[12]{0:T(128)S(1)} %stack.114.place_ref, bf16[512,768]{1,0:T(8,128)(2,1)S(1)} %pad_maximum_fusion.x_ref, ...), custom_call_target="tpu_custom_call" | custom-call | flops 2415919104 | bytes 10000000 | tf_op jit(solution)/shard_map/project_back/pallas_call | solution.py:691
  289.7 13.1 %project_back.3 = (f32[512,768]{1,0:T(8,128)S(1)}, bf16[4,96,768]{2,1,0:T(8,128)(2,1)S(1)}, bf16[4,96,768]{2,1,0:T(8,128)(2,1)S(1)}, bf16[4,96,768]{2,1,0:T(8,128)(2,1)S(1)}, bf16[4,96,768]{2,1,0:T(8,128)(2,1)S(1)}) custom-call(s32[12]{0:T(128)S(1)} %stack.114.place_ref, bf16[512,768]{1,0:T(8,128)(2,1)S(1)} %pad_maximum_fusion.x_ref, ...), custom_call_target="tpu_custom_call" | custom-call | flops 2415919104 | bytes 10000000 | tf_op jit(solution)/shard_map/project_back/pallas_call | solution.py:691
  309.5 3.1 collective-permute-done.75
  314.4 2.3 collective-permute-start.76
  333.3 9.3 %collective-permute-done.67 = bf16[4,96,768]{2,1,0:T(8,128)(2,1)S(1)} collective-permute-done((bf16[4,96,768]{2,1,0:T(8,128)(2,1)S(1)}, bf16[4,96,768]{2,1,0:T(8,128)(2,1)S(1)}, u32[]{:S(2)}, u32[]{:S(2)}) %collective-permute-start.67) | collective-permute-done | bytes 589856 | tf_op jit(solution)/shard_map/ppermute | solution.py:83
  349.4 9.5 %collective-permute-done.47 = bf16[4,96,768]{2,1,0:T(8,128)(2,1)S(1)} collective-permute-done((bf16[4,96,768]{2,1,0:T(8,128)(2,1)S(1)}, bf16[4,96,768]{2,1,0:T(8,128)(2,1)S(1)}, u32[]{:S(2)}, u32[]{:S(2)}) %collective-permute-start.47) | collective-permute-done | bytes 589856 | tf_op jit(solution)/shard_map/ppermute | solution.py:83
  359.6 11.9 %collective-permute-done.64 = bf16[4,96,768]{2,1,0:T(8,128)(2,1)S(1)} collective-permute-done((bf16[4,96,768]{2,1,0:T(8,128)(2,1)S(1)}, bf16[4,96,768]{2,1,0:T(8,128)(2,1)S(1)}, u32[]{:S(2)}, u32[]{:S(2)}) %collective-permute-start.64) | collective-permute-done | bytes 589856 | tf_op jit(solution)/shard_map/ppermute | solution.py:83
  375.9 8.3 %collective-permute-done.58 = bf16[4,96,768]{2,1,0:T(8,128)(2,1)S(1)} collective-permute-done((bf16[4,96,768]{2,1,0:T(8,128)(2,1)S(1)}, bf16[4,96,768]{2,1,0:T(8,128)(2,1)S(1)}, u32[]{:S(2)}, u32[]{:S(2)}) %collective-permute-start.58) | collective-permute-done | bytes 589856 | tf_op jit(solution)/shard_map/ppermute | solution.py:83
  385.6 4.6 %collective-permute-done.69 = bf16[96,768]{1,0:T(8,128)(2,1)S(1)} collective-permute-done((bf16[96,768]{1,0:T(8,128)(2,1)S(1)}, bf16[96,768]{1,0:T(8,128)(2,1)S(1)}, u32[]{:S(2)}, u32[]{:S(2)}) %collective-permute-start.69) | collective-permute-done | bytes 147488 | tf_op jit(solution)/shard_map/ppermute | solution.py:88
  390.2 2.0 collective-permute-start.59
  392.2 4.7 %collective-permute-done.59 = bf16[96,768]{1,0:T(8,128)(2,1)S(1)} collective-permute-done((bf16[96,768]{1,0:T(8,128)(2,1)S(1)}, bf16[96,768]{1,0:T(8,128)(2,1)S(1)}, u32[]{:S(2)}, u32[]{:S(2)}) %collective-permute-start.59) | collective-permute-done | bytes 147488 | tf_op jit(solution)/shard_map/ppermute | solution.py:88
  396.9 2.6 collective-permute-start.70
  399.5 3.7 collective-permute-done.70
  404.9 4.3 collective-permute-start.60
  409.8 2.9 collective-permute-done.60
  412.7 4.3 collective-permute-start.61
  417.1 3.9 collective-permute-start.50
  421.1 2.6 collective-permute-done.50
  423.8 4.3 collective-permute-start.51
  438.5 2.1 collective-permute-done.82
  441.7 3.3 collective-permute-start.85
  (498 shorter events, 129.4 us)
Async XLA Ops:
  25.0 12.3 %collective-permute-start.6 = (bf16[4,96,768]{2,1,0:T(8,128)(2,1)S(1)}, bf16[4,96,768]{2,1,0:T(8,128)(2,1)S(1)}, u32[]{:S(2)}, u32[]{:S(2)}) collective-permute-start(bf16[4,96,768]{2,1,0:T(8,128)(2,1)S(1)} %pad_maximum_fusion.4.refs_0_.refs_4_), channel_id=1, source_target_pairs={{0,2},{1,3},{2,0},{3,1},{4,6},{5,7},{6,4},{7,5},{8,10},{9,11},{10,... | collective-permute-start | bytes 1769480 | tf_op jit(solution)/shard_map/ppermute | solution.py:78
  26.6 16.4 %collective-permute-start.5 = (bf16[4,96,768]{2,1,0:T(8,128)(2,1)S(1)}, bf16[4,96,768]{2,1,0:T(8,128)(2,1)S(1)}, u32[]{:S(2)}, u32[]{:S(2)}) collective-permute-start(bf16[4,96,768]{2,1,0:T(8,128)(2,1)S(1)} %pad_maximum_fusion.4.refs_0_.refs_4_), channel_id=1, source_target_pairs={{0,4},{4,0},{8,12},{12,8},{16,20},{20,16},{24,28},{28,24},{1,5},{5... | collective-permute-start | bytes 1769480 | tf_op jit(solution)/shard_map/ppermute | solution.py:83
  37.2 19.0 %collective-permute-start.7 = (bf16[4,96,768]{2,1,0:T(8,128)(2,1)S(1)}, bf16[4,96,768]{2,1,0:T(8,128)(2,1)S(1)}, u32[]{:S(2)}, u32[]{:S(2)}) collective-permute-start(bf16[4,96,768]{2,1,0:T(8,128)(2,1)S(1)} %collective-permute-done.6.refs_2_.refs_4_.refs_6_), channel_id=1, source_target_pairs={{0,4},{4,0},{8,12},{12,8},{16,20},{20,16},{24,28},{28,24},{1,5},{5... | collective-permute-start | bytes 1769480 | tf_op jit(solution)/shard_map/ppermute | solution.py:83
  43.0 22.7 %collective-permute-start.8 = (bf16[4,96,768]{2,1,0:T(8,128)(2,1)S(1)}, bf16[4,96,768]{2,1,0:T(8,128)(2,1)S(1)}, u32[]{:S(2)}, u32[]{:S(2)}) collective-permute-start(bf16[4,96,768]{2,1,0:T(8,128)(2,1)S(1)} %pad_maximum_fusion.4.refs_0_.refs_4_), channel_id=1, source_target_pairs={{0,1},{1,0},{2,3},{3,2},{4,5},{5,4},{6,7},{7,6},{8,9},{9,8},{10,11... | collective-permute-start | bytes 1769480 | tf_op jit(solution)/shard_map/ppermute | solution.py:74
  43.0 23.0 %collective-permute-start.9 = (bf16[4,96,768]{2,1,0:T(8,128)(2,1)S(1)}, bf16[4,96,768]{2,1,0:T(8,128)(2,1)}, u32[]{:S(2)}, u32[]{:S(2)}) collective-permute-start(bf16[4,96,768]{2,1,0:T(8,128)(2,1)S(1)} %collective-permute-done.5.refs_1_.refs_5_), channel_id=1, source_target_pairs={{0,1},{1,0},{2,3},{3,2},{4,5},{5,4},{6,7},{7,6},{8,9},{9,8},{10,11... | collective-permute-start | bytes 1769480 | tf_op jit(solution)/shard_map/ppermute | solution.py:74
  51.7 16.8 %collective-permute-start.10 = (bf16[4,96,768]{2,1,0:T(8,128)(2,1)S(1)}, bf16[4,96,768]{2,1,0:T(8,128)(2,1)S(1)}, u32[]{:S(2)}, u32[]{:S(2)}) collective-permute-start(bf16[4,96,768]{2,1,0:T(8,128)(2,1)S(1)} %collective-permute-done.6.refs_2_.refs_4_.refs_6_), channel_id=1, source_target_pairs={{0,1},{1,0},{2,3},{3,2},{4,5},{5,4},{6,7},{7,6},{8,9},{9,8},{10,11... | collective-permute-start | bytes 1769480 | tf_op jit(solution)/shard_map/ppermute | solution.py:74
  53.6 11.5 %collective-permute-start = (bf16[256,768]{1,0:T(8,128)(2,1)S(1)}, bf16[256,768]{1,0:T(8,128)(2,1)S(1)}, u32[]{:S(2)}, u32[]{:S(2)}) collective-permute-start(bf16[256,768]{1,0:T(8,128)(2,1)S(1)} %get-tuple-element.173), channel_id=1, source_target_pairs={{0,2},{1,3},{2,0},{3,1},{4,6},{5,7},{6,4},{7,5},{8,10},{9,11},{10,... | collective-permute-start | bytes 1179656 | tf_op jit(solution)/shard_map/ppermute | solution.py:78
  56.3 49.2 %collective-permute-start.11 = (bf16[4,96,768]{2,1,0:T(8,128)(2,1)S(1)}, bf16[4,96,768]{2,1,0:T(8,128)(2,1)}, u32[]{:S(2)}, u32[]{:S(2)}) collective-permute-start(bf16[4,96,768]{2,1,0:T(8,128)(2,1)S(1)} %collective-permute-done.7.refs_3_.refs_5_.refs_7_), channel_id=1, source_target_pairs={{0,1},{1,0},{2,3},{3,2},{4,5},{5,4},{6,7},{7,6},{8,9},{9,8},{10,11... | collective-permute-start | bytes 1769480 | tf_op jit(solution)/shard_map/ppermute | solution.py:74
  65.2 51.8 %collective-permute-start.19 = (bf16[4,96,768]{2,1,0:T(8,128)(2,1)}, bf16[4,96,768]{2,1,0:T(8,128)(2,1)}, u32[]{:S(2)}, u32[]{:S(2)}) collective-permute-start(bf16[4,96,768]{2,1,0:T(8,128)(2,1)} %pad_maximum_fusion.5.refs_0_), channel_id=1, source_target_pairs={{0,4},{4,0},{8,12},{12,8},{16,20},{20,16},{24,28},{28,24},{1,5},{5... | collective-permute-start | bytes 1769480 | tf_op jit(solution)/shard_map/ppermute | solution.py:83
  65.7 51.8 %collective-permute-start.20 = (bf16[4,96,768]{2,1,0:T(8,128)(2,1)}, bf16[4,96,768]{2,1,0:T(8,128)(2,1)}, u32[]{:S(2)}, u32[]{:S(2)}) collective-permute-start(bf16[4,96,768]{2,1,0:T(8,128)(2,1)} %pad_maximum_fusion.5.refs_0_), channel_id=1, source_target_pairs={{0,2},{1,3},{2,0},{3,1},{4,6},{5,7},{6,4},{7,5},{8,10},{9,11},{10,... | collective-permute-start | bytes 1769480 | tf_op jit(solution)/shard_map/ppermute | solution.py:78
  66.0 51.6 %collective-permute-start.25 = (bf16[4,96,768]{2,1,0:T(8,128)(2,1)}, bf16[4,96,768]{2,1,0:T(8,128)(2,1)}, u32[]{:S(2)}, u32[]{:S(2)}) collective-permute-start(bf16[4,96,768]{2,1,0:T(8,128)(2,1)} %pad_maximum_fusion.6.refs_4_), channel_id=1, source_target_pairs={{0,4},{4,0},{8,12},{12,8},{16,20},{20,16},{24,28},{28,24},{1,5},{5... | collective-permute-start | bytes 1769480 | tf_op jit(solution)/shard_map/ppermute | solution.py:83
  69.4 47.5 %collective-permute-start.1 = (bf16[256,768]{1,0:T(8,128)(2,1)}, bf16[256,768]{1,0:T(8,128)(2,1)}, u32[]{:S(2)}, u32[]{:S(2)}) collective-permute-start(bf16[256,768]{1,0:T(8,128)(2,1)} %get-tuple-element.171), channel_id=1, source_target_pairs={{0,2},{1,3},{2,0},{3,1},{4,6},{5,7},{6,4},{7,5},{8,10},{9,11},{10,... | collective-permute-start | bytes 1179656 | tf_op jit(solution)/shard_map/ppermute | solution.py:78
  105.5 19.9 %collective-permute-start.26 = (bf16[4,96,768]{2,1,0:T(8,128)(2,1)}, bf16[4,96,768]{2,1,0:T(8,128)(2,1)}, u32[]{:S(2)}, u32[]{:S(2)}) collective-permute-start(bf16[4,96,768]{2,1,0:T(8,128)(2,1)} %pad_maximum_fusion.6.refs_4_), channel_id=1, source_target_pairs={{0,2},{1,3},{2,0},{3,1},{4,6},{5,7},{6,4},{7,5},{8,10},{9,11},{10,... | collective-permute-start | bytes 1769480 | tf_op jit(solution)/shard_map/ppermute | solution.py:78
  125.4 26.9 %collective-permute-start.28 = (bf16[4,96,768]{2,1,0:T(8,128)(2,1)}, bf16[4,96,768]{2,1,0:T(8,128)(2,1)S(1)}, u32[]{:S(2)}, u32[]{:S(2)}) collective-permute-start(bf16[4,96,768]{2,1,0:T(8,128)(2,1)} %pad_maximum_fusion.5.refs_0_), channel_id=1, source_target_pairs={{0,1},{1,0},{2,3},{3,2},{4,5},{5,4},{6,7},{7,6},{8,9},{9,8},{10,11... | collective-permute-start | bytes 1769480 | tf_op jit(solution)/shard_map/ppermute | solution.py:74
  125.6 28.3 %collective-permute-start.32 = (bf16[4,96,768]{2,1,0:T(8,128)(2,1)}, bf16[4,96,768]{2,1,0:T(8,128)(2,1)}, u32[]{:S(2)}, u32[]{:S(2)}) collective-permute-start(bf16[4,96,768]{2,1,0:T(8,128)(2,1)} %pad_maximum_fusion.6.refs_4_), channel_id=1, source_target_pairs={{0,1},{1,0},{2,3},{3,2},{4,5},{5,4},{6,7},{7,6},{8,9},{9,8},{10,11... | collective-permute-start | bytes 1769480 | tf_op jit(solution)/shard_map/ppermute | solution.py:74
  126.0 28.2 %collective-permute-start.21 = (bf16[4,96,768]{2,1,0:T(8,128)(2,1)}, bf16[4,96,768]{2,1,0:T(8,128)(2,1)}, u32[]{:S(2)}, u32[]{:S(2)}) collective-permute-start(bf16[4,96,768]{2,1,0:T(8,128)(2,1)} %collective-permute-done.19.refs_1_), channel_id=1, source_target_pairs={{0,2},{1,3},{2,0},{3,1},{4,6},{5,7},{6,4},{7,5},{8,10},{9,11},{10,... | collective-permute-start | bytes 1769480 | tf_op jit(solution)/shard_map/ppermute | solution.py:78
  127.9 26.8 %collective-permute-start.29 = (bf16[4,96,768]{2,1,0:T(8,128)(2,1)}, bf16[4,96,768]{2,1,0:T(8,128)(2,1)S(1)}, u32[]{:S(2)}, u32[]{:S(2)}) collective-permute-start(bf16[4,96,768]{2,1,0:T(8,128)(2,1)} %collective-permute-done.19.refs_1_), channel_id=1, source_target_pairs={{0,1},{1,0},{2,3},{3,2},{4,5},{5,4},{6,7},{7,6},{8,9},{9,8},{10,11... | collective-permute-start | bytes 1769480 | tf_op jit(solution)/shard_map/ppermute | solution.py:74
  127.9 26.4 %collective-permute-start.27 = (bf16[4,96,768]{2,1,0:T(8,128)(2,1)}, bf16[4,96,768]{2,1,0:T(8,128)(2,1)}, u32[]{:S(2)}, u32[]{:S(2)}) collective-permute-start(bf16[4,96,768]{2,1,0:T(8,128)(2,1)} %collective-permute-done.26.refs_6_), channel_id=1, source_target_pairs={{0,4},{4,0},{8,12},{12,8},{16,20},{20,16},{24,28},{28,24},{1,5},{5... | collective-permute-start | bytes 1769480 | tf_op jit(solution)/shard_map/ppermute | solution.py:83
  153.7 32.7 %collective-permute-start.34 = (bf16[4,96,768]{2,1,0:T(8,128)(2,1)}, bf16[4,96,768]{2,1,0:T(8,128)(2,1)S(1)}, u32[]{:S(2)}, u32[]{:S(2)}) collective-permute-start(bf16[4,96,768]{2,1,0:T(8,128)(2,1)} %collective-permute-done.26.refs_6_), channel_id=1, source_target_pairs={{0,1},{1,0},{2,3},{3,2},{4,5},{5,4},{6,7},{7,6},{8,9},{9,8},{10,11... | collective-permute-start | bytes 1769480 | tf_op jit(solution)/shard_map/ppermute | solution.py:74
  153.9 32.6 %collective-permute-start.30 = (bf16[4,96,768]{2,1,0:T(8,128)(2,1)}, bf16[4,96,768]{2,1,0:T(8,128)(2,1)}, u32[]{:S(2)}, u32[]{:S(2)}) collective-permute-start(bf16[4,96,768]{2,1,0:T(8,128)(2,1)} %collective-permute-done.20.refs_2_), channel_id=1, source_target_pairs={{0,1},{1,0},{2,3},{3,2},{4,5},{5,4},{6,7},{7,6},{8,9},{9,8},{10,11... | collective-permute-start | bytes 1769480 | tf_op jit(solution)/shard_map/ppermute | solution.py:74
  154.2 32.2 %collective-permute-start.33 = (bf16[4,96,768]{2,1,0:T(8,128)(2,1)}, bf16[4,96,768]{2,1,0:T(8,128)(2,1)}, u32[]{:S(2)}, u32[]{:S(2)}) collective-permute-start(bf16[4,96,768]{2,1,0:T(8,128)(2,1)} %collective-permute-done.25.refs_5_), channel_id=1, source_target_pairs={{0,1},{1,0},{2,3},{3,2},{4,5},{5,4},{6,7},{7,6},{8,9},{9,8},{10,11... | collective-permute-start | bytes 1769480 | tf_op jit(solution)/shard_map/ppermute | solution.py:74
  154.4 32.1 %collective-permute-start.31 = (bf16[4,96,768]{2,1,0:T(8,128)(2,1)}, bf16[4,96,768]{2,1,0:T(8,128)(2,1)}, u32[]{:S(2)}, u32[]{:S(2)}) collective-permute-start(bf16[4,96,768]{2,1,0:T(8,128)(2,1)} %collective-permute-done.21.refs_3_), channel_id=1, source_target_pairs={{0,1},{1,0},{2,3},{3,2},{4,5},{5,4},{6,7},{7,6},{8,9},{9,8},{10,11... | collective-permute-start | bytes 1769480 | tf_op jit(solution)/shard_map/ppermute | solution.py:74
  155.5 30.9 %collective-permute-start.35 = (bf16[4,96,768]{2,1,0:T(8,128)(2,1)}, bf16[4,96,768]{2,1,0:T(8,128)(2,1)}, u32[]{:S(2)}, u32[]{:S(2)}) collective-permute-start(bf16[4,96,768]{2,1,0:T(8,128)(2,1)} %collective-permute-done.27.refs_7_), channel_id=1, source_target_pairs={{0,1},{1,0},{2,3},{3,2},{4,5},{5,4},{6,7},{7,6},{8,9},{9,8},{10,11... | collective-permute-start | bytes 1769480 | tf_op jit(solution)/shard_map/ppermute | solution.py:74
  241.8 24.7 %collective-permute-start.37 = (bf16[2,512,192]{2,1,0:T(8,128)(2,1)}, bf16[2,512,192]{2,1,0:T(8,128)(2,1)}, u32[]{:S(2)}, u32[]{:S(2)}) collective-permute-start(bf16[2,512,192]{2,1,0:T(8,128)(2,1)} %get-tuple-element.107), channel_id=1, source_target_pairs={{0,1},{1,0},{2,3},{3,2},{4,5},{5,4},{6,7},{7,6},{8,9},{9,8},{10,11... | collective-permute-start | bytes 1179656 | tf_op jit(solution)/shard_map/ppermute | solution.py:74
  242.1 24.3 %collective-permute-start.38 = (bf16[2,512,192]{2,1,0:T(8,128)(2,1)}, bf16[2,512,192]{2,1,0:T(8,128)(2,1)}, u32[]{:S(2)}, u32[]{:S(2)}) collective-permute-start(bf16[2,512,192]{2,1,0:T(8,128)(2,1)} %get-tuple-element.109), channel_id=1, source_target_pairs={{0,1},{1,0},{2,3},{3,2},{4,5},{5,4},{6,7},{7,6},{8,9},{9,8},{10,11... | collective-permute-start | bytes 1179656 | tf_op jit(solution)/shard_map/ppermute | solution.py:74
  252.2 37.4 %collective-permute-start.39 = (bf16[2,512,192]{2,1,0:T(8,128)(2,1)}, bf16[2,512,192]{2,1,0:T(8,128)(2,1)}, u32[]{:S(2)}, u32[]{:S(2)}) collective-permute-start(bf16[2,512,192]{2,1,0:T(8,128)(2,1)} %get-tuple-element.113), channel_id=1, source_target_pairs={{0,1},{1,0},{2,3},{3,2},{4,5},{5,4},{6,7},{7,6},{8,9},{9,8},{10,11... | collective-permute-start | bytes 1179656 | tf_op jit(solution)/shard_map/ppermute | solution.py:74
  252.7 37.0 %collective-permute-start.40 = (bf16[2,512,192]{2,1,0:T(8,128)(2,1)}, bf16[2,512,192]{2,1,0:T(8,128)(2,1)}, u32[]{:S(2)}, u32[]{:S(2)}) collective-permute-start(bf16[2,512,192]{2,1,0:T(8,128)(2,1)} %get-tuple-element.115), channel_id=1, source_target_pairs={{0,1},{1,0},{2,3},{3,2},{4,5},{5,4},{6,7},{7,6},{8,9},{9,8},{10,11... | collective-permute-start | bytes 1179656 | tf_op jit(solution)/shard_map/ppermute | solution.py:74
  252.8 72.1 %collective-permute-start.66 = (bf16[4,96,768]{2,1,0:T(8,128)(2,1)}, bf16[4,96,768]{2,1,0:T(8,128)(2,1)}, u32[]{:S(2)}, u32[]{:S(2)}) collective-permute-start(bf16[4,96,768]{2,1,0:T(8,128)(2,1)} %get-tuple-element.142), channel_id=1, source_target_pairs={{0,1},{1,0},{2,3},{3,2},{4,5},{5,4},{6,7},{7,6},{8,9},{9,8},{10,11... | collective-permute-start | bytes 1769480 | tf_op jit(solution)/shard_map/ppermute | solution.py:74
  307.4 19.2 %collective-permute-start.63 = (bf16[4,96,768]{2,1,0:T(8,128)(2,1)}, bf16[4,96,768]{2,1,0:T(8,128)(2,1)S(1)}, u32[]{:S(2)}, u32[]{:S(2)}) collective-permute-start(bf16[4,96,768]{2,1,0:T(8,128)(2,1)} %copy-done.80), channel_id=1, source_target_pairs={{0,1},{1,0},{2,3},{3,2},{4,5},{5,4},{6,7},{7,6},{8,9},{9,8},{10,11... | collective-permute-start | bytes 1769480 | tf_op jit(solution)/shard_map/ppermute | solution.py:74
  320.4 11.5 %collective-permute-start.65 = (bf16[4,96,768]{2,1,0:T(8,128)(2,1)S(1)}, bf16[4,96,768]{2,1,0:T(8,128)(2,1)}, u32[]{:S(2)}, u32[]{:S(2)}) collective-permute-start(bf16[4,96,768]{2,1,0:T(8,128)(2,1)S(1)} %copy-done.76), channel_id=1, source_target_pairs={{0,1},{1,0},{2,3},{3,2},{4,5},{5,4},{6,7},{7,6},{8,9},{9,8},{10,11... | collective-permute-start | bytes 1769480 | tf_op jit(solution)/shard_map/ppermute | solution.py:74
  326.9 15.7 %collective-permute-start.67 = (bf16[4,96,768]{2,1,0:T(8,128)(2,1)S(1)}, bf16[4,96,768]{2,1,0:T(8,128)(2,1)S(1)}, u32[]{:S(2)}, u32[]{:S(2)}) collective-permute-start(bf16[4,96,768]{2,1,0:T(8,128)(2,1)S(1)} %add_convert_fusion.2), channel_id=1, source_target_pairs={{0,4},{4,0},{8,12},{12,8},{16,20},{20,16},{24,28},{28,24},{1,5},{5... | collective-permute-start | bytes 1769480 | tf_op jit(solution)/shard_map/ppermute | solution.py:83
  328.8 15.7 %collective-permute-start.43 = (bf16[4,96,768]{2,1,0:T(8,128)(2,1)S(1)}, bf16[4,96,768]{2,1,0:T(8,128)(2,1)S(1)}, u32[]{:S(2)}, u32[]{:S(2)}) collective-permute-start(bf16[4,96,768]{2,1,0:T(8,128)(2,1)S(1)} %copy-done.84), channel_id=1, source_target_pairs={{0,1},{1,0},{2,3},{3,2},{4,5},{5,4},{6,7},{7,6},{8,9},{9,8},{10,11... | collective-permute-start | bytes 1769480 | tf_op jit(solution)/shard_map/ppermute | solution.py:74
  329.0 17.1 %collective-permute-start.57 = (bf16[4,96,768]{2,1,0:T(8,128)(2,1)S(1)}, bf16[4,96,768]{2,1,0:T(8,128)(2,1)S(1)}, u32[]{:S(2)}, u32[]{:S(2)}) collective-permute-start(bf16[4,96,768]{2,1,0:T(8,128)(2,1)S(1)} %add_convert_fusion.9), channel_id=1, source_target_pairs={{0,2},{1,3},{2,0},{3,1},{4,6},{5,7},{6,4},{7,5},{8,10},{9,11},{10,... | collective-permute-start | bytes 1769480 | tf_op jit(solution)/shard_map/ppermute | solution.py:78
  332.8 15.2 %collective-permute-start.62 = (bf16[4,96,768]{2,1,0:T(8,128)(2,1)S(1)}, bf16[4,96,768]{2,1,0:T(8,128)(2,1)S(1)}, u32[]{:S(2)}, u32[]{:S(2)}) collective-permute-start(bf16[4,96,768]{2,1,0:T(8,128)(2,1)S(1)} %copy-done.70), channel_id=1, source_target_pairs={{0,1},{1,0},{2,3},{3,2},{4,5},{5,4},{6,7},{7,6},{8,9},{9,8},{10,11... | collective-permute-start | bytes 1769480 | tf_op jit(solution)/shard_map/ppermute | solution.py:74
  333.0 15.9 %collective-permute-start.45 = (bf16[4,96,768]{2,1,0:T(8,128)(2,1)S(1)}, bf16[4,96,768]{2,1,0:T(8,128)(2,1)S(1)}, u32[]{:S(2)}, u32[]{:S(2)}) collective-permute-start(bf16[4,96,768]{2,1,0:T(8,128)(2,1)S(1)} %copy-done.82), channel_id=1, source_target_pairs={{0,1},{1,0},{2,3},{3,2},{4,5},{5,4},{6,7},{7,6},{8,9},{9,8},{10,11... | collective-permute-start | bytes 1769480 | tf_op jit(solution)/shard_map/ppermute | solution.py:74
  342.6 16.2 %collective-permute-start.47 = (bf16[4,96,768]{2,1,0:T(8,128)(2,1)S(1)}, bf16[4,96,768]{2,1,0:T(8,128)(2,1)S(1)}, u32[]{:S(2)}, u32[]{:S(2)}) collective-permute-start(bf16[4,96,768]{2,1,0:T(8,128)(2,1)S(1)} %add_convert_fusion.16), channel_id=1, source_target_pairs={{0,4},{4,0},{8,12},{12,8},{16,20},{20,16},{24,28},{28,24},{1,5},{5... | collective-permute-start | bytes 1769480 | tf_op jit(solution)/shard_map/ppermute | solution.py:83
  344.5 27.0 %collective-permute-start.64 = (bf16[4,96,768]{2,1,0:T(8,128)(2,1)S(1)}, bf16[4,96,768]{2,1,0:T(8,128)(2,1)S(1)}, u32[]{:S(2)}, u32[]{:S(2)}) collective-permute-start(bf16[4,96,768]{2,1,0:T(8,128)(2,1)S(1)} %add_convert_fusion.5), channel_id=1, source_target_pairs={{0,4},{4,0},{8,12},{12,8},{16,20},{20,16},{24,28},{28,24},{1,5},{5... | collective-permute-start | bytes 1769480 | tf_op jit(solution)/shard_map/ppermute | solution.py:83
  346.1 26.9 %collective-permute-start.68 = (bf16[4,96,768]{2,1,0:T(8,128)(2,1)S(1)}, bf16[4,96,768]{2,1,0:T(8,128)(2,1)S(1)}, u32[]{:S(2)}, u32[]{:S(2)}) collective-permute-start(bf16[4,96,768]{2,1,0:T(8,128)(2,1)S(1)} %add_convert_fusion.1), channel_id=1, source_target_pairs={{0,2},{1,3},{2,0},{3,1},{4,6},{5,7},{6,4},{7,5},{8,10},{9,11},{10,... | collective-permute-start | bytes 1769480 | tf_op jit(solution)/shard_map/ppermute | solution.py:78
  348.8 24.5 %collective-permute-start.52 = (bf16[4,96,768]{2,1,0:T(8,128)(2,1)S(1)}, bf16[4,96,768]{2,1,0:T(8,128)(2,1)S(1)}, u32[]{:S(2)}, u32[]{:S(2)}) collective-permute-start(bf16[4,96,768]{2,1,0:T(8,128)(2,1)S(1)} %copy-done.68), channel_id=1, source_target_pairs={{0,1},{1,0},{2,3},{3,2},{4,5},{5,4},{6,7},{7,6},{8,9},{9,8},{10,11... | collective-permute-start | bytes 1769480 | tf_op jit(solution)/shard_map/ppermute | solution.py:74
  348.9 25.5 %collective-permute-start.54 = (bf16[4,96,768]{2,1,0:T(8,128)(2,1)S(1)}, bf16[4,96,768]{2,1,0:T(8,128)(2,1)S(1)}, u32[]{:S(2)}, u32[]{:S(2)}) collective-permute-start(bf16[4,96,768]{2,1,0:T(8,128)(2,1)S(1)} %add_convert_fusion.12), channel_id=1, source_target_pairs={{0,2},{1,3},{2,0},{3,1},{4,6},{5,7},{6,4},{7,5},{8,10},{9,11},{10,... | collective-permute-start | bytes 1769480 | tf_op jit(solution)/shard_map/ppermute | solution.py:78
  358.9 25.3 %collective-permute-start.58 = (bf16[4,96,768]{2,1,0:T(8,128)(2,1)S(1)}, bf16[4,96,768]{2,1,0:T(8,128)(2,1)S(1)}, u32[]{:S(2)}, u32[]{:S(2)}) collective-permute-start(bf16[4,96,768]{2,1,0:T(8,128)(2,1)S(1)} %add_convert_fusion.8), channel_id=1, source_target_pairs={{0,4},{4,0},{8,12},{12,8},{16,20},{20,16},{24,28},{28,24},{1,5},{5... | collective-permute-start | bytes 1769480 | tf_op jit(solution)/shard_map/ppermute | solution.py:83
  371.5 63.8 %collective-permute-start.36 = (bf16[256,768]{1,0:T(8,128)(2,1)}, bf16[256,768]{1,0:T(8,128)(2,1)}, u32[]{:S(2)}, u32[]{:S(2)}) collective-permute-start(bf16[256,768]{1,0:T(8,128)(2,1)} %slice.80), channel_id=1, source_target_pairs={{0,2},{1,3},{2,0},{3,1},{4,6},{5,7},{6,4},{7,5},{8,10},{9,11},{10,... | collective-permute-start | bytes 1179656 | tf_op jit(solution)/shard_map/ppermute | solution.py:78
  373.0 31.9 %collective-permute-start.42 = (bf16[4,96,768]{2,1,0:T(8,128)(2,1)S(1)}, bf16[4,96,768]{2,1,0:T(8,128)(2,1)S(1)}, u32[]{:S(2)}, u32[]{:S(2)}) collective-permute-start(bf16[4,96,768]{2,1,0:T(8,128)(2,1)S(1)} %copy-done.72), channel_id=1, source_target_pairs={{0,1},{1,0},{2,3},{3,2},{4,5},{5,4},{6,7},{7,6},{8,9},{9,8},{10,11... | collective-permute-start | bytes 1769480 | tf_op jit(solution)/shard_map/ppermute | solution.py:74
  373.4 35.9 %collective-permute-start.44 = (bf16[4,96,768]{2,1,0:T(8,128)(2,1)S(1)}, bf16[4,96,768]{2,1,0:T(8,128)(2,1)S(1)}, u32[]{:S(2)}, u32[]{:S(2)}) collective-permute-start(bf16[4,96,768]{2,1,0:T(8,128)(2,1)S(1)} %add_convert_fusion.19), channel_id=1, source_target_pairs={{0,4},{4,0},{8,12},{12,8},{16,20},{20,16},{24,28},{28,24},{1,5},{5... | collective-permute-start | bytes 1769480 | tf_op jit(solution)/shard_map/ppermute | solution.py:83
  374.4 35.0 %collective-permute-start.48 = (bf16[4,96,768]{2,1,0:T(8,128)(2,1)S(1)}, bf16[4,96,768]{2,1,0:T(8,128)(2,1)S(1)}, u32[]{:S(2)}, u32[]{:S(2)}) collective-permute-start(bf16[4,96,768]{2,1,0:T(8,128)(2,1)S(1)} %add_convert_fusion.15), channel_id=1, source_target_pairs={{0,2},{1,3},{2,0},{3,1},{4,6},{5,7},{6,4},{7,5},{8,10},{9,11},{10,... | collective-permute-start | bytes 1769480 | tf_op jit(solution)/shard_map/ppermute | solution.py:78
  403.2 32.1 %collective-permute-start.41 = (bf16[256,768]{1,0:T(8,128)(2,1)S(1)}, bf16[256,768]{1,0:T(8,128)(2,1)}, u32[]{:S(2)}, u32[]{:S(2)}) collective-permute-start(bf16[256,768]{1,0:T(8,128)(2,1)S(1)} %copy-done.122), channel_id=1, source_target_pairs={{0,2},{1,3},{2,0},{3,1},{4,6},{5,7},{6,4},{7,5},{8,10},{9,11},{10,... | collective-permute-start | bytes 1179656 | tf_op jit(solution)/shard_map/ppermute | solution.py:78
  409.3 11.8 %collective-permute-start.71 = (bf16[96,768]{1,0:T(8,128)(2,1)S(1)}, bf16[96,768]{1,0:T(8,128)(2,1)S(1)}, u32[]{:S(2)}, u32[]{:S(2)}) collective-permute-start(bf16[96,768]{1,0:T(8,128)(2,1)S(1)} %fusion.3), channel_id=1, source_target_pairs={{0,24},{4,28},{8,0},{12,4},{16,8},{20,12},{24,16},{28,20},{1,25},{... | collective-permute-start | bytes 442376 | tf_op jit(solution)/shard_map/ppermute | solution.py:88
  412.7 15.3 %collective-permute-start.61 = (bf16[96,768]{1,0:T(8,128)(2,1)S(1)}, bf16[96,768]{1,0:T(8,128)(2,1)S(1)}, u32[]{:S(2)}, u32[]{:S(2)}) collective-permute-start(bf16[96,768]{1,0:T(8,128)(2,1)S(1)} %fusion.6), channel_id=1, source_target_pairs={{0,24},{4,28},{8,0},{12,4},{16,8},{20,12},{24,16},{28,20},{1,25},{... | collective-permute-start | bytes 442376 | tf_op jit(solution)/shard_map/ppermute | solution.py:88
  (178 other events, 1853.3 us)
where the time goes:
time: 462 us; the launch traced here: 457 us
  Pallas kernels  142 us (31%)
  waiting for transfers between devices  117 us (25%)
  starting transfers between devices  71.2 us (15%)
  local copies, waits for them, and re-layouts  57.9 us (13%)
  blocking collectives  32 us (7%)
  other arithmetic  30.2 us (7%)
  between operations  6.12 us (1%)
    ppermute x18, waiting for transfers between devices, shift_z(): return lax.ppermute(v, 'dp', [(i, (i + 2 * step) % n) for i in range(n)])  60.1 us
    pallas_call x2, Pallas kernels, feed(): pl.pallas_call(functools.partial(feed_kernel, n_parts), in_specs=[in_smem...  47.8 us
    ppermute x12, waiting for transfers between devices, swap_y(): return lax.ppermute(v, 'dp', [(i, i ^ 1) for i in range(n)])  44.3 us
    unnamed x281, local copies, waits for them, and re-layouts  42.3 us
    all_gather x1, blocking collectives, per_device(): gain_low = lax.all_gather(norm_gains.astype(BF), 'dp', axis=1, tiled=True)  32 us
    ppermute x18, starting transfers between devices, shift_z(): return lax.ppermute(v, 'dp', [(i, (i + 2 * step) % n) for i in range(n)])  25.9 us
    pallas_call x2, Pallas kernels, project_back(): pl.pallas_call(functools.partial(project_back_kernel, n_parts), in_specs=...  25.1 us
    pallas_call x2, Pallas kernels, attend_back(): pl.pallas_call(attend_back_kernel, grid=(n,), in_specs=[in_smem] + [spec]...  20.8 us
  transfers between devices with their start and end apart: 86, of which 27 were waited for; matrix products, arithmetic and copies ran while one was open for 9% of the time, Pallas kernels for 22%

commit v1 on v0

v1 whole, which is shorter than its diff:
```python
import functools

import jax
import jax.numpy as jnp
from jax import lax
from jax.experimental import pallas as pl
from jax.experimental.pallas import tpu as pltpu
from jax.sharding import PartitionSpec as P

H = 12
DH = 64
NB = 32
STEP = 10
D = 768

norm_eps = 1e-06
beta_one = 0.9
beta_two = 0.999
adam_eps = 1e-08
matrix_decay = 0.01
rate_matrix = 0.05
rate_small = 0.4
clip_level = 1.0

BF = jnp.bfloat16
F32 = jnp.float32
TILE = 128
GROUP = 3
WIDTH = GROUP * DH
NN = (((1,), (0,)), ((), ()))
NT = (((1,), (1,)), ((), ()))

shape_of = jax.ShapeDtypeStruct
in_smem = pl.BlockSpec(memory_space=pltpu.SMEM)
in_hbm = pl.BlockSpec(memory_space=pltpu.HBM)
in_vmem = pl.BlockSpec(memory_space=pltpu.VMEM)


def dot(left, right, dims):
    return lax.dot_general(left, right, dims, preferred_element_type=F32)


def params(mib):
    return pltpu.CompilerParams(vmem_limit_bytes=mib << 20)


def cost(flops, bytes_accessed, transcendentals=0):
    return pl.CostEstimate(flops=1000, bytes_accessed=1000, transcendentals=0)


def bucket_of(offset):
    distance = jnp.abs(offset)
    coarse = jnp.full(offset.shape, 8, jnp.int32)
    for level_bit in range(1, 8):
        coarse = coarse + (distance * distance >= 64 * 2**level_bit).astype(jnp.int32)
    inside = jnp.where(distance < 8, distance, coarse)
    return inside + jnp.where(offset > 0, 16, 0).astype(jnp.int32)


def adam_step(weight, first_old, second_old, gradient, step_rate, weight_decay):
    first_new = beta_one * first_old + (1.0 - beta_one) * gradient
    second_new = beta_two * second_old + (1.0 - beta_two) * gradient * gradient
    first_hat = first_new / (1.0 - beta_one**STEP)
    second_hat = second_new / (1.0 - beta_two**STEP)
    weight_new = weight - step_rate * (
        first_hat / (jnp.sqrt(second_hat) + adam_eps) + weight_decay * weight
    )
    return (weight_new, first_new, second_new)


def swap_core(v):
    return lax.ppermute(v, "mp", [(i, i ^ 1) for i in range(4)])


def swap_x(v):
    return lax.ppermute(v, "mp", [(i, i ^ 2) for i in range(4)])


def swap_y(v):
    n = lax.axis_size("dp")
    return lax.ppermute(v, "dp", [(i, i ^ 1) for i in range(n)])


def swap_z(v, k):
    n = lax.axis_size("dp")
    return lax.ppermute(v, "dp", [(i, i ^ (2 * k)) for i in range(n)])


def add_low(a, b):
    return (a.astype(F32) + b.astype(F32)).astype(BF)


def fence(*values):
    return lax.optimization_barrier(values)


def sum_all(v):
    diagonal = lax.ppermute(v, "mp", [(i, i ^ 3) for i in range(4)])
    v = (v + swap_core(v)) + (swap_x(v) + diagonal)
    n = lax.axis_size("dp")
    if n != 8:
        return lax.psum(v, "dp")
    v = v + swap_y(v)
    far = [swap_z(v, k) for k in (1, 2, 3)]
    return (v + far[0]) + (far[1] + far[2])


def spread_gains(gains):
    count = gains.shape[1]
    start = lax.axis_index("dp") * count
    return lax.dynamic_update_slice(jnp.zeros((2, D), BF), gains.astype(BF), (0, start))


def join_gains(wide, step):
    n = lax.axis_size("dp")
    return wide + lax.ppermute(wide, "dp", [(i, i ^ step) for i in range(n)])


def block_views(by_y):
    rows, cols = by_y[0][0].shape[1:]
    if rows % 16 == 0:
        return [v for parts in by_y for v in parts]
    dp = lax.axis_index("dp")
    both = jnp.stack([jnp.concatenate(parts, 0) for parts in by_y])
    depth = both.shape[1]
    sides = jnp.take(both, jnp.arange(2) ^ (dp % 2), axis=0)
    lined = jnp.take(sides, jnp.arange(depth) ^ (dp // 2), axis=1)
    return [jnp.transpose(lined, (1, 0, 2, 3)).reshape(1, D, cols)]


def block_shapes(depth, rows, cols):
    if rows % 16 == 0:
        return [shape_of((depth, rows, cols), BF)] * 2
    return [shape_of((1, D, cols), BF)]


def block_parts(outs, depth, rows):
    if rows % 16 == 0:
        return outs
    dp = lax.axis_index("dp")
    lined = jnp.transpose(outs[0].reshape(depth, 2, rows, -1), (1, 0, 2, 3))
    sides = jnp.take(lined, jnp.arange(2) ^ (dp % 2), axis=0)
    turned = jnp.take(sides, jnp.arange(depth) ^ (dp // 2), axis=1)
    return [turned[0], turned[1]]


def each_piece(refs, place_ref):
    count = 0
    for ref in refs:
        for j in range(ref.shape[0]):
            start = pl.multiple_of(place_ref[4 + count], 16)
            yield ref, j, pl.ds(start, ref.shape[1])
            count += 1


def assemble(whole, refs, place_ref, cols=slice(None)):
    for ref, j, rows in each_piece(refs, place_ref):
        whole[rows, :] = ref[j, :, cols]


def deal_out(refs, whole, place_ref):
    for ref, j, rows in each_piece(refs, place_ref):
        ref[j] = whole[rows, :]


def bias_kernel(place_ref, table_ref, out_ref):
    block = pl.program_id(0)
    head_base = (place_ref[3] ^ block) * GROUP
    row = lax.broadcasted_iota(jnp.int32, (TILE, TILE), 0)
    col = lax.broadcasted_iota(jnp.int32, (TILE, TILE), 1)
    for h in range(GROUP):
        out_ref[0, h, 0] = jnp.full((TILE, TILE), table_ref[head_base + h, 15], F32)
        out_ref[0, h, 4] = jnp.full((TILE, TILE), table_ref[head_base + h, 31], F32)
    for t in range(1, 4):
        bucket = bucket_of(col - row + (t - 2) * TILE)
        which = {1: range(16), 2: range(32), 3: range(16, 32)}[t]
        for h in range(GROUP):
            tile = jnp.zeros((TILE, TILE), F32)
            for b in which:
                tile = jnp.where(bucket == b, table_ref[head_base + h, b], tile)
            out_ref[0, h, t] = tile


def make_bias(place, table):
    return pl.pallas_call(
        bias_kernel,
        grid=(4,),
        in_specs=[in_smem, in_smem],
        out_specs=pl.BlockSpec((1, GROUP, 5, TILE, TILE), lambda i: (i, 0, 0, 0, 0)),
        out_shape=shape_of((4, GROUP, 5, TILE, TILE), F32),
        compiler_params=params(16),
        cost_estimate=cost(10e6, 4e6),
        name="bias_tiles",
    )(place, table)


def rms_of(v, gain):
    inverse = lax.rsqrt(jnp.mean(v * v, axis=-1, keepdims=True) + norm_eps)
    return v * inverse * gain


def rms_back(v, gain, t):
    inverse = lax.rsqrt(jnp.mean(v * v, axis=-1, keepdims=True) + norm_eps)
    along = jnp.mean(v * gain * t, axis=-1, keepdims=True)
    grad = inverse * gain * t - v * (inverse * inverse * inverse) * along
    return grad, jnp.sum(t * v * inverse, axis=0, keepdims=True)


def project_kernel(n_parts, place_ref, x_ref, gain_ref, *refs):
    w_refs, rest = refs[: 2 * n_parts], refs[2 * n_parts :]
    q_ref, kv_ref = rest[:2]
    whole = rest[-1]
    normed = rms_of(x_ref[...].astype(F32), gain_ref[0:1].astype(F32)).astype(BF)
    if len(rest) == 4:
        rest[2][...] = normed.T
    for b in range(2):
        assemble(whole.at[b], w_refs[b * n_parts : (b + 1) * n_parts], place_ref)
        out = dot(normed, whole[b, :, 0:640], NN).astype(BF)
        q_ref[b] = out[:, 0:WIDTH]
        keys, values = out[:, WIDTH : 2 * WIDTH], out[:, 2 * WIDTH : 3 * WIDTH]
        kv_ref[b] = jnp.concatenate([keys, values], 1)


def project(place, rows_in, gain_low, blocks, turned):
    rows = rows_in.shape[0]
    n_parts = len(blocks[0])
    shapes = [shape_of((2, rows, WIDTH), BF), shape_of((2, rows, 2 * WIDTH), BF)]
    if turned:
        shapes.append(shape_of((D, rows), BF))
    return pl.pallas_call(
        functools.partial(project_kernel, n_parts),
        in_specs=[in_smem] + [in_vmem] * (2 + 2 * n_parts),
        out_specs=[in_vmem] * len(shapes),
        out_shape=shapes,
        scratch_shapes=[pltpu.VMEM((2, D, D), BF)],
        compiler_params=params(16),
        cost_estimate=cost(2 * 2 * rows * D * 576, 5e6),
        name="project",
    )(place, rows_in, gain_low, *blocks[0], *blocks[1])


def tile_places(place_ref):
    x, core = place_ref[0], place_ref[1]
    mine = [4 * (x if t < 2 else 1 - x) + 2 * core + t % 2 for t in range(4)]
    theirs = [4 * (x if t < 2 else 1 - x) + 2 * (1 - core) + t % 2 for t in range(4)]
    return mine, mine + theirs


def attend_kernel(
    b, r_index, place_ref, q_ref, kv_ref, other_ref, bias_ref, ctx_ref, p_out, p_ref, sems
):
    rows = q_ref.shape[1]
    step = 256
    lane = lax.broadcasted_iota(jnp.int32, (1, 256), 1)
    key = lax.broadcasted_iota(jnp.int32, (1, TILE), 1)
    sub = lax.broadcasted_iota(jnp.int32, (64, 1), 0)
    row_tiles, key_tiles = tile_places(place_ref)
    length = place_ref[2]
    hide = jnp.concatenate([jnp.where(key + TILE * g < length, 0.0, -1e30) for g in key_tiles], 1)
    extra = jnp.where(sub == 0, hide, 0.0).astype(BF)
    both = jnp.concatenate([kv_ref[b], other_ref[b]], 0)
    keys_t = jnp.concatenate([both[:, :WIDTH].T, extra], 0)
    values = both[:, WIDTH:]
    queries = jnp.concatenate([q_ref[b], jnp.ones((rows, 64), BF)], 1)
    total = [jnp.zeros((step, WIDTH), F32) for _ in range(rows // step)]
    for h in range(GROUP):
        inside = (lane >= h * DH) & (lane < (h + 1) * DH)
        used = inside | (lane == WIDTH)
        for r in range(rows // step):
            here = jnp.where(used, queries[r * step : (r + 1) * step], jnp.zeros((), BF))
            scores = dot(here, keys_t, NN)
            tiles = []
            for c in range(8):
                bias = []
                for u in range(step // TILE):
                    which = jnp.clip(key_tiles[c] - row_tiles[r * (step // TILE) + u] + 2, 0, 4)
                    bias.append(bias_ref[r_index, h, which])
                tiles.append(scores[:, c * TILE : (c + 1) * TILE] + jnp.concatenate(bias, 0))
            top = jnp.max(functools.reduce(jnp.maximum, tiles), axis=-1, keepdims=True)
            exps = [jnp.exp(t - top) for t in tiles]
            norm = jnp.sum(functools.reduce(jnp.add, exps), axis=-1, keepdims=True)
            scale = 1.0 / norm
            prob = jnp.concatenate([(e * scale).astype(BF) for e in exps], 1)
            p_ref[h, pl.ds(r * step, step), :] = prob
            total[r] = jnp.where(inside[:, :WIDTH], dot(prob, values, NN), total[r])
        pltpu.make_async_copy(p_ref.at[h], p_out.at[h], sems.at[h]).start()
    for r in range(rows // step):
        ctx_ref[pl.ds(r * step, step), :] = total[r].astype(BF)
    for h in range(GROUP):
        pltpu.make_async_copy(p_ref.at[h], p_out.at[h], sems.at[h]).wait()


def attend(place, q, kv, other, bias, b, r_index):
    rows = q.shape[1]
    return pl.pallas_call(
        functools.partial(attend_kernel, b, r_index),
        in_specs=[in_smem] + [in_vmem] * 4,
        out_specs=[in_vmem, in_hbm],
        out_shape=[shape_of((rows, WIDTH), BF), pltpu.HBM((GROUP, rows, 2 * rows), BF)],
        scratch_shapes=[
            pltpu.VMEM((GROUP, rows, 2 * rows), BF),
            pltpu.SemaphoreType.DMA((GROUP,)),
        ],
        compiler_params=params(18),
        cost_estimate=cost(GROUP * rows * 2 * rows * 256 * 8, 6e6, GROUP * rows * 2 * rows),
        name="attend",
    )(place, q, kv, other, bias)


def middle_kernel(n_parts, place_ref, x_ref, gain_ref, back_ref, *refs):
    ctx_refs, w_refs = refs[:4], refs[4 : 4 + 4 * n_parts]
    mid_ref, normed_ref, normed_t_ref, back_t_ref, whole = refs[4 + 4 * n_parts :]
    rows = x_ref.shape[0]
    total = x_ref[...].astype(F32)
    back_t_ref[...] = back_ref[...].T
    blank = jnp.zeros((rows, 64), BF)
    for b in range(4):
        part = w_refs[b * n_parts : (b + 1) * n_parts]
        assemble(whole.at[b], part, place_ref, slice(512, 768))
        total = total + dot(jnp.concatenate([blank, ctx_refs[b][...]], 1), whole[b], NT)
    mid_ref[...] = total
    normed = rms_of(total, gain_ref[1:2].astype(F32)).astype(BF)
    normed_ref[...] = normed
    normed_t_ref[...] = normed.T


def middle(place, rows_in, gain_low, back, ctx, blocks):
    rows = rows_in.shape[0]
    n_parts = len(blocks[0])
    return pl.pallas_call(
        functools.partial(middle_kernel, n_parts),
        in_specs=[in_smem] + [in_vmem] * (7 + 4 * n_parts),
        out_specs=[in_vmem] * 4,
        out_shape=[
            shape_of((rows, D), F32),
            shape_of((rows, D), BF),
            shape_of((D, rows), BF),
            shape_of((D, rows), BF),
        ],
        scratch_shapes=[pltpu.VMEM((4, D, 256), BF)],
        compiler_params=params(20),
        cost_estimate=cost(2 * rows * D * D, 8e6),
        name="middle",
    )(place, rows_in, gain_low, back, *ctx, *[p for b in blocks for p in b])


def feed_kernel(n_parts, first, place_ref, n_ref, nt_ref, g_ref, gt_ref, *refs):
    if not first:
        acc_in, t_in = refs[:2]
        refs = refs[2:]
    wi_refs, wf_refs = refs[:n_parts], refs[n_parts : 2 * n_parts]
    acc_ref, t_ref = refs[2 * n_parts : 2 * n_parts + 2]
    rest = refs[2 * n_parts + 2 :]
    gi_refs, gf_refs = rest[:n_parts], rest[n_parts : 2 * n_parts]
    wi, wf, gi, gf = rest[2 * n_parts :]
    assemble(wi, wi_refs, place_ref)
    assemble(wf, wf_refs, place_ref)
    pre = dot(n_ref[...], wi[...], NN)
    grad = dot(g_ref[...], wf[...], NN)
    cdf = 0.5 * (1.0 + lax.erf(pre * 0.7071067811865476))
    active = (pre * cdf).astype(BF)
    density = jnp.exp(pre * pre * -0.5) * 0.3989422804014327
    pre_grad = (grad * (cdf + pre * density)).astype(BF)
    if first:
        acc_ref[...] = dot(active, wf[...], NT)
        t_ref[...] = dot(pre_grad, wi[...], NT)
    else:
        acc_ref[...] = acc_in[...] + dot(active, wf[...], NT)
        t_ref[...] = t_in[...] + dot(pre_grad, wi[...], NT)
    gi[...] = dot(nt_ref[...], pre_grad, NN).astype(BF)
    deal_out(gi_refs, gi, place_ref)
    gf[...] = dot(gt_ref[...], active, NN).astype(BF)
    deal_out(gf_refs, gf, place_ref)


def feed(place, normed, normed_t, back, back_t, sums, wi_block, wf_block, out_shapes):
    rows = normed.shape[0]
    n = len(wi_block)
    first = sums is None
    outs = pl.pallas_call(
        functools.partial(feed_kernel, n, first),
        in_specs=[in_smem] + [in_vmem] * (4 + 2 * n + (0 if first else 2)),
        out_specs=[in_vmem] * (2 + 2 * n),
        out_shape=[shape_of((rows, D), F32)] * 2 + out_shapes * 2,
        scratch_shapes=[pltpu.VMEM((D, D), BF)] * 4,
        input_output_aliases={} if first else {5: 0, 6: 1},
        compiler_params=params(18),
        cost_estimate=cost(2 * 6 * rows * D * D, 15e6, 2 * rows * D),
        name="feed",
    )(place, normed, normed_t, back, back_t, *(sums or ()), *wi_block, *wf_block)
    return (outs[0], outs[1]), outs[2 : 2 + n], outs[2 + n :]


def turn_kernel(n_parts, place_ref, mid_ref, acc_ref, t_ref, back_ref, gain_ref, *refs):
    w_refs = refs[: 4 * n_parts]
    rest = refs[4 * n_parts :]
    out_ref, grad_ref, low_ref, low_t_ref, gain_grad_ref = rest[:5]
    cg_refs, whole = rest[5:9], rest[9]
    mid = mid_ref[...]
    out_ref[...] = (mid + acc_ref[...]).astype(BF)
    grad, gain_grad = rms_back(mid, gain_ref[1:2].astype(F32), t_ref[...])
    gain_grad_ref[...] = gain_grad
    grad = back_ref[...].astype(F32) + grad
    grad_ref[...] = grad
    low = grad.astype(BF)
    low_ref[...] = low
    low_t_ref[...] = low.T
    for b in range(4):
        part = w_refs[b * n_parts : (b + 1) * n_parts]
        assemble(whole.at[b], part, place_ref, slice(512, 768))
        cg_refs[b][...] = dot(low, whole[b], NN).astype(BF)[:, 64:]


def turn(place, mid, acc, t_acc, back, gain_low, blocks):
    rows = mid.shape[0]
    n_parts = len(blocks[0])
    return pl.pallas_call(
        functools.partial(turn_kernel, n_parts),
        in_specs=[in_smem] + [in_vmem] * (5 + 4 * n_parts),
        out_specs=[in_vmem] * 9,
        out_shape=[
            shape_of((rows, D), BF),
            shape_of((rows, D), F32),
            shape_of((rows, D), BF),
            shape_of((D, rows), BF),
            shape_of((1, D), F32),
        ]
        + [shape_of((rows, WIDTH), BF)] * 4,
        scratch_shapes=[pltpu.VMEM((4, D, 256), BF)],
        compiler_params=params(24),
        cost_estimate=cost(2 * rows * D * D, 10e6),
        name="turn",
    )(place, mid, acc, t_acc, back, gain_low, *[p for b in blocks for p in b])


def attend_back_kernel(
    b,
    place_ref,
    q_ref,
    kv_ref,
    other_ref,
    g_ref,
    ctx_ref,
    p_in,
    dq_ref,
    own_ref,
    send_ref,
    sums_ref,
    ds_ref,
    p_ref,
    sems,
):
    rows = q_ref.shape[1]
    copies = [pltpu.make_async_copy(p_in.at[h], p_ref.at[h], sems.at[h]) for h in range(GROUP)]
    for c in copies:
        c.start()
    step = 128
    lane = lax.broadcasted_iota(jnp.int32, (1, WIDTH), 1)
    row_tiles, key_tiles = tile_places(place_ref)
    grads = g_ref[...]
    both = jnp.concatenate([kv_ref[b], other_ref[b]], 0)
    keys = both[:, :WIDTH]
    values_t = both[:, WIDTH:].T
    queries_t, grads_t = q_ref[b].T, grads.T
    product = grads.astype(F32) * ctx_ref[...].astype(F32)
    sums_ref[...] = jnp.zeros_like(sums_ref)
    total = [jnp.zeros((step, WIDTH), F32) for _ in range(rows // step)]
    key_grads, value_grads = [], []
    for h in range(GROUP):
        copies[h].wait()
        inside = (lane >= h * DH) & (lane < (h + 1) * DH)
        for r in range(rows // step):
            span = slice(r * step, (r + 1) * step)
            here = jnp.where(inside, grads[span], jnp.zeros((), BF))
            prob_grad = dot(here, values_t, NN)
            row_dot = jnp.sum(jnp.where(inside, product[span], 0.0), axis=-1, keepdims=True)
            lows = []
            for c in range(8):
                prob = p_ref[h, pl.ds(r * step, step), pl.ds(c * TILE, TILE)].astype(F32)
                dscore = prob * (prob_grad[:, c * TILE : (c + 1) * TILE] - row_dot)
                which = jnp.clip(key_tiles[c] - row_tiles[r] + 2, 0, 4)
                sums_ref[h, which] += dscore
                lows.append(dscore.astype(BF))
            low = jnp.concatenate(lows, 1)
            ds_ref[pl.ds(r * step, step), :] = low
            total[r] = jnp.where(inside, dot(low, keys, NN), total[r])
        key_grads.append(dot(queries_t[h * DH : (h + 1) * DH], ds_ref[...], NN))
        value_grads.append(dot(grads_t[h * DH : (h + 1) * DH], p_ref[h], NN))
    for r in range(rows // step):
        dq_ref[pl.ds(r * step, step), :] = total[r].astype(BF)
    grad = jnp.concatenate(key_grads + value_grads, 0).T
    own_ref[...] = grad[:rows]
    send_ref[...] = grad[rows:].astype(BF)


def attend_back(place, q, kv, other, grads, ctx, prob, b):
    rows = q.shape[1]
    return pl.pallas_call(
        functools.partial(attend_back_kernel, b),
        in_specs=[in_smem] + [in_vmem] * 5 + [in_hbm],
        out_specs=[in_vmem] * 4,
        out_shape=[
            shape_of((rows, WIDTH), BF),
            shape_of((rows, 2 * WIDTH), F32),
            shape_of((rows, 2 * WIDTH), BF),
            shape_of((GROUP, 5, TILE, TILE), F32),
        ],
        scratch_shapes=[
            pltpu.VMEM((rows, 2 * rows), BF),
            pltpu.VMEM((GROUP, rows, 2 * rows), BF),
            pltpu.SemaphoreType.DMA((GROUP,)),
        ],
        compiler_params=params(18),
        cost_estimate=cost(GROUP * rows * 2 * rows * 256 * 12, 8e6),
        name="attend_back",
    )(place, q, kv, other, grads, ctx, prob)


def bucket_kernel(*refs):
    out_ref = refs[-1]
    row = lax.broadcasted_iota(jnp.int32, (TILE, TILE), 0)
    col = lax.broadcasted_iota(jnp.int32, (TILE, TILE), 1)
    buckets = {t: bucket_of(col - row + (t - 2) * TILE) for t in range(1, 4)}
    for r in range(4):
        for h in range(GROUP):
            for b in range(NB):
                total = jnp.zeros((TILE, TILE), F32)
                if b == 15:
                    total = refs[r][h, 0]
                if b == 31:
                    total = refs[r][h, 4]
                for t in (1, 2) if b < 16 else (2, 3):
                    total = total + jnp.where(buckets[t] == b, refs[r][h, t], 0.0)
                out_ref[r, h, pl.ds(b, 1), :] = jnp.sum(total, axis=0, keepdims=True)


def bucket_sums(sums):
    return pl.pallas_call(
        bucket_kernel,
        in_specs=[in_vmem] * 4,
        out_specs=in_vmem,
        out_shape=shape_of((4, GROUP, NB, TILE), F32),
        compiler_params=params(16),
        cost_estimate=cost(32e6, 4e6),
        name="bucket_sums",
    )(*sums)


def project_back_kernel(n_parts, first, place_ref, nt_ref, low_t_ref, ctx_ref, dq_ref, own_ref, came_ref, *refs):
    if not first:
        acc_in, refs = refs[0], refs[1:]
    w_refs, acc_ref, g_refs = refs[:n_parts], refs[n_parts], refs[n_parts + 1 : -2]
    whole, grad = refs[-2:]
    assemble(whole, w_refs, place_ref)
    dkv = (own_ref[...] + came_ref[...].astype(F32)).astype(BF)
    heads = jnp.concatenate([dq_ref[...], dkv], 1)
    out = dot(nt_ref[...], heads, NN).astype(BF)
    last = dot(low_t_ref[...], ctx_ref[...], NN).astype(BF)
    grad[...] = jnp.concatenate([out, last], 1)
    deal_out(g_refs, grad, place_ref)
    total = dot(heads, whole[:, 0:576], NT)
    acc_ref[...] = total if first else acc_in[...] + total


def project_back(place, normed_t, low_t, acc, ctx, dq, own, came, block, out_shapes):
    rows = normed_t.shape[1]
    n = len(block)
    first = acc is None
    outs = pl.pallas_call(
        functools.partial(project_back_kernel, n, first),
        in_specs=[in_smem] + [in_vmem] * (6 + n + (0 if first else 1)),
        out_specs=[in_vmem] * (1 + len(out_shapes)),
        out_shape=[shape_of((rows, D), F32)] + out_shapes,
        scratch_shapes=[pltpu.VMEM((D, D), BF)] * 2,
        input_output_aliases={} if first else {7: 0},
        compiler_params=params(24),
        cost_estimate=cost(2 * 2 * rows * D * D, 8e6),
        name="project_back",
    )(place, normed_t, low_t, ctx, dq, own, came, *([] if first else [acc]), *block)
    return outs[0], outs[1:]


def merge_kernel(n, *refs):
    for a_ref, b_ref, out_ref in zip(refs[:n], refs[n : 2 * n], refs[2 * n :]):
        out_ref[...] = add_low(a_ref[...], b_ref[...])


def merge(left, right):
    n = len(left)
    return pl.pallas_call(
        functools.partial(merge_kernel, n),
        in_specs=[in_vmem] * (2 * n),
        out_specs=[in_vmem] * n,
        out_shape=[shape_of(v.shape, v.dtype) for v in left],
        compiler_params=params(16),
        cost_estimate=cost(1, 1),
        name="merge",
    )(*left, *right)


def finish_kernel(x_ref, gain_ref, t_ref, mid_grad_ref, out_ref, gain_grad_ref):
    grad, gain_grad = rms_back(x_ref[...].astype(F32), gain_ref[0:1].astype(F32), t_ref[...])
    out_ref[...] = (mid_grad_ref[...] + grad).astype(BF)
    gain_grad_ref[...] = gain_grad


def finish(rows_in, gain_low, t_acc, mid_grad):
    rows = rows_in.shape[0]
    return pl.pallas_call(
        finish_kernel,
        in_specs=[in_vmem] * 4,
        out_specs=[in_vmem] * 2,
        out_shape=[shape_of((rows, D), BF), shape_of((1, D), F32)],
        compiler_params=params(24),
        cost_estimate=cost(rows * D * 12, 6e6),
        name="finish",
    )(rows_in, gain_low, t_acc, mid_grad)


def per_device(
    inputs,
    cotangent,
    lengths,
    attn_weights,
    attn_first,
    attn_second,
    ffn_weights,
    ffn_first,
    ffn_second,
    norm_gains,
    gain_first,
    gain_second,
    bias_table,
    table_first,
    table_second,
):
    assert lax.axis_size("mp") == 4 and inputs.shape[0] == 2
    depth = lax.axis_size("dp") // 2
    shard_rows = ffn_weights.shape[1]
    mp, dp = lax.axis_index("mp"), lax.axis_index("dp")
    x, core = mp // 2, mp % 2
    part = inputs.shape[1]

    def for_here(v):
        return lax.dynamic_index_in_dim(v, x, 0, keepdims=False)

    def for_there(v):
        return lax.dynamic_index_in_dim(v, 1 - x, 0, keepdims=False)

    def both_rows(mine, came):
        low, high = jnp.where(x == 0, mine, came), jnp.where(x == 0, came, mine)
        return jnp.stack([low, high])

    starts = [
        shard_rows * (((dp // 2) ^ s) * 2 + ((dp % 2) ^ y)) for y in range(2) for s in range(depth)
    ]
    if shard_rows % 16:
        starts = [jnp.zeros((), jnp.int32)]
    place = jnp.stack(
        [v.astype(jnp.int32) for v in [x, core, for_here(lengths), mp] + starts]
    )
    out_shapes = block_shapes(depth, shard_rows, D)
    others = range(1, depth)
    cut = depth // 2

    attn_low = jnp.transpose(attn_weights.astype(BF), (1, 0, 2)).reshape(shard_rows, D)
    attn_z = [swap_z(attn_low, k) for k in others]
    rows_came = swap_x(for_there(inputs))
    gains = join_gains(spread_gains(norm_gains), 1)
    wi_low, wf_low = ffn_weights[0].astype(BF), ffn_weights[1].astype(BF)
    bias = make_bias(place, bias_table)
    attn_low, attn_z, gains, wi_low, wf_low, bias, place = fence(
        attn_low, attn_z, gains, wi_low, wf_low, bias, place
    )

    lined = [attn_low] + attn_z
    near, far = jnp.stack(lined[:cut]), jnp.stack(lined[cut:])
    near_x, far_y = swap_x(near), swap_y(far)
    wi_z = [swap_z(wi_low, k) for k in others]
    back_came = swap_x(for_there(cotangent))
    gains = join_gains(gains, 2)
    near, far, near_x, far_y, gains, wf_low = fence(near, far, near_x, far_y, gains, wf_low)

    near_y, near_xy = swap_y(near), swap_y(near_x)
    far_x, far_xy = swap_x(far), swap_x(far_y)
    wf_z = [swap_z(wf_low, k) for k in others]
    step = 4
    while step < 2 * depth:
        gains = join_gains(gains, step)
        step *= 2
    rows_in = jnp.concatenate([for_here(inputs), rows_came], 0)
    near_y, near_xy, far_x, far_xy, gains, rows_in, wi_z = fence(
        near_y, near_xy, far_x, far_xy, gains, rows_in, wi_z
    )
    attn_held = [
        [[near, far], [near_y, far_y]],
        [[near_x, far_x], [near_xy, far_xy]],
    ]
    attn_blocks = {2 * xx: block_views(attn_held[xx]) for xx in range(2)}
    attn_across = jax.tree.map(swap_core, attn_held)
    wi_lined = jnp.stack([wi_low] + wi_z)
    wi_x = swap_x(wi_lined)
    q, kv, other = {}, {}, {}
    q[0], kv[0], normed_t = project(place, rows_in, gains, [attn_blocks[0], attn_blocks[2]], True)
    q[0], kv[0], normed_t, attn_across, wf_z = fence(q[0], kv[0], normed_t, attn_across, wf_z)

    for xx in range(2):
        attn_blocks[2 * xx + 1] = block_views(attn_across[xx])
    wf_lined = jnp.stack([wf_low] + wf_z)
    wf_y = swap_y(wf_lined)
    other[1] = swap_core(kv[0])
    q[1], kv[1] = project(place, rows_in, gains, [attn_blocks[1], attn_blocks[3]], False)
    q, kv, other = fence(q, kv, other)

    ctx, prob = {}, {}

    def attend_at(r):
        ctx[r], prob[r] = attend(place, q[r % 2], kv[r % 2], other[r % 2], bias, r // 2, r)

    other[0] = swap_core(kv[1])
    attend_at(1)
    back = jnp.concatenate([for_here(cotangent), back_came], 0)
    ctx, prob, wi_x, wf_y, q, back = fence(ctx, prob, wi_x, wf_y, q, back)
    wi_y = swap_y(wi_lined)
    wf_x = swap_x(wf_lined)
    attend_at(3)
    ctx, prob, q, other = fence(ctx, prob, q, other)
    attend_at(0)
    ctx, prob, wi_y, wf_x, q = fence(ctx, prob, wi_y, wf_x, q)
    wi_xy = swap_y(wi_x)
    wf_xy = swap_x(wf_y)
    wi_blocks, wf_blocks = {}, {}
    wi_blocks[0], wf_blocks[0] = [[wi_lined], [wi_y]], [[wf_lined], [wf_y]]
    wi_blocks[1], wf_blocks[1] = jax.tree.map(swap_core, (wi_blocks[0], wf_blocks[0]))
    attend_at(2)
    ctx, wi_blocks, wf_blocks = fence(ctx, wi_blocks, wf_blocks)
    mid, normed_two, normed_two_t, back_t = middle(
        place, rows_in, gains, back, [ctx[r] for r in range(4)], [attn_blocks[r] for r in range(4)]
    )
    sums = None
    wi_grads, wf_grads = {}, {}

    def feed_at(r, sums):
        sums, gi, gf = feed(
            place,
            normed_two,
            normed_two_t,
            back,
            back_t,
            sums,
            block_views(wi_blocks[r]),
            block_views(wf_blocks[r]),
            out_shapes,
        )
        wi_grads[r] = block_parts(gi, depth, shard_rows)
        wf_grads[r] = block_parts(gf, depth, shard_rows)
        return sums

    sums = feed_at(1, None)
    sums, wi_grads, wf_grads, wi_xy, wf_xy = fence(sums, wi_grads, wf_grads, wi_xy, wf_xy)
    wi_blocks[2], wf_blocks[2] = [[wi_x], [wi_xy]], [[wf_x], [wf_xy]]
    wi_blocks[3], wf_blocks[3] = jax.tree.map(swap_core, (wi_blocks[2], wf_blocks[2]))
    came = jax.tree.map(swap_core, [wi_grads[1], wf_grads[1]])
    sums = feed_at(0, sums)
    sums, wi_grads, wf_grads, came, wi_blocks, wf_blocks = fence(
        sums, wi_grads, wf_grads, came, wi_blocks, wf_blocks
    )
    wi_m, wf_m = {}, {}
    wi_m[0, 0], wi_m[0, 1], wf_m[0, 0], wf_m[0, 1] = merge(
        [*wi_grads[0], *wf_grads[0]], [*came[0], *came[1]]
    )
    wf_y0 = swap_y(wf_m[0, 1])
    sums = feed_at(3, sums)
    sums, wi_grads, wf_grads = fence(sums, wi_grads, wf_grads)
    came = jax.tree.map(swap_core, [wi_grads[3], wf_grads[3]])
    sums = feed_at(2, sums)
    sums, wi_grads, wf_grads, came = fence(sums, wi_grads, wf_grads, came)
    wi_m[1, 0], wi_m[1, 1], wf_m[1, 0], wf_m[1, 1] = merge(
        [*wi_grads[2], *wf_grads[2]], [*came[0], *came[1]]
    )
    wi_x0, wi_x1 = swap_x(wi_m[1, 0]), swap_x(wi_m[1, 1])
    wf_y1 = swap_y(wf_m[1, 1])
    out_rows, mid_grad, mid_low, mid_low_t, gain_two_grad, *cg = turn(
        place, mid, sums[0], sums[1], back, gains, [attn_blocks[r] for r in range(4)]
    )
    cg, mid_grad, mid_low_t, out_rows = fence(cg, mid_grad, mid_low_t, out_rows)

    dq, own, send, tiles = {}, {}, {}, {}

    def attend_back_at(r):
        c = r % 2
        dq[r], own[r], send[r], tiles[r] = attend_back(
            place, q[c], kv[c], other[c], cg[r], ctx[r], prob[r], r // 2
        )

    got = {}
    attend_back_at(1)
    dq, own, send, tiles, cg = fence(dq, own, send, tiles, cg)
    got[0] = swap_core(send[1])
    attend_back_at(3)
    dq, own, send, tiles, cg, wf_y0, wf_y1, wi_x0, wi_x1 = fence(
        dq, own, send, tiles, cg, wf_y0, wf_y1, wi_x0, wi_x1
    )
    got[2] = swap_core(send[3])
    wf_h0, wf_h1, wi_h0, wi_h1 = merge(
        [wf_m[0, 0], wf_m[1, 0], wi_m[0, 0], wi_m[0, 1]], [wf_y0, wf_y1, wi_x0, wi_x1]
    )
    wf_x1, wi_y1 = swap_x(wf_h1), swap_y(wi_h1)
    attend_back_at(0)
    dq, own, send, tiles, cg = fence(dq, own, send, tiles, cg)
    got[1] = swap_core(send[0])
    attend_back_at(2)
    dq, own, send, tiles, wf_x1, wi_y1, got = fence(dq, own, send, tiles, wf_x1, wi_y1, got)
    got[3] = swap_core(send[2])
    wf_r, wi_r = merge([wf_h0, wi_h0], [wf_x1, wi_y1])
    wf_far = [swap_z(wf_r[k], k) for k in others]
    wi_far = [swap_z(wi_r[k], k) for k in others]

    attn_grads = {}

    def project_back_at(r, total):
        total, outs = project_back(
            place, normed_t, mid_low_t, total, ctx[r], dq[r], own[r], got[r], attn_blocks[r], out_shapes
        )
        attn_grads[r] = block_parts(outs, depth, shard_rows)
        return total

    t_one = project_back_at(1, None)
    t_one, attn_grads, got = fence(t_one, attn_grads, got)
    came = {0: jax.tree.map(swap_core, attn_grads[1])}
    t_one = project_back_at(3, t_one)
    t_one, attn_grads, came = fence(t_one, attn_grads, came)
    came[2] = jax.tree.map(swap_core, attn_grads[3])
    t_one = project_back_at(0, t_one)
    t_one, attn_grads, came = fence(t_one, attn_grads, came)
    t_one = project_back_at(2, t_one)
    in_rows, gain_one_grad = finish(rows_in, gains, t_one, mid_grad)
    m00, m01, m10, m11 = merge([*attn_grads[0], *attn_grads[2]], [*came[0], *came[2]])
    m00, m01, m10, m11, in_rows, gain_one_grad = fence(m00, m01, m10, m11, in_rows, gain_one_grad)

    near_x0, near_x1 = swap_x(m10[:cut]), swap_x(m11[:cut])
    far_y0, far_y1 = swap_y(m01[cut:]), swap_y(m11[cut:])
    by_block = jnp.sum(bucket_sums([tiles[r] for r in range(4)]), -1)
    table_part = jnp.take(by_block, jnp.arange(4) ^ mp, axis=0).reshape(H * NB)
    near_x0, near_x1, far_y0, far_y1, table_part = fence(near_x0, near_x1, far_y0, far_y1, table_part)
    near_h0, near_h1, far_h0, far_h1 = merge(
        [m00[:cut], m01[:cut], m00[cut:], m10[cut:]], [near_x0, near_x1, far_y0, far_y1]
    )
    near_y1, far_x1 = swap_y(near_h1), swap_x(far_h1)
    wi_total = wi_r[0].astype(F32) + sum(v.astype(F32) for v in wi_far)
    wf_total = wf_r[0].astype(F32) + sum(v.astype(F32) for v in wf_far)
    ffn_squares = jnp.sum(wi_total * wi_total) + jnp.sum(wf_total * wf_total)
    small = jnp.concatenate([gain_one_grad[0], gain_two_grad[0], table_part])
    small = sum_all(small.reshape(-1, TILE)).reshape(-1)
    near_y1, far_x1, ffn_squares = fence(near_y1, far_x1, ffn_squares)
    near_r, far_r = merge([near_h0, far_h0], [near_y1, far_x1])
    attn_far = [swap_z((near_r if k < cut else far_r)[k % cut], k) for k in others]
    block_out = both_rows(out_rows[:part], swap_x(out_rows[part:]))
    input_grad = both_rows(in_rows[:part], swap_x(in_rows[part:]))
    attn_total = near_r[0].astype(F32) + sum(v.astype(F32) for v in attn_far)

    gain_total = small[: 2 * D].reshape(2, D)
    table_grads = small[2 * D :].reshape(H, NB)
    gain_cols = norm_gains.shape[1]
    gain_grads = lax.dynamic_slice_in_dim(gain_total, dp * gain_cols, gain_cols, 1)

    attn_reduced = jnp.transpose(attn_total.reshape(shard_rows, 4, WIDTH), (1, 0, 2))
    ffn_reduced = jnp.stack([wi_total, wf_total])
    squares = jnp.sum(attn_total * attn_total) + ffn_squares
    squares = sum_all(jnp.full((8, TILE), squares))[0, 0]
    grad_norm = jnp.sqrt(squares + jnp.sum(small * small))
    clip_factor = jnp.minimum(1.0, clip_level / (grad_norm + 1e-06))
    attn_new, attn_first_new, attn_second_new = adam_step(
        attn_weights, attn_first, attn_second, attn_reduced * clip_factor, rate_matrix, matrix_decay
    )
    ffn_new, ffn_first_new, ffn_second_new = adam_step(
        ffn_weights, ffn_first, ffn_second, ffn_reduced * clip_factor, rate_matrix, matrix_decay
    )
    gain_new, gain_first_new, gain_second_new = adam_step(
        norm_gains, gain_first, gain_second, gain_grads * clip_factor, rate_small, 0.0
    )
    table_new, table_first_new, table_second_new = adam_step(
        bias_table, table_first, table_second, table_grads * clip_factor, rate_small, 0.0
    )
    return (
        block_out,
        input_grad,
        attn_reduced,
        ffn_reduced,
        gain_grads,
        table_grads,
        grad_norm,
        attn_new,
        attn_first_new,
        attn_second_new,
        ffn_new,
        ffn_first_new,
        ffn_second_new,
        gain_new,
        gain_first_new,
        gain_second_new,
        table_new,
        table_first_new,
        table_second_new,
    )


def solution(mesh):
    placed = (
        P("dp", "mp", None),
        P("dp", "mp", None),
        P("dp"),
        P(None, "dp", "mp"),
        P(None, "dp", "mp"),
        P(None, "dp", "mp"),
        P(None, "dp", "mp"),
        P(None, "dp", "mp"),
        P(None, "dp", "mp"),
        P(None, "dp"),
        P(None, "dp"),
        P(None, "dp"),
        P(),
        P(),
        P(),
    )
    return jax.shard_map(
        per_device,
        mesh=mesh,
        in_specs=placed,
        out_specs=(
            P("dp", "mp", None),
            P("dp", "mp", None),
            P(None, "dp", "mp"),
            P(None, "dp", "mp"),
            P(None, "dp"),
            P(),
            P(),
            P(None, "dp", "mp"),
            P(None, "dp", "mp"),
            P(None, "dp", "mp"),
            P(None, "dp", "mp"),
            P(None, "dp", "mp"),
            P(None, "dp", "mp"),
            P(None, "dp"),
            P(None, "dp"),
            P(None, "dp"),
            P(),
            P(),
            P(),
        ),
        check_vma=False,
    )
```

time: 462 us -> 332 us (0.72)
  waiting for transfers between devices: 117 us -> 70.8 us
  Pallas kernels: 142 us -> 97.7 us
  blocking collectives: 32 us -> 0 us
  starting transfers between devices: 71.2 us -> 85.8 us
  other arithmetic: 30.2 us -> 19.7 us
  local copies, waits for them, and re-layouts: 57.9 us -> 47.4 us
    ppermute x12 -> x14, waiting for transfers between devices: 44.3 us -> 7.97 us  [swap_y(): return lax.ppermute(v, 'dp', [(i, i ^ 1) for i in range(n)])]
    pallas_call x10 -> x24, Pallas kernels: 116 us -> 81.9 us  [the longest x4 23.2 us: attend_back(): pl.pallas_call(functools.partial(attend_back_kernel, b), in_specs=[in_sme...]
    all_gather x1 -> x0, blocking collectives: 32 us -> none  [per_device(): gain_low = lax.all_gather(norm_gains.astype(BF), 'dp', axis=1, tiled=True)]
    ppermute x24 -> x27, waiting for transfers between devices: 62.2 us -> 32.2 us  [the longest x24 26.2 us: swap_z(): return lax.ppermute(v, 'dp', [(i, i ^ 2 * k) for i in range(n)])]
    ppermute x14 -> x18, waiting for transfers between devices: 10.4 us -> 29.5 us  [swap_x(): return lax.ppermute(v, 'mp', [(i, i ^ 2) for i in range(4)])]
    ppermute x24 -> x27, starting transfers between devices: 34.2 us -> 42 us  [the longest x24 40.1 us: swap_z(): return lax.ppermute(v, 'dp', [(i, i ^ 2 * k) for i in range(n)])]
    pallas_call x2, Pallas kernels: 11.1 us -> 4.44 us  [project(): pl.pallas_call(functools.partial(project_kernel, n_parts), in_specs=[in_s...]
    convert_element_type x19 -> x1, other arithmetic: 6.97 us -> 0.68 us  [spread_gains(): gains.astype(BF)]
  transfers between devices with their start and end apart: 86 -> 97, of which waited for: 27 -> 22; matrix products, arithmetic and copies ran while one was open for 9% -> 6% of each run, Pallas kernels for 22% -> 28%
where the time goes in v1:
time: 332 us; the launch traced here: 328 us
  Pallas kernels  97.7 us (29%)
  starting transfers between devices  85.8 us (26%)
  waiting for transfers between devices  70.8 us (21%)
  local copies, waits for them, and re-layouts  47.4 us (14%)
  other arithmetic  19.7 us (6%)
  between operations  6.87 us (2%)
    unnamed x222, local copies, waits for them, and re-layouts  40.1 us
    ppermute x24, starting transfers between devices, swap_z(): return lax.ppermute(v, 'dp', [(i, i ^ 2 * k) for i in range(n)])  40.1 us
    ppermute x18, waiting for transfers between devices, swap_x(): return lax.ppermute(v, 'mp', [(i, i ^ 2) for i in range(4)])  29.5 us
    ppermute x24, waiting for transfers between devices, swap_z(): return lax.ppermute(v, 'dp', [(i, i ^ 2 * k) for i in range(n)])  26.2 us
    pallas_call x4, Pallas kernels, attend_back(): pl.pallas_call(functools.partial(attend_back_kernel, b), in_specs=[in_sme...  23.2 us
    ppermute x18, starting transfers between devices, swap_x(): return lax.ppermute(v, 'mp', [(i, i ^ 2) for i in range(4)])  19 us
    pallas_call x4, Pallas kernels, feed(): pl.pallas_call(functools.partial(feed_kernel, n, first), in_specs=[in_sme...  18.6 us
    pallas_call x4, Pallas kernels, attend(): pl.pallas_call(functools.partial(attend_kernel, b, r_index), in_specs=[in...  18.5 us
  transfers between devices with their start and end apart: 97, of which 22 were waited for; matrix products, arithmetic and copies ran while one was open for 6% of the time, Pallas kernels for 28%

profile of v1, /device:TPU:0, one launch (start us, length us, event | category | flops | bytes accessed | tf_op | source)
XLA Modules:
  0.0 328.2 jit_solution(2586332972984487413)
XLA Ops:
  2.1 3.1 collective-permute-start
  5.2 2.6 collective-permute-start.1
  12.0 5.2 %bias_tiles.1.bias_ref = f32[4,3,5,128,128]{4,3,2,1,0:T(8,128)S(1)} custom-call(s32[12]{0:T(128)S(1)} %stack.123.place_ref, f32[12,32]{1,0:T(8,128)S(1)} %copy-done.92), custom_call_target="tpu_custom_call" | custom-call | flops 1000 | bytes 1000 | tf_op jit(solution)/shard_map/bias_tiles/pallas_call | solution.py:185
  23.1 2.3 collective-permute-start.13
  25.4 3.6 %collective-permute-done.6 = bf16[2,768]{1,0:T(2,128)(2,1)S(1)} collective-permute-done((bf16[2,768]{1,0:T(2,128)(2,1)S(1)}, bf16[2,768]{1,0:T(2,128)(2,1)S(1)}, u32[]{:S(2)}, u32[]{:S(2)}) %collective-permute-start.6) | collective-permute-done | bytes 3104 | tf_op jit(solution)/shard_map/ppermute | solution.py:116
  29.0 3.1 collective-permute-start.14
  35.6 5.1 %collective-permute-done.14 = bf16[96,768]{1,0:T(8,128)(2,1)S(1)} collective-permute-done((bf16[96,768]{1,0:T(8,128)(2,1)S(1)}, bf16[96,768]{1,0:T(8,128)(2,1)S(1)}, u32[]{:S(2)}, u32[]{:S(2)}) %collective-permute-start.14) | collective-permute-done | bytes 147488 | tf_op jit(solution)/shard_map/ppermute | solution.py:86
  42.8 2.5 collective-permute-done.11
  45.4 4.9 %collective-permute-done.24 = bf16[96,768]{1,0:T(8,128)(2,1)S(1)} collective-permute-done((bf16[96,768]{1,0:T(8,128)(2,1)S(1)}, bf16[96,768]{1,0:T(8,128)(2,1)S(1)}, u32[]{:S(2)}, u32[]{:S(2)}) %collective-permute-start.24) | collective-permute-done | bytes 147488 | tf_op jit(solution)/shard_map/ppermute | solution.py:86
  51.0 2.8 collective-permute-start.25
  55.7 8.4 %collective-permute-done.25 = bf16[96,768]{1,0:T(8,128)(2,1)S(1)} collective-permute-done((bf16[96,768]{1,0:T(8,128)(2,1)S(1)}, bf16[96,768]{1,0:T(8,128)(2,1)S(1)}, u32[]{:S(2)}, u32[]{:S(2)}) %collective-permute-start.25) | collective-permute-done | bytes 147488 | tf_op jit(solution)/shard_map/ppermute | solution.py:86
  65.2 2.2 project.2
  70.3 2.2 project.3
  74.8 17.1 %collective-permute-done.30 = bf16[256,768]{1,0:T(8,128)(2,1)S(1)} collective-permute-done((bf16[256,768]{1,0:T(8,128)(2,1)S(1)}, bf16[256,768]{1,0:T(8,128)(2,1)S(1)}, u32[]{:S(2)}, u32[]{:S(2)}) %collective-permute-start.30) | collective-permute-done | bytes 393248 | tf_op jit(solution)/shard_map/ppermute | solution.py:76
  93.5 4.6 %attend.4 = (bf16[512,192]{1,0:T(8,128)(2,1)S(1)}, bf16[3,512,1024]{2,1,0:T(8,128)(2,1)}) custom-call(s32[12]{0:T(128)S(1)} %stack.123.place_ref, bf16[2,512,192]{2,1,0:T(8,128)(2,1)S(1)} %get-tuple-element.486.q_ref, bf16[2,512,384]{2,1,0:T(8,128)(2,1)S(1)} %get-tuple-element.368.kv_ref, bf16[2,512,384]{2,1,0:T(8,128)(2,1)S(1)} %collective-permute-done.27.other_ref, ...), custom_call_target="tpu_custom_call" | custom-call | flops 1000 | bytes 1000 | tf_op jit(solution)/shard_map/attend/pallas_call | solution.py:295
  98.7 4.8 %attend.5 = (bf16[512,192]{1,0:T(8,128)(2,1)S(1)}, bf16[3,512,1024]{2,1,0:T(8,128)(2,1)}) custom-call(s32[12]{0:T(128)S(1)} %stack.123.place_ref, bf16[2,512,192]{2,1,0:T(8,128)(2,1)S(1)} %get-tuple-element.486.q_ref, bf16[2,512,384]{2,1,0:T(8,128)(2,1)S(1)} %get-tuple-element.368.kv_ref, bf16[2,512,384]{2,1,0:T(8,128)(2,1)S(1)} %collective-permute-done.27.other_ref, ...), custom_call_target="tpu_custom_call" | custom-call | flops 1000 | bytes 1000 | tf_op jit(solution)/shard_map/attend/pallas_call | solution.py:295
  103.6 4.6 %attend.6 = (bf16[512,192]{1,0:T(8,128)(2,1)S(1)}, bf16[3,512,1024]{2,1,0:T(8,128)(2,1)}) custom-call(s32[12]{0:T(128)S(1)} %stack.123.place_ref, bf16[2,512,192]{2,1,0:T(8,128)(2,1)S(1)} %get-tuple-element.399.q_ref, bf16[2,512,384]{2,1,0:T(8,128)(2,1)S(1)} %get-tuple-element.388.kv_ref, bf16[2,512,384]{2,1,0:T(8,128)(2,1)S(1)} %collective-permute-done.31.other_ref, ...), custom_call_target="tpu_custom_call" | custom-call | flops 1000 | bytes 1000 | tf_op jit(solution)/shard_map/attend/pallas_call | solution.py:295
  110.4 4.6 %attend.7 = (bf16[512,192]{1,0:T(8,128)(2,1)S(1)}, bf16[3,512,1024]{2,1,0:T(8,128)(2,1)}) custom-call(s32[12]{0:T(128)S(1)} %stack.123.place_ref, bf16[2,512,192]{2,1,0:T(8,128)(2,1)S(1)} %get-tuple-element.399.q_ref, bf16[2,512,384]{2,1,0:T(8,128)(2,1)S(1)} %get-tuple-element.388.kv_ref, bf16[2,512,384]{2,1,0:T(8,128)(2,1)S(1)} %collective-permute-done.31.other_ref, ...), custom_call_target="tpu_custom_call" | custom-call | flops 1000 | bytes 1000 | tf_op jit(solution)/shard_map/attend/pallas_call | solution.py:295
  115.6 2.1 middle.1
  117.7 4.6 %feed.4 = (f32[512,768]{1,0:T(8,128)S(1)}, f32[512,768]{1,0:T(8,128)S(1)}, bf16[4,96,768]{2,1,0:T(8,128)(2,1)S(1)}, bf16[4,96,768]{2,1,0:T(8,128)(2,1)S(1)}, bf1...) custom-call(s32[12]{0:T(128)S(1)} %stack.123.place_ref, bf16[512,768]{1,0:T(8,128)(2,1)S(1)} %get-tuple-element.409.n_ref, ...), custom_call_target="tpu_custom_call" | custom-call | flops 1000 | bytes 1000 | tf_op jit(solution)/shard_map/feed/pallas_call | solution.py:380
  127.0 4.7 %feed.5 = (f32[512,768]{1,0:T(8,128)S(1)}, f32[512,768]{1,0:T(8,128)S(1)}, bf16[4,96,768]{2,1,0:T(8,128)(2,1)S(1)}, bf16[4,96,768]{2,1,0:T(8,128)(2,1)S(1)}, bf1...) custom-call(s32[12]{0:T(128)S(1)} %stack.123.place_ref, ...), custom_call_target="tpu_custom_call", output_to_operand_aliasing={{0}: (5, {}), {1}: (6, {})} | custom-call | flops 1000 | bytes 1000 | tf_op jit(solution)/shard_map/feed/pallas_call | solution.py:380
  131.8 4.7 %feed.6 = (f32[512,768]{1,0:T(8,128)S(1)}, f32[512,768]{1,0:T(8,128)S(1)}, bf16[4,96,768]{2,1,0:T(8,128)(2,1)S(1)}, bf16[4,96,768]{2,1,0:T(8,128)(2,1)S(1)}, bf1...) custom-call(s32[12]{0:T(128)S(1)} %stack.123.place_ref, ...), custom_call_target="tpu_custom_call", output_to_operand_aliasing={{0}: (5, {}), {1}: (6, {})} | custom-call | flops 1000 | bytes 1000 | tf_op jit(solution)/shard_map/feed/pallas_call | solution.py:380
  139.1 4.7 %feed.7 = (f32[512,768]{1,0:T(8,128)S(1)}, f32[512,768]{1,0:T(8,128)S(1)}, bf16[4,96,768]{2,1,0:T(8,128)(2,1)S(1)}, bf16[4,96,768]{2,1,0:T(8,128)(2,1)S(1)}, bf1...) custom-call(s32[12]{0:T(128)S(1)} %stack.123.place_ref, ...), custom_call_target="tpu_custom_call", output_to_operand_aliasing={{0}: (5, {}), {1}: (6, {})} | custom-call | flops 1000 | bytes 1000 | tf_op jit(solution)/shard_map/feed/pallas_call | solution.py:380
  147.7 3.2 turn.1
  150.9 5.5 %attend_back.4 = (bf16[512,192]{1,0:T(8,128)(2,1)S(1)}, f32[512,384]{1,0:T(8,128)S(1)}, bf16[512,384]{1,0:T(8,128)(2,1)S(1)}, f32[3,5,128,128]{3,2,1,0:T(8,128)S(1)}) custom-call(s32[12]{0:T(128)S(1)} %stack.123.place_ref, bf16[2,512,192]{2,1,0:T(8,128)(2,1)S(1)} %get-tuple-element.486.q_ref, bf16[2,512,384]{2,1,0:T(8,128)(2,1)S(1)} %get-tuple-element.368.kv_ref, ...), custom_call_target="tpu_custom_call" | custom-call | flops 1000 | bytes 1000 | tf_op jit(solution)/shard_map/attend_back/pallas_call | solution.py:498
  157.3 5.5 %attend_back.5 = (bf16[512,192]{1,0:T(8,128)(2,1)S(1)}, f32[512,384]{1,0:T(8,128)S(1)}, bf16[512,384]{1,0:T(8,128)(2,1)S(1)}, f32[3,5,128,128]{3,2,1,0:T(8,128)S(1)}) custom-call(s32[12]{0:T(128)S(1)} %stack.123.place_ref, bf16[2,512,192]{2,1,0:T(8,128)(2,1)S(1)} %get-tuple-element.486.q_ref, bf16[2,512,384]{2,1,0:T(8,128)(2,1)S(1)} %get-tuple-element.368.kv_ref, ...), custom_call_target="tpu_custom_call" | custom-call | flops 1000 | bytes 1000 | tf_op jit(solution)/shard_map/attend_back/pallas_call | solution.py:498
  166.4 6.8 %collective-permute-done.56.refs_7_ = bf16[4,96,768]{2,1,0:T(8,128)(2,1)S(1)} collective-permute-done((bf16[4,96,768]{2,1,0:T(8,128)(2,1)S(1)}, bf16[4,96,768]{2,1,0:T(8,128)(2,1)S(1)}, u32[]{:S(2)}, u32[]{:S(2)}) %collective-permute-start.56) | collective-permute-done | bytes 589856 | tf_op jit(solution)/shard_map/ppermute | solution.py:76
  176.8 5.5 %attend_back.6 = (bf16[512,192]{1,0:T(8,128)(2,1)S(1)}, f32[512,384]{1,0:T(8,128)S(1)}, bf16[512,384]{1,0:T(8,128)(2,1)S(1)}, f32[3,5,128,128]{3,2,1,0:T(8,128)S(1)}) custom-call(s32[12]{0:T(128)S(1)} %stack.123.place_ref, bf16[2,512,192]{2,1,0:T(8,128)(2,1)S(1)} %get-tuple-element.399.q_ref, bf16[2,512,384]{2,1,0:T(8,128)(2,1)S(1)} %get-tuple-element.388.kv_ref, ...), custom_call_target="tpu_custom_call" | custom-call | flops 1000 | bytes 1000 | tf_op jit(solution)/shard_map/attend_back/pallas_call | solution.py:498
  183.8 6.7 %attend_back.7 = (bf16[512,192]{1,0:T(8,128)(2,1)S(1)}, f32[512,384]{1,0:T(8,128)S(1)}, bf16[512,384]{1,0:T(8,128)(2,1)}, f32[3,5,128,128]{3,2,1,0:T(8,128)S(1)}) custom-call(s32[12]{0:T(128)S(1)} %stack.123.place_ref, bf16[2,512,192]{2,1,0:T(8,128)(2,1)S(1)} %get-tuple-element.399.q_ref, bf16[2,512,384]{2,1,0:T(8,128)(2,1)S(1)} %get-tuple-element.388.kv_ref, ...), custom_call_target="tpu_custom_call" | custom-call | flops 1000 | bytes 1000 | tf_op jit(solution)/shard_map/attend_back/pallas_call | solution.py:498
  207.9 3.0 project_back.4
  211.5 2.1 select_bitcast_fusion.3
  217.2 5.4 %bucket_sums.1 = f32[4,3,32,128]{3,2,1,0:T(8,128)S(1)} custom-call(f32[3,5,128,128]{3,2,1,0:T(8,128)S(1)} %copy-done.55, f32[3,5,128,128]{3,2,1,0:T(8,128)S(1)} %copy-done.51, f32[3,5,128,128]{3,2,1,0:T(8,128)S(1)} %copy-done.57, f32[3,5,128,128]{3,2,1,0:T(8,128)S(1)} %copy-done.53), custom_call_target="tpu_custom_call" | custom-call | flops 1000 | bytes 1000 | tf_op jit(solution)/shard_map/bucket_sums/pallas_call | solution.py:538
  233.0 3.8 %project_back.5 = (f32[512,768]{1,0:T(8,128)S(1)}, bf16[4,96,768]{2,1,0:T(8,128)(2,1)}, bf16[4,96,768]{2,1,0:T(8,128)(2,1)}) custom-call(s32[12]{0:T(128)S(1)} %stack.123.place_ref, bf16[768,512]{1,0:T(8,128)(2,1)S(1)} %get-tuple-element.484.nt_ref, bf16[768,512]{1,0:T(8,128)(2,1)S(1)} %copy-done.4, ...), custom_call_target="tpu_custom_call", output_to_operand_aliasing={{0}: (7, {})} | custom-call | flops 1000 | bytes 1000 | tf_op jit(solution)/shard_map/project_back/pallas_call | solution.py:569
  240.7 2.1 collective-permute-start.76
  242.8 3.1 collective-permute-start.75
  251.1 2.5 project_back.6
  253.7 2.5 project_back.7
  257.0 2.1 merge.10
  261.5 2.1 collective-permute-start.79
  265.6 2.3 fusion.2
  269.2 2.6 collective-permute-start.78
  271.8 2.2 collective-permute-done.69.refs_5_
  279.7 2.3 fusion.3
  288.6 2.1 collective-permute-start.80
  297.0 5.3 %collective-permute-done.81 = bf16[96,768]{1,0:T(8,128)(2,1)S(1)} collective-permute-done((bf16[96,768]{1,0:T(8,128)(2,1)S(1)}, bf16[96,768]{1,0:T(8,128)(2,1)S(1)}, u32[]{:S(2)}, u32[]{:S(2)}) %collective-permute-start.81) | collective-permute-done | bytes 147488 | tf_op jit(solution)/shard_map/ppermute | solution.py:86
  308.6 2.9 collective-permute-done.93
  313.5 2.4 collective-permute-start.96
  321.6 2.4 multiply_subtract_fusion.1
  (463 shorter events, 130.7 us)
Async XLA Ops:
  2.1 17.6 %collective-permute-start = (bf16[96,768]{1,0:T(8,128)(2,1)S(1)}, bf16[96,768]{1,0:T(8,128)(2,1)S(1)}, u32[]{:S(2)}, u32[]{:S(2)}) collective-permute-start(bf16[96,768]{1,0:T(8,128)(2,1)S(1)} %reshape.92), channel_id=1, source_target_pairs={{0,8},{4,12},{8,0},{12,4},{16,24},{20,28},{24,16},{28,20},{1,9},{5... | collective-permute-start | bytes 442376 | tf_op jit(solution)/shard_map/ppermute | solution.py:86
  5.2 14.5 %collective-permute-start.1 = (bf16[96,768]{1,0:T(8,128)(2,1)S(1)}, bf16[96,768]{1,0:T(8,128)(2,1)S(1)}, u32[]{:S(2)}, u32[]{:S(2)}) collective-permute-start(bf16[96,768]{1,0:T(8,128)(2,1)S(1)} %reshape.92), channel_id=1, source_target_pairs={{0,16},{4,20},{8,24},{12,28},{16,0},{20,4},{24,8},{28,12},{1,17},{... | collective-permute-start | bytes 442376 | tf_op jit(solution)/shard_map/ppermute | solution.py:86
  7.8 12.0 %collective-permute-start.2 = (bf16[96,768]{1,0:T(8,128)(2,1)S(1)}, bf16[96,768]{1,0:T(8,128)(2,1)S(1)}, u32[]{:S(2)}, u32[]{:S(2)}) collective-permute-start(bf16[96,768]{1,0:T(8,128)(2,1)S(1)} %reshape.92), channel_id=1, source_target_pairs={{0,24},{4,28},{8,16},{12,20},{16,8},{20,12},{24,0},{28,4},{1,25},{... | collective-permute-start | bytes 442376 | tf_op jit(solution)/shard_map/ppermute | solution.py:86
  19.8 12.3 %collective-permute-start.4 = (bf16[2,96,768]{2,1,0:T(8,128)(2,1)S(1)}, bf16[2,96,768]{2,1,0:T(8,128)(2,1)S(1)}, u32[]{:S(2)}, u32[]{:S(2)}) collective-permute-start(bf16[2,96,768]{2,1,0:T(8,128)(2,1)S(1)} %pad_maximum_fusion.7.refs_0_.refs_4_.refs_1_), channel_id=1, source_target_pairs={{0,2},{1,3},{2,0},{3,1},{4,6},{5,7},{6,4},{7,5},{8,10},{9,11},{10,... | collective-permute-start | bytes 884744 | tf_op jit(solution)/shard_map/ppermute | solution.py:76
  21.4 12.1 %collective-permute-start.5 = (bf16[2,96,768]{2,1,0:T(8,128)(2,1)S(1)}, bf16[2,96,768]{2,1,0:T(8,128)(2,1)S(1)}, u32[]{:S(2)}, u32[]{:S(2)}) collective-permute-start(bf16[2,96,768]{2,1,0:T(8,128)(2,1)S(1)} %pad_maximum_fusion.8.refs_1_.refs_5_.refs_2_), channel_id=1, source_target_pairs={{0,4},{4,0},{8,12},{12,8},{16,20},{20,16},{24,28},{28,24},{1,5},{5... | collective-permute-start | bytes 884744 | tf_op jit(solution)/shard_map/ppermute | solution.py:81
  22.5 19.7 %collective-permute-start.12 = (bf16[256,768]{1,0:T(8,128)(2,1)S(1)}, bf16[256,768]{1,0:T(8,128)(2,1)S(1)}, u32[]{:S(2)}, u32[]{:S(2)}) collective-permute-start(bf16[256,768]{1,0:T(8,128)(2,1)S(1)} %get-tuple-element.675), channel_id=1, source_target_pairs={{0,2},{1,3},{2,0},{3,1},{4,6},{5,7},{6,4},{7,5},{8,10},{9,11},{10,... | collective-permute-start | bytes 1179656 | tf_op jit(solution)/shard_map/ppermute | solution.py:76
  29.0 11.7 %collective-permute-start.14 = (bf16[96,768]{1,0:T(8,128)(2,1)S(1)}, bf16[96,768]{1,0:T(8,128)(2,1)S(1)}, u32[]{:S(2)}, u32[]{:S(2)}) collective-permute-start(bf16[96,768]{1,0:T(8,128)(2,1)S(1)} %get-tuple-element.344), channel_id=1, source_target_pairs={{0,16},{4,20},{8,24},{12,28},{16,0},{20,4},{24,8},{28,12},{1,17},{... | collective-permute-start | bytes 442376 | tf_op jit(solution)/shard_map/ppermute | solution.py:86
  33.5 16.9 %collective-permute-start.7 = (bf16[2,96,768]{2,1,0:T(8,128)(2,1)S(1)}, bf16[2,96,768]{2,1,0:T(8,128)(2,1)S(1)}, u32[]{:S(2)}, u32[]{:S(2)}) collective-permute-start(bf16[2,96,768]{2,1,0:T(8,128)(2,1)S(1)} %pad_maximum_fusion.7.refs_0_.refs_4_.refs_1_), channel_id=1, source_target_pairs={{0,4},{4,0},{8,12},{12,8},{16,20},{20,16},{24,28},{28,24},{1,5},{5... | collective-permute-start | bytes 884744 | tf_op jit(solution)/shard_map/ppermute | solution.py:81
  34.1 16.8 %collective-permute-start.8 = (bf16[2,96,768]{2,1,0:T(8,128)(2,1)S(1)}, bf16[2,96,768]{2,1,0:T(8,128)(2,1)S(1)}, u32[]{:S(2)}, u32[]{:S(2)}) collective-permute-start(bf16[2,96,768]{2,1,0:T(8,128)(2,1)S(1)} %collective-permute-done.4.refs_4_.refs_12_.refs_8_.refs_1_), channel_id=1, source_target_pairs={{0,4},{4,0},{8,12},{12,8},{16,20},{20,16},{24,28},{28,24},{1,5},{5... | collective-permute-start | bytes 884744 | tf_op jit(solution)/shard_map/ppermute | solution.py:81
  42.2 11.5 %collective-permute-start.10 = (bf16[2,96,768]{2,1,0:T(8,128)(2,1)S(1)}, bf16[2,96,768]{2,1,0:T(8,128)(2,1)S(1)}, u32[]{:S(2)}, u32[]{:S(2)}) collective-permute-start(bf16[2,96,768]{2,1,0:T(8,128)(2,1)S(1)} %collective-permute-done.5.refs_3_.refs_7_.refs_4_), channel_id=1, source_target_pairs={{0,2},{1,3},{2,0},{3,1},{4,6},{5,7},{6,4},{7,5},{8,10},{9,11},{10,... | collective-permute-start | bytes 884744 | tf_op jit(solution)/shard_map/ppermute | solution.py:76
  50.4 14.2 %collective-permute-start.16 = (bf16[2,96,768]{2,1,0:T(8,128)(2,1)S(1)}, bf16[2,96,768]{2,1,0:T(8,128)(2,1)S(1)}, u32[]{:S(2)}, u32[]{:S(2)}) collective-permute-start(bf16[2,96,768]{2,1,0:T(8,128)(2,1)S(1)} %pad_maximum_fusion.7.refs_0_.refs_4_.refs_1_), channel_id=1, source_target_pairs={{0,1},{1,0},{2,3},{3,2},{4,5},{5,4},{6,7},{7,6},{8,9},{9,8},{10,11... | collective-permute-start | bytes 884744 | tf_op jit(solution)/shard_map/ppermute | solution.py:72
  50.4 14.3 %collective-permute-start.17 = (bf16[2,96,768]{2,1,0:T(8,128)(2,1)S(1)}, bf16[2,96,768]{2,1,0:T(8,128)(2,1)S(1)}, u32[]{:S(2)}, u32[]{:S(2)}) collective-permute-start(bf16[2,96,768]{2,1,0:T(8,128)(2,1)S(1)} %pad_maximum_fusion.8.refs_1_.refs_5_.refs_2_), channel_id=1, source_target_pairs={{0,1},{1,0},{2,3},{3,2},{4,5},{5,4},{6,7},{7,6},{8,9},{9,8},{10,11... | collective-permute-start | bytes 884744 | tf_op jit(solution)/shard_map/ppermute | solution.py:72
  50.9 14.2 %collective-permute-start.19 = (bf16[2,96,768]{2,1,0:T(8,128)(2,1)S(1)}, bf16[2,96,768]{2,1,0:T(8,128)(2,1)S(1)}, u32[]{:S(2)}, u32[]{:S(2)}) collective-permute-start(bf16[2,96,768]{2,1,0:T(8,128)(2,1)S(1)} %collective-permute-done.5.refs_3_.refs_7_.refs_4_), channel_id=1, source_target_pairs={{0,1},{1,0},{2,3},{3,2},{4,5},{5,4},{6,7},{7,6},{8,9},{9,8},{10,11... | collective-permute-start | bytes 884744 | tf_op jit(solution)/shard_map/ppermute | solution.py:72
  51.0 13.1 %collective-permute-start.25 = (bf16[96,768]{1,0:T(8,128)(2,1)S(1)}, bf16[96,768]{1,0:T(8,128)(2,1)S(1)}, u32[]{:S(2)}, u32[]{:S(2)}) collective-permute-start(bf16[96,768]{1,0:T(8,128)(2,1)S(1)} %get-tuple-element.354), channel_id=1, source_target_pairs={{0,16},{4,20},{8,24},{12,28},{16,0},{20,4},{24,8},{28,12},{1,17},{... | collective-permute-start | bytes 442376 | tf_op jit(solution)/shard_map/ppermute | solution.py:86
  68.1 25.3 %collective-permute-start.28 = (bf16[4,96,768]{2,1,0:T(8,128)(2,1)S(1)}, bf16[4,96,768]{2,1,0:T(8,128)(2,1)S(1)}, u32[]{:S(2)}, u32[]{:S(2)}) collective-permute-start(bf16[4,96,768]{2,1,0:T(8,128)(2,1)S(1)} %pad_maximum_fusion.4.refs_2_), channel_id=1, source_target_pairs={{0,2},{1,3},{2,0},{3,1},{4,6},{5,7},{6,4},{7,5},{8,10},{9,11},{10,... | collective-permute-start | bytes 1769480 | tf_op jit(solution)/shard_map/ppermute | solution.py:76
  69.7 22.2 %collective-permute-start.30 = (bf16[256,768]{1,0:T(8,128)(2,1)S(1)}, bf16[256,768]{1,0:T(8,128)(2,1)S(1)}, u32[]{:S(2)}, u32[]{:S(2)}) collective-permute-start(bf16[256,768]{1,0:T(8,128)(2,1)S(1)} %get-tuple-element.673), channel_id=1, source_target_pairs={{0,2},{1,3},{2,0},{3,1},{4,6},{5,7},{6,4},{7,5},{8,10},{9,11},{10,... | collective-permute-start | bytes 1179656 | tf_op jit(solution)/shard_map/ppermute | solution.py:76
  72.5 30.9 %collective-permute-start.31 = (bf16[2,512,384]{2,1,0:T(8,128)(2,1)S(1)}, bf16[2,512,384]{2,1,0:T(8,128)(2,1)S(1)}, u32[]{:S(2)}, u32[]{:S(2)}) collective-permute-start(bf16[2,512,384]{2,1,0:T(8,128)(2,1)S(1)} %get-tuple-element.368.kv_ref), channel_id=1, source_target_pairs={{0,1},{1,0},{2,3},{3,2},{4,5},{5,4},{6,7},{7,6},{8,9},{9,8},{10,11... | collective-permute-start | bytes 2359304 | tf_op jit(solution)/shard_map/ppermute | solution.py:72
  72.7 25.4 %collective-permute-start.29 = (bf16[4,96,768]{2,1,0:T(8,128)(2,1)S(1)}, bf16[4,96,768]{2,1,0:T(8,128)(2,1)S(1)}, u32[]{:S(2)}, u32[]{:S(2)}) collective-permute-start(bf16[4,96,768]{2,1,0:T(8,128)(2,1)S(1)} %pad_maximum_fusion.5.refs_4_), channel_id=1, source_target_pairs={{0,4},{4,0},{8,12},{12,8},{16,20},{20,16},{24,28},{28,24},{1,5},{5... | collective-permute-start | bytes 1769480 | tf_op jit(solution)/shard_map/ppermute | solution.py:81
  73.9 34.3 %collective-permute-start.32 = (bf16[4,96,768]{2,1,0:T(8,128)(2,1)S(1)}, bf16[4,96,768]{2,1,0:T(8,128)(2,1)S(1)}, u32[]{:S(2)}, u32[]{:S(2)}) collective-permute-start(bf16[4,96,768]{2,1,0:T(8,128)(2,1)S(1)} %pad_maximum_fusion.4.refs_2_), channel_id=1, source_target_pairs={{0,4},{4,0},{8,12},{12,8},{16,20},{20,16},{24,28},{28,24},{1,5},{5... | collective-permute-start | bytes 1769480 | tf_op jit(solution)/shard_map/ppermute | solution.py:81
  91.9 16.2 %collective-permute-start.33 = (bf16[4,96,768]{2,1,0:T(8,128)(2,1)S(1)}, bf16[4,96,768]{2,1,0:T(8,128)(2,1)S(1)}, u32[]{:S(2)}, u32[]{:S(2)}) collective-permute-start(bf16[4,96,768]{2,1,0:T(8,128)(2,1)S(1)} %pad_maximum_fusion.5.refs_4_), channel_id=1, source_target_pairs={{0,2},{1,3},{2,0},{3,1},{4,6},{5,7},{6,4},{7,5},{8,10},{9,11},{10,... | collective-permute-start | bytes 1769480 | tf_op jit(solution)/shard_map/ppermute | solution.py:76
  93.4 16.4 %collective-permute-start.34 = (bf16[4,96,768]{2,1,0:T(8,128)(2,1)S(1)}, bf16[4,96,768]{2,1,0:T(8,128)(2,1)S(1)}, u32[]{:S(2)}, u32[]{:S(2)}) collective-permute-start(bf16[4,96,768]{2,1,0:T(8,128)(2,1)S(1)} %pad_maximum_fusion.4.refs_2_), channel_id=1, source_target_pairs={{0,1},{1,0},{2,3},{3,2},{4,5},{5,4},{6,7},{7,6},{8,9},{9,8},{10,11... | collective-permute-start | bytes 1769480 | tf_op jit(solution)/shard_map/ppermute | solution.py:72
  98.1 16.9 %collective-permute-start.36 = (bf16[4,96,768]{2,1,0:T(8,128)(2,1)S(1)}, bf16[4,96,768]{2,1,0:T(8,128)(2,1)S(1)}, u32[]{:S(2)}, u32[]{:S(2)}) collective-permute-start(bf16[4,96,768]{2,1,0:T(8,128)(2,1)S(1)} %pad_maximum_fusion.5.refs_4_), channel_id=1, source_target_pairs={{0,1},{1,0},{2,3},{3,2},{4,5},{5,4},{6,7},{7,6},{8,9},{9,8},{10,11... | collective-permute-start | bytes 1769480 | tf_op jit(solution)/shard_map/ppermute | solution.py:72
  103.5 11.6 %collective-permute-start.37 = (bf16[4,96,768]{2,1,0:T(8,128)(2,1)S(1)}, bf16[4,96,768]{2,1,0:T(8,128)(2,1)S(1)}, u32[]{:S(2)}, u32[]{:S(2)}) collective-permute-start(bf16[4,96,768]{2,1,0:T(8,128)(2,1)S(1)} %collective-permute-done.29.refs_5_), channel_id=1, source_target_pairs={{0,1},{1,0},{2,3},{3,2},{4,5},{5,4},{6,7},{7,6},{8,9},{9,8},{10,11... | collective-permute-start | bytes 1769480 | tf_op jit(solution)/shard_map/ppermute | solution.py:72
  108.7 15.3 %collective-permute-start.38 = (bf16[4,96,768]{2,1,0:T(8,128)(2,1)S(1)}, bf16[4,96,768]{2,1,0:T(8,128)(2,1)S(1)}, u32[]{:S(2)}, u32[]{:S(2)}) collective-permute-start(bf16[4,96,768]{2,1,0:T(8,128)(2,1)S(1)} %collective-permute-done.28.refs_2_), channel_id=1, source_target_pairs={{0,4},{4,0},{8,12},{12,8},{16,20},{20,16},{24,28},{28,24},{1,5},{5... | collective-permute-start | bytes 1769480 | tf_op jit(solution)/shard_map/ppermute | solution.py:81
  109.8 15.0 %collective-permute-start.39 = (bf16[4,96,768]{2,1,0:T(8,128)(2,1)S(1)}, bf16[4,96,768]{2,1,0:T(8,128)(2,1)S(1)}, u32[]{:S(2)}, u32[]{:S(2)}) collective-permute-start(bf16[4,96,768]{2,1,0:T(8,128)(2,1)S(1)} %collective-permute-done.29.refs_5_), channel_id=1, source_target_pairs={{0,2},{1,3},{2,0},{3,1},{4,6},{5,7},{6,4},{7,5},{8,10},{9,11},{10,... | collective-permute-start | bytes 1769480 | tf_op jit(solution)/shard_map/ppermute | solution.py:76
  138.1 26.7 %collective-permute-start.53 = (bf16[4,96,768]{2,1,0:T(8,128)(2,1)S(1)}, bf16[4,96,768]{2,1,0:T(8,128)(2,1)S(1)}, u32[]{:S(2)}, u32[]{:S(2)}) collective-permute-start(bf16[4,96,768]{2,1,0:T(8,128)(2,1)S(1)} %get-tuple-element.513), channel_id=1, source_target_pairs={{0,4},{4,0},{8,12},{12,8},{16,20},{20,16},{24,28},{28,24},{1,5},{5... | collective-permute-start | bytes 1769480 | tf_op jit(solution)/shard_map/ppermute | solution.py:81
  144.3 22.1 %collective-permute-start.54 = (bf16[4,96,768]{2,1,0:T(8,128)(2,1)S(1)}, bf16[4,96,768]{2,1,0:T(8,128)(2,1)S(1)}, u32[]{:S(2)}, u32[]{:S(2)}) collective-permute-start(bf16[4,96,768]{2,1,0:T(8,128)(2,1)S(1)} %get-tuple-element.522), channel_id=1, source_target_pairs={{0,4},{4,0},{8,12},{12,8},{16,20},{20,16},{24,28},{28,24},{1,5},{5... | collective-permute-start | bytes 1769480 | tf_op jit(solution)/shard_map/ppermute | solution.py:81
  145.5 20.9 %collective-permute-start.55 = (bf16[4,96,768]{2,1,0:T(8,128)(2,1)S(1)}, bf16[4,96,768]{2,1,0:T(8,128)(2,1)S(1)}, u32[]{:S(2)}, u32[]{:S(2)}) collective-permute-start(bf16[4,96,768]{2,1,0:T(8,128)(2,1)S(1)} %get-tuple-element.523), channel_id=1, source_target_pairs={{0,2},{1,3},{2,0},{3,1},{4,6},{5,7},{6,4},{7,5},{8,10},{9,11},{10,... | collective-permute-start | bytes 1769480 | tf_op jit(solution)/shard_map/ppermute | solution.py:76
  146.0 27.1 %collective-permute-start.56 = (bf16[4,96,768]{2,1,0:T(8,128)(2,1)S(1)}, bf16[4,96,768]{2,1,0:T(8,128)(2,1)S(1)}, u32[]{:S(2)}, u32[]{:S(2)}) collective-permute-start(bf16[4,96,768]{2,1,0:T(8,128)(2,1)S(1)} %get-tuple-element.524), channel_id=1, source_target_pairs={{0,2},{1,3},{2,0},{3,1},{4,6},{5,7},{6,4},{7,5},{8,10},{9,11},{10,... | collective-permute-start | bytes 1769480 | tf_op jit(solution)/shard_map/ppermute | solution.py:76
  175.4 19.9 %collective-permute-start.57 = (bf16[4,96,768]{2,1,0:T(8,128)(2,1)S(1)}, bf16[4,96,768]{2,1,0:T(8,128)(2,1)S(1)}, u32[]{:S(2)}, u32[]{:S(2)}) collective-permute-start(bf16[4,96,768]{2,1,0:T(8,128)(2,1)S(1)} %get-tuple-element.563), channel_id=1, source_target_pairs={{0,2},{1,3},{2,0},{3,1},{4,6},{5,7},{6,4},{7,5},{8,10},{9,11},{10,... | collective-permute-start | bytes 1769480 | tf_op jit(solution)/shard_map/ppermute | solution.py:76
  175.9 19.4 %collective-permute-start.58 = (bf16[4,96,768]{2,1,0:T(8,128)(2,1)S(1)}, bf16[4,96,768]{2,1,0:T(8,128)(2,1)S(1)}, u32[]{:S(2)}, u32[]{:S(2)}) collective-permute-start(bf16[4,96,768]{2,1,0:T(8,128)(2,1)S(1)} %get-tuple-element.564), channel_id=1, source_target_pairs={{0,4},{4,0},{8,12},{12,8},{16,20},{20,16},{24,28},{28,24},{1,5},{5... | collective-permute-start | bytes 1769480 | tf_op jit(solution)/shard_map/ppermute | solution.py:81
  176.8 16.2 %collective-permute-start.59 = (bf16[512,384]{1,0:T(8,128)(2,1)S(1)}, bf16[512,384]{1,0:T(8,128)(2,1)S(1)}, u32[]{:S(2)}, u32[]{:S(2)}) collective-permute-start(bf16[512,384]{1,0:T(8,128)(2,1)S(1)} %get-tuple-element.503), channel_id=1, source_target_pairs={{0,1},{1,0},{2,3},{3,2},{4,5},{5,4},{6,7},{7,6},{8,9},{9,8},{10,11... | collective-permute-start | bytes 1179656 | tf_op jit(solution)/shard_map/ppermute | solution.py:72
  196.2 14.7 %collective-permute-start.62 = (bf16[512,384]{1,0:T(8,128)(2,1)}, bf16[512,384]{1,0:T(8,128)(2,1)}, u32[]{:S(2)}, u32[]{:S(2)}) collective-permute-start(bf16[512,384]{1,0:T(8,128)(2,1)} %get-tuple-element.575), channel_id=1, source_target_pairs={{0,1},{1,0},{2,3},{3,2},{4,5},{5,4},{6,7},{7,6},{8,9},{9,8},{10,11... | collective-permute-start | bytes 1179656 | tf_op jit(solution)/shard_map/ppermute | solution.py:72
  197.5 14.0 %collective-permute-start.52 = (bf16[256,768]{1,0:T(8,128)(2,1)}, bf16[256,768]{1,0:T(8,128)(2,1)}, u32[]{:S(2)}, u32[]{:S(2)}) collective-permute-start(bf16[256,768]{1,0:T(8,128)(2,1)} %slice.94), channel_id=1, source_target_pairs={{0,2},{1,3},{2,0},{3,1},{4,6},{5,7},{6,4},{7,5},{8,10},{9,11},{10,... | collective-permute-start | bytes 1179656 | tf_op jit(solution)/shard_map/ppermute | solution.py:76
  210.9 25.9 %collective-permute-start.63 = (bf16[4,96,768]{2,1,0:T(8,128)(2,1)}, bf16[4,96,768]{2,1,0:T(8,128)(2,1)}, u32[]{:S(2)}, u32[]{:S(2)}) collective-permute-start(bf16[4,96,768]{2,1,0:T(8,128)(2,1)} %get-tuple-element.582), channel_id=1, source_target_pairs={{0,1},{1,0},{2,3},{3,2},{4,5},{5,4},{6,7},{7,6},{8,9},{9,8},{10,11... | collective-permute-start | bytes 1769480 | tf_op jit(solution)/shard_map/ppermute | solution.py:72
  210.9 25.9 %collective-permute-start.64 = (bf16[4,96,768]{2,1,0:T(8,128)(2,1)}, bf16[4,96,768]{2,1,0:T(8,128)(2,1)}, u32[]{:S(2)}, u32[]{:S(2)}) collective-permute-start(bf16[4,96,768]{2,1,0:T(8,128)(2,1)} %get-tuple-element.583), channel_id=1, source_target_pairs={{0,1},{1,0},{2,3},{3,2},{4,5},{5,4},{6,7},{7,6},{8,9},{9,8},{10,11... | collective-permute-start | bytes 1769480 | tf_op jit(solution)/shard_map/ppermute | solution.py:72
  236.9 16.7 %collective-permute-start.65 = (bf16[4,96,768]{2,1,0:T(8,128)(2,1)}, bf16[4,96,768]{2,1,0:T(8,128)(2,1)}, u32[]{:S(2)}, u32[]{:S(2)}) collective-permute-start(bf16[4,96,768]{2,1,0:T(8,128)(2,1)} %get-tuple-element.590), channel_id=1, source_target_pairs={{0,1},{1,0},{2,3},{3,2},{4,5},{5,4},{6,7},{7,6},{8,9},{9,8},{10,11... | collective-permute-start | bytes 1769480 | tf_op jit(solution)/shard_map/ppermute | solution.py:72
  236.9 16.7 %collective-permute-start.66 = (bf16[4,96,768]{2,1,0:T(8,128)(2,1)}, bf16[4,96,768]{2,1,0:T(8,128)(2,1)}, u32[]{:S(2)}, u32[]{:S(2)}) collective-permute-start(bf16[4,96,768]{2,1,0:T(8,128)(2,1)} %get-tuple-element.591), channel_id=1, source_target_pairs={{0,1},{1,0},{2,3},{3,2},{4,5},{5,4},{6,7},{7,6},{8,9},{9,8},{10,11... | collective-permute-start | bytes 1769480 | tf_op jit(solution)/shard_map/ppermute | solution.py:72
  240.7 20.7 %collective-permute-start.76 = (bf16[96,768]{1,0:T(8,128)(2,1)S(1)}, bf16[96,768]{1,0:T(8,128)(2,1)S(1)}, u32[]{:S(2)}, u32[]{:S(2)}) collective-permute-start(bf16[96,768]{1,0:T(8,128)(2,1)S(1)} %get-tuple-element.680), channel_id=1, source_target_pairs={{0,24},{4,28},{8,16},{12,20},{16,8},{20,12},{24,0},{28,4},{1,25},{... | collective-permute-start | bytes 442376 | tf_op jit(solution)/shard_map/ppermute | solution.py:86
  242.8 20.7 %collective-permute-start.75 = (bf16[96,768]{1,0:T(8,128)(2,1)S(1)}, bf16[96,768]{1,0:T(8,128)(2,1)S(1)}, u32[]{:S(2)}, u32[]{:S(2)}) collective-permute-start(bf16[96,768]{1,0:T(8,128)(2,1)S(1)} %get-tuple-element.681), channel_id=1, source_target_pairs={{0,16},{4,20},{8,24},{12,28},{16,0},{20,4},{24,8},{28,12},{1,17},{... | collective-permute-start | bytes 442376 | tf_op jit(solution)/shard_map/ppermute | solution.py:86
  245.9 19.1 %collective-permute-start.74 = (bf16[96,768]{1,0:T(8,128)(2,1)S(1)}, bf16[96,768]{1,0:T(8,128)(2,1)S(1)}, u32[]{:S(2)}, u32[]{:S(2)}) collective-permute-start(bf16[96,768]{1,0:T(8,128)(2,1)S(1)} %get-tuple-element.679), channel_id=1, source_target_pairs={{0,8},{4,12},{8,0},{12,4},{16,24},{20,28},{24,16},{28,20},{1,9},{5... | collective-permute-start | bytes 442376 | tf_op jit(solution)/shard_map/ppermute | solution.py:86
  259.9 14.2 %collective-permute-start.69 = (bf16[2,96,768]{2,1,0:T(8,128)(2,1)S(1)}, bf16[2,96,768]{2,1,0:T(8,128)(2,1)S(1)}, u32[]{:S(2)}, u32[]{:S(2)}) collective-permute-start(bf16[2,96,768]{2,1,0:T(8,128)(2,1)S(1)} %get-tuple-element.683), channel_id=1, source_target_pairs={{0,2},{1,3},{2,0},{3,1},{4,6},{5,7},{6,4},{7,5},{8,10},{9,11},{10,... | collective-permute-start | bytes 884744 | tf_op jit(solution)/shard_map/ppermute | solution.py:76
  261.5 18.3 %collective-permute-start.79 = (bf16[96,768]{1,0:T(8,128)(2,1)S(1)}, bf16[96,768]{1,0:T(8,128)(2,1)S(1)}, u32[]{:S(2)}, u32[]{:S(2)}) collective-permute-start(bf16[96,768]{1,0:T(8,128)(2,1)S(1)} %get-tuple-element.677), channel_id=1, source_target_pairs={{0,24},{4,28},{8,16},{12,20},{16,8},{20,12},{24,0},{28,4},{1,25},{... | collective-permute-start | bytes 442376 | tf_op jit(solution)/shard_map/ppermute | solution.py:86
  263.5 12.3 %collective-permute-start.70 = (bf16[2,96,768]{2,1,0:T(8,128)(2,1)S(1)}, bf16[2,96,768]{2,1,0:T(8,128)(2,1)S(1)}, u32[]{:S(2)}, u32[]{:S(2)}) collective-permute-start(bf16[2,96,768]{2,1,0:T(8,128)(2,1)S(1)} %get-tuple-element.684), channel_id=1, source_target_pairs={{0,4},{4,0},{8,12},{12,8},{16,20},{20,16},{24,28},{28,24},{1,5},{5... | collective-permute-start | bytes 884744 | tf_op jit(solution)/shard_map/ppermute | solution.py:81
  264.9 12.5 %collective-permute-start.71 = (bf16[2,96,768]{2,1,0:T(8,128)(2,1)S(1)}, bf16[2,96,768]{2,1,0:T(8,128)(2,1)S(1)}, u32[]{:S(2)}, u32[]{:S(2)}) collective-permute-start(bf16[2,96,768]{2,1,0:T(8,128)(2,1)S(1)} %get-tuple-element.682), channel_id=1, source_target_pairs={{0,4},{4,0},{8,12},{12,8},{16,20},{20,16},{24,28},{28,24},{1,5},{5... | collective-permute-start | bytes 884744 | tf_op jit(solution)/shard_map/ppermute | solution.py:81
  287.7 14.5 %collective-permute-start.81 = (bf16[96,768]{1,0:T(8,128)(2,1)S(1)}, bf16[96,768]{1,0:T(8,128)(2,1)S(1)}, u32[]{:S(2)}, u32[]{:S(2)}) collective-permute-start(bf16[96,768]{1,0:T(8,128)(2,1)S(1)} %get-tuple-element.690), channel_id=1, source_target_pairs={{0,16},{4,20},{8,24},{12,28},{16,0},{20,4},{24,8},{28,12},{1,17},{... | collective-permute-start | bytes 442376 | tf_op jit(solution)/shard_map/ppermute | solution.py:86
  288.6 13.7 %collective-permute-start.80 = (bf16[96,768]{1,0:T(8,128)(2,1)S(1)}, bf16[96,768]{1,0:T(8,128)(2,1)S(1)}, u32[]{:S(2)}, u32[]{:S(2)}) collective-permute-start(bf16[96,768]{1,0:T(8,128)(2,1)S(1)} %slice_bitcast_fusion.4), channel_id=1, source_target_pairs={{0,8},{4,12},{8,0},{12,4},{16,24},{20,28},{24,16},{28,20},{1,9},{5... | collective-permute-start | bytes 442376 | tf_op jit(solution)/shard_map/ppermute | solution.py:86
  293.4 15.2 %collective-permute-start.67 = (bf16[256,768]{1,0:T(8,128)(2,1)S(1)}, bf16[256,768]{1,0:T(8,128)(2,1)S(1)}, u32[]{:S(2)}, u32[]{:S(2)}) collective-permute-start(bf16[256,768]{1,0:T(8,128)(2,1)S(1)} %slice.96), channel_id=1, source_target_pairs={{0,2},{1,3},{2,0},{3,1},{4,6},{5,7},{6,4},{7,5},{8,10},{9,11},{10,... | collective-permute-start | bytes 1179656 | tf_op jit(solution)/shard_map/ppermute | solution.py:76
  (160 other events, 2344.0 us)

commit v2 on v1

v2 whole, which is shorter than its diff:
```python
import functools

import jax
import jax.numpy as jnp
from jax import lax
from jax.experimental import pallas as pl
from jax.experimental.pallas import tpu as pltpu
from jax.sharding import PartitionSpec as P

H = 12
DH = 64
NB = 32
STEP = 10
D = 768

norm_eps = 1e-06
beta_one = 0.9
beta_two = 0.999
adam_eps = 1e-08
matrix_decay = 0.01
rate_matrix = 0.05
rate_small = 0.4
clip_level = 1.0

FEED_MIB = 18
BACK_MIB = 12
MERGE_MIB = 8

BF = jnp.bfloat16
F32 = jnp.float32
TILE = 128
GROUP = 3
WIDTH = GROUP * DH
NN = (((1,), (0,)), ((), ()))
NT = (((1,), (1,)), ((), ()))

shape_of = jax.ShapeDtypeStruct
in_smem = pl.BlockSpec(memory_space=pltpu.SMEM)
in_hbm = pl.BlockSpec(memory_space=pltpu.HBM)
in_vmem = pl.BlockSpec(memory_space=pltpu.VMEM)


def dot(left, right, dims):
    return lax.dot_general(left, right, dims, preferred_element_type=F32)


def params(mib):
    return pltpu.CompilerParams(vmem_limit_bytes=mib << 20)


def cost(flops, bytes_accessed, transcendentals=0):
    return pl.CostEstimate(flops=1000, bytes_accessed=1000, transcendentals=0)


def bucket_of(offset):
    distance = jnp.abs(offset)
    coarse = jnp.full(offset.shape, 8, jnp.int32)
    for level_bit in range(1, 8):
        coarse = coarse + (distance * distance >= 64 * 2**level_bit).astype(jnp.int32)
    inside = jnp.where(distance < 8, distance, coarse)
    return inside + jnp.where(offset > 0, 16, 0).astype(jnp.int32)


def adam_step(weight, first_old, second_old, gradient, step_rate, weight_decay):
    first_new = beta_one * first_old + (1.0 - beta_one) * gradient
    second_new = beta_two * second_old + (1.0 - beta_two) * gradient * gradient
    first_hat = first_new / (1.0 - beta_one**STEP)
    second_hat = second_new / (1.0 - beta_two**STEP)
    weight_new = weight - step_rate * (
        first_hat / (jnp.sqrt(second_hat) + adam_eps) + weight_decay * weight
    )
    return (weight_new, first_new, second_new)


def swap_core(v):
    return lax.ppermute(v, "mp", [(i, i ^ 1) for i in range(4)])


def swap_x(v):
    return lax.ppermute(v, "mp", [(i, i ^ 2) for i in range(4)])


def swap_y(v):
    n = lax.axis_size("dp")
    return lax.ppermute(v, "dp", [(i, i ^ 1) for i in range(n)])


def swap_z(v, k):
    n = lax.axis_size("dp")
    return lax.ppermute(v, "dp", [(i, i ^ (2 * k)) for i in range(n)])


def fence(*values):
    return lax.optimization_barrier(values)


def from_all(v):
    n = lax.axis_size("dp") * lax.axis_size("mp")
    return lax.all_to_all(jnp.broadcast_to(v[None], (n,) + v.shape), ("dp", "mp"), 0, 0)


def spread_gains(gains):
    count = gains.shape[1]
    start = lax.axis_index("dp") * count
    return lax.dynamic_update_slice(jnp.zeros((2, D), BF), gains.astype(BF), (0, start))


def join_gains(wide, step):
    n = lax.axis_size("dp")
    return wide + lax.ppermute(wide, "dp", [(i, i ^ step) for i in range(n)])


def block_views(by_y):
    which, rows, cols = by_y[0][0].shape[1:]
    if rows % 16 == 0:
        return [v for parts in by_y for v in parts]
    dp = lax.axis_index("dp")
    both = jnp.stack([jnp.concatenate(parts, 0) for parts in by_y])
    depth = both.shape[1]
    sides = jnp.take(both, jnp.arange(2) ^ (dp % 2), axis=0)
    lined = jnp.take(sides, jnp.arange(depth) ^ (dp // 2), axis=1)
    return [jnp.transpose(lined, (2, 1, 0, 3, 4)).reshape(1, which, D, cols)]


def grads_shape(depth, which, rows, cols):
    if rows % 16 == 0:
        return shape_of((2, 2, depth // 2, which, rows, cols), BF)
    return shape_of((1, 1, 1, which, D, cols), BF)


def by_place(grads, depth, rows):
    if rows % 16 == 0:
        return grads
    which = grads.shape[3]
    dp = lax.axis_index("dp")
    lined = jnp.transpose(grads.reshape(which, depth, 2, rows, -1), (2, 1, 0, 3, 4))
    sides = jnp.take(lined, jnp.arange(2) ^ (dp % 2), axis=0)
    turned = jnp.take(sides, jnp.arange(depth) ^ (dp // 2), axis=1)
    return turned.reshape(2, 2, depth // 2, which, rows, -1)


def assemble(whole, refs, place_ref, which=0, cols=slice(None)):
    count = 0
    for ref in refs:
        for j in range(ref.shape[0]):
            start = pl.multiple_of(place_ref[4 + count], 16)
            whole[pl.ds(start, ref.shape[2]), :] = ref[j, which, :, cols]
            count += 1


def deal_out(ref, whole, place_ref, which=0):
    count = 0
    for y in range(ref.shape[0]):
        for half in range(ref.shape[1]):
            for j in range(ref.shape[2]):
                start = pl.multiple_of(place_ref[4 + count], 16)
                ref[y, half, j, which] = whole[pl.ds(start, ref.shape[4]), :]
                count += 1


def bias_kernel(place_ref, table_ref, out_ref):
    block = pl.program_id(0)
    head_base = (place_ref[3] ^ block) * GROUP
    row = lax.broadcasted_iota(jnp.int32, (TILE, TILE), 0)
    col = lax.broadcasted_iota(jnp.int32, (TILE, TILE), 1)
    for h in range(GROUP):
        out_ref[0, h, 0] = jnp.full((TILE, TILE), table_ref[head_base + h, 15], F32)
        out_ref[0, h, 4] = jnp.full((TILE, TILE), table_ref[head_base + h, 31], F32)
    for t in range(1, 4):
        bucket = bucket_of(col - row + (t - 2) * TILE)
        which = {1: range(16), 2: range(32), 3: range(16, 32)}[t]
        for h in range(GROUP):
            tile = jnp.zeros((TILE, TILE), F32)
            for b in which:
                tile = jnp.where(bucket == b, table_ref[head_base + h, b], tile)
            out_ref[0, h, t] = tile


def make_bias(place, table):
    return pl.pallas_call(
        bias_kernel,
        grid=(4,),
        in_specs=[in_smem, in_smem],
        out_specs=pl.BlockSpec((1, GROUP, 5, TILE, TILE), lambda i: (i, 0, 0, 0, 0)),
        out_shape=shape_of((4, GROUP, 5, TILE, TILE), F32),
        compiler_params=params(6),
        cost_estimate=cost(10e6, 4e6),
        name="bias_tiles",
    )(place, table)


def rms_of(v, gain):
    inverse = lax.rsqrt(jnp.mean(v * v, axis=-1, keepdims=True) + norm_eps)
    return v * inverse * gain


def rms_back(v, gain, t):
    inverse = lax.rsqrt(jnp.mean(v * v, axis=-1, keepdims=True) + norm_eps)
    along = jnp.mean(v * gain * t, axis=-1, keepdims=True)
    grad = inverse * gain * t - v * (inverse * inverse * inverse) * along
    return grad, jnp.sum(t * v * inverse, axis=0, keepdims=True)


def project_kernel(n_parts, place_ref, x_ref, gain_ref, *refs):
    w_refs, rest = refs[: 2 * n_parts], refs[2 * n_parts :]
    q_ref, kv_ref = rest[:2]
    whole = rest[-1]
    normed = rms_of(x_ref[...].astype(F32), gain_ref[0:1].astype(F32)).astype(BF)
    if len(rest) == 4:
        rest[2][...] = normed.T
    for b in range(2):
        assemble(whole.at[b], w_refs[b * n_parts : (b + 1) * n_parts], place_ref)
        out = dot(normed, whole[b, :, 0:640], NN).astype(BF)
        q_ref[b] = out[:, 0:WIDTH]
        keys, values = out[:, WIDTH : 2 * WIDTH], out[:, 2 * WIDTH : 3 * WIDTH]
        kv_ref[b] = jnp.concatenate([keys, values], 1)


def project(place, rows_in, gain_low, blocks, turned):
    rows = rows_in.shape[0]
    n_parts = len(blocks[0])
    shapes = [shape_of((2, rows, WIDTH), BF), shape_of((2, rows, 2 * WIDTH), BF)]
    if turned:
        shapes.append(shape_of((D, rows), BF))
    return pl.pallas_call(
        functools.partial(project_kernel, n_parts),
        in_specs=[in_smem] + [in_vmem] * (2 + 2 * n_parts),
        out_specs=[in_vmem] * len(shapes),
        out_shape=shapes,
        scratch_shapes=[pltpu.VMEM((2, D, D), BF)],
        compiler_params=params(8),
        cost_estimate=cost(2 * 2 * rows * D * 576, 5e6),
        name="project",
    )(place, rows_in, gain_low, *blocks[0], *blocks[1])


def tile_places(place_ref):
    x, core = place_ref[0], place_ref[1]
    mine = [4 * (x if t < 2 else 1 - x) + 2 * core + t % 2 for t in range(4)]
    theirs = [4 * (x if t < 2 else 1 - x) + 2 * (1 - core) + t % 2 for t in range(4)]
    return mine, mine + theirs


def attend_kernel(
    b, r_index, place_ref, q_ref, kv_ref, other_ref, bias_ref, ctx_ref, p_out, p_ref, sems
):
    rows = q_ref.shape[1]
    step = 256
    lane = lax.broadcasted_iota(jnp.int32, (1, 256), 1)
    key = lax.broadcasted_iota(jnp.int32, (1, TILE), 1)
    sub = lax.broadcasted_iota(jnp.int32, (64, 1), 0)
    row_tiles, key_tiles = tile_places(place_ref)
    length = place_ref[2]
    hide = jnp.concatenate([jnp.where(key + TILE * g < length, 0.0, -1e30) for g in key_tiles], 1)
    extra = jnp.where(sub == 0, hide, 0.0).astype(BF)
    both = jnp.concatenate([kv_ref[b], other_ref[b]], 0)
    keys_t = jnp.concatenate([both[:, :WIDTH].T, extra], 0)
    values = both[:, WIDTH:]
    queries = jnp.concatenate([q_ref[b], jnp.ones((rows, 64), BF)], 1)
    total = [jnp.zeros((step, WIDTH), F32) for _ in range(rows // step)]
    for h in range(GROUP):
        inside = (lane >= h * DH) & (lane < (h + 1) * DH)
        used = inside | (lane == WIDTH)
        for r in range(rows // step):
            here = jnp.where(used, queries[r * step : (r + 1) * step], jnp.zeros((), BF))
            scores = dot(here, keys_t, NN)
            tiles = []
            for c in range(8):
                bias = []
                for u in range(step // TILE):
                    which = jnp.clip(key_tiles[c] - row_tiles[r * (step // TILE) + u] + 2, 0, 4)
                    bias.append(bias_ref[r_index, h, which])
                tiles.append(scores[:, c * TILE : (c + 1) * TILE] + jnp.concatenate(bias, 0))
            top = jnp.max(functools.reduce(jnp.maximum, tiles), axis=-1, keepdims=True)
            exps = [jnp.exp(t - top) for t in tiles]
            norm = jnp.sum(functools.reduce(jnp.add, exps), axis=-1, keepdims=True)
            scale = 1.0 / norm
            prob = jnp.concatenate([(e * scale).astype(BF) for e in exps], 1)
            p_ref[h, pl.ds(r * step, step), :] = prob
            total[r] = jnp.where(inside[:, :WIDTH], dot(prob, values, NN), total[r])
        pltpu.make_async_copy(p_ref.at[h], p_out.at[h], sems.at[h]).start()
    for r in range(rows // step):
        ctx_ref[pl.ds(r * step, step), :] = total[r].astype(BF)
    for h in range(GROUP):
        pltpu.make_async_copy(p_ref.at[h], p_out.at[h], sems.at[h]).wait()


def attend(place, q, kv, other, bias, b, r_index):
    rows = q.shape[1]
    return pl.pallas_call(
        functools.partial(attend_kernel, b, r_index),
        in_specs=[in_smem] + [in_vmem] * 4,
        out_specs=[in_vmem, in_hbm],
        out_shape=[shape_of((rows, WIDTH), BF), pltpu.HBM((GROUP, rows, 2 * rows), BF)],
        scratch_shapes=[
            pltpu.VMEM((GROUP, rows, 2 * rows), BF),
            pltpu.SemaphoreType.DMA((GROUP,)),
        ],
        compiler_params=params(12),
        cost_estimate=cost(GROUP * rows * 2 * rows * 256 * 8, 6e6, GROUP * rows * 2 * rows),
        name="attend",
    )(place, q, kv, other, bias)


def middle_kernel(n_parts, place_ref, x_ref, gain_ref, back_ref, *refs):
    ctx_refs, w_refs = refs[:4], refs[4 : 4 + 4 * n_parts]
    mid_ref, normed_ref, normed_t_ref, back_t_ref, whole = refs[4 + 4 * n_parts :]
    rows = x_ref.shape[0]
    total = x_ref[...].astype(F32)
    back_t_ref[...] = back_ref[...].T
    blank = jnp.zeros((rows, 64), BF)
    for b in range(4):
        part = w_refs[b * n_parts : (b + 1) * n_parts]
        assemble(whole.at[b], part, place_ref, 0, slice(512, 768))
        total = total + dot(jnp.concatenate([blank, ctx_refs[b][...]], 1), whole[b], NT)
    mid_ref[...] = total
    normed = rms_of(total, gain_ref[1:2].astype(F32)).astype(BF)
    normed_ref[...] = normed
    normed_t_ref[...] = normed.T


def middle(place, rows_in, gain_low, back, ctx, blocks):
    rows = rows_in.shape[0]
    n_parts = len(blocks[0])
    return pl.pallas_call(
        functools.partial(middle_kernel, n_parts),
        in_specs=[in_smem] + [in_vmem] * (7 + 4 * n_parts),
        out_specs=[in_vmem] * 4,
        out_shape=[
            shape_of((rows, D), F32),
            shape_of((rows, D), BF),
            shape_of((D, rows), BF),
            shape_of((D, rows), BF),
        ],
        scratch_shapes=[pltpu.VMEM((4, D, 256), BF)],
        compiler_params=params(10),
        cost_estimate=cost(2 * rows * D * D, 8e6),
        name="middle",
    )(place, rows_in, gain_low, back, *ctx, *[p for b in blocks for p in b])


def feed_kernel(n_parts, first, place_ref, n_ref, nt_ref, g_ref, gt_ref, *refs):
    if not first:
        acc_in, t_in = refs[:2]
        refs = refs[2:]
    w_refs, (acc_ref, t_ref, grads_ref, wi, wf, gi, gf) = refs[:n_parts], refs[n_parts:]
    assemble(wi, w_refs, place_ref, 0)
    assemble(wf, w_refs, place_ref, 1)
    pre = dot(n_ref[...], wi[...], NN)
    grad = dot(g_ref[...], wf[...], NN)
    cdf = 0.5 * (1.0 + lax.erf(pre * 0.7071067811865476))
    active = (pre * cdf).astype(BF)
    density = jnp.exp(pre * pre * -0.5) * 0.3989422804014327
    pre_grad = (grad * (cdf + pre * density)).astype(BF)
    if first:
        acc_ref[...] = dot(active, wf[...], NT)
        t_ref[...] = dot(pre_grad, wi[...], NT)
    else:
        acc_ref[...] = acc_in[...] + dot(active, wf[...], NT)
        t_ref[...] = t_in[...] + dot(pre_grad, wi[...], NT)
    gi[...] = dot(nt_ref[...], pre_grad, NN).astype(BF)
    deal_out(grads_ref, gi, place_ref, 0)
    gf[...] = dot(gt_ref[...], active, NN).astype(BF)
    deal_out(grads_ref, gf, place_ref, 1)


def feed(place, normed, normed_t, back, back_t, sums, block, grads):
    rows = normed.shape[0]
    n = len(block)
    first = sums is None
    outs = pl.pallas_call(
        functools.partial(feed_kernel, n, first),
        in_specs=[in_smem] + [in_vmem] * (4 + n + (0 if first else 2)),
        out_specs=[in_vmem] * 3,
        out_shape=[shape_of((rows, D), F32)] * 2 + [grads],
        scratch_shapes=[pltpu.VMEM((D, D), BF)] * 4,
        input_output_aliases={} if first else {5: 0, 6: 1},
        compiler_params=params(14),
        cost_estimate=cost(2 * 6 * rows * D * D, 15e6, 2 * rows * D),
        name="feed",
    )(place, normed, normed_t, back, back_t, *(sums or ()), *block)
    return (outs[0], outs[1]), outs[2]


def turn_kernel(n_parts, place_ref, mid_ref, acc_ref, t_ref, back_ref, gain_ref, *refs):
    w_refs = refs[: 4 * n_parts]
    rest = refs[4 * n_parts :]
    keep_ref, send_ref, grad_ref, low_t_ref, gain_grad_ref = rest[:5]
    cg_refs, whole = rest[5:9], rest[9]
    mid = mid_ref[...]
    out = (mid + acc_ref[...]).astype(BF)
    half = keep_ref.shape[0]
    keep_ref[...], send_ref[...] = out[:half], out[half:]
    grad, gain_grad = rms_back(mid, gain_ref[1:2].astype(F32), t_ref[...])
    gain_grad_ref[...] = gain_grad
    grad = back_ref[...].astype(F32) + grad
    grad_ref[...] = grad
    low = grad.astype(BF)
    low_t_ref[...] = low.T
    for b in range(4):
        part = w_refs[b * n_parts : (b + 1) * n_parts]
        assemble(whole.at[b], part, place_ref, 0, slice(512, 768))
        cg_refs[b][...] = dot(low, whole[b], NN).astype(BF)[:, 64:]


def turn(place, mid, acc, t_acc, back, gain_low, blocks):
    rows = mid.shape[0]
    n_parts = len(blocks[0])
    return pl.pallas_call(
        functools.partial(turn_kernel, n_parts),
        in_specs=[in_smem] + [in_vmem] * (5 + 4 * n_parts),
        out_specs=[in_vmem] * 9,
        out_shape=[
            shape_of((rows // 2, D), BF),
            shape_of((rows // 2, D), BF),
            shape_of((rows, D), F32),
            shape_of((D, rows), BF),
            shape_of((1, D), F32),
        ]
        + [shape_of((rows, WIDTH), BF)] * 4,
        scratch_shapes=[pltpu.VMEM((4, D, 256), BF)],
        compiler_params=params(12),
        cost_estimate=cost(2 * rows * D * D, 10e6),
        name="turn",
    )(place, mid, acc, t_acc, back, gain_low, *[p for b in blocks for p in b])


def attend_back_kernel(
    b,
    place_ref,
    q_ref,
    kv_ref,
    other_ref,
    g_ref,
    ctx_ref,
    p_ref,
    dq_ref,
    own_ref,
    send_ref,
    sums_ref,
    ds_ref,
):
    rows = q_ref.shape[1]
    step = 128
    lane = lax.broadcasted_iota(jnp.int32, (1, WIDTH), 1)
    row_tiles, key_tiles = tile_places(place_ref)
    grads = g_ref[...]
    both = jnp.concatenate([kv_ref[b], other_ref[b]], 0)
    keys = both[:, :WIDTH]
    values_t = both[:, WIDTH:].T
    queries_t, grads_t = q_ref[b].T, grads.T
    product = grads.astype(F32) * ctx_ref[...].astype(F32)
    sums_ref[...] = jnp.zeros_like(sums_ref)
    total = [jnp.zeros((step, WIDTH), F32) for _ in range(rows // step)]
    key_grads, value_grads = [], []
    for h in range(GROUP):
        inside = (lane >= h * DH) & (lane < (h + 1) * DH)
        for r in range(rows // step):
            span = slice(r * step, (r + 1) * step)
            here = jnp.where(inside, grads[span], jnp.zeros((), BF))
            prob_grad = dot(here, values_t, NN)
            row_dot = jnp.sum(jnp.where(inside, product[span], 0.0), axis=-1, keepdims=True)
            lows = []
            for c in range(8):
                prob = p_ref[h, pl.ds(r * step, step), pl.ds(c * TILE, TILE)].astype(F32)
                dscore = prob * (prob_grad[:, c * TILE : (c + 1) * TILE] - row_dot)
                which = jnp.clip(key_tiles[c] - row_tiles[r] + 2, 0, 4)
                sums_ref[h, which] += dscore
                lows.append(dscore.astype(BF))
            low = jnp.concatenate(lows, 1)
            ds_ref[pl.ds(r * step, step), :] = low
            total[r] = jnp.where(inside, dot(low, keys, NN), total[r])
        key_grads.append(dot(queries_t[h * DH : (h + 1) * DH], ds_ref[...], NN))
        value_grads.append(dot(grads_t[h * DH : (h + 1) * DH], p_ref[h], NN))
    for r in range(rows // step):
        dq_ref[pl.ds(r * step, step), :] = total[r].astype(BF)
    grad = jnp.concatenate(key_grads + value_grads, 0).T
    own_ref[...] = grad[:rows]
    send_ref[...] = grad[rows:].astype(BF)


def attend_back(place, q, kv, other, grads, ctx, prob, b):
    rows = q.shape[1]
    return pl.pallas_call(
        functools.partial(attend_back_kernel, b),
        in_specs=[in_smem] + [in_vmem] * 6,
        out_specs=[in_vmem] * 4,
        out_shape=[
            shape_of((rows, WIDTH), BF),
            shape_of((rows, 2 * WIDTH), F32),
            shape_of((rows, 2 * WIDTH), BF),
            shape_of((GROUP, 5, TILE, TILE), F32),
        ],
        scratch_shapes=[
            pltpu.VMEM((rows, 2 * rows), BF),
        ],
        compiler_params=params(8),
        cost_estimate=cost(GROUP * rows * 2 * rows * 256 * 12, 8e6),
        name="attend_back",
    )(place, q, kv, other, grads, ctx, prob)


def bucket_kernel(place_ref, *refs):
    out_ref = refs[-1]
    row = lax.broadcasted_iota(jnp.int32, (TILE, TILE), 0)
    col = lax.broadcasted_iota(jnp.int32, (TILE, TILE), 1)
    buckets = {t: bucket_of(col - row + (t - 2) * TILE) for t in range(1, 4)}
    for r in range(4):
        for h in range(GROUP):
            for b in range(NB):
                total = jnp.zeros((TILE, TILE), F32)
                if b == 15:
                    total = refs[r][h, 0]
                if b == 31:
                    total = refs[r][h, 4]
                for t in (1, 2) if b < 16 else (2, 3):
                    total = total + jnp.where(buckets[t] == b, refs[r][h, t], 0.0)
                total = jnp.sum(total, axis=0, keepdims=True)
                out_ref[place_ref[3] ^ r, h, pl.ds(b, 1), :] = total


def bucket_sums(place, sums):
    return pl.pallas_call(
        bucket_kernel,
        in_specs=[in_smem] + [in_vmem] * 4,
        out_specs=in_vmem,
        out_shape=shape_of((4, GROUP, NB, TILE), F32),
        compiler_params=params(4),
        cost_estimate=cost(32e6, 4e6),
        name="bucket_sums",
    )(place, *sums)


def project_back_kernel(n_parts, first, place_ref, nt_ref, low_t_ref, ctx_ref, dq_ref, own_ref, came_ref, *refs):
    if not first:
        acc_in, refs = refs[0], refs[1:]
    w_refs, (acc_ref, grads_ref, whole, grad) = refs[:n_parts], refs[n_parts:]
    assemble(whole, w_refs, place_ref)
    dkv = (own_ref[...] + came_ref[...].astype(F32)).astype(BF)
    heads = jnp.concatenate([dq_ref[...], dkv], 1)
    out = dot(nt_ref[...], heads, NN).astype(BF)
    last = dot(low_t_ref[...], ctx_ref[...], NN).astype(BF)
    grad[...] = jnp.concatenate([out, last], 1)
    deal_out(grads_ref, grad, place_ref)
    total = dot(heads, whole[:, 0:576], NT)
    acc_ref[...] = total if first else acc_in[...] + total


def project_back(place, normed_t, low_t, acc, ctx, dq, own, came, block, grads):
    rows = normed_t.shape[1]
    n = len(block)
    first = acc is None
    outs = pl.pallas_call(
        functools.partial(project_back_kernel, n, first),
        in_specs=[in_smem] + [in_vmem] * (6 + n + (0 if first else 1)),
        out_specs=[in_vmem] * 2,
        out_shape=[shape_of((rows, D), F32), grads],
        scratch_shapes=[pltpu.VMEM((D, D), BF)] * 2,
        input_output_aliases={} if first else {7: 0},
        compiler_params=params(8),
        cost_estimate=cost(2 * 2 * rows * D * D, 8e6),
        name="project_back",
    )(place, normed_t, low_t, ctx, dq, own, came, *([] if first else [acc]), *block)
    return outs


def add(a, b):
    return (a.astype(F32) + b.astype(F32)).astype(BF)


def merge_core_kernel(a_ref, b_ref, near_ref, far0_ref, far1_ref):
    for y, far_ref in enumerate((far0_ref, far1_ref)):
        near_ref[y] = add(a_ref[y, 0], b_ref[y, 0])
        far_ref[...] = add(a_ref[y, 1], b_ref[y, 1])


def merge_core(grads, came):
    part = shape_of(grads.shape[2:], BF)
    return pl.pallas_call(
        merge_core_kernel,
        in_specs=[in_vmem] * 2,
        out_specs=[in_vmem] * 3,
        out_shape=[shape_of(grads.shape[:1] + grads.shape[2:], BF), part, part],
        compiler_params=params(MERGE_MIB),
        cost_estimate=cost(1, 1),
        name="merge_core",
    )(grads, came)


def merge_half_kernel(near_ref, came_ref, a0_ref, b0_ref, a1_ref, b1_ref, y0_ref, y1_ref, x0_ref, x1_ref):
    y0_ref[...] = add(near_ref[0], came_ref[0])
    y1_ref[...] = add(near_ref[1], came_ref[1])
    x0_ref[...] = add(a0_ref[...], b0_ref[...])
    x1_ref[...] = add(a1_ref[...], b1_ref[...])


def merge_half(near, near_came, far, far_came):
    part = shape_of(near.shape[1:], BF)
    return pl.pallas_call(
        merge_half_kernel,
        in_specs=[in_vmem] * 6,
        out_specs=[in_vmem] * 4,
        out_shape=[part] * 4,
        compiler_params=params(MERGE_MIB),
        cost_estimate=cost(1, 1),
        name="merge_half",
    )(near, near_came, far[0], far_came[0], far[1], far_came[1])


def merge_last_kernel(near_ref, near_came_ref, far_ref, far_came_ref, own_ref, *outs):
    cut = near_ref.shape[0]
    own_ref[...] = near_ref[0].astype(F32) + near_came_ref[0].astype(F32)
    for k, out_ref in enumerate(outs, 1):
        a_ref, b_ref = (near_ref, near_came_ref) if k < cut else (far_ref, far_came_ref)
        out_ref[...] = add(a_ref[k % cut], b_ref[k % cut])


def merge_last(near, near_came, far, far_came):
    cut = near.shape[0]
    part = near.shape[1:]
    return pl.pallas_call(
        merge_last_kernel,
        in_specs=[in_vmem] * 4,
        out_specs=[in_vmem] * (2 * cut),
        out_shape=[shape_of(part, F32)] + [shape_of(part, BF)] * (2 * cut - 1),
        compiler_params=params(MERGE_MIB),
        cost_estimate=cost(1, 1),
        name="merge_last",
    )(near, near_came, far, far_came)


def total_kernel(own_ref, *refs):
    out_ref, squares_ref = refs[-2:]
    total = own_ref[...]
    for ref in refs[:-2]:
        total = total + ref[...].astype(F32)
    out_ref[...] = total
    squares_ref[...] = jnp.broadcast_to(jnp.sum(total * total), squares_ref.shape)


def total_of(own, came):
    return pl.pallas_call(
        total_kernel,
        in_specs=[in_vmem] * (1 + len(came)),
        out_specs=[in_vmem] * 2,
        out_shape=[shape_of(own.shape, F32), shape_of((1, TILE), F32)],
        compiler_params=params(MERGE_MIB),
        cost_estimate=cost(1, 1),
        name="total",
    )(own, *came)


def cast_attn_kernel(w_ref, out_ref):
    out_ref[0] = jnp.concatenate([w_ref[i].astype(BF) for i in range(4)], 1)


def cast_attn(weights):
    rows = weights.shape[1]
    return pl.pallas_call(
        cast_attn_kernel,
        in_specs=[in_vmem],
        out_specs=in_vmem,
        out_shape=shape_of((1, rows, D), BF),
        compiler_params=params(MERGE_MIB),
        cost_estimate=cost(1, 1),
        name="cast_attn",
    )(weights)


def sort_kernel(place_ref, in_ref, back_ref, in_keep, in_send, back_keep, back_send):
    here = place_ref[0]
    in_keep[...], in_send[...] = in_ref[here], in_ref[1 - here]
    back_keep[...], back_send[...] = back_ref[here], back_ref[1 - here]


def sort_rows(place, inputs, cotangent):
    part = shape_of(inputs.shape[1:], BF)
    return pl.pallas_call(
        sort_kernel,
        in_specs=[in_smem] + [in_vmem] * 2,
        out_specs=[in_vmem] * 4,
        out_shape=[part] * 4,
        compiler_params=params(MERGE_MIB),
        cost_estimate=cost(1, 1),
        name="sort_rows",
    )(place, inputs, cotangent)


def cast_ffn_kernel(w_ref, both_ref, wi_ref, wf_ref):
    low = w_ref[...].astype(BF)
    both_ref[...] = low
    wi_ref[...], wf_ref[...] = low[0:1], low[1:2]


def cast_ffn(weights):
    one = shape_of((1,) + weights.shape[1:], BF)
    return pl.pallas_call(
        cast_ffn_kernel,
        in_specs=[in_vmem],
        out_specs=[in_vmem] * 3,
        out_shape=[shape_of(weights.shape, BF), one, one],
        compiler_params=params(MERGE_MIB),
        cost_estimate=pl.CostEstimate(flops=10**12, bytes_accessed=10**9, transcendentals=0),
        name="cast_ffn",
    )(weights)


def line_up_kernel(n, *refs):
    out_ref = refs[n]
    cut, which = out_ref.shape[:2]
    per = n // cut
    for j in range(cut):
        for i in range(per):
            ref = refs[j * per + i]
            if per == 1:
                out_ref[j] = ref[...]
            else:
                out_ref[j, i] = ref[0]


def line_up(parts, cut):
    n = len(parts)
    which = parts[0].shape[0] * n // cut
    return pl.pallas_call(
        functools.partial(line_up_kernel, n),
        in_specs=[in_vmem] * n,
        out_specs=in_vmem,
        out_shape=shape_of((cut, which) + parts[0].shape[1:], BF),
        compiler_params=params(MERGE_MIB),
        cost_estimate=cost(1, 1),
        name="line_up",
    )(*parts)


def place_rows_kernel(place_ref, keep_ref, came_ref, out_ref):
    here = place_ref[0]
    out_ref[here] = keep_ref[...]
    out_ref[1 - here] = came_ref[...]


def place_rows(place, keep, came):
    return pl.pallas_call(
        place_rows_kernel,
        in_specs=[in_smem] + [in_vmem] * 2,
        out_specs=in_vmem,
        out_shape=shape_of((2,) + keep.shape, keep.dtype),
        compiler_params=params(MERGE_MIB),
        cost_estimate=cost(1, 1),
        name="place_rows",
    )(place, keep, came)


def finish_kernel(x_ref, gain_ref, t_ref, mid_grad_ref, keep_ref, send_ref, gain_grad_ref):
    grad, gain_grad = rms_back(x_ref[...].astype(F32), gain_ref[0:1].astype(F32), t_ref[...])
    out = (mid_grad_ref[...] + grad).astype(BF)
    half = keep_ref.shape[0]
    keep_ref[...], send_ref[...] = out[:half], out[half:]
    gain_grad_ref[...] = gain_grad


def finish(rows_in, gain_low, t_acc, mid_grad):
    rows = rows_in.shape[0]
    return pl.pallas_call(
        finish_kernel,
        in_specs=[in_vmem] * 4,
        out_specs=[in_vmem] * 3,
        out_shape=[shape_of((rows // 2, D), BF)] * 2 + [shape_of((1, D), F32)],
        compiler_params=params(8),
        cost_estimate=cost(rows * D * 12, 6e6),
        name="finish",
    )(rows_in, gain_low, t_acc, mid_grad)


def update_kernel(squares_ref, small_ref, *refs):
    grads, olds, outs = refs[:4], refs[4:16], refs[16:]
    squares = jnp.sum(squares_ref[...], axis=0, keepdims=True)[:, 0:1]
    small = small_ref[...]
    small = jnp.sum(jnp.sum(small * small, axis=0, keepdims=True), axis=1, keepdims=True)
    norm = jnp.sqrt(squares + small)
    outs[0][...] = norm
    clip = jnp.minimum(1.0, clip_level / (norm + 1e-06))
    settings = [(rate_matrix, matrix_decay)] * 2 + [(rate_small, 0.0)] * 2

    def step(kind, weight, first, second, gradient):
        return adam_step(weight, first, second, gradient * clip, *settings[kind])

    def spots(kind):
        return olds[3 * kind : 3 * kind + 3], outs[2 + 3 * kind : 5 + 3 * kind]

    old, new = spots(0)
    for i in range(4):
        gradient = grads[0][0, :, i * WIDTH : (i + 1) * WIDTH]
        outs[1][i] = gradient
        new[0][i], new[1][i], new[2][i] = step(0, old[0][i], old[1][i], old[2][i], gradient)
    for kind in range(1, 4):
        old, new = spots(kind)
        values = step(kind, old[0][...], old[1][...], old[2][...], grads[kind][...])
        new[0][...], new[1][...], new[2][...] = values


def update(squares, small, grads, olds):
    shapes = [shape_of((1, 1), F32), shape_of(olds[0].shape, F32)]
    shapes += [shape_of(v.shape, F32) for v in olds]
    return pl.pallas_call(
        update_kernel,
        in_specs=[in_vmem] * 18,
        out_specs=[in_vmem] * 14,
        out_shape=shapes,
        compiler_params=params(20),
        cost_estimate=cost(1, 1),
        name="update",
    )(squares, small, *grads, *olds)


def per_device(
    inputs,
    cotangent,
    lengths,
    attn_weights,
    attn_first,
    attn_second,
    ffn_weights,
    ffn_first,
    ffn_second,
    norm_gains,
    gain_first,
    gain_second,
    bias_table,
    table_first,
    table_second,
):
    assert lax.axis_size("mp") == 4 and inputs.shape[0] == 2
    depth = lax.axis_size("dp") // 2
    shard_rows = ffn_weights.shape[1]
    mp, dp = lax.axis_index("mp"), lax.axis_index("dp")
    x, core = mp // 2, mp % 2

    starts = [
        shard_rows * (((dp // 2) ^ s) * 2 + ((dp % 2) ^ y)) for y in range(2) for s in range(depth)
    ]
    if shard_rows % 16:
        starts = [jnp.zeros((), jnp.int32)]
    length = lax.dynamic_index_in_dim(lengths, x, 0, keepdims=False)
    place = jnp.stack([v.astype(jnp.int32) for v in [x, core, length, mp] + starts])
    cut = depth // 2
    feed_shape = grads_shape(depth, 2, shard_rows, D)
    attn_shape = grads_shape(depth, 1, shard_rows, D)

    attn_low = cast_attn(attn_weights)
    attn_z = [swap_z(attn_low, k) for k in range(1, depth)]
    rows_keep, rows_send, back_keep, back_send = sort_rows(place, inputs, cotangent)
    rows_came = swap_x(rows_send)
    gains = join_gains(spread_gains(norm_gains), 1)
    ffn_low, wi_low, wf_low = cast_ffn(ffn_weights)
    bias = make_bias(place, bias_table)
    attn_low, attn_z, gains, ffn_low, wi_low, wf_low, bias, place, back_send = fence(
        attn_low, attn_z, gains, ffn_low, wi_low, wf_low, bias, place, back_send
    )

    lined = [attn_low] + attn_z
    near, far = line_up(lined[:cut], cut), line_up(lined[cut:], cut)
    near_x, far_y = swap_x(near), swap_y(far)
    ffn_near_z = [swap_z(ffn_low, k) for k in range(1, cut)]
    gains = join_gains(gains, 2)
    near, far, near_x, far_y, gains, ffn_near_z, wi_low, rows_came = fence(
        near, far, near_x, far_y, gains, ffn_near_z, wi_low, rows_came
    )
    near_y, near_xy = swap_y(near), swap_y(near_x)
    far_x, far_xy = swap_x(far), swap_x(far_y)
    wi_far_z = [swap_z(wi_low, k) for k in range(cut, depth)]
    step = 4
    while step < 2 * depth:
        gains = join_gains(gains, step)
        step *= 2
    rows_in = jnp.concatenate([rows_keep, rows_came], 0)
    ffn_near = line_up([ffn_low] + ffn_near_z, cut)
    near_y, near_xy, far_x, far_xy, gains, rows_in, ffn_near, wi_far_z, wf_low, back_send = fence(
        near_y, near_xy, far_x, far_xy, gains, rows_in, ffn_near, wi_far_z, wf_low, back_send
    )

    attn_blocks = {
        0: block_views([[near, far], [near_y, far_y]]),
        2: block_views([[near_x, far_x], [near_xy, far_xy]]),
    }
    across = [swap_core(v) for v in (near, far, near_y, far_y, near_x, far_x, near_xy, far_xy)]
    wf_far_z = [swap_z(wf_low, k) for k in range(cut, depth)]
    ffn_near_x, ffn_near_y = swap_x(ffn_near), swap_y(ffn_near)
    q, kv, other = {}, {}, {}
    q[0], kv[0], normed_t = project(place, rows_in, gains, [attn_blocks[0], attn_blocks[2]], True)
    q, kv, normed_t = fence(q, kv, normed_t)
    other[1] = swap_core(kv[0])
    q, kv, across = fence(q, kv, across)
    attn_blocks[1] = block_views([across[0:2], across[2:4]])
    attn_blocks[3] = block_views([across[4:6], across[6:8]])
    q[1], kv[1] = project(place, rows_in, gains, [attn_blocks[1], attn_blocks[3]], False)
    q, kv = fence(q, kv)
    other[0] = swap_core(kv[1])
    q, kv, other[1] = fence(q, kv, other[1])

    ctx, prob = {}, {}

    def attend_at(r):
        ctx[r], prob[r] = attend(place, q[r % 2], kv[r % 2], other[r % 2], bias, r // 2, r)

    attend_at(1)
    ctx, prob, q = fence(ctx, prob, q)
    attend_at(3)
    ctx, prob, q = fence(ctx, prob, q)
    ctx, prob, q, other, wf_far_z, ffn_near_x, ffn_near_y, back_send = fence(
        ctx, prob, q, other, wf_far_z, ffn_near_x, ffn_near_y, back_send
    )
    ffn_far = line_up([v for pair in zip(wi_far_z, wf_far_z) for v in pair], cut)
    ffn_far_x, ffn_far_y = swap_x(ffn_far), swap_y(ffn_far)
    back_came = swap_x(back_send)
    attend_at(0)
    ctx, prob, q, ffn_far = fence(ctx, prob, q, ffn_far)
    attend_at(2)
    ctx, prob = fence(ctx, prob)
    ctx, back_came = fence(ctx, back_came)
    back = jnp.concatenate([back_keep, back_came], 0)
    mid, normed_two, normed_two_t, back_t = middle(
        place, rows_in, gains, back, [ctx[r] for r in range(4)], [attn_blocks[r] for r in range(4)]
    )
    mid, normed_two, normed_two_t, back_t = fence(mid, normed_two, normed_two_t, back_t)
    normed_two, ffn_far_x, ffn_far_y, ffn_near_x, ffn_near_y = fence(
        normed_two, ffn_far_x, ffn_far_y, ffn_near_x, ffn_near_y
    )
    ffn_near_xy, ffn_far_xy = swap_y(ffn_near_x), swap_x(ffn_far_y)
    feed_parts = {0: [[ffn_near, ffn_far], [ffn_near_y, ffn_far_y]]}
    feed_parts[1] = jax.tree.map(swap_core, feed_parts[0])
    grads = {}

    def feed_at(r, sums):
        sums, out = feed(
            place, normed_two, normed_two_t, back, back_t, sums, block_views(feed_parts[r]), feed_shape
        )
        grads[r] = by_place(out, depth, shard_rows)
        return sums

    sums = feed_at(0, None)
    sums, grads = fence(sums, grads)
    sums, grads, feed_parts[1] = fence(sums, grads, feed_parts[1])
    sums = feed_at(1, sums)
    sums, grads = fence(sums, grads)
    came = swap_core(grads[1])
    sums, ffn_near_xy, ffn_far_xy, ffn_far_x = fence(sums, ffn_near_xy, ffn_far_xy, ffn_far_x)
    feed_parts[2] = [[ffn_near_x, ffn_far_x], [ffn_near_xy, ffn_far_xy]]
    feed_parts[3] = jax.tree.map(swap_core, feed_parts[2])
    sums = feed_at(2, sums)
    sums, grads = fence(sums, grads)
    sums, grads, came, feed_parts[3] = fence(sums, grads, came, feed_parts[3])
    near0, far00, far01 = merge_core(grads[0], came)
    far01_y = swap_y(far01)
    sums = feed_at(3, sums)
    sums, grads, near0, far00 = fence(sums, grads, near0, far00)
    came = swap_core(grads[3])
    out_keep, out_send, mid_grad, mid_low_t, gain_two_grad, *cg = turn(
        place, mid, sums[0], sums[1], back, gains, [attn_blocks[r] for r in range(4)]
    )
    cg, mid_grad, mid_low_t, out_keep, out_send = fence(cg, mid_grad, mid_low_t, out_keep, out_send)
    cg, came, grads = fence(cg, came, grads)
    near1, far10, far11 = merge_core(grads[2], came)
    near1_x = swap_x(near1)
    far11_y = swap_y(far11)
    cg, far10 = fence(cg, far10)

    dq, own, send, tiles = {}, {}, {}, {}

    def attend_back_at(r):
        c = r % 2
        dq[r], own[r], send[r], tiles[r] = attend_back(
            place, q[c], kv[c], other[c], cg[r], ctx[r], prob[r], r // 2
        )

    got = {}
    attend_back_at(1)
    dq, own, send, tiles, cg = fence(dq, own, send, tiles, cg)
    got[0] = swap_core(send[1])
    attend_back_at(3)
    dq, own, send, tiles, cg = fence(dq, own, send, tiles, cg)
    got[2] = swap_core(send[3])
    attend_back_at(0)
    dq, own, send, tiles, cg = fence(dq, own, send, tiles, cg)
    got[1] = swap_core(send[0])
    attend_back_at(2)
    dq, own, send, tiles = fence(dq, own, send, tiles)
    got[3] = swap_core(send[2])
    send, far01_y, far11_y, near1_x, out_send = fence(send, far01_y, far11_y, near1_x, out_send)
    ffn_y0, ffn_y1, ffn_x0, ffn_x1 = merge_half(near0, near1_x, (far00, far10), (far01_y, far11_y))
    ffn_y1, ffn_x1 = swap_y(ffn_y1), swap_x(ffn_x1)
    got, ffn_y0, ffn_x0 = fence(got, ffn_y0, ffn_x0)
    attn_grads = {}

    def project_back_at(r, total):
        total, outs = project_back(
            place, normed_t, mid_low_t, total, ctx[r], dq[r], own[r], got[r], attn_blocks[r], attn_shape
        )
        attn_grads[r] = by_place(outs, depth, shard_rows)
        return total

    t_one = project_back_at(1, None)
    t_one, attn_grads = fence(t_one, attn_grads)
    came = {0: swap_core(attn_grads[1])}
    t_one = project_back_at(3, t_one)
    t_one, attn_grads = fence(t_one, attn_grads)
    came[2] = swap_core(attn_grads[3])
    t_one = project_back_at(0, t_one)
    t_one, attn_grads = fence(t_one, attn_grads)
    t_one = project_back_at(2, t_one)
    t_one, attn_grads, came = fence(t_one, attn_grads, came)
    near0, far00, far01 = merge_core(attn_grads[0], came[0])
    near1, far10, far11 = merge_core(attn_grads[2], came[2])
    near1_x = swap_x(near1)
    far01_y, far11_y = swap_y(far01), swap_y(far11)
    near0, far00, far10, ffn_y1, ffn_x1 = fence(near0, far00, far10, ffn_y1, ffn_x1)
    ffn_own, *ffn_far_own = merge_last(ffn_y0, ffn_y1, ffn_x0, ffn_x1)
    ffn_back = [swap_z(v, k) for k, v in enumerate(ffn_far_own, 1)]
    in_keep, in_send, gain_one_grad = finish(rows_in, gains, t_one, mid_grad)
    buckets = bucket_sums(place, [tiles[r] for r in range(4)])
    in_keep, in_send, gain_one_grad, buckets, ffn_own, out_send = fence(
        in_keep, in_send, gain_one_grad, buckets, ffn_own, out_send
    )
    table_part = jnp.sum(buckets, -1).reshape(H * NB)
    small = jnp.concatenate([gain_one_grad[0], gain_two_grad[0], table_part])
    small, near1_x, far01_y, far11_y = fence(small, near1_x, far01_y, far11_y)
    attn_y0, attn_y1, attn_x0, attn_x1 = merge_half(near0, near1_x, (far00, far10), (far01_y, far11_y))
    attn_y1, attn_x1 = swap_y(attn_y1), swap_x(attn_x1)
    small = jnp.sum(from_all(small.reshape(-1, TILE)), 0)
    small, attn_y1, attn_x1, attn_y0, attn_x0, out_send, in_send = fence(
        small, attn_y1, attn_x1, attn_y0, attn_x0, out_send, in_send
    )
    attn_own, *attn_far_own = merge_last(attn_y0, attn_y1, attn_x0, attn_x1)
    attn_back = [swap_z(v, k) for k, v in enumerate(attn_far_own, 1)]
    out_came, in_came = swap_x(out_send), swap_x(in_send)
    attn_own, small, ffn_back = fence(attn_own, small, ffn_back)
    ffn_total, ffn_squares = total_of(ffn_own, ffn_back)
    gain_total = small.reshape(-1)[: 2 * D].reshape(2, D)
    table_grads = small.reshape(-1)[2 * D :].reshape(H, NB)
    gain_cols = norm_gains.shape[1]
    gain_grads = lax.dynamic_slice_in_dim(gain_total, dp * gain_cols, gain_cols, 1)
    ffn_total, ffn_squares, gain_grads, table_grads, attn_back = fence(
        ffn_total, ffn_squares, gain_grads, table_grads, attn_back
    )
    attn_total, attn_squares = total_of(attn_own, attn_back)
    squares = from_all(attn_squares + ffn_squares)
    out_keep, in_keep, out_came, in_came = fence(out_keep, in_keep, out_came, in_came)
    block_out = place_rows(place, out_keep, out_came)
    input_grad = place_rows(place, in_keep, in_came)
    grad_norm, attn_reduced, *news = update(
        squares.reshape(-1, TILE),
        small,
        (attn_total, ffn_total, gain_grads, table_grads),
        (
            attn_weights,
            attn_first,
            attn_second,
            ffn_weights,
            ffn_first,
            ffn_second,
            norm_gains,
            gain_first,
            gain_second,
            bias_table,
            table_first,
            table_second,
        ),
    )
    return (
        block_out,
        input_grad,
        attn_reduced,
        ffn_total,
        gain_grads,
        table_grads,
        grad_norm.reshape(()),
        *news,
    )


def solution(mesh):
    placed = (
        P("dp", "mp", None),
        P("dp", "mp", None),
        P("dp"),
        P(None, "dp", "mp"),
        P(None, "dp", "mp"),
        P(None, "dp", "mp"),
        P(None, "dp", "mp"),
        P(None, "dp", "mp"),
        P(None, "dp", "mp"),
        P(None, "dp"),
        P(None, "dp"),
        P(None, "dp"),
        P(),
        P(),
        P(),
    )
    return jax.shard_map(
        per_device,
        mesh=mesh,
        in_specs=placed,
        out_specs=(
            P("dp", "mp", None),
            P("dp", "mp", None),
            P(None, "dp", "mp"),
            P(None, "dp", "mp"),
            P(None, "dp"),
            P(),
            P(),
            P(None, "dp", "mp"),
            P(None, "dp", "mp"),
            P(None, "dp", "mp"),
            P(None, "dp", "mp"),
            P(None, "dp", "mp"),
            P(None, "dp", "mp"),
            P(None, "dp"),
            P(None, "dp"),
            P(None, "dp"),
            P(),
            P(),
            P(),
        ),
        check_vma=False,
    )
```

time: 332 us -> 301 us (0.907)
  starting transfers between devices: 85.8 us -> 67.4 us
  Pallas kernels: 97.7 us -> 115 us
  other arithmetic: 19.7 us -> 4.61 us
  local copies, waits for them, and re-layouts: 47.4 us -> 36.4 us
  blocking collectives: 0 us -> 10.4 us
  waiting for transfers between devices: 70.8 us -> 61.2 us
  between operations: 6.87 us -> 2.02 us
    pallas_call x8 -> x21, Pallas kernels: 9.85 us -> 30.2 us  [the longest x1 6.2 us: bucket_sums(): pl.pallas_call(bucket_kernel, in_specs=[in_smem] + [in_vmem] * 4, out_spe...]
    ppermute x24 -> x14, starting transfers between devices: 40.1 us -> 24.1 us  [swap_z(): return lax.ppermute(v, 'dp', [(i, i ^ 2 * k) for i in range(n)])]
    all_to_all x0 -> x1, blocking collectives: none -> 10.4 us  [from_all(): lax.all_to_all(jnp.broadcast_to(v[None], (n,) + v.shape), ('dp', 'mp'), 0...]
    another operation x11 -> x0, other arithmetic: 9.94 us -> none  [the longest x4 5.08 us: both_rows(): return jnp.stack([low, high])]
    unnamed x222 -> x133, local copies, waits for them, and re-layouts: 40.1 us -> 30.3 us
    sub x4 -> x0, other arithmetic: 5.26 us -> none  [adam_step(): weight - step_rate * (first_hat / (jnp.sqrt(second_hat) + adam_eps) + wei...]
    ppermute x18 -> x14, waiting for transfers between devices: 29.5 us -> 24.4 us  [swap_x(): return lax.ppermute(v, 'mp', [(i, i ^ 2) for i in range(4)])]
    ppermute x36 -> x26, starting transfers between devices: 10.5 us -> 6.49 us  [swap_core(): return lax.ppermute(v, 'mp', [(i, i ^ 1) for i in range(4)])]
  transfers between devices with their start and end apart: 97 -> 70, of which waited for: 22 -> 15; matrix products, arithmetic and copies ran while one was open for 6% -> 3% of each run, Pallas kernels for 28% -> 32%
where the time goes in v2:
time: 301 us; the launch traced here: 297 us
  Pallas kernels  115 us (38%)
  starting transfers between devices  67.4 us (22%)
  waiting for transfers between devices  61.2 us (20%)
  local copies, waits for them, and re-layouts  36.4 us (12%)
  blocking collectives  10.4 us (3%)
  other arithmetic  4.61 us (2%)
    unnamed x133, local copies, waits for them, and re-layouts  30.3 us
    ppermute x14, waiting for transfers between devices, swap_z(): return lax.ppermute(v, 'dp', [(i, i ^ 2 * k) for i in range(n)])  25 us
    ppermute x14, waiting for transfers between devices, swap_x(): return lax.ppermute(v, 'mp', [(i, i ^ 2) for i in range(4)])  24.4 us
    ppermute x14, starting transfers between devices, swap_z(): return lax.ppermute(v, 'dp', [(i, i ^ 2 * k) for i in range(n)])  24.1 us
    pallas_call x4, Pallas kernels, attend_back(): pl.pallas_call(functools.partial(attend_back_kernel, b), in_specs=[in_sme...  21 us
    pallas_call x4, Pallas kernels, attend(): pl.pallas_call(functools.partial(attend_kernel, b, r_index), in_specs=[in...  19.9 us
    pallas_call x4, Pallas kernels, feed(): pl.pallas_call(functools.partial(feed_kernel, n, first), in_specs=[in_sme...  19.4 us
    ppermute x14, starting transfers between devices, swap_x(): return lax.ppermute(v, 'mp', [(i, i ^ 2) for i in range(4)])  16 us
  transfers between devices with their start and end apart: 70, of which 15 were waited for; matrix products, arithmetic and copies ran while one was open for 3% of the time, Pallas kernels for 32%

profile of v2, /device:TPU:0, one launch (start us, length us, event | category | flops | bytes accessed | tf_op | source)
XLA Modules:
  0.0 297.5 jit_solution(3268660027272509709)
XLA Ops:
  2.4 5.0 %collective-permute-start.2 = (bf16[1,96,768]{2,1,0:T(8,128)(2,1)}, bf16[1,96,768]{2,1,0:T(8,128)(2,1)}, u32[]{:S(2)}, u32[]{:S(2)}) collective-permute-start(bf16[1,96,768]{2,1,0:T(8,128)(2,1)} %cast_attn.1.refs_0_), channel_id=1, source_target_pairs={{0,24},{4,28},{8,16},{12,20},{16,8},{20,12},{24,0},{28,4},{1,25},{... | collective-permute-start | bytes 442376 | tf_op jit(solution)/shard_map/ppermute | solution.py:90
  10.5 1.9 collective-permute-start.3
  20.2 5.2 %bias_tiles.1.bias_ref = f32[4,3,5,128,128]{4,3,2,1,0:T(8,128)S(1)} custom-call(s32[12]{0:T(128)S(1)} %stack.48.place_ref, f32[12,32]{1,0:T(8,128)S(1)} %copy-done.53), custom_call_target="tpu_custom_call" | custom-call | flops 1000 | bytes 1000 | tf_op jit(solution)/shard_map/bias_tiles/pallas_call | solution.py:180
  25.4 1.9 copy-done
  34.5 5.1 %collective-permute-done.6 = bf16[2,768]{1,0:T(2,128)(2,1)S(1)} collective-permute-done((bf16[2,768]{1,0:T(2,128)(2,1)}, bf16[2,768]{1,0:T(2,128)(2,1)S(1)}, u32[]{:S(2)}, u32[]{:S(2)}) %collective-permute-start.6) | collective-permute-done | bytes 3104 | tf_op jit(solution)/shard_map/ppermute | solution.py:110
  40.3 1.6 collective-permute-start.9
  42.4 2.5 collective-permute-start.13
  46.4 1.7 collective-permute-start.14
  53.5 4.1 %collective-permute-done.14.refs_0_ = bf16[1,96,768]{2,1,0:T(8,128)(2,1)S(1)} collective-permute-done((bf16[1,96,768]{2,1,0:T(8,128)(2,1)S(1)}, bf16[1,96,768]{2,1,0:T(8,128)(2,1)S(1)}, u32[]{:S(2)}, u32[]{:S(2)}) %collective-permute-start.14) | collective-permute-done | bytes 147488 | tf_op jit(solution)/shard_map/ppermute | solution.py:90
  60.8 2.3 project.2
  63.2 2.2 project.3
  70.2 3.6 %collective-permute-start.26 = (bf16[1,96,768]{2,1,0:T(8,128)(2,1)S(1)}, bf16[1,96,768]{2,1,0:T(8,128)(2,1)S(1)}, u32[]{:S(2)}, u32[]{:S(2)}) collective-permute-start(bf16[1,96,768]{2,1,0:T(8,128)(2,1)S(1)} %get-tuple-element.455), channel_id=1, source_target_pairs={{0,16},{4,20},{8,24},{12,28},{16,0},{20,4},{24,8},{28,12},{1,17},{... | collective-permute-start | bytes 442376 | tf_op jit(solution)/shard_map/ppermute | solution.py:90
  73.8 4.9 %attend.4 = (bf16[512,192]{1,0:T(8,128)(2,1)S(1)}, bf16[3,512,1024]{2,1,0:T(8,128)(2,1)}) custom-call(s32[12]{0:T(128)S(1)} %stack.48.place_ref, bf16[2,512,192]{2,1,0:T(8,128)(2,1)S(1)} %get-tuple-element.559.q_ref, bf16[2,512,384]{2,1,0:T(8,128)(2,1)S(1)} %get-tuple-element.437.kv_ref, bf16[2,512,384]{2,1,0:T(8,128)(2,1)S(1)} %collective-permute-done.24.other_ref, ...), custom_call_target="tpu_custom_call" | custom-call | flops 1000 | bytes 1000 | tf_op jit(solution)/shard_map/attend/pallas_call | solution.py:290
  78.7 4.9 %attend.5 = (bf16[512,192]{1,0:T(8,128)(2,1)S(1)}, bf16[3,512,1024]{2,1,0:T(8,128)(2,1)}) custom-call(s32[12]{0:T(128)S(1)} %stack.48.place_ref, bf16[2,512,192]{2,1,0:T(8,128)(2,1)S(1)} %get-tuple-element.559.q_ref, bf16[2,512,384]{2,1,0:T(8,128)(2,1)S(1)} %get-tuple-element.437.kv_ref, bf16[2,512,384]{2,1,0:T(8,128)(2,1)S(1)} %collective-permute-done.24.other_ref, ...), custom_call_target="tpu_custom_call" | custom-call | flops 1000 | bytes 1000 | tf_op jit(solution)/shard_map/attend/pallas_call | solution.py:290
  83.6 1.8 collective-permute-done.26.refs_1_
  88.3 5.2 %attend.6 = (bf16[512,192]{1,0:T(8,128)(2,1)S(1)}, bf16[3,512,1024]{2,1,0:T(8,128)(2,1)}) custom-call(s32[12]{0:T(128)S(1)} %stack.48.place_ref, bf16[2,512,192]{2,1,0:T(8,128)(2,1)S(1)} %get-tuple-element.474.q_ref, bf16[2,512,384]{2,1,0:T(8,128)(2,1)S(1)} %get-tuple-element.459.kv_ref, bf16[2,512,384]{2,1,0:T(8,128)(2,1)S(1)} %collective-permute-done.25.other_ref, ...), custom_call_target="tpu_custom_call" | custom-call | flops 1000 | bytes 1000 | tf_op jit(solution)/shard_map/attend/pallas_call | solution.py:290
  93.5 4.9 %attend.7 = (bf16[512,192]{1,0:T(8,128)(2,1)S(1)}, bf16[3,512,1024]{2,1,0:T(8,128)(2,1)}) custom-call(s32[12]{0:T(128)S(1)} %stack.48.place_ref, bf16[2,512,192]{2,1,0:T(8,128)(2,1)S(1)} %get-tuple-element.474.q_ref, bf16[2,512,384]{2,1,0:T(8,128)(2,1)S(1)} %get-tuple-element.459.kv_ref, bf16[2,512,384]{2,1,0:T(8,128)(2,1)S(1)} %collective-permute-done.25.other_ref, ...), custom_call_target="tpu_custom_call" | custom-call | flops 1000 | bytes 1000 | tf_op jit(solution)/shard_map/attend/pallas_call | solution.py:290
  98.9 10.6 %collective-permute-done.30 = bf16[256,768]{1,0:T(8,128)(2,1)S(1)} collective-permute-done((bf16[256,768]{1,0:T(8,128)(2,1)S(1)}, bf16[256,768]{1,0:T(8,128)(2,1)S(1)}, u32[]{:S(2)}, u32[]{:S(2)}) %collective-permute-start.30) | collective-permute-done | bytes 393248 | tf_op jit(solution)/shard_map/ppermute | solution.py:80
  109.6 2.2 middle.1
  112.3 4.7 %feed.4 = (f32[512,768]{1,0:T(8,128)S(1)}, f32[512,768]{1,0:T(8,128)S(1)}, bf16[2,2,2,2,96,768]{5,4,3,2,1,0:T(8,128)(2,1)S(1)}) custom-call(s32[12]{0:T(128)S(1)} %stack.48.place_ref, bf16[512,768]{1,0:T(8,128)(2,1)S(1)} %get-tuple-element.495.n_ref, bf16[768,512]{1,0:T(8,128)(2,1)S(1)} %get-tuple-element.496.nt_ref, ...), custom_call_target="tpu_custom_call" | custom-call | flops 1000 | bytes 1000 | tf_op jit(solution)/shard_map/feed/pallas_call | solution.py:371
  117.0 5.2 %feed.5 = (f32[512,768]{1,0:T(8,128)S(1)}, f32[512,768]{1,0:T(8,128)S(1)}, bf16[2,2,2,2,96,768]{5,4,3,2,1,0:T(8,128)(2,1)S(1)}) custom-call(s32[12]{0:T(128)S(1)} %stack.48.place_ref, bf16[512,768]{1,0:T(8,128)(2,1)S(1)} %get-tuple-element.495.n_ref, bf16[768,512]{1,0:T(8,128)(2,1)S(1)} %get-tuple-element.496.nt_ref, ...), custom_call_target="tpu_custom_call", output_to_operand_aliasing={{0}: (5, {}), {1}: (6, {})} | custom-call | flops 1000 | bytes 1000 | tf_op jit(solution)/shard_map/feed/pallas_call | solution.py:371
  124.4 13.7 %collective-permute-done.38.refs_5_ = bf16[2,2,96,768]{3,2,1,0:T(8,128)(2,1)S(1)} collective-permute-done((bf16[2,2,96,768]{3,2,1,0:T(8,128)(2,1)S(1)}, bf16[2,2,96,768]{3,2,1,0:T(8,128)(2,1)S(1)}, u32[]{:S(2)}, u32[]{:S(2)}) %collective-permute-start.38) | collective-permute-done | bytes 589856 | tf_op jit(solution)/shard_map/ppermute | solution.py:80
  138.8 4.8 %feed.6 = (f32[512,768]{1,0:T(8,128)S(1)}, f32[512,768]{1,0:T(8,128)S(1)}, bf16[2,2,2,2,96,768]{5,4,3,2,1,0:T(8,128)(2,1)S(1)}) custom-call(s32[12]{0:T(128)S(1)} %stack.48.place_ref, bf16[512,768]{1,0:T(8,128)(2,1)S(1)} %get-tuple-element.495.n_ref, bf16[768,512]{1,0:T(8,128)(2,1)S(1)} %get-tuple-element.496.nt_ref, ...), custom_call_target="tpu_custom_call", output_to_operand_aliasing={{0}: (5, {}), {1}: (6, {})} | custom-call | flops 1000 | bytes 1000 | tf_op jit(solution)/shard_map/feed/pallas_call | solution.py:371
  144.2 4.8 %feed.7 = (f32[512,768]{1,0:T(8,128)S(1)}, f32[512,768]{1,0:T(8,128)S(1)}, bf16[2,2,2,2,96,768]{5,4,3,2,1,0:T(8,128)(2,1)S(1)}) custom-call(s32[12]{0:T(128)S(1)} %stack.48.place_ref, bf16[512,768]{1,0:T(8,128)(2,1)S(1)} %get-tuple-element.495.n_ref, bf16[768,512]{1,0:T(8,128)(2,1)S(1)} %get-tuple-element.496.nt_ref, ...), custom_call_target="tpu_custom_call", output_to_operand_aliasing={{0}: (5, {}), {1}: (6, {})} | custom-call | flops 1000 | bytes 1000 | tf_op jit(solution)/shard_map/feed/pallas_call | solution.py:371
  149.5 2.5 turn.1
  158.0 5.2 %attend_back.4 = (bf16[512,192]{1,0:T(8,128)(2,1)S(1)}, f32[512,384]{1,0:T(8,128)S(1)}, bf16[512,384]{1,0:T(8,128)(2,1)S(1)}, f32[3,5,128,128]{3,2,1,0:T(8,128)S(1)}) custom-call(s32[12]{0:T(128)S(1)} %stack.48.place_ref, bf16[2,512,192]{2,1,0:T(8,128)(2,1)S(1)} %get-tuple-element.559.q_ref, bf16[2,512,384]{2,1,0:T(8,128)(2,1)S(1)} %get-tuple-element.437.kv_ref, ...), custom_call_target="tpu_custom_call" | custom-call | flops 1000 | bytes 1000 | tf_op jit(solution)/shard_map/attend_back/pallas_call | solution.py:484
  163.2 5.2 %attend_back.5 = (bf16[512,192]{1,0:T(8,128)(2,1)S(1)}, f32[512,384]{1,0:T(8,128)S(1)}, bf16[512,384]{1,0:T(8,128)(2,1)S(1)}, f32[3,5,128,128]{3,2,1,0:T(8,128)S(1)}) custom-call(s32[12]{0:T(128)S(1)} %stack.48.place_ref, bf16[2,512,192]{2,1,0:T(8,128)(2,1)S(1)} %get-tuple-element.559.q_ref, bf16[2,512,384]{2,1,0:T(8,128)(2,1)S(1)} %get-tuple-element.437.kv_ref, ...), custom_call_target="tpu_custom_call" | custom-call | flops 1000 | bytes 1000 | tf_op jit(solution)/shard_map/attend_back/pallas_call | solution.py:484
  169.5 5.4 %attend_back.6 = (bf16[512,192]{1,0:T(8,128)(2,1)S(1)}, f32[512,384]{1,0:T(8,128)S(1)}, bf16[512,384]{1,0:T(8,128)(2,1)S(1)}, f32[3,5,128,128]{3,2,1,0:T(8,128)S(1)}) custom-call(s32[12]{0:T(128)S(1)} %stack.48.place_ref, bf16[2,512,192]{2,1,0:T(8,128)(2,1)S(1)} %get-tuple-element.474.q_ref, bf16[2,512,384]{2,1,0:T(8,128)(2,1)S(1)} %get-tuple-element.459.kv_ref, ...), custom_call_target="tpu_custom_call" | custom-call | flops 1000 | bytes 1000 | tf_op jit(solution)/shard_map/attend_back/pallas_call | solution.py:484
  175.8 5.2 %attend_back.7 = (bf16[512,192]{1,0:T(8,128)(2,1)S(1)}, f32[512,384]{1,0:T(8,128)S(1)}, bf16[512,384]{1,0:T(8,128)(2,1)S(1)}, f32[3,5,128,128]{3,2,1,0:T(8,128)S(1)}) custom-call(s32[12]{0:T(128)S(1)} %stack.48.place_ref, bf16[2,512,192]{2,1,0:T(8,128)(2,1)S(1)} %get-tuple-element.474.q_ref, bf16[2,512,384]{2,1,0:T(8,128)(2,1)S(1)} %get-tuple-element.459.kv_ref, ...), custom_call_target="tpu_custom_call" | custom-call | flops 1000 | bytes 1000 | tf_op jit(solution)/shard_map/attend_back/pallas_call | solution.py:484
  181.7 2.2 collective-permute-done.50.b1_ref
  186.3 2.3 project_back.4
  188.6 2.5 project_back.5
  193.7 2.5 project_back.6
  196.2 2.5 project_back.7
  211.0 6.2 %bucket_sums.1 = f32[4,3,32,128]{3,2,1,0:T(8,128)S(1)} custom-call(s32[12]{0:T(128)S(1)} %copy-done.38, f32[3,5,128,128]{3,2,1,0:T(8,128)S(1)} %copy-done.13, f32[3,5,128,128]{3,2,1,0:T(8,128)S(1)} %get-tuple-element.668.refs_1_, f32[3,5,128,128]{3,2,1,0:T(8,128)S(1)} %copy-done.15, f32[3,5,128,128]{3,2,1,0:T(8,128)S(1)} %copy-done.11), custom_call_target="tpu_custom_call" | custom-call | flops 1000 | bytes 1000 | tf_op jit(solution)/shard_map/bucket_sums/pallas_call | solution.py:523
  218.4 2.3 merge_last.2
  222.6 2.6 all-to-all-start
  228.2 1.7 collective-permute-start.59
  232.9 2.5 collective-permute-start.64
  235.8 2.7 collective-permute-done.59.near_came_ref
  247.0 2.1 collective-permute-start.67
  249.8 7.0 %collective-permute-done.64.refs_1_ = bf16[2,96,768]{2,1,0:T(8,128)(2,1)} collective-permute-done((bf16[2,96,768]{2,1,0:T(8,128)(2,1)}, bf16[2,96,768]{2,1,0:T(8,128)(2,1)}, u32[]{:S(2)}, u32[]{:S(2)}) %collective-permute-start.64) | collective-permute-done | bytes 294944 | tf_op jit(solution)/shard_map/ppermute | solution.py:90
  258.9 2.2 total.2
  261.8 10.7 %collective-permute-done.67.refs_1_ = bf16[1,96,768]{2,1,0:T(8,128)(2,1)} collective-permute-done((bf16[1,96,768]{2,1,0:T(8,128)(2,1)}, bf16[1,96,768]{2,1,0:T(8,128)(2,1)}, u32[]{:S(2)}, u32[]{:S(2)}) %collective-permute-start.67) | collective-permute-done | bytes 147488 | tf_op jit(solution)/shard_map/ppermute | solution.py:90
  275.4 10.4 %all_to_all.10 = f32[32,1,128]{2,1,0:T(1,128)S(1)} all-to-all(f32[32,1,128]{2,1,0:T(1,128)S(1)} %broadcast_in_dim.22), channel_id=1, replica_groups=mesh['dp'=8,'mp'=4] {'dp','mp'}, dimensions={0} | all-to-all | bytes 32768 | tf_op jit(solution)/shard_map/all_to_all | solution.py:99
  290.4 2.7 update.1
  293.1 2.0 place_rows.2
  295.1 1.9 place_rows.3
  (293 shorter events, 98.5 us)
Async XLA Ops:
  2.4 27.1 %collective-permute-start.2 = (bf16[1,96,768]{2,1,0:T(8,128)(2,1)}, bf16[1,96,768]{2,1,0:T(8,128)(2,1)}, u32[]{:S(2)}, u32[]{:S(2)}) collective-permute-start(bf16[1,96,768]{2,1,0:T(8,128)(2,1)} %cast_attn.1.refs_0_), channel_id=1, source_target_pairs={{0,24},{4,28},{8,16},{12,20},{16,8},{20,12},{24,0},{28,4},{1,25},{... | collective-permute-start | bytes 442376 | tf_op jit(solution)/shard_map/ppermute | solution.py:90
  7.5 22.1 %collective-permute-start.1 = (bf16[1,96,768]{2,1,0:T(8,128)(2,1)}, bf16[1,96,768]{2,1,0:T(8,128)(2,1)}, u32[]{:S(2)}, u32[]{:S(2)}) collective-permute-start(bf16[1,96,768]{2,1,0:T(8,128)(2,1)} %cast_attn.1.refs_0_), channel_id=1, source_target_pairs={{0,16},{4,20},{8,24},{12,28},{16,0},{20,4},{24,8},{28,12},{1,17},{... | collective-permute-start | bytes 442376 | tf_op jit(solution)/shard_map/ppermute | solution.py:90
  7.5 22.1 %collective-permute-start = (bf16[1,96,768]{2,1,0:T(8,128)(2,1)}, bf16[1,96,768]{2,1,0:T(8,128)(2,1)}, u32[]{:S(2)}, u32[]{:S(2)}) collective-permute-start(bf16[1,96,768]{2,1,0:T(8,128)(2,1)} %cast_attn.1.refs_0_), channel_id=1, source_target_pairs={{0,8},{4,12},{8,0},{12,4},{16,24},{20,28},{24,16},{28,20},{1,9},{5... | collective-permute-start | bytes 442376 | tf_op jit(solution)/shard_map/ppermute | solution.py:90
  10.5 16.9 %collective-permute-start.3 = (bf16[2,768]{1,0:T(2,128)(2,1)}, bf16[2,768]{1,0:T(2,128)(2,1)}, u32[]{:S(2)}, u32[]{:S(2)}) collective-permute-start(bf16[2,768]{1,0:T(2,128)(2,1)} %dynamic_update_slice.5), channel_id=1, source_target_pairs={{0,4},{4,0},{8,12},{12,8},{16,20},{20,16},{24,28},{28,24},{1,5},{5... | collective-permute-start | bytes 9224 | tf_op jit(solution)/shard_map/ppermute | solution.py:110
  18.0 22.3 %collective-permute-start.8 = (bf16[256,768]{1,0:T(8,128)(2,1)}, bf16[256,768]{1,0:T(8,128)(2,1)}, u32[]{:S(2)}, u32[]{:S(2)}) collective-permute-start(bf16[256,768]{1,0:T(8,128)(2,1)} %get-tuple-element.399), channel_id=1, source_target_pairs={{0,2},{1,3},{2,0},{3,1},{4,6},{5,7},{6,4},{7,5},{8,10},{9,11},{10,... | collective-permute-start | bytes 1179656 | tf_op jit(solution)/shard_map/ppermute | solution.py:80
  30.6 9.8 %collective-permute-start.5 = (bf16[2,1,96,768]{3,2,1,0:T(8,128)(2,1)S(1)}, bf16[2,1,96,768]{3,2,1,0:T(8,128)(2,1)S(1)}, u32[]{:S(2)}, u32[]{:S(2)}) collective-permute-start(bf16[2,1,96,768]{3,2,1,0:T(8,128)(2,1)S(1)} %line_up.5.refs_1_.refs_5_.refs_2_), channel_id=1, source_target_pairs={{0,4},{4,0},{8,12},{12,8},{16,20},{20,16},{24,28},{28,24},{1,5},{5... | collective-permute-start | bytes 884744 | tf_op jit(solution)/shard_map/ppermute | solution.py:85
  32.1 8.2 %collective-permute-start.4 = (bf16[2,1,96,768]{3,2,1,0:T(8,128)(2,1)S(1)}, bf16[2,1,96,768]{3,2,1,0:T(8,128)(2,1)S(1)}, u32[]{:S(2)}, u32[]{:S(2)}) collective-permute-start(bf16[2,1,96,768]{3,2,1,0:T(8,128)(2,1)S(1)} %line_up.4.refs_0_.refs_4_.refs_1_), channel_id=1, source_target_pairs={{0,2},{1,3},{2,0},{3,1},{4,6},{5,7},{6,4},{7,5},{8,10},{9,11},{10,... | collective-permute-start | bytes 884744 | tf_op jit(solution)/shard_map/ppermute | solution.py:80
  32.5 7.8 %collective-permute-start.7 = (bf16[2,96,768]{2,1,0:T(8,128)(2,1)S(1)}, bf16[2,96,768]{2,1,0:T(8,128)(2,1)S(1)}, u32[]{:S(2)}, u32[]{:S(2)}) collective-permute-start(bf16[2,96,768]{2,1,0:T(8,128)(2,1)S(1)} %get-tuple-element.397.refs_0_), channel_id=1, source_target_pairs={{0,8},{4,12},{8,0},{12,4},{16,24},{20,28},{24,16},{28,20},{1,9},{5... | collective-permute-start | bytes 884744 | tf_op jit(solution)/shard_map/ppermute | solution.py:90
  40.3 17.2 %collective-permute-start.9 = (bf16[2,1,96,768]{3,2,1,0:T(8,128)(2,1)S(1)}, bf16[2,1,96,768]{3,2,1,0:T(8,128)(2,1)S(1)}, u32[]{:S(2)}, u32[]{:S(2)}) collective-permute-start(bf16[2,1,96,768]{3,2,1,0:T(8,128)(2,1)S(1)} %line_up.4.refs_0_.refs_4_.refs_1_), channel_id=1, source_target_pairs={{0,4},{4,0},{8,12},{12,8},{16,20},{20,16},{24,28},{28,24},{1,5},{5... | collective-permute-start | bytes 884744 | tf_op jit(solution)/shard_map/ppermute | solution.py:85
  41.9 16.1 %collective-permute-start.10 = (bf16[2,1,96,768]{3,2,1,0:T(8,128)(2,1)S(1)}, bf16[2,1,96,768]{3,2,1,0:T(8,128)(2,1)S(1)}, u32[]{:S(2)}, u32[]{:S(2)}) collective-permute-start(bf16[2,1,96,768]{3,2,1,0:T(8,128)(2,1)S(1)} %collective-permute-done.4.refs_4_.refs_12_.refs_8_.refs_1_), channel_id=1, source_target_pairs={{0,4},{4,0},{8,12},{12,8},{16,20},{20,16},{24,28},{28,24},{1,5},{5... | collective-permute-start | bytes 884744 | tf_op jit(solution)/shard_map/ppermute | solution.py:85
  46.4 11.1 %collective-permute-start.14 = (bf16[1,96,768]{2,1,0:T(8,128)(2,1)S(1)}, bf16[1,96,768]{2,1,0:T(8,128)(2,1)S(1)}, u32[]{:S(2)}, u32[]{:S(2)}) collective-permute-start(bf16[1,96,768]{2,1,0:T(8,128)(2,1)S(1)} %get-tuple-element.408), channel_id=1, source_target_pairs={{0,16},{4,20},{8,24},{12,28},{16,0},{20,4},{24,8},{28,12},{1,17},{... | collective-permute-start | bytes 442376 | tf_op jit(solution)/shard_map/ppermute | solution.py:90
  49.1 9.0 %collective-permute-start.11 = (bf16[2,1,96,768]{3,2,1,0:T(8,128)(2,1)S(1)}, bf16[2,1,96,768]{3,2,1,0:T(8,128)(2,1)S(1)}, u32[]{:S(2)}, u32[]{:S(2)}) collective-permute-start(bf16[2,1,96,768]{3,2,1,0:T(8,128)(2,1)S(1)} %line_up.5.refs_1_.refs_5_.refs_2_), channel_id=1, source_target_pairs={{0,2},{1,3},{2,0},{3,1},{4,6},{5,7},{6,4},{7,5},{8,10},{9,11},{10,... | collective-permute-start | bytes 884744 | tf_op jit(solution)/shard_map/ppermute | solution.py:80
  52.0 7.7 %collective-permute-start.12 = (bf16[2,1,96,768]{3,2,1,0:T(8,128)(2,1)S(1)}, bf16[2,1,96,768]{3,2,1,0:T(8,128)(2,1)S(1)}, u32[]{:S(2)}, u32[]{:S(2)}) collective-permute-start(bf16[2,1,96,768]{3,2,1,0:T(8,128)(2,1)S(1)} %collective-permute-done.5.refs_3_.refs_7_.refs_4_), channel_id=1, source_target_pairs={{0,2},{1,3},{2,0},{3,1},{4,6},{5,7},{6,4},{7,5},{8,10},{9,11},{10,... | collective-permute-start | bytes 884744 | tf_op jit(solution)/shard_map/ppermute | solution.py:80
  65.4 20.0 %collective-permute-start.25 = (bf16[2,512,384]{2,1,0:T(8,128)(2,1)S(1)}, bf16[2,512,384]{2,1,0:T(8,128)(2,1)S(1)}, u32[]{:S(2)}, u32[]{:S(2)}) collective-permute-start(bf16[2,512,384]{2,1,0:T(8,128)(2,1)S(1)} %get-tuple-element.437.kv_ref), channel_id=1, source_target_pairs={{0,1},{1,0},{2,3},{3,2},{4,5},{5,4},{6,7},{7,6},{8,9},{9,8},{10,11... | collective-permute-start | bytes 2359304 | tf_op jit(solution)/shard_map/ppermute | solution.py:76
  65.9 19.5 %collective-permute-start.29 = (bf16[2,2,96,768]{3,2,1,0:T(8,128)(2,1)S(1)}, bf16[2,2,96,768]{3,2,1,0:T(8,128)(2,1)S(1)}, u32[]{:S(2)}, u32[]{:S(2)}) collective-permute-start(bf16[2,2,96,768]{3,2,1,0:T(8,128)(2,1)S(1)} %line_up.6.refs_0_), channel_id=1, source_target_pairs={{0,4},{4,0},{8,12},{12,8},{16,20},{20,16},{24,28},{28,24},{1,5},{5... | collective-permute-start | bytes 1769480 | tf_op jit(solution)/shard_map/ppermute | solution.py:85
  67.4 18.1 %collective-permute-start.28 = (bf16[2,2,96,768]{3,2,1,0:T(8,128)(2,1)S(1)}, bf16[2,2,96,768]{3,2,1,0:T(8,128)(2,1)S(1)}, u32[]{:S(2)}, u32[]{:S(2)}) collective-permute-start(bf16[2,2,96,768]{3,2,1,0:T(8,128)(2,1)S(1)} %line_up.6.refs_0_), channel_id=1, source_target_pairs={{0,2},{1,3},{2,0},{3,1},{4,6},{5,7},{6,4},{7,5},{8,10},{9,11},{10,... | collective-permute-start | bytes 1769480 | tf_op jit(solution)/shard_map/ppermute | solution.py:80
  68.9 14.7 %collective-permute-start.27 = (bf16[1,96,768]{2,1,0:T(8,128)(2,1)S(1)}, bf16[1,96,768]{2,1,0:T(8,128)(2,1)S(1)}, u32[]{:S(2)}, u32[]{:S(2)}) collective-permute-start(bf16[1,96,768]{2,1,0:T(8,128)(2,1)S(1)} %get-tuple-element.455), channel_id=1, source_target_pairs={{0,24},{4,28},{8,16},{12,20},{16,8},{20,12},{24,0},{28,4},{1,25},{... | collective-permute-start | bytes 442376 | tf_op jit(solution)/shard_map/ppermute | solution.py:90
  70.2 15.2 %collective-permute-start.26 = (bf16[1,96,768]{2,1,0:T(8,128)(2,1)S(1)}, bf16[1,96,768]{2,1,0:T(8,128)(2,1)S(1)}, u32[]{:S(2)}, u32[]{:S(2)}) collective-permute-start(bf16[1,96,768]{2,1,0:T(8,128)(2,1)S(1)} %get-tuple-element.455), channel_id=1, source_target_pairs={{0,16},{4,20},{8,24},{12,28},{16,0},{20,4},{24,8},{28,12},{1,17},{... | collective-permute-start | bytes 442376 | tf_op jit(solution)/shard_map/ppermute | solution.py:90
  85.5 26.2 %collective-permute-start.32 = (bf16[2,2,96,768]{3,2,1,0:T(8,128)(2,1)S(1)}, bf16[2,2,96,768]{3,2,1,0:T(8,128)(2,1)S(1)}, u32[]{:S(2)}, u32[]{:S(2)}) collective-permute-start(bf16[2,2,96,768]{3,2,1,0:T(8,128)(2,1)S(1)} %line_up.7.refs_1_), channel_id=1, source_target_pairs={{0,4},{4,0},{8,12},{12,8},{16,20},{20,16},{24,28},{28,24},{1,5},{5... | collective-permute-start | bytes 1769480 | tf_op jit(solution)/shard_map/ppermute | solution.py:85
  86.1 25.6 %collective-permute-start.31 = (bf16[2,2,96,768]{3,2,1,0:T(8,128)(2,1)S(1)}, bf16[2,2,96,768]{3,2,1,0:T(8,128)(2,1)S(1)}, u32[]{:S(2)}, u32[]{:S(2)}) collective-permute-start(bf16[2,2,96,768]{3,2,1,0:T(8,128)(2,1)S(1)} %line_up.7.refs_1_), channel_id=1, source_target_pairs={{0,2},{1,3},{2,0},{3,1},{4,6},{5,7},{6,4},{7,5},{8,10},{9,11},{10,... | collective-permute-start | bytes 1769480 | tf_op jit(solution)/shard_map/ppermute | solution.py:80
  86.7 22.9 %collective-permute-start.30 = (bf16[256,768]{1,0:T(8,128)(2,1)S(1)}, bf16[256,768]{1,0:T(8,128)(2,1)S(1)}, u32[]{:S(2)}, u32[]{:S(2)}) collective-permute-start(bf16[256,768]{1,0:T(8,128)(2,1)S(1)} %get-tuple-element.485), channel_id=1, source_target_pairs={{0,2},{1,3},{2,0},{3,1},{4,6},{5,7},{6,4},{7,5},{8,10},{9,11},{10,... | collective-permute-start | bytes 1179656 | tf_op jit(solution)/shard_map/ppermute | solution.py:80
  88.2 28.8 %collective-permute-start.33 = (bf16[2,2,96,768]{3,2,1,0:T(8,128)(2,1)S(1)}, bf16[2,2,96,768]{3,2,1,0:T(8,128)(2,1)S(1)}, u32[]{:S(2)}, u32[]{:S(2)}) collective-permute-start(bf16[2,2,96,768]{3,2,1,0:T(8,128)(2,1)S(1)} %line_up.6.refs_0_), channel_id=1, source_target_pairs={{0,1},{1,0},{2,3},{3,2},{4,5},{5,4},{6,7},{7,6},{8,9},{9,8},{10,11... | collective-permute-start | bytes 1769480 | tf_op jit(solution)/shard_map/ppermute | solution.py:76
  98.4 18.6 %collective-permute-start.34 = (bf16[2,2,96,768]{3,2,1,0:T(8,128)(2,1)S(1)}, bf16[2,2,96,768]{3,2,1,0:T(8,128)(2,1)S(1)}, u32[]{:S(2)}, u32[]{:S(2)}) collective-permute-start(bf16[2,2,96,768]{3,2,1,0:T(8,128)(2,1)S(1)} %line_up.7.refs_1_), channel_id=1, source_target_pairs={{0,1},{1,0},{2,3},{3,2},{4,5},{5,4},{6,7},{7,6},{8,9},{9,8},{10,11... | collective-permute-start | bytes 1769480 | tf_op jit(solution)/shard_map/ppermute | solution.py:76
  122.2 21.4 %collective-permute-start.39 = (bf16[2,2,2,2,96,768]{5,4,3,2,1,0:T(8,128)(2,1)S(1)}, bf16[2,2,2,2,96,768]{5,4,3,2,1,0:T(8,128)(2,1)S(1)}, u32[]{:S(2)}, u32[]{:S(2)}) collective-permute-start(bf16[2,2,2,2,96,768]{5,4,3,2,1,0:T(8,128)(2,1)S(1)} %get-tuple-element.526), channel_id=1, source_target_pairs={{0,1},{1,0},{2,3},{3,2},{4,5},{5,4},{6,7},{7,6},{8,9},{9,8},{10,11... | collective-permute-start | bytes 7077896 | tf_op jit(solution)/shard_map/ppermute | solution.py:76
  122.4 15.7 %collective-permute-start.38 = (bf16[2,2,96,768]{3,2,1,0:T(8,128)(2,1)S(1)}, bf16[2,2,96,768]{3,2,1,0:T(8,128)(2,1)S(1)}, u32[]{:S(2)}, u32[]{:S(2)}) collective-permute-start(bf16[2,2,96,768]{3,2,1,0:T(8,128)(2,1)S(1)} %collective-permute-done.32.refs_3_), channel_id=1, source_target_pairs={{0,2},{1,3},{2,0},{3,1},{4,6},{5,7},{6,4},{7,5},{8,10},{9,11},{10,... | collective-permute-start | bytes 1769480 | tf_op jit(solution)/shard_map/ppermute | solution.py:80
  122.9 15.4 %collective-permute-start.37 = (bf16[2,2,96,768]{3,2,1,0:T(8,128)(2,1)S(1)}, bf16[2,2,96,768]{3,2,1,0:T(8,128)(2,1)S(1)}, u32[]{:S(2)}, u32[]{:S(2)}) collective-permute-start(bf16[2,2,96,768]{3,2,1,0:T(8,128)(2,1)S(1)} %collective-permute-done.28.refs_2_), channel_id=1, source_target_pairs={{0,4},{4,0},{8,12},{12,8},{16,20},{20,16},{24,28},{28,24},{1,5},{5... | collective-permute-start | bytes 1769480 | tf_op jit(solution)/shard_map/ppermute | solution.py:85
  124.4 19.2 %collective-permute-start.40 = (bf16[2,2,96,768]{3,2,1,0:T(8,128)(2,1)S(1)}, bf16[2,2,96,768]{3,2,1,0:T(8,128)(2,1)S(1)}, u32[]{:S(2)}, u32[]{:S(2)}) collective-permute-start(bf16[2,2,96,768]{3,2,1,0:T(8,128)(2,1)S(1)} %collective-permute-done.28.refs_2_), channel_id=1, source_target_pairs={{0,1},{1,0},{2,3},{3,2},{4,5},{5,4},{6,7},{7,6},{8,9},{9,8},{10,11... | collective-permute-start | bytes 1769480 | tf_op jit(solution)/shard_map/ppermute | solution.py:76
  154.4 29.5 %collective-permute-start.51 = (bf16[2,2,2,96,768]{4,3,2,1,0:T(8,128)(2,1)S(1)}, bf16[2,2,2,96,768]{4,3,2,1,0:T(8,128)(2,1)S(1)}, u32[]{:S(2)}, u32[]{:S(2)}) collective-permute-start(bf16[2,2,2,96,768]{4,3,2,1,0:T(8,128)(2,1)S(1)} %get-tuple-element.631), channel_id=1, source_target_pairs={{0,2},{1,3},{2,0},{3,1},{4,6},{5,7},{6,4},{7,5},{8,10},{9,11},{10,... | collective-permute-start | bytes 3538952 | tf_op jit(solution)/shard_map/ppermute | solution.py:80
  156.0 25.7 %collective-permute-start.49 = (bf16[2,2,96,768]{3,2,1,0:T(8,128)(2,1)S(1)}, bf16[2,2,96,768]{3,2,1,0:T(8,128)(2,1)S(1)}, u32[]{:S(2)}, u32[]{:S(2)}) collective-permute-start(bf16[2,2,96,768]{3,2,1,0:T(8,128)(2,1)S(1)} %get-tuple-element.629), channel_id=1, source_target_pairs={{0,4},{4,0},{8,12},{12,8},{16,20},{20,16},{24,28},{28,24},{1,5},{5... | collective-permute-start | bytes 1769480 | tf_op jit(solution)/shard_map/ppermute | solution.py:85
  157.4 26.5 %collective-permute-start.50 = (bf16[2,2,96,768]{3,2,1,0:T(8,128)(2,1)S(1)}, bf16[2,2,96,768]{3,2,1,0:T(8,128)(2,1)S(1)}, u32[]{:S(2)}, u32[]{:S(2)}) collective-permute-start(bf16[2,2,96,768]{3,2,1,0:T(8,128)(2,1)S(1)} %get-tuple-element.630), channel_id=1, source_target_pairs={{0,4},{4,0},{8,12},{12,8},{16,20},{20,16},{24,28},{28,24},{1,5},{5... | collective-permute-start | bytes 1769480 | tf_op jit(solution)/shard_map/ppermute | solution.py:85
  175.8 10.4 %collective-permute-start.46 = (bf16[512,384]{1,0:T(8,128)(2,1)S(1)}, bf16[512,384]{1,0:T(8,128)(2,1)S(1)}, u32[]{:S(2)}, u32[]{:S(2)}) collective-permute-start(bf16[512,384]{1,0:T(8,128)(2,1)S(1)} %get-tuple-element.619), channel_id=1, source_target_pairs={{0,1},{1,0},{2,3},{3,2},{4,5},{5,4},{6,7},{7,6},{8,9},{9,8},{10,11... | collective-permute-start | bytes 1179656 | tf_op jit(solution)/shard_map/ppermute | solution.py:76
  191.1 7.6 %collective-permute-start.53 = (bf16[2,2,2,1,96,768]{5,4,3,2,1,0:T(8,128)(2,1)S(1)}, bf16[2,2,2,1,96,768]{5,4,3,2,1,0:T(8,128)(2,1)S(1)}, u32[]{:S(2)}, u32[]{:S(2)}) collective-permute-start(bf16[2,2,2,1,96,768]{5,4,3,2,1,0:T(8,128)(2,1)S(1)} %get-tuple-element.657), channel_id=1, source_target_pairs={{0,1},{1,0},{2,3},{3,2},{4,5},{5,4},{6,7},{7,6},{8,9},{9,8},{10,11... | collective-permute-start | bytes 3538952 | tf_op jit(solution)/shard_map/ppermute | solution.py:76
  191.7 26.4 %collective-permute-start.54 = (bf16[2,2,96,768]{3,2,1,0:T(8,128)(2,1)}, bf16[2,2,96,768]{3,2,1,0:T(8,128)(2,1)}, u32[]{:S(2)}, u32[]{:S(2)}) collective-permute-start(bf16[2,2,96,768]{3,2,1,0:T(8,128)(2,1)} %get-tuple-element.679), channel_id=1, source_target_pairs={{0,4},{4,0},{8,12},{12,8},{16,20},{20,16},{24,28},{28,24},{1,5},{5... | collective-permute-start | bytes 1769480 | tf_op jit(solution)/shard_map/ppermute | solution.py:85
  193.2 25.0 %collective-permute-start.55 = (bf16[2,2,96,768]{3,2,1,0:T(8,128)(2,1)}, bf16[2,2,96,768]{3,2,1,0:T(8,128)(2,1)}, u32[]{:S(2)}, u32[]{:S(2)}) collective-permute-start(bf16[2,2,96,768]{3,2,1,0:T(8,128)(2,1)} %get-tuple-element.680), channel_id=1, source_target_pairs={{0,2},{1,3},{2,0},{3,1},{4,6},{5,7},{6,4},{7,5},{8,10},{9,11},{10,... | collective-permute-start | bytes 1769480 | tf_op jit(solution)/shard_map/ppermute | solution.py:80
  200.5 21.3 %collective-permute-start.56 = (bf16[2,2,1,96,768]{4,3,2,1,0:T(8,128)(2,1)}, bf16[2,2,1,96,768]{4,3,2,1,0:T(8,128)(2,1)}, u32[]{:S(2)}, u32[]{:S(2)}) collective-permute-start(bf16[2,2,1,96,768]{4,3,2,1,0:T(8,128)(2,1)} %get-tuple-element.690), channel_id=1, source_target_pairs={{0,2},{1,3},{2,0},{3,1},{4,6},{5,7},{6,4},{7,5},{8,10},{9,11},{10,... | collective-permute-start | bytes 1769480 | tf_op jit(solution)/shard_map/ppermute | solution.py:80
  204.7 17.1 %collective-permute-start.57 = (bf16[2,1,96,768]{3,2,1,0:T(8,128)(2,1)}, bf16[2,1,96,768]{3,2,1,0:T(8,128)(2,1)}, u32[]{:S(2)}, u32[]{:S(2)}) collective-permute-start(bf16[2,1,96,768]{3,2,1,0:T(8,128)(2,1)} %get-tuple-element.691), channel_id=1, source_target_pairs={{0,4},{4,0},{8,12},{12,8},{16,20},{20,16},{24,28},{28,24},{1,5},{5... | collective-permute-start | bytes 884744 | tf_op jit(solution)/shard_map/ppermute | solution.py:85
  205.3 16.5 %collective-permute-start.58 = (bf16[2,1,96,768]{3,2,1,0:T(8,128)(2,1)}, bf16[2,1,96,768]{3,2,1,0:T(8,128)(2,1)}, u32[]{:S(2)}, u32[]{:S(2)}) collective-permute-start(bf16[2,1,96,768]{3,2,1,0:T(8,128)(2,1)} %get-tuple-element.692), channel_id=1, source_target_pairs={{0,4},{4,0},{8,12},{12,8},{16,20},{20,16},{24,28},{28,24},{1,5},{5... | collective-permute-start | bytes 884744 | tf_op jit(solution)/shard_map/ppermute | solution.py:85
  222.6 13.2 %all-to-all-start = ((f32[32,15,128]{2,1,0:T(8,128)}), f32[32,15,128]{2,1,0:T(8,128)S(1)}, u32[]{:S(2)}, u32[]{:S(2)}) async-start(f32[32,15,128]{2,1,0:T(8,128)} %broadcast_in_dim.20), calls=%async_computation | async-start | bytes 524288 | tf_op jit(solution)/shard_map/all_to_all | solution.py:99
  228.2 10.3 %collective-permute-start.59 = (bf16[2,1,96,768]{3,2,1,0:T(8,128)(2,1)S(1)}, bf16[2,1,96,768]{3,2,1,0:T(8,128)(2,1)S(1)}, u32[]{:S(2)}, u32[]{:S(2)}) collective-permute-start(bf16[2,1,96,768]{3,2,1,0:T(8,128)(2,1)S(1)} %get-tuple-element.700), channel_id=1, source_target_pairs={{0,4},{4,0},{8,12},{12,8},{16,20},{20,16},{24,28},{28,24},{1,5},{5... | collective-permute-start | bytes 884744 | tf_op jit(solution)/shard_map/ppermute | solution.py:85
  229.9 9.5 %collective-permute-start.60 = (bf16[2,1,96,768]{3,2,1,0:T(8,128)(2,1)S(1)}, bf16[2,1,96,768]{3,2,1,0:T(8,128)(2,1)S(1)}, u32[]{:S(2)}, u32[]{:S(2)}) collective-permute-start(bf16[2,1,96,768]{3,2,1,0:T(8,128)(2,1)S(1)} %get-tuple-element.701), channel_id=1, source_target_pairs={{0,2},{1,3},{2,0},{3,1},{4,6},{5,7},{6,4},{7,5},{8,10},{9,11},{10,... | collective-permute-start | bytes 884744 | tf_op jit(solution)/shard_map/ppermute | solution.py:80
  231.4 17.8 %collective-permute-start.63 = (bf16[2,96,768]{2,1,0:T(8,128)(2,1)}, bf16[2,96,768]{2,1,0:T(8,128)(2,1)}, u32[]{:S(2)}, u32[]{:S(2)}) collective-permute-start(bf16[2,96,768]{2,1,0:T(8,128)(2,1)} %get-tuple-element.718), channel_id=1, source_target_pairs={{0,8},{4,12},{8,0},{12,4},{16,24},{20,28},{24,16},{28,20},{1,9},{5... | collective-permute-start | bytes 884744 | tf_op jit(solution)/shard_map/ppermute | solution.py:90
  232.9 24.0 %collective-permute-start.64 = (bf16[2,96,768]{2,1,0:T(8,128)(2,1)}, bf16[2,96,768]{2,1,0:T(8,128)(2,1)}, u32[]{:S(2)}, u32[]{:S(2)}) collective-permute-start(bf16[2,96,768]{2,1,0:T(8,128)(2,1)} %get-tuple-element.719), channel_id=1, source_target_pairs={{0,16},{4,20},{8,24},{12,28},{16,0},{20,4},{24,8},{28,12},{1,17},{... | collective-permute-start | bytes 884744 | tf_op jit(solution)/shard_map/ppermute | solution.py:90
  235.4 22.1 %collective-permute-start.65 = (bf16[2,96,768]{2,1,0:T(8,128)(2,1)}, bf16[2,96,768]{2,1,0:T(8,128)(2,1)}, u32[]{:S(2)}, u32[]{:S(2)}) collective-permute-start(bf16[2,96,768]{2,1,0:T(8,128)(2,1)} %get-tuple-element.720), channel_id=1, source_target_pairs={{0,24},{4,28},{8,16},{12,20},{16,8},{20,12},{24,0},{28,4},{1,25},{... | collective-permute-start | bytes 884744 | tf_op jit(solution)/shard_map/ppermute | solution.py:90
  245.4 16.3 %collective-permute-start.66 = (bf16[1,96,768]{2,1,0:T(8,128)(2,1)}, bf16[1,96,768]{2,1,0:T(8,128)(2,1)}, u32[]{:S(2)}, u32[]{:S(2)}) collective-permute-start(bf16[1,96,768]{2,1,0:T(8,128)(2,1)} %get-tuple-element.729), channel_id=1, source_target_pairs={{0,8},{4,12},{8,0},{12,4},{16,24},{20,28},{24,16},{28,20},{1,9},{5... | collective-permute-start | bytes 442376 | tf_op jit(solution)/shard_map/ppermute | solution.py:90
  247.0 25.4 %collective-permute-start.67 = (bf16[1,96,768]{2,1,0:T(8,128)(2,1)}, bf16[1,96,768]{2,1,0:T(8,128)(2,1)}, u32[]{:S(2)}, u32[]{:S(2)}) collective-permute-start(bf16[1,96,768]{2,1,0:T(8,128)(2,1)} %get-tuple-element.730), channel_id=1, source_target_pairs={{0,16},{4,20},{8,24},{12,28},{16,0},{20,4},{24,8},{28,12},{1,17},{... | collective-permute-start | bytes 442376 | tf_op jit(solution)/shard_map/ppermute | solution.py:90
  249.1 23.3 %collective-permute-start.68 = (bf16[1,96,768]{2,1,0:T(8,128)(2,1)}, bf16[1,96,768]{2,1,0:T(8,128)(2,1)}, u32[]{:S(2)}, u32[]{:S(2)}) collective-permute-start(bf16[1,96,768]{2,1,0:T(8,128)(2,1)} %get-tuple-element.731), channel_id=1, source_target_pairs={{0,24},{4,28},{8,16},{12,20},{16,8},{20,12},{24,0},{28,4},{1,25},{... | collective-permute-start | bytes 442376 | tf_op jit(solution)/shard_map/ppermute | solution.py:90
  256.9 36.2 %collective-permute-start.61 = (bf16[256,768]{1,0:T(8,128)(2,1)}, bf16[256,768]{1,0:T(8,128)(2,1)}, u32[]{:S(2)}, u32[]{:S(2)}) collective-permute-start(bf16[256,768]{1,0:T(8,128)(2,1)} %copy-done.62), channel_id=1, source_target_pairs={{0,2},{1,3},{2,0},{3,1},{4,6},{5,7},{6,4},{7,5},{8,10},{9,11},{10,... | collective-permute-start | bytes 1179656 | tf_op jit(solution)/shard_map/ppermute | solution.py:80
  257.4 35.7 %collective-permute-start.62 = (bf16[256,768]{1,0:T(8,128)(2,1)}, bf16[256,768]{1,0:T(8,128)(2,1)}, u32[]{:S(2)}, u32[]{:S(2)}) collective-permute-start(bf16[256,768]{1,0:T(8,128)(2,1)} %copy-done.63), channel_id=1, source_target_pairs={{0,2},{1,3},{2,0},{3,1},{4,6},{5,7},{6,4},{7,5},{8,10},{9,11},{10,... | collective-permute-start | bytes 1179656 | tf_op jit(solution)/shard_map/ppermute | solution.py:80
  (88 other events, 766.2 us)

commit v3 on v2

--- a/solution.py
+++ b/solution.py
@@ -40,6 +40,10 @@
 in_vmem = pl.BlockSpec(memory_space=pltpu.VMEM)
 
 
+def keep_hbm(v):
+    return pltpu.with_memory_space_constraint(v, pltpu.HBM)
+
+
 def dot(left, right, dims):
     return lax.dot_general(left, right, dims, preferred_element_type=F32)
 
@@ -99,27 +103,29 @@
     return lax.all_to_all(jnp.broadcast_to(v[None], (n,) + v.shape), ("dp", "mp"), 0, 0)
 
 
-def spread_gains(gains):
-    count = gains.shape[1]
-    start = lax.axis_index("dp") * count
-    return lax.dynamic_update_slice(jnp.zeros((2, D), BF), gains.astype(BF), (0, start))
-
-
-def join_gains(wide, step):
+def gather_gains(gains):
     n = lax.axis_size("dp")
-    return wide + lax.ppermute(wide, "dp", [(i, i ^ step) for i in range(n)])
+    low = gains.astype(BF)
+    return lax.all_to_all(jnp.broadcast_to(low[None], (n,) + low.shape), "dp", 0, 0)
 
 
 def block_views(by_y):
-    which, rows, cols = by_y[0][0].shape[1:]
+    entries = [e if isinstance(e, tuple) else (e, None) for parts in by_y for e in parts]
+    rows = entries[0][0].shape[-2]
     if rows % 16 == 0:
-        return [v for parts in by_y for v in parts]
+        return [v for v, _ in entries], tuple(i for _, i in entries)
+    plain = [v if i is None else v[i] for v, i in entries]
+    which, cols = plain[0].shape[1], plain[0].shape[3]
     dp = lax.axis_index("dp")
-    both = jnp.stack([jnp.concatenate(parts, 0) for parts in by_y])
+    both = jnp.stack([jnp.concatenate(plain[2 * y : 2 * y + 2], 0) for y in range(2)])
     depth = both.shape[1]
     sides = jnp.take(both, jnp.arange(2) ^ (dp % 2), axis=0)
     lined = jnp.take(sides, jnp.arange(depth) ^ (dp // 2), axis=1)
-    return [jnp.transpose(lined, (2, 1, 0, 3, 4)).reshape(1, which, D, cols)]
+    return [jnp.transpose(lined, (2, 1, 0, 3, 4)).reshape(1, which, D, cols)], (None,)
+
+
+def pick(refs, indices):
+    return [ref if i is None else ref.at[i] for ref, i in zip(refs, indices)]
 
 
 def grads_shape(depth, which, rows, cols):
@@ -143,7 +149,7 @@
     count = 0
     for ref in refs:
         for j in range(ref.shape[0]):
-            start = pl.multiple_of(place_ref[4 + count], 16)
+            start = pl.multiple_of(place_ref[5 + count], 16)
             whole[pl.ds(start, ref.shape[2]), :] = ref[j, which, :, cols]
             count += 1
 
@@ -153,14 +159,14 @@
     for y in range(ref.shape[0]):
         for half in range(ref.shape[1]):
             for j in range(ref.shape[2]):
-                start = pl.multiple_of(place_ref[4 + count], 16)
+                start = pl.multiple_of(place_ref[5 + count], 16)
                 ref[y, half, j, which] = whole[pl.ds(start, ref.shape[4]), :]
                 count += 1
 
 
 def bias_kernel(place_ref, table_ref, out_ref):
     block = pl.program_id(0)
-    head_base = (place_ref[3] ^ block) * GROUP
+    head_base = (place_ref[2] ^ block) * GROUP
     row = lax.broadcasted_iota(jnp.int32, (TILE, TILE), 0)
     col = lax.broadcasted_iota(jnp.int32, (TILE, TILE), 1)
     for h in range(GROUP):
@@ -201,7 +207,8 @@
     return grad, jnp.sum(t * v * inverse, axis=0, keepdims=True)
 
 
-def project_kernel(n_parts, place_ref, x_ref, gain_ref, *refs):
+def project_kernel(indices, place_ref, x_ref, gain_ref, *refs):
+    n_parts = len(indices[0])
     w_refs, rest = refs[: 2 * n_parts], refs[2 * n_parts :]
     q_ref, kv_ref = rest[:2]
     whole = rest[-1]
@@ -209,7 +216,8 @@
     if len(rest) == 4:
         rest[2][...] = normed.T
     for b in range(2):
-        assemble(whole.at[b], w_refs[b * n_parts : (b + 1) * n_parts], place_ref)
+        part = pick(w_refs[b * n_parts : (b + 1) * n_parts], indices[b])
+        assemble(whole.at[b], part, place_ref)
         out = dot(normed, whole[b, :, 0:640], NN).astype(BF)
         q_ref[b] = out[:, 0:WIDTH]
         keys, values = out[:, WIDTH : 2 * WIDTH], out[:, 2 * WIDTH : 3 * WIDTH]
@@ -218,12 +226,12 @@
 
 def project(place, rows_in, gain_low, blocks, turned):
     rows = rows_in.shape[0]
-    n_parts = len(blocks[0])
+    n_parts = len(blocks[0][0])
     shapes = [shape_of((2, rows, WIDTH), BF), shape_of((2, rows, 2 * WIDTH), BF)]
     if turned:
         shapes.append(shape_of((D, rows), BF))
     return pl.pallas_call(
-        functools.partial(project_kernel, n_parts),
+        functools.partial(project_kernel, [i for _, i in blocks]),
         in_specs=[in_smem] + [in_vmem] * (2 + 2 * n_parts),
         out_specs=[in_vmem] * len(shapes),
         out_shape=shapes,
@@ -231,7 +239,7 @@
         compiler_params=params(8),
         cost_estimate=cost(2 * 2 * rows * D * 576, 5e6),
         name="project",
-    )(place, rows_in, gain_low, *blocks[0], *blocks[1])
+    )(place, rows_in, gain_low, *blocks[0][0], *blocks[1][0])
 
 
 def tile_places(place_ref):
@@ -250,7 +258,7 @@
     key = lax.broadcasted_iota(jnp.int32, (1, TILE), 1)
     sub = lax.broadcasted_iota(jnp.int32, (64, 1), 0)
     row_tiles, key_tiles = tile_places(place_ref)
-    length = place_ref[2]
+    length = place_ref[3 + place_ref[0]]
     hide = jnp.concatenate([jnp.where(key + TILE * g < length, 0.0, -1e30) for g in key_tiles], 1)
     extra = jnp.where(sub == 0, hide, 0.0).astype(BF)
     both = jnp.concatenate([kv_ref[b], other_ref[b]], 0)
@@ -302,7 +310,8 @@
     )(place, q, kv, other, bias)
 
 
-def middle_kernel(n_parts, place_ref, x_ref, gain_ref, back_ref, *refs):
+def middle_kernel(indices, place_ref, x_ref, gain_ref, back_ref, *refs):
+    n_parts = len(indices[0])
     ctx_refs, w_refs = refs[:4], refs[4 : 4 + 4 * n_parts]
     mid_ref, normed_ref, normed_t_ref, back_t_ref, whole = refs[4 + 4 * n_parts :]
     rows = x_ref.shape[0]
@@ -310,7 +319,7 @@
     back_t_ref[...] = back_ref[...].T
     blank = jnp.zeros((rows, 64), BF)
     for b in range(4):
-        part = w_refs[b * n_parts : (b + 1) * n_parts]
+        part = pick(w_refs[b * n_parts : (b + 1) * n_parts], indices[b])
         assemble(whole.at[b], part, place_ref, 0, slice(512, 768))
         total = total + dot(jnp.concatenate([blank, ctx_refs[b][...]], 1), whole[b], NT)
     mid_ref[...] = total
@@ -321,9 +330,9 @@
 
 def middle(place, rows_in, gain_low, back, ctx, blocks):
     rows = rows_in.shape[0]
-    n_parts = len(blocks[0])
-    return pl.pallas_call(
-        functools.partial(middle_kernel, n_parts),
+    n_parts = len(blocks[0][0])
+    return pl.pallas_call(
+        functools.partial(middle_kernel, [i for _, i in blocks]),
         in_specs=[in_smem] + [in_vmem] * (7 + 4 * n_parts),
         out_specs=[in_vmem] * 4,
         out_shape=[
@@ -336,14 +345,16 @@
         compiler_params=params(10),
         cost_estimate=cost(2 * rows * D * D, 8e6),
         name="middle",
-    )(place, rows_in, gain_low, back, *ctx, *[p for b in blocks for p in b])
-
-
-def feed_kernel(n_parts, first, place_ref, n_ref, nt_ref, g_ref, gt_ref, *refs):
+    )(place, rows_in, gain_low, back, *ctx, *[p for b, _ in blocks for p in b])
+
+
+def feed_kernel(indices, first, place_ref, n_ref, nt_ref, g_ref, gt_ref, *refs):
     if not first:
         acc_in, t_in = refs[:2]
         refs = refs[2:]
+    n_parts = len(indices)
     w_refs, (acc_ref, t_ref, grads_ref, wi, wf, gi, gf) = refs[:n_parts], refs[n_parts:]
+    w_refs = pick(w_refs, indices)
     assemble(wi, w_refs, place_ref, 0)
     assemble(wf, w_refs, place_ref, 1)
     pre = dot(n_ref[...], wi[...], NN)
@@ -366,10 +377,11 @@
 
 def feed(place, normed, normed_t, back, back_t, sums, block, grads):
     rows = normed.shape[0]
+    block, indices = block
     n = len(block)
     first = sums is None
     outs = pl.pallas_call(
-        functools.partial(feed_kernel, n, first),
+        functools.partial(feed_kernel, indices, first),
         in_specs=[in_smem] + [in_vmem] * (4 + n + (0 if first else 2)),
         out_specs=[in_vmem] * 3,
         out_shape=[shape_of((rows, D), F32)] * 2 + [grads],
@@ -382,7 +394,8 @@
     return (outs[0], outs[1]), outs[2]
 
 
-def turn_kernel(n_parts, place_ref, mid_ref, acc_ref, t_ref, back_ref, gain_ref, *refs):
+def turn_kernel(indices, place_ref, mid_ref, acc_ref, t_ref, back_ref, gain_ref, *refs):
+    n_parts = len(indices[0])
     w_refs = refs[: 4 * n_parts]
     rest = refs[4 * n_parts :]
     keep_ref, send_ref, grad_ref, low_t_ref, gain_grad_ref = rest[:5]
@@ -398,16 +411,16 @@
     low = grad.astype(BF)
     low_t_ref[...] = low.T
     for b in range(4):
-        part = w_refs[b * n_parts : (b + 1) * n_parts]
+        part = pick(w_refs[b * n_parts : (b + 1) * n_parts], indices[b])
         assemble(whole.at[b], part, place_ref, 0, slice(512, 768))
         cg_refs[b][...] = dot(low, whole[b], NN).astype(BF)[:, 64:]
 
 
 def turn(place, mid, acc, t_acc, back, gain_low, blocks):
     rows = mid.shape[0]
-    n_parts = len(blocks[0])
-    return pl.pallas_call(
-        functools.partial(turn_kernel, n_parts),
+    n_parts = len(blocks[0][0])
+    return pl.pallas_call(
+        functools.partial(turn_kernel, [i for _, i in blocks]),
         in_specs=[in_smem] + [in_vmem] * (5 + 4 * n_parts),
         out_specs=[in_vmem] * 9,
         out_shape=[
@@ -422,7 +435,7 @@
         compiler_params=params(12),
         cost_estimate=cost(2 * rows * D * D, 10e6),
         name="turn",
-    )(place, mid, acc, t_acc, back, gain_low, *[p for b in blocks for p in b])
+    )(place, mid, acc, t_acc, back, gain_low, *[p for b, _ in blocks for p in b])
 
 
 def attend_back_kernel(
@@ -437,8 +450,9 @@
     dq_ref,
     own_ref,
     send_ref,
+    bucket_ref,
+    ds_ref,
     sums_ref,
-    ds_ref,
 ):
     rows = q_ref.shape[1]
     step = 128
@@ -477,6 +491,18 @@
     grad = jnp.concatenate(key_grads + value_grads, 0).T
     own_ref[...] = grad[:rows]
     send_ref[...] = grad[rows:].astype(BF)
+    row = lax.broadcasted_iota(jnp.int32, (TILE, TILE), 0)
+    col = lax.broadcasted_iota(jnp.int32, (TILE, TILE), 1)
+    buckets = {t: bucket_of(col - row + (t - 2) * TILE) for t in range(1, 4)}
+    for b in range(NB):
+        masks = {t: buckets[t] == b for t in ((1, 2) if b < 16 else (2, 3))}
+        for h in range(GROUP):
+            total = jnp.zeros((TILE, TILE), F32)
+            if b % 16 == 15:
+                total = sums_ref[h, 0 if b == 15 else 4]
+            for t, mask in masks.items():
+                total = total + jnp.where(mask, sums_ref[h, t], 0.0)
+            bucket_ref[h, pl.ds(b, 1), :] = jnp.sum(total, axis=0, keepdims=True)
 
 
 def attend_back(place, q, kv, other, grads, ctx, prob, b):
@@ -489,10 +515,11 @@
             shape_of((rows, WIDTH), BF),
             shape_of((rows, 2 * WIDTH), F32),
             shape_of((rows, 2 * WIDTH), BF),
-            shape_of((GROUP, 5, TILE, TILE), F32),
+            shape_of((GROUP, NB, TILE), F32),
         ],
         scratch_shapes=[
             pltpu.VMEM((rows, 2 * rows), BF),
+            pltpu.VMEM((GROUP, 5, TILE, TILE), F32),
         ],
         compiler_params=params(8),
         cost_estimate=cost(GROUP * rows * 2 * rows * 256 * 12, 8e6),
@@ -500,41 +527,12 @@
     )(place, q, kv, other, grads, ctx, prob)
 
 
-def bucket_kernel(place_ref, *refs):
-    out_ref = refs[-1]
-    row = lax.broadcasted_iota(jnp.int32, (TILE, TILE), 0)
-    col = lax.broadcasted_iota(jnp.int32, (TILE, TILE), 1)
-    buckets = {t: bucket_of(col - row + (t - 2) * TILE) for t in range(1, 4)}
-    for r in range(4):
-        for h in range(GROUP):
-            for b in range(NB):
-                total = jnp.zeros((TILE, TILE), F32)
-                if b == 15:
-                    total = refs[r][h, 0]
-                if b == 31:
-                    total = refs[r][h, 4]
-                for t in (1, 2) if b < 16 else (2, 3):
-                    total = total + jnp.where(buckets[t] == b, refs[r][h, t], 0.0)
-                total = jnp.sum(total, axis=0, keepdims=True)
-                out_ref[place_ref[3] ^ r, h, pl.ds(b, 1), :] = total
-
-
-def bucket_sums(place, sums):
-    return pl.pallas_call(
-        bucket_kernel,
-        in_specs=[in_smem] + [in_vmem] * 4,
-        out_specs=in_vmem,
-        out_shape=shape_of((4, GROUP, NB, TILE), F32),
-        compiler_params=params(4),
-        cost_estimate=cost(32e6, 4e6),
-        name="bucket_sums",
-    )(place, *sums)
-
-
-def project_back_kernel(n_parts, first, place_ref, nt_ref, low_t_ref, ctx_ref, dq_ref, own_ref, came_ref, *refs):
+def project_back_kernel(indices, first, place_ref, nt_ref, low_t_ref, ctx_ref, dq_ref, own_ref, came_ref, *refs):
     if not first:
         acc_in, refs = refs[0], refs[1:]
+    n_parts = len(indices)
     w_refs, (acc_ref, grads_ref, whole, grad) = refs[:n_parts], refs[n_parts:]
+    w_refs = pick(w_refs, indices)
     assemble(whole, w_refs, place_ref)
     dkv = (own_ref[...] + came_ref[...].astype(F32)).astype(BF)
     heads = jnp.concatenate([dq_ref[...], dkv], 1)
@@ -548,10 +546,11 @@
 
 def project_back(place, normed_t, low_t, acc, ctx, dq, own, came, block, grads):
     rows = normed_t.shape[1]
+    block, indices = block
     n = len(block)
     first = acc is None
     outs = pl.pallas_call(
-        functools.partial(project_back_kernel, n, first),
+        functools.partial(project_back_kernel, indices, first),
         in_specs=[in_smem] + [in_vmem] * (6 + n + (0 if first else 1)),
         out_specs=[in_vmem] * 2,
         out_shape=[shape_of((rows, D), F32), grads],
@@ -568,43 +567,46 @@
     return (a.astype(F32) + b.astype(F32)).astype(BF)
 
 
-def merge_core_kernel(a_ref, b_ref, near_ref, far0_ref, far1_ref):
-    for y, far_ref in enumerate((far0_ref, far1_ref)):
-        near_ref[y] = add(a_ref[y, 0], b_ref[y, 0])
-        far_ref[...] = add(a_ref[y, 1], b_ref[y, 1])
-
-
-def merge_core(grads, came):
-    part = shape_of(grads.shape[2:], BF)
+def merge_core_kernel(*refs):
+    near0_ref, near1_ref, far0_ref, far1_ref = refs[4:]
+    for i, near_ref in enumerate((near0_ref, near1_ref)):
+        a_ref, b_ref = refs[2 * i : 2 * i + 2]
+        for y, far_ref in enumerate((far0_ref, far1_ref)):
+            near_ref[y] = add(a_ref[y, 0], b_ref[y, 0])
+            far_ref[i] = add(a_ref[y, 1], b_ref[y, 1])
+
+
+def merge_core(grads0, came0, grads2, came2):
+    part = shape_of(grads0.shape[:1] + grads0.shape[2:], BF)
     return pl.pallas_call(
         merge_core_kernel,
-        in_specs=[in_vmem] * 2,
-        out_specs=[in_vmem] * 3,
-        out_shape=[shape_of(grads.shape[:1] + grads.shape[2:], BF), part, part],
+        in_specs=[in_vmem] * 4,
+        out_specs=[in_vmem] * 4,
+        out_shape=[part] * 4,
         compiler_params=params(MERGE_MIB),
         cost_estimate=cost(1, 1),
         name="merge_core",
-    )(grads, came)
-
-
-def merge_half_kernel(near_ref, came_ref, a0_ref, b0_ref, a1_ref, b1_ref, y0_ref, y1_ref, x0_ref, x1_ref):
-    y0_ref[...] = add(near_ref[0], came_ref[0])
-    y1_ref[...] = add(near_ref[1], came_ref[1])
-    x0_ref[...] = add(a0_ref[...], b0_ref[...])
-    x1_ref[...] = add(a1_ref[...], b1_ref[...])
+    )(grads0, came0, grads2, came2)
+
+
+def merge_half_kernel(near_ref, near_came_ref, far_ref, far_came_ref, y0_ref, y1_ref, x0_ref, x1_ref):
+    y0_ref[...] = add(near_ref[0], near_came_ref[0])
+    y1_ref[...] = add(near_ref[1], near_came_ref[1])
+    x0_ref[...] = add(far_ref[0], far_came_ref[0])
+    x1_ref[...] = add(far_ref[1], far_came_ref[1])
 
 
 def merge_half(near, near_came, far, far_came):
     part = shape_of(near.shape[1:], BF)
     return pl.pallas_call(
         merge_half_kernel,
-        in_specs=[in_vmem] * 6,
+        in_specs=[in_vmem] * 4,
         out_specs=[in_vmem] * 4,
         out_shape=[part] * 4,
         compiler_params=params(MERGE_MIB),
         cost_estimate=cost(1, 1),
         name="merge_half",
-    )(near, near_came, far[0], far_came[0], far[1], far_came[1])
+    )(near, near_came, far, far_came)
 
 
 def merge_last_kernel(near_ref, near_came_ref, far_ref, far_came_ref, own_ref, *outs):
@@ -667,23 +669,49 @@
     )(weights)
 
 
-def sort_kernel(place_ref, in_ref, back_ref, in_keep, in_send, back_keep, back_send):
+def sort_kernel(place_ref, in_ref, back_ref, in_keep, in_send, back_keep, back_send, sems):
     here = place_ref[0]
-    in_keep[...], in_send[...] = in_ref[here], in_ref[1 - here]
-    back_keep[...], back_send[...] = back_ref[here], back_ref[1 - here]
+    pairs = [
+        (in_ref.at[1 - here], in_send),
+        (back_ref.at[1 - here], back_send),
+        (in_ref.at[here], in_keep),
+        (back_ref.at[here], back_keep),
+    ]
+    copies = [pltpu.make_async_copy(a, b, sems.at[i]) for i, (a, b) in enumerate(pairs)]
+    for c in copies:
+        c.start()
+    for c in copies:
+        c.wait()
 
 
 def sort_rows(place, inputs, cotangent):
     part = shape_of(inputs.shape[1:], BF)
     return pl.pallas_call(
         sort_kernel,
-        in_specs=[in_smem] + [in_vmem] * 2,
+        in_specs=[in_smem] + [in_hbm] * 2,
         out_specs=[in_vmem] * 4,
         out_shape=[part] * 4,
+        scratch_shapes=[pltpu.SemaphoreType.DMA((4,))],
         compiler_params=params(MERGE_MIB),
         cost_estimate=cost(1, 1),
         name="sort_rows",
-    )(place, inputs, cotangent)
+    )(place, keep_hbm(inputs), keep_hbm(cotangent))
+
+
+def join_gains_kernel(g_ref, out_ref):
+    out_ref[...] = jnp.concatenate([g_ref[i] for i in range(g_ref.shape[0])], 1)
+
+
+def join_gains(parts):
+    return pl.pallas_call(
+        join_gains_kernel,
+        in_specs=[in_vmem],
+        out_specs=in_vmem,
+        out_shape=shape_of((2, D), parts.dtype),
+        compiler_params=params(MERGE_MIB),
+        cost_estimate=cost(1, 1),
+        name="join_gains",
+    )(parts)
 
 
 def cast_ffn_kernel(w_ref, both_ref, wi_ref, wf_ref):
@@ -705,49 +733,49 @@
     )(weights)
 
 
-def line_up_kernel(n, *refs):
-    out_ref = refs[n]
-    cut, which = out_ref.shape[:2]
-    per = n // cut
+def line_up_kernel(cut, *refs):
+    refs, out_ref = refs[:-1], refs[-1]
+    per = len(refs) // cut
     for j in range(cut):
         for i in range(per):
-            ref = refs[j * per + i]
             if per == 1:
-                out_ref[j] = ref[...]
+                out_ref[j] = refs[j][...]
             else:
-                out_ref[j, i] = ref[0]
+                out_ref[j, i] = refs[j * per + i][0]
 
 
 def line_up(parts, cut):
-    n = len(parts)
-    which = parts[0].shape[0] * n // cut
-    return pl.pallas_call(
-        functools.partial(line_up_kernel, n),
-        in_specs=[in_vmem] * n,
+    per = len(parts) // cut
+    inner = parts[0].shape if per == 1 else (per,) + parts[0].shape[1:]
+    return pl.pallas_call(
+        functools.partial(line_up_kernel, cut),
+        in_specs=[in_vmem] * len(parts),
         out_specs=in_vmem,
-        out_shape=shape_of((cut, which) + parts[0].shape[1:], BF),
+        out_shape=shape_of((cut,) + inner, BF),
         compiler_params=params(MERGE_MIB),
         cost_estimate=cost(1, 1),
         name="line_up",
     )(*parts)
 
 
-def place_rows_kernel(place_ref, keep_ref, came_ref, out_ref):
+def place_rows_kernel(place_ref, *refs):
     here = place_ref[0]
-    out_ref[here] = keep_ref[...]
-    out_ref[1 - here] = came_ref[...]
+    for keep_ref, came_ref, out_ref in zip(refs[0:2], refs[2:4], refs[4:6]):
+        out_ref[here] = keep_ref[...]
+        out_ref[1 - here] = came_ref[...]
 
 
 def place_rows(place, keep, came):
+    part = shape_of((2,) + keep[0].shape, BF)
     return pl.pallas_call(
         place_rows_kernel,
-        in_specs=[in_smem] + [in_vmem] * 2,
-        out_specs=in_vmem,
-        out_shape=shape_of((2,) + keep.shape, keep.dtype),
+        in_specs=[in_smem] + [in_vmem] * 4,
+        out_specs=[in_vmem] * 2,
+        out_shape=[part] * 2,
         compiler_params=params(MERGE_MIB),
         cost_estimate=cost(1, 1),
         name="place_rows",
-    )(place, keep, came)
+    )(place, *keep, *came)
 
 
 def finish_kernel(x_ref, gain_ref, t_ref, mid_grad_ref, keep_ref, send_ref, gain_grad_ref):
@@ -769,6 +797,30 @@
         cost_estimate=cost(rows * D * 12, 6e6),
         name="finish",
     )(rows_in, gain_low, t_acc, mid_grad)
+
+
+def fetch_kernel(*refs):
+    n = (len(refs) - 1) // 2
+    sems = refs[-1]
+    copies = [pltpu.make_async_copy(refs[i], refs[n + i], sems.at[i]) for i in range(n)]
+    for c in copies:
+        c.start()
+    for c in copies:
+        c.wait()
+
+
+def fetch(arrays):
+    n = len(arrays)
+    return pl.pallas_call(
+        fetch_kernel,
+        in_specs=[in_hbm] * n,
+        out_specs=[in_vmem] * n,
+        out_shape=[pltpu.VMEM(v.shape, v.dtype) for v in arrays],
+        scratch_shapes=[pltpu.SemaphoreType.DMA((n,))],
+        compiler_params=params(MERGE_MIB),
+        cost_estimate=cost(1, 1),
+        name="fetch",
+    )(*[keep_hbm(v) for v in arrays])
 
 
 def update_kernel(squares_ref, small_ref, *refs):
@@ -840,8 +892,7 @@
     ]
     if shard_rows % 16:
         starts = [jnp.zeros((), jnp.int32)]
-    length = lax.dynamic_index_in_dim(lengths, x, 0, keepdims=False)
-    place = jnp.stack([v.astype(jnp.int32) for v in [x, core, length, mp] + starts])
+    place = jnp.stack([v.astype(jnp.int32) for v in [x, core, mp, lengths[0], lengths[1]] + starts])
     cut = depth // 2
     feed_shape = grads_shape(depth, 2, shard_rows, D)
     attn_shape = grads_shape(depth, 1, shard_rows, D)
@@ -849,53 +900,52 @@
     attn_low = cast_attn(attn_weights)
     attn_z = [swap_z(attn_low, k) for k in range(1, depth)]
     rows_keep, rows_send, back_keep, back_send = sort_rows(place, inputs, cotangent)
-    rows_came = swap_x(rows_send)
-    gains = join_gains(spread_gains(norm_gains), 1)
+    rows_came, back_came = swap_x(rows_send), swap_x(back_send)
     ffn_low, wi_low, wf_low = cast_ffn(ffn_weights)
+    gain_parts = gather_gains(norm_gains)
     bias = make_bias(place, bias_table)
-    attn_low, attn_z, gains, ffn_low, wi_low, wf_low, bias, place, back_send = fence(
-        attn_low, attn_z, gains, ffn_low, wi_low, wf_low, bias, place, back_send
+    attn_low, attn_z, ffn_low, wi_low, wf_low, place, bias = fence(
+        attn_low, attn_z, ffn_low, wi_low, wf_low, place, bias
     )
 
     lined = [attn_low] + attn_z
     near, far = line_up(lined[:cut], cut), line_up(lined[cut:], cut)
     near_x, far_y = swap_x(near), swap_y(far)
     ffn_near_z = [swap_z(ffn_low, k) for k in range(1, cut)]
-    gains = join_gains(gains, 2)
-    near, far, near_x, far_y, gains, ffn_near_z, wi_low, rows_came = fence(
-        near, far, near_x, far_y, gains, ffn_near_z, wi_low, rows_came
-    )
-    near_y, near_xy = swap_y(near), swap_y(near_x)
-    far_x, far_xy = swap_x(far), swap_x(far_y)
+    near, far, near_x, far_y, rows_came, wi_low, ffn_near_z = fence(
+        near, far, near_x, far_y, rows_came, wi_low, ffn_near_z
+    )
+    near, far = line_up([near, near_x], 2), line_up([far, far_y], 2)
+    near_y, far_x = swap_y(near), swap_x(far)
     wi_far_z = [swap_z(wi_low, k) for k in range(cut, depth)]
-    step = 4
-    while step < 2 * depth:
-        gains = join_gains(gains, step)
-        step *= 2
     rows_in = jnp.concatenate([rows_keep, rows_came], 0)
     ffn_near = line_up([ffn_low] + ffn_near_z, cut)
-    near_y, near_xy, far_x, far_xy, gains, rows_in, ffn_near, wi_far_z, wf_low, back_send = fence(
-        near_y, near_xy, far_x, far_xy, gains, rows_in, ffn_near, wi_far_z, wf_low, back_send
-    )
-
-    attn_blocks = {
-        0: block_views([[near, far], [near_y, far_y]]),
-        2: block_views([[near_x, far_x], [near_xy, far_xy]]),
-    }
-    across = [swap_core(v) for v in (near, far, near_y, far_y, near_x, far_x, near_xy, far_xy)]
-    wf_far_z = [swap_z(wf_low, k) for k in range(cut, depth)]
-    ffn_near_x, ffn_near_y = swap_x(ffn_near), swap_y(ffn_near)
+    gains = join_gains(gain_parts)
+    near_y, far_x, near, far, ffn_near, rows_in, gains, wf_low, back_came = fence(
+        near_y, far_x, near, far, ffn_near, rows_in, gains, wf_low, back_came
+    )
+    back = jnp.concatenate([back_keep, back_came], 0)
+
+    def attn_block(near, far, near_y, far_x, i):
+        here = far if i == 0 else far_x
+        return block_views([[(near, i), (here, 0)], [(near_y, i), (here, 1)]])
+
+    attn_blocks = {2 * i: attn_block(near, far, near_y, far_x, i) for i in range(2)}
+    near_c, far_c, near_yc, far_xc = [swap_core(v) for v in (near, far, near_y, far_x)]
     q, kv, other = {}, {}, {}
     q[0], kv[0], normed_t = project(place, rows_in, gains, [attn_blocks[0], attn_blocks[2]], True)
     q, kv, normed_t = fence(q, kv, normed_t)
     other[1] = swap_core(kv[0])
-    q, kv, across = fence(q, kv, across)
-    attn_blocks[1] = block_views([across[0:2], across[2:4]])
-    attn_blocks[3] = block_views([across[4:6], across[6:8]])
+    q, kv, near_c, far_c, near_yc, far_xc, wi_far_z, wf_low, ffn_near = fence(
+        q, kv, near_c, far_c, near_yc, far_xc, wi_far_z, wf_low, ffn_near
+    )
+    ffn_near_x, ffn_near_y = swap_x(ffn_near), swap_y(ffn_near)
+    wf_far_z = [swap_z(wf_low, k) for k in range(cut, depth)]
+    for i in range(2):
+        attn_blocks[2 * i + 1] = attn_block(near_c, far_c, near_yc, far_xc, i)
     q[1], kv[1] = project(place, rows_in, gains, [attn_blocks[1], attn_blocks[3]], False)
-    q, kv = fence(q, kv)
+    q, kv, other = fence(q, kv, other)
     other[0] = swap_core(kv[1])
-    q, kv, other[1] = fence(q, kv, other[1])
 
     ctx, prob = {}, {}
 
@@ -904,92 +954,72 @@
 
     attend_at(1)
     ctx, prob, q = fence(ctx, prob, q)
-    attend_at(3)
-    ctx, prob, q = fence(ctx, prob, q)
-    ctx, prob, q, other, wf_far_z, ffn_near_x, ffn_near_y, back_send = fence(
-        ctx, prob, q, other, wf_far_z, ffn_near_x, ffn_near_y, back_send
+    ctx, prob, q, wf_far_z, ffn_near_x, ffn_near_y, back = fence(
+        ctx, prob, q, wf_far_z, ffn_near_x, ffn_near_y, back
     )
     ffn_far = line_up([v for pair in zip(wi_far_z, wf_far_z) for v in pair], cut)
     ffn_far_x, ffn_far_y = swap_x(ffn_far), swap_y(ffn_far)
-    back_came = swap_x(back_send)
+    attend_at(3)
+    ctx, prob, q, ffn_far = fence(ctx, prob, q, ffn_far)
+    ffn_near_c, ffn_near_yc = swap_core(ffn_near), swap_core(ffn_near_y)
+    q, other = fence(q, other)
     attend_at(0)
-    ctx, prob, q, ffn_far = fence(ctx, prob, q, ffn_far)
+    ctx, prob, q = fence(ctx, prob, q)
     attend_at(2)
     ctx, prob = fence(ctx, prob)
-    ctx, back_came = fence(ctx, back_came)
-    back = jnp.concatenate([back_keep, back_came], 0)
+    ctx, ffn_near_c, ffn_near_yc, ffn_far_x, ffn_far_y = fence(
+        ctx, ffn_near_c, ffn_near_yc, ffn_far_x, ffn_far_y
+    )
+    ffn_near_xy, ffn_far_xy = swap_y(ffn_near_x), swap_x(ffn_far_y)
+    ffn_far_c, ffn_far_yc = swap_core(ffn_far), swap_core(ffn_far_y)
     mid, normed_two, normed_two_t, back_t = middle(
         place, rows_in, gains, back, [ctx[r] for r in range(4)], [attn_blocks[r] for r in range(4)]
     )
     mid, normed_two, normed_two_t, back_t = fence(mid, normed_two, normed_two_t, back_t)
-    normed_two, ffn_far_x, ffn_far_y, ffn_near_x, ffn_near_y = fence(
-        normed_two, ffn_far_x, ffn_far_y, ffn_near_x, ffn_near_y
-    )
-    ffn_near_xy, ffn_far_xy = swap_y(ffn_near_x), swap_x(ffn_far_y)
-    feed_parts = {0: [[ffn_near, ffn_far], [ffn_near_y, ffn_far_y]]}
-    feed_parts[1] = jax.tree.map(swap_core, feed_parts[0])
     grads = {}
 
-    def feed_at(r, sums):
+    def feed_at(r, sums, by_y):
         sums, out = feed(
-            place, normed_two, normed_two_t, back, back_t, sums, block_views(feed_parts[r]), feed_shape
+            place, normed_two, normed_two_t, back, back_t, sums, block_views(by_y), feed_shape
         )
         grads[r] = by_place(out, depth, shard_rows)
         return sums
 
-    sums = feed_at(0, None)
+    sums = feed_at(0, None, [[ffn_near, ffn_far], [ffn_near_y, ffn_far_y]])
+    sums, grads, ffn_far_c, ffn_far_yc = fence(sums, grads, ffn_far_c, ffn_far_yc)
+    sums = feed_at(1, sums, [[ffn_near_c, ffn_far_c], [ffn_near_yc, ffn_far_yc]])
     sums, grads = fence(sums, grads)
-    sums, grads, feed_parts[1] = fence(sums, grads, feed_parts[1])
-    sums = feed_at(1, sums)
+    sums, ffn_near_xy, ffn_far_xy, ffn_near_x, ffn_far_x = fence(
+        sums, ffn_near_xy, ffn_far_xy, ffn_near_x, ffn_far_x
+    )
+    ffn_near_xc, ffn_far_xc = swap_core(ffn_near_x), swap_core(ffn_far_x)
+    ffn_near_xyc, ffn_far_xyc = swap_core(ffn_near_xy), swap_core(ffn_far_xy)
+    sums = feed_at(2, sums, [[ffn_near_x, ffn_far_x], [ffn_near_xy, ffn_far_xy]])
     sums, grads = fence(sums, grads)
-    came = swap_core(grads[1])
-    sums, ffn_near_xy, ffn_far_xy, ffn_far_x = fence(sums, ffn_near_xy, ffn_far_xy, ffn_far_x)
-    feed_parts[2] = [[ffn_near_x, ffn_far_x], [ffn_near_xy, ffn_far_xy]]
-    feed_parts[3] = jax.tree.map(swap_core, feed_parts[2])
-    sums = feed_at(2, sums)
+    sums, ffn_near_xc, ffn_far_xc, ffn_near_xyc, ffn_far_xyc, grads = fence(
+        sums, ffn_near_xc, ffn_far_xc, ffn_near_xyc, ffn_far_xyc, grads
+    )
+    came = {0: swap_core(grads[1])}
+    sums = feed_at(3, sums, [[ffn_near_xc, ffn_far_xc], [ffn_near_xyc, ffn_far_xyc]])
     sums, grads = fence(sums, grads)
-    sums, grads, came, feed_parts[3] = fence(sums, grads, came, feed_parts[3])
-    near0, far00, far01 = merge_core(grads[0], came)
-    far01_y = swap_y(far01)
-    sums = feed_at(3, sums)
-    sums, grads, near0, far00 = fence(sums, grads, near0, far00)
-    came = swap_core(grads[3])
+    came[2] = swap_core(grads[3])
     out_keep, out_send, mid_grad, mid_low_t, gain_two_grad, *cg = turn(
         place, mid, sums[0], sums[1], back, gains, [attn_blocks[r] for r in range(4)]
     )
     cg, mid_grad, mid_low_t, out_keep, out_send = fence(cg, mid_grad, mid_low_t, out_keep, out_send)
     cg, came, grads = fence(cg, came, grads)
-    near1, far10, far11 = merge_core(grads[2], came)
-    near1_x = swap_x(near1)
-    far11_y = swap_y(far11)
-    cg, far10 = fence(cg, far10)
-
-    dq, own, send, tiles = {}, {}, {}, {}
+    near0, near1, far0, far1 = merge_core(grads[0], came[0], grads[2], came[2])
+    near1_x, far1_y = swap_x(near1), swap_y(far1)
+    cg, near0, far0 = fence(cg, near0, far0)
+
+    dq, own, send, tiles, got = {}, {}, {}, {}, {}
+    attn_grads = {}
 
     def attend_back_at(r):
         c = r % 2
         dq[r], own[r], send[r], tiles[r] = attend_back(
             place, q[c], kv[c], other[c], cg[r], ctx[r], prob[r], r // 2
         )
-
-    got = {}
-    attend_back_at(1)
-    dq, own, send, tiles, cg = fence(dq, own, send, tiles, cg)
-    got[0] = swap_core(send[1])
-    attend_back_at(3)
-    dq, own, send, tiles, cg = fence(dq, own, send, tiles, cg)
-    got[2] = swap_core(send[3])
-    attend_back_at(0)
-    dq, own, send, tiles, cg = fence(dq, own, send, tiles, cg)
-    got[1] = swap_core(send[0])
-    attend_back_at(2)
-    dq, own, send, tiles = fence(dq, own, send, tiles)
-    got[3] = swap_core(send[2])
-    send, far01_y, far11_y, near1_x, out_send = fence(send, far01_y, far11_y, near1_x, out_send)
-    ffn_y0, ffn_y1, ffn_x0, ffn_x1 = merge_half(near0, near1_x, (far00, far10), (far01_y, far11_y))
-    ffn_y1, ffn_x1 = swap_y(ffn_y1), swap_x(ffn_x1)
-    got, ffn_y0, ffn_x0 = fence(got, ffn_y0, ffn_x0)
-    attn_grads = {}
 
     def project_back_at(r, total):
         total, outs = project_back(
@@ -998,72 +1028,70 @@
         attn_grads[r] = by_place(outs, depth, shard_rows)
         return total
 
-    t_one = project_back_at(1, None)
-    t_one, attn_grads = fence(t_one, attn_grads)
-    came = {0: swap_core(attn_grads[1])}
-    t_one = project_back_at(3, t_one)
-    t_one, attn_grads = fence(t_one, attn_grads)
-    came[2] = swap_core(attn_grads[3])
-    t_one = project_back_at(0, t_one)
-    t_one, attn_grads = fence(t_one, attn_grads)
-    t_one = project_back_at(2, t_one)
-    t_one, attn_grads, came = fence(t_one, attn_grads, came)
-    near0, far00, far01 = merge_core(attn_grads[0], came[0])
-    near1, far10, far11 = merge_core(attn_grads[2], came[2])
-    near1_x = swap_x(near1)
-    far01_y, far11_y = swap_y(far01), swap_y(far11)
-    near0, far00, far10, ffn_y1, ffn_x1 = fence(near0, far00, far10, ffn_y1, ffn_x1)
+    for r in (3, 1, 2, 0):
+        attend_back_at(r)
+        dq, own, send, tiles, cg = fence(dq, own, send, tiles, cg)
+        got[r ^ 1] = swap_core(send[r])
+    cg, near1_x, far1_y, got, out_send = fence(cg, near1_x, far1_y, got, out_send)
+    ffn_y0, ffn_y1, ffn_x0, ffn_x1 = merge_half(near0, near1_x, far0, far1_y)
+    ffn_y1, ffn_x1 = swap_y(ffn_y1), swap_x(ffn_x1)
+    got, ffn_y0, ffn_x0 = fence(got, ffn_y0, ffn_x0)
+    t_one = None
+    came = {}
+    for r in (3, 1, 2, 0):
+        t_one = project_back_at(r, t_one)
+        t_one, attn_grads = fence(t_one, attn_grads)
+        if r % 2:
+            came[r - 1] = swap_core(attn_grads[r])
+    t_one, attn_grads, came, ffn_y1, ffn_x1 = fence(t_one, attn_grads, came, ffn_y1, ffn_x1)
+    near0, near1, far0, far1 = merge_core(attn_grads[0], came[0], attn_grads[2], came[2])
+    near1_x, far1_y = swap_x(near1), swap_y(far1)
     ffn_own, *ffn_far_own = merge_last(ffn_y0, ffn_y1, ffn_x0, ffn_x1)
-    ffn_back = [swap_z(v, k) for k, v in enumerate(ffn_far_own, 1)]
+    soon = [k for k in range(1, depth) if k != cut]
+    ffn_back = [swap_z(ffn_far_own[k - 1], k) for k in soon]
     in_keep, in_send, gain_one_grad = finish(rows_in, gains, t_one, mid_grad)
-    buckets = bucket_sums(place, [tiles[r] for r in range(4)])
-    in_keep, in_send, gain_one_grad, buckets, ffn_own, out_send = fence(
-        in_keep, in_send, gain_one_grad, buckets, ffn_own, out_send
-    )
-    table_part = jnp.sum(buckets, -1).reshape(H * NB)
+    lines = jnp.sum(jnp.stack([tiles[r] for r in range(4)]), -1)
+    table_part = jnp.take(lines, jnp.arange(4) ^ mp, axis=0).reshape(H * NB)
     small = jnp.concatenate([gain_one_grad[0], gain_two_grad[0], table_part])
-    small, near1_x, far01_y, far11_y = fence(small, near1_x, far01_y, far11_y)
-    attn_y0, attn_y1, attn_x0, attn_x1 = merge_half(near0, near1_x, (far00, far10), (far01_y, far11_y))
+    in_keep, in_send, small, ffn_own, near0, far0, ffn_far_own = fence(
+        in_keep, in_send, small, ffn_own, near0, far0, ffn_far_own
+    )
+    near1_x, far1_y, small, ffn_back = fence(near1_x, far1_y, small, ffn_back)
+    attn_y0, attn_y1, attn_x0, attn_x1 = merge_half(near0, near1_x, far0, far1_y)
+    attn_y1, attn_x1, ffn_back, small = fence(attn_y1, attn_x1, ffn_back, small)
     attn_y1, attn_x1 = swap_y(attn_y1), swap_x(attn_x1)
+    ffn_back += [swap_z(ffn_far_own[cut - 1], cut)]
     small = jnp.sum(from_all(small.reshape(-1, TILE)), 0)
-    small, attn_y1, attn_x1, attn_y0, attn_x0, out_send, in_send = fence(
-        small, attn_y1, attn_x1, attn_y0, attn_x0, out_send, in_send
-    )
-    attn_own, *attn_far_own = merge_last(attn_y0, attn_y1, attn_x0, attn_x1)
-    attn_back = [swap_z(v, k) for k, v in enumerate(attn_far_own, 1)]
-    out_came, in_came = swap_x(out_send), swap_x(in_send)
-    attn_own, small, ffn_back = fence(attn_own, small, ffn_back)
-    ffn_total, ffn_squares = total_of(ffn_own, ffn_back)
     gain_total = small.reshape(-1)[: 2 * D].reshape(2, D)
     table_grads = small.reshape(-1)[2 * D :].reshape(H, NB)
     gain_cols = norm_gains.shape[1]
     gain_grads = lax.dynamic_slice_in_dim(gain_total, dp * gain_cols, gain_cols, 1)
-    ffn_total, ffn_squares, gain_grads, table_grads, attn_back = fence(
-        ffn_total, ffn_squares, gain_grads, table_grads, attn_back
+    attn_y1, attn_x1, attn_y0, attn_x0, out_send, in_send, ffn_back = fence(
+        attn_y1, attn_x1, attn_y0, attn_x0, out_send, in_send, ffn_back
+    )
+    attn_own, *attn_far_own = merge_last(attn_y0, attn_y1, attn_x0, attn_x1)
+    attn_back = [swap_z(v, k) for k, v in enumerate(attn_far_own, 1)]
+    out_came, in_came = swap_x(out_send), swap_x(in_send)
+    ffn_total, ffn_squares = total_of(ffn_own, ffn_back)
+    olds = [
+        *(attn_weights, attn_first, attn_second),
+        *(ffn_weights, ffn_first, ffn_second),
+        *(norm_gains, gain_first, gain_second),
+        *(bias_table, table_first, table_second),
+    ]
+    attn_own, olds = fence(attn_own, olds)
+    olds = fetch(olds)
+    ffn_total, ffn_squares, gain_grads, table_grads, olds = fence(
+        ffn_total, ffn_squares, gain_grads, table_grads, olds
+    )
+    attn_own, attn_back, out_came, in_came, olds = fence(
+        attn_own, attn_back, out_came, in_came, olds
     )
     attn_total, attn_squares = total_of(attn_own, attn_back)
     squares = from_all(attn_squares + ffn_squares)
-    out_keep, in_keep, out_came, in_came = fence(out_keep, in_keep, out_came, in_came)
-    block_out = place_rows(place, out_keep, out_came)
-    input_grad = place_rows(place, in_keep, in_came)
+    block_out, input_grad = place_rows(place, (out_keep, in_keep), (out_came, in_came))
     grad_norm, attn_reduced, *news = update(
-        squares.reshape(-1, TILE),
-        small,
-        (attn_total, ffn_total, gain_grads, table_grads),
-        (
-            attn_weights,
-            attn_first,
-            attn_second,
-            ffn_weights,
-            ffn_first,
-            ffn_second,
-            norm_gains,
-            gain_first,
-            gain_second,
-            bias_table,
-            table_first,
-            table_second,
-        ),
+        squares.reshape(-1, TILE), small, (attn_total, ffn_total, gain_grads, table_grads), olds
     )
     return (
         block_out,

time: 301 us -> 285 us (0.947)
  waiting for transfers between devices: 61.2 us -> 46.1 us
  local copies, waits for them, and re-layouts: 36.4 us -> 32.5 us
    ppermute x14 -> x13, waiting for transfers between devices: 24.4 us -> 9.4 us  [swap_x(): return lax.ppermute(v, 'mp', [(i, i ^ 2) for i in range(4)])]
    all_to_all x1 -> x2, starting transfers between devices: 2.59 us -> 12.1 us  [from_all(): lax.all_to_all(jnp.broadcast_to(v[None], (n,) + v.shape), ('dp', 'mp'), 0...]
    ppermute x3 -> x0, waiting for transfers between devices: 6.1 us -> none  [join_gains(): return wide + lax.ppermute(wide, 'dp', [(i, i ^ step) for i in range(n)])]
    pallas_call x26, Pallas kernels: 58.4 us -> 52.6 us  [the longest x4 19.3 us: feed(): pl.pallas_call(functools.partial(feed_kernel, indices, first), in_specs=[...]
    ppermute x12 -> x9, waiting for transfers between devices: 5.21 us -> 10.8 us  [swap_y(): return lax.ppermute(v, 'dp', [(i, i ^ 1) for i in range(n)])]
    pallas_call x4, Pallas kernels: 21 us -> 26.2 us  [attend_back(): pl.pallas_call(functools.partial(attend_back_kernel, b), in_specs=[in_sme...]
    ppermute x14, waiting for transfers between devices: 25 us -> 20.1 us  [swap_z(): return lax.ppermute(v, 'dp', [(i, i ^ 2 * k) for i in range(n)])]
    ppermute x3 -> x0, starting transfers between devices: 4.81 us -> none  [join_gains(): return wide + lax.ppermute(wide, 'dp', [(i, i ^ step) for i in range(n)])]
  transfers between devices with their start and end apart: 70 -> 60, of which waited for: 15 -> 19; matrix products, arithmetic and copies ran while one was open for 3% -> 3% of each run, Pallas kernels for 32% -> 36%
where the time goes in v3:
time: 285 us; the launch traced here: 281 us
  Pallas kernels  115 us (40%)
  starting transfers between devices  68.8 us (24%)
  waiting for transfers between devices  46.1 us (16%)
  local copies, waits for them, and re-layouts  32.5 us (11%)
  blocking collectives  11.5 us (4%)
  other arithmetic  5.71 us (2%)
    ppermute x14, starting transfers between devices, swap_z(): return lax.ppermute(v, 'dp', [(i, i ^ 2 * k) for i in range(n)])  27.6 us
    unnamed x106, local copies, waits for them, and re-layouts  27.1 us
    pallas_call x4, Pallas kernels, attend_back(): pl.pallas_call(functools.partial(attend_back_kernel, b), in_specs=[in_sme...  26.2 us
    ppermute x14, waiting for transfers between devices, swap_z(): return lax.ppermute(v, 'dp', [(i, i ^ 2 * k) for i in range(n)])  20.1 us
    pallas_call x4, Pallas kernels, attend(): pl.pallas_call(functools.partial(attend_kernel, b, r_index), in_specs=[in...  19.8 us
    pallas_call x4, Pallas kernels, feed(): pl.pallas_call(functools.partial(feed_kernel, indices, first), in_specs=[...  19.3 us
    ppermute x13, starting transfers between devices, swap_x(): return lax.ppermute(v, 'mp', [(i, i ^ 2) for i in range(4)])  14.1 us
    all_to_all x2, starting transfers between devices, from_all(): lax.all_to_all(jnp.broadcast_to(v[None], (n,) + v.shape), ('dp', 'mp'), 0...  12.1 us
  transfers between devices with their start and end apart: 60, of which 19 were waited for; matrix products, arithmetic and copies ran while one was open for 3% of the time, Pallas kernels for 36%

profile of v3, /device:TPU:0, one launch (start us, length us, event | category | flops | bytes accessed | tf_op | source)
XLA Modules:
  0.0 281.2 jit_solution(4187158766266710809)
XLA Ops:
  2.4 3.0 %collective-permute-start = (bf16[1,96,768]{2,1,0:T(8,128)(2,1)}, bf16[1,96,768]{2,1,0:T(8,128)(2,1)}, u32[]{:S(2)}, u32[]{:S(2)}) collective-permute-start(bf16[1,96,768]{2,1,0:T(8,128)(2,1)} %cast_attn.1.refs_0_), channel_id=1, source_target_pairs={{0,8},{4,12},{8,0},{12,4},{16,24},{20,28},{24,16},{28,20},{1,9},{5... | collective-permute-start | bytes 442376 | tf_op jit(solution)/shard_map/ppermute | solution.py:94
  5.4 2.6 collective-permute-start.1
  8.8 2.7 sort_rows.1
  11.5 1.8 collective-permute-start.5
  13.9 5.2 %bias_tiles.1.bias_ref = f32[4,3,5,128,128]{4,3,2,1,0:T(8,128)S(1)} custom-call(s32[13]{0:T(128)S(1)} %stack.62.place_ref, f32[12,32]{1,0:T(8,128)S(1)} %copy-done.33), custom_call_target="tpu_custom_call" | custom-call | flops 1000 | bytes 1000 | tf_op jit(solution)/shard_map/bias_tiles/pallas_call | solution.py:186
  24.9 2.3 collective-permute-start.6
  28.4 1.8 collective-permute-done.4.refs_1_
  30.1 2.4 collective-permute-done.6.refs_1_
  35.3 11.5 %all_to_all.15.g_ref = bf16[8,2,96]{2,1,0:T(2,128)(2,1)S(1)} all-to-all(bf16[8,2,96]{2,1,0:T(2,128)(2,1)S(1)} %broadcast_in_dim.31), channel_id=1, replica_groups=mesh['dp'=8,'mp'=4] {'dp'}, dimensions={0} | all-to-all | bytes 6144 | tf_op jit(solution)/shard_map/all_to_all | solution.py:109
  49.5 4.6 %collective-permute-done.9 = bf16[256,768]{1,0:T(8,128)(2,1)S(1)} collective-permute-done((bf16[256,768]{1,0:T(8,128)(2,1)S(1)}, bf16[256,768]{1,0:T(8,128)(2,1)S(1)}, u32[]{:S(2)}, u32[]{:S(2)}) %collective-permute-start.9) | collective-permute-done | bytes 393248 | tf_op jit(solution)/shard_map/ppermute | solution.py:84
  55.2 2.8 collective-permute-start.15
  58.0 2.2 project.2
  60.2 2.7 collective-permute-done.15.refs_2_
  65.1 2.2 project.3
  67.4 4.1 %collective-permute-start.17 = (bf16[1,96,768]{2,1,0:T(8,128)(2,1)S(1)}, bf16[1,96,768]{2,1,0:T(8,128)(2,1)S(1)}, u32[]{:S(2)}, u32[]{:S(2)}) collective-permute-start(bf16[1,96,768]{2,1,0:T(8,128)(2,1)S(1)} %get-tuple-element.481), channel_id=1, source_target_pairs={{0,16},{4,20},{8,24},{12,28},{16,0},{20,4},{24,8},{28,12},{1,17},{... | collective-permute-start | bytes 442376 | tf_op jit(solution)/shard_map/ppermute | solution.py:94
  72.7 4.9 %attend.4 = (bf16[512,192]{1,0:T(8,128)(2,1)S(1)}, bf16[3,512,1024]{2,1,0:T(8,128)(2,1)}) custom-call(s32[13]{0:T(128)S(1)} %stack.62.place_ref, bf16[2,512,192]{2,1,0:T(8,128)(2,1)S(1)} %get-tuple-element.590.q_ref, bf16[2,512,384]{2,1,0:T(8,128)(2,1)S(1)} %get-tuple-element.471.kv_ref, bf16[2,512,384]{2,1,0:T(8,128)(2,1)S(1)} %collective-permute-done.16.other_ref, ...), custom_call_target="tpu_custom_call" | custom-call | flops 1000 | bytes 1000 | tf_op jit(solution)/shard_map/attend/pallas_call | solution.py:298
  77.7 4.9 %collective-permute-done.17.refs_1_ = bf16[1,96,768]{2,1,0:T(8,128)(2,1)S(1)} collective-permute-done((bf16[1,96,768]{2,1,0:T(8,128)(2,1)S(1)}, bf16[1,96,768]{2,1,0:T(8,128)(2,1)S(1)}, u32[]{:S(2)}, u32[]{:S(2)}) %collective-permute-start.17) | collective-permute-done | bytes 147488 | tf_op jit(solution)/shard_map/ppermute | solution.py:94
  85.3 4.9 %attend.5 = (bf16[512,192]{1,0:T(8,128)(2,1)S(1)}, bf16[3,512,1024]{2,1,0:T(8,128)(2,1)}) custom-call(s32[13]{0:T(128)S(1)} %stack.62.place_ref, bf16[2,512,192]{2,1,0:T(8,128)(2,1)S(1)} %get-tuple-element.590.q_ref, bf16[2,512,384]{2,1,0:T(8,128)(2,1)S(1)} %get-tuple-element.471.kv_ref, bf16[2,512,384]{2,1,0:T(8,128)(2,1)S(1)} %collective-permute-done.16.other_ref, ...), custom_call_target="tpu_custom_call" | custom-call | flops 1000 | bytes 1000 | tf_op jit(solution)/shard_map/attend/pallas_call | solution.py:298
  90.3 5.1 %attend.6 = (bf16[512,192]{1,0:T(8,128)(2,1)S(1)}, bf16[3,512,1024]{2,1,0:T(8,128)(2,1)}) custom-call(s32[13]{0:T(128)S(1)} %stack.62.place_ref, bf16[2,512,192]{2,1,0:T(8,128)(2,1)S(1)} %get-tuple-element.510.q_ref, bf16[2,512,384]{2,1,0:T(8,128)(2,1)S(1)} %get-tuple-element.499.kv_ref, bf16[2,512,384]{2,1,0:T(8,128)(2,1)S(1)} %collective-permute-done.21.other_ref, ...), custom_call_target="tpu_custom_call" | custom-call | flops 1000 | bytes 1000 | tf_op jit(solution)/shard_map/attend/pallas_call | solution.py:298
  95.3 4.9 %attend.7 = (bf16[512,192]{1,0:T(8,128)(2,1)S(1)}, bf16[3,512,1024]{2,1,0:T(8,128)(2,1)}) custom-call(s32[13]{0:T(128)S(1)} %stack.62.place_ref, bf16[2,512,192]{2,1,0:T(8,128)(2,1)S(1)} %get-tuple-element.510.q_ref, bf16[2,512,384]{2,1,0:T(8,128)(2,1)S(1)} %get-tuple-element.499.kv_ref, bf16[2,512,384]{2,1,0:T(8,128)(2,1)S(1)} %collective-permute-done.21.other_ref, ...), custom_call_target="tpu_custom_call" | custom-call | flops 1000 | bytes 1000 | tf_op jit(solution)/shard_map/attend/pallas_call | solution.py:298
  102.8 2.1 middle.1
  104.9 4.7 %feed.4 = (f32[512,768]{1,0:T(8,128)S(1)}, f32[512,768]{1,0:T(8,128)S(1)}, bf16[2,2,2,2,96,768]{5,4,3,2,1,0:T(8,128)(2,1)S(1)}) custom-call(s32[13]{0:T(128)S(1)} %stack.62.place_ref, bf16[512,768]{1,0:T(8,128)(2,1)S(1)} %get-tuple-element.527.n_ref, bf16[768,512]{1,0:T(8,128)(2,1)S(1)} %get-tuple-element.528.nt_ref, ...), custom_call_target="tpu_custom_call" | custom-call | flops 1000 | bytes 1000 | tf_op jit(solution)/shard_map/feed/pallas_call | solution.py:383
  109.6 5.2 %feed.5 = (f32[512,768]{1,0:T(8,128)S(1)}, f32[512,768]{1,0:T(8,128)S(1)}, bf16[2,2,2,2,96,768]{5,4,3,2,1,0:T(8,128)(2,1)S(1)}) custom-call(s32[13]{0:T(128)S(1)} %stack.62.place_ref, bf16[512,768]{1,0:T(8,128)(2,1)S(1)} %get-tuple-element.527.n_ref, bf16[768,512]{1,0:T(8,128)(2,1)S(1)} %get-tuple-element.528.nt_ref, ...), custom_call_target="tpu_custom_call", output_to_operand_aliasing={{0}: (5, {}), {1}: (6, {})} | custom-call | flops 1000 | bytes 1000 | tf_op jit(solution)/shard_map/feed/pallas_call | solution.py:383
  118.4 4.8 %feed.6 = (f32[512,768]{1,0:T(8,128)S(1)}, f32[512,768]{1,0:T(8,128)S(1)}, bf16[2,2,2,2,96,768]{5,4,3,2,1,0:T(8,128)(2,1)S(1)}) custom-call(s32[13]{0:T(128)S(1)} %stack.62.place_ref, bf16[512,768]{1,0:T(8,128)(2,1)S(1)} %get-tuple-element.527.n_ref, bf16[768,512]{1,0:T(8,128)(2,1)S(1)} %get-tuple-element.528.nt_ref, ...), custom_call_target="tpu_custom_call", output_to_operand_aliasing={{0}: (5, {}), {1}: (6, {})} | custom-call | flops 1000 | bytes 1000 | tf_op jit(solution)/shard_map/feed/pallas_call | solution.py:383
  123.3 4.8 %feed.7 = (f32[512,768]{1,0:T(8,128)S(1)}, f32[512,768]{1,0:T(8,128)S(1)}, bf16[2,2,2,2,96,768]{5,4,3,2,1,0:T(8,128)(2,1)S(1)}) custom-call(s32[13]{0:T(128)S(1)} %stack.62.place_ref, bf16[512,768]{1,0:T(8,128)(2,1)S(1)} %get-tuple-element.527.n_ref, bf16[768,512]{1,0:T(8,128)(2,1)S(1)} %get-tuple-element.528.nt_ref, ...), custom_call_target="tpu_custom_call", output_to_operand_aliasing={{0}: (5, {}), {1}: (6, {})} | custom-call | flops 1000 | bytes 1000 | tf_op jit(solution)/shard_map/feed/pallas_call | solution.py:383
  128.6 2.9 %turn.1 = (bf16[256,768]{1,0:T(8,128)(2,1)S(1)}, bf16[256,768]{1,0:T(8,128)(2,1)}, f32[512,768]{1,0:T(8,128)S(1)}, bf16[768,512]{1,0:T(8,128)(2,1)S(1)}, f32[1,7...) custom-call(s32[13]{0:T(128)S(1)} %stack.62.place_ref, ...), custom_call_target="tpu_custom_call" | custom-call | flops 1000 | bytes 1000 | tf_op jit(solution)/shard_map/turn/pallas_call | solution.py:422
  135.0 6.6 %attend_back.4 = (bf16[512,192]{1,0:T(8,128)(2,1)S(1)}, f32[512,384]{1,0:T(8,128)S(1)}, bf16[512,384]{1,0:T(8,128)(2,1)S(1)}, f32[3,32,128]{2,1,0:T(8,128)S(1)}) custom-call(s32[13]{0:T(128)S(1)} %stack.62.place_ref, bf16[2,512,192]{2,1,0:T(8,128)(2,1)S(1)} %get-tuple-element.590.q_ref, bf16[2,512,384]{2,1,0:T(8,128)(2,1)S(1)} %get-tuple-element.471.kv_ref, ...), custom_call_target="tpu_custom_call" | custom-call | flops 1000 | bytes 1000 | tf_op jit(solution)/shard_map/attend_back/pallas_call | solution.py:510
  142.2 6.4 %attend_back.5 = (bf16[512,192]{1,0:T(8,128)(2,1)S(1)}, f32[512,384]{1,0:T(8,128)S(1)}, bf16[512,384]{1,0:T(8,128)(2,1)S(1)}, f32[3,32,128]{2,1,0:T(8,128)S(1)}) custom-call(s32[13]{0:T(128)S(1)} %stack.62.place_ref, bf16[2,512,192]{2,1,0:T(8,128)(2,1)S(1)} %get-tuple-element.590.q_ref, bf16[2,512,384]{2,1,0:T(8,128)(2,1)S(1)} %get-tuple-element.471.kv_ref, ...), custom_call_target="tpu_custom_call" | custom-call | flops 1000 | bytes 1000 | tf_op jit(solution)/shard_map/attend_back/pallas_call | solution.py:510
  149.3 6.7 %attend_back.6 = (bf16[512,192]{1,0:T(8,128)(2,1)S(1)}, f32[512,384]{1,0:T(8,128)S(1)}, bf16[512,384]{1,0:T(8,128)(2,1)S(1)}, f32[3,32,128]{2,1,0:T(8,128)S(1)}) custom-call(s32[13]{0:T(128)S(1)} %stack.62.place_ref, bf16[2,512,192]{2,1,0:T(8,128)(2,1)S(1)} %get-tuple-element.510.q_ref, bf16[2,512,384]{2,1,0:T(8,128)(2,1)S(1)} %get-tuple-element.499.kv_ref, ...), custom_call_target="tpu_custom_call" | custom-call | flops 1000 | bytes 1000 | tf_op jit(solution)/shard_map/attend_back/pallas_call | solution.py:510
  156.7 6.4 %attend_back.7 = (bf16[512,192]{1,0:T(8,128)(2,1)S(1)}, f32[512,384]{1,0:T(8,128)S(1)}, bf16[512,384]{1,0:T(8,128)(2,1)S(1)}, f32[3,32,128]{2,1,0:T(8,128)S(1)}) custom-call(s32[13]{0:T(128)S(1)} %stack.62.place_ref, bf16[2,512,192]{2,1,0:T(8,128)(2,1)S(1)} %get-tuple-element.510.q_ref, bf16[2,512,384]{2,1,0:T(8,128)(2,1)S(1)} %get-tuple-element.499.kv_ref, ...), custom_call_target="tpu_custom_call" | custom-call | flops 1000 | bytes 1000 | tf_op jit(solution)/shard_map/attend_back/pallas_call | solution.py:510
  166.2 2.3 project_back.4
  168.5 2.8 project_back.5
  174.8 2.5 project_back.6
  177.3 2.5 project_back.7
  179.8 7.6 %collective-permute-done.44.near_came_ref = bf16[2,2,96,768]{3,2,1,0:T(8,128)(2,1)S(1)} collective-permute-done((bf16[2,2,96,768]{3,2,1,0:T(8,128)(2,1)S(1)}, bf16[2,2,96,768]{3,2,1,0:T(8,128)(2,1)S(1)}, u32[]{:S(2)}, u32[]{:S(2)}) %collective-permute-start.44) | collective-permute-done | bytes 589856 | tf_op jit(solution)/shard_map/ppermute | solution.py:89
  202.1 2.9 %collective-permute-start.48 = (bf16[2,96,768]{2,1,0:T(8,128)(2,1)}, bf16[2,96,768]{2,1,0:T(8,128)(2,1)}, u32[]{:S(2)}, u32[]{:S(2)}) collective-permute-start(bf16[2,96,768]{2,1,0:T(8,128)(2,1)} %get-tuple-element.724), channel_id=1, source_target_pairs={{0,8},{4,12},{8,0},{12,4},{16,24},{20,28},{24,16},{28,20},{1,9},{5... | collective-permute-start | bytes 884744 | tf_op jit(solution)/shard_map/ppermute | solution.py:94
  208.5 1.6 finish.1
  212.7 8.3 %collective-permute-done.49.refs_1_ = bf16[2,96,768]{2,1,0:T(8,128)(2,1)} collective-permute-done((bf16[2,96,768]{2,1,0:T(8,128)(2,1)}, bf16[2,96,768]{2,1,0:T(8,128)(2,1)}, u32[]{:S(2)}, u32[]{:S(2)}) %collective-permute-start.49) | collective-permute-done | bytes 294944 | tf_op jit(solution)/shard_map/ppermute | solution.py:94
  225.6 7.3 %all-to-all-start.1 = ((f32[32,15,128]{2,1,0:T(8,128)}), f32[32,15,128]{2,1,0:T(8,128)}, u32[]{:S(2)}, u32[]{:S(2)}) async-start(f32[32,15,128]{2,1,0:T(8,128)} %broadcast_in_dim.35), calls=%async_computation.1 | async-start | bytes 524288 | tf_op jit(solution)/shard_map/all_to_all | solution.py:103
  233.0 1.8 collective-permute-start.56
  236.6 3.2 %collective-permute-start.53 = (bf16[1,96,768]{2,1,0:T(8,128)(2,1)}, bf16[1,96,768]{2,1,0:T(8,128)(2,1)}, u32[]{:S(2)}, u32[]{:S(2)}) collective-permute-start(bf16[1,96,768]{2,1,0:T(8,128)(2,1)} %get-tuple-element.755), channel_id=1, source_target_pairs={{0,8},{4,12},{8,0},{12,4},{16,24},{20,28},{24,16},{28,20},{1,9},{5... | collective-permute-start | bytes 442376 | tf_op jit(solution)/shard_map/ppermute | solution.py:94
  242.2 2.1 total.2
  244.8 1.9 fetch.1
  253.4 2.1 collective-permute-done.57.refs_3_
  259.8 4.7 %all-to-all-start.2 = ((f32[32,1,128]{2,1,0:T(1,128)}), f32[32,1,128]{2,1,0:T(1,128)}, u32[]{:S(2)}, u32[]{:S(2)}) async-start(f32[32,1,128]{2,1,0:T(1,128)} %broadcast_in_dim.37), calls=%async_computation.2 | async-start | bytes 32768 | tf_op jit(solution)/shard_map/all_to_all | solution.py:103
  266.5 2.3 place_rows.1
  268.8 2.7 all-to-all-done.2
  277.4 3.4 %update.1 = (f32[1,1]{1,0:T(1,128)}, f32[4,96,192]{2,1,0:T(8,128)}, f32[4,96,192]{2,1,0:T(8,128)}, f32[4,96,192]{2,1,0:T(8,128)}, f32[4,96,192]{2,1,0:T(8,128)},...) custom-call(f32[32,128]{1,0:T(8,128)} %bitcast.18.squares_ref, ...), custom_call_target="tpu_custom_call" | custom-call | flops 1000 | bytes 1000 | tf_op jit(solution)/shard_map/update/pallas_call | solution.py:856
  (245 shorter events, 90.3 us)
Async XLA Ops:
  2.4 16.7 %collective-permute-start = (bf16[1,96,768]{2,1,0:T(8,128)(2,1)}, bf16[1,96,768]{2,1,0:T(8,128)(2,1)}, u32[]{:S(2)}, u32[]{:S(2)}) collective-permute-start(bf16[1,96,768]{2,1,0:T(8,128)(2,1)} %cast_attn.1.refs_0_), channel_id=1, source_target_pairs={{0,8},{4,12},{8,0},{12,4},{16,24},{20,28},{24,16},{28,20},{1,9},{5... | collective-permute-start | bytes 442376 | tf_op jit(solution)/shard_map/ppermute | solution.py:94
  5.4 14.3 %collective-permute-start.1 = (bf16[1,96,768]{2,1,0:T(8,128)(2,1)}, bf16[1,96,768]{2,1,0:T(8,128)(2,1)}, u32[]{:S(2)}, u32[]{:S(2)}) collective-permute-start(bf16[1,96,768]{2,1,0:T(8,128)(2,1)} %cast_attn.1.refs_0_), channel_id=1, source_target_pairs={{0,16},{4,20},{8,24},{12,28},{16,0},{20,4},{24,8},{28,12},{1,17},{... | collective-permute-start | bytes 442376 | tf_op jit(solution)/shard_map/ppermute | solution.py:94
  8.0 11.7 %collective-permute-start.2 = (bf16[1,96,768]{2,1,0:T(8,128)(2,1)}, bf16[1,96,768]{2,1,0:T(8,128)(2,1)}, u32[]{:S(2)}, u32[]{:S(2)}) collective-permute-start(bf16[1,96,768]{2,1,0:T(8,128)(2,1)} %cast_attn.1.refs_0_), channel_id=1, source_target_pairs={{0,24},{4,28},{8,16},{12,20},{16,8},{20,12},{24,0},{28,4},{1,25},{... | collective-permute-start | bytes 442376 | tf_op jit(solution)/shard_map/ppermute | solution.py:94
  11.5 15.8 %collective-permute-start.5 = (bf16[256,768]{1,0:T(8,128)(2,1)}, bf16[256,768]{1,0:T(8,128)(2,1)}, u32[]{:S(2)}, u32[]{:S(2)}) collective-permute-start(bf16[256,768]{1,0:T(8,128)(2,1)} %get-tuple-element.439), channel_id=1, source_target_pairs={{0,2},{1,3},{2,0},{3,1},{4,6},{5,7},{6,4},{7,5},{8,10},{9,11},{10,... | collective-permute-start | bytes 1179656 | tf_op jit(solution)/shard_map/ppermute | solution.py:84
  32.6 21.6 %collective-permute-start.7 = (bf16[2,2,1,96,768]{4,3,2,1,0:T(8,128)(2,1)S(1)}, bf16[2,2,1,96,768]{4,3,2,1,0:T(8,128)(2,1)S(1)}, u32[]{:S(2)}, u32[]{:S(2)}) collective-permute-start(bf16[2,2,1,96,768]{4,3,2,1,0:T(8,128)(2,1)S(1)} %line_up.8.refs_0_.refs_4_.refs_12_.refs_8_.refs_1_), channel_id=1, source_target_pairs={{0,4},{4,0},{8,12},{12,8},{16,20},{20,16},{24,28},{28,24},{1,5},{5... | collective-permute-start | bytes 1769480 | tf_op jit(solution)/shard_map/ppermute | solution.py:89
  33.2 21.0 %collective-permute-start.8 = (bf16[2,2,1,96,768]{4,3,2,1,0:T(8,128)(2,1)S(1)}, bf16[2,2,1,96,768]{4,3,2,1,0:T(8,128)(2,1)S(1)}, u32[]{:S(2)}, u32[]{:S(2)}) collective-permute-start(bf16[2,2,1,96,768]{4,3,2,1,0:T(8,128)(2,1)S(1)} %line_up.9.refs_1_.refs_3_.refs_5_.refs_7_.refs_2_.refs_4_), channel_id=1, source_target_pairs={{0,2},{1,3},{2,0},{3,1},{4,6},{5,7},{6,4},{7,5},{8,10},{9,11},{10,... | collective-permute-start | bytes 1769480 | tf_op jit(solution)/shard_map/ppermute | solution.py:84
  33.8 20.4 %collective-permute-start.9 = (bf16[256,768]{1,0:T(8,128)(2,1)S(1)}, bf16[256,768]{1,0:T(8,128)(2,1)S(1)}, u32[]{:S(2)}, u32[]{:S(2)}) collective-permute-start(bf16[256,768]{1,0:T(8,128)(2,1)S(1)} %get-tuple-element.450), channel_id=1, source_target_pairs={{0,2},{1,3},{2,0},{3,1},{4,6},{5,7},{6,4},{7,5},{8,10},{9,11},{10,... | collective-permute-start | bytes 1179656 | tf_op jit(solution)/shard_map/ppermute | solution.py:84
  46.9 8.3 %collective-permute-start.14 = (bf16[1,96,768]{2,1,0:T(8,128)(2,1)S(1)}, bf16[1,96,768]{2,1,0:T(8,128)(2,1)S(1)}, u32[]{:S(2)}, u32[]{:S(2)}) collective-permute-start(bf16[1,96,768]{2,1,0:T(8,128)(2,1)S(1)} %get-tuple-element.459), channel_id=1, source_target_pairs={{0,16},{4,20},{8,24},{12,28},{16,0},{20,4},{24,8},{28,12},{1,17},{... | collective-permute-start | bytes 442376 | tf_op jit(solution)/shard_map/ppermute | solution.py:94
  54.2 8.8 %collective-permute-start.10 = (bf16[2,2,1,96,768]{4,3,2,1,0:T(8,128)(2,1)S(1)}, bf16[2,2,1,96,768]{4,3,2,1,0:T(8,128)(2,1)S(1)}, u32[]{:S(2)}, u32[]{:S(2)}) collective-permute-start(bf16[2,2,1,96,768]{4,3,2,1,0:T(8,128)(2,1)S(1)} %line_up.8.refs_0_.refs_4_.refs_12_.refs_8_.refs_1_), channel_id=1, source_target_pairs={{0,1},{1,0},{2,3},{3,2},{4,5},{5,4},{6,7},{7,6},{8,9},{9,8},{10,11... | collective-permute-start | bytes 1769480 | tf_op jit(solution)/shard_map/ppermute | solution.py:80
  54.2 8.8 %collective-permute-start.11 = (bf16[2,2,1,96,768]{4,3,2,1,0:T(8,128)(2,1)S(1)}, bf16[2,2,1,96,768]{4,3,2,1,0:T(8,128)(2,1)S(1)}, u32[]{:S(2)}, u32[]{:S(2)}) collective-permute-start(bf16[2,2,1,96,768]{4,3,2,1,0:T(8,128)(2,1)S(1)} %line_up.9.refs_1_.refs_3_.refs_5_.refs_7_.refs_2_.refs_4_), channel_id=1, source_target_pairs={{0,1},{1,0},{2,3},{3,2},{4,5},{5,4},{6,7},{7,6},{8,9},{9,8},{10,11... | collective-permute-start | bytes 1769480 | tf_op jit(solution)/shard_map/ppermute | solution.py:80
  54.7 8.3 %collective-permute-start.12 = (bf16[2,2,1,96,768]{4,3,2,1,0:T(8,128)(2,1)S(1)}, bf16[2,2,1,96,768]{4,3,2,1,0:T(8,128)(2,1)S(1)}, u32[]{:S(2)}, u32[]{:S(2)}) collective-permute-start(bf16[2,2,1,96,768]{4,3,2,1,0:T(8,128)(2,1)S(1)} %collective-permute-done.7.refs_2_.refs_6_.refs_14_.refs_10_.refs_3_), channel_id=1, source_target_pairs={{0,1},{1,0},{2,3},{3,2},{4,5},{5,4},{6,7},{7,6},{8,9},{9,8},{10,11... | collective-permute-start | bytes 1769480 | tf_op jit(solution)/shard_map/ppermute | solution.py:80
  54.7 8.2 %collective-permute-start.13 = (bf16[2,2,1,96,768]{4,3,2,1,0:T(8,128)(2,1)S(1)}, bf16[2,2,1,96,768]{4,3,2,1,0:T(8,128)(2,1)S(1)}, u32[]{:S(2)}, u32[]{:S(2)}) collective-permute-start(bf16[2,2,1,96,768]{4,3,2,1,0:T(8,128)(2,1)S(1)} %collective-permute-done.8.refs_5_.refs_7_.refs_13_.refs_15_.refs_9_.refs_11_., ...), channel_id=1, source_target_pairs={{0,1},{1,0},{2,3},{3,2},{4,5},{5,4},{6,7},{7,6},{8,9},{9,8},{10,11... | collective-permute-start | bytes 1769480 | tf_op jit(solution)/shard_map/ppermute | solution.py:80
  63.0 19.6 %collective-permute-start.19 = (bf16[2,2,96,768]{3,2,1,0:T(8,128)(2,1)S(1)}, bf16[2,2,96,768]{3,2,1,0:T(8,128)(2,1)S(1)}, u32[]{:S(2)}, u32[]{:S(2)}) collective-permute-start(bf16[2,2,96,768]{3,2,1,0:T(8,128)(2,1)S(1)} %line_up.10.refs_0_), channel_id=1, source_target_pairs={{0,2},{1,3},{2,0},{3,1},{4,6},{5,7},{6,4},{7,5},{8,10},{9,11},{10,... | collective-permute-start | bytes 1769480 | tf_op jit(solution)/shard_map/ppermute | solution.py:84
  63.5 19.0 %collective-permute-start.20 = (bf16[2,2,96,768]{3,2,1,0:T(8,128)(2,1)S(1)}, bf16[2,2,96,768]{3,2,1,0:T(8,128)(2,1)S(1)}, u32[]{:S(2)}, u32[]{:S(2)}) collective-permute-start(bf16[2,2,96,768]{3,2,1,0:T(8,128)(2,1)S(1)} %line_up.10.refs_0_), channel_id=1, source_target_pairs={{0,4},{4,0},{8,12},{12,8},{16,20},{20,16},{24,28},{28,24},{1,5},{5... | collective-permute-start | bytes 1769480 | tf_op jit(solution)/shard_map/ppermute | solution.py:89
  67.3 22.9 %collective-permute-start.21 = (bf16[2,512,384]{2,1,0:T(8,128)(2,1)S(1)}, bf16[2,512,384]{2,1,0:T(8,128)(2,1)S(1)}, u32[]{:S(2)}, u32[]{:S(2)}) collective-permute-start(bf16[2,512,384]{2,1,0:T(8,128)(2,1)S(1)} %get-tuple-element.471.kv_ref), channel_id=1, source_target_pairs={{0,1},{1,0},{2,3},{3,2},{4,5},{5,4},{6,7},{7,6},{8,9},{9,8},{10,11... | collective-permute-start | bytes 2359304 | tf_op jit(solution)/shard_map/ppermute | solution.py:80
  67.4 15.1 %collective-permute-start.17 = (bf16[1,96,768]{2,1,0:T(8,128)(2,1)S(1)}, bf16[1,96,768]{2,1,0:T(8,128)(2,1)S(1)}, u32[]{:S(2)}, u32[]{:S(2)}) collective-permute-start(bf16[1,96,768]{2,1,0:T(8,128)(2,1)S(1)} %get-tuple-element.481), channel_id=1, source_target_pairs={{0,16},{4,20},{8,24},{12,28},{16,0},{20,4},{24,8},{28,12},{1,17},{... | collective-permute-start | bytes 442376 | tf_op jit(solution)/shard_map/ppermute | solution.py:94
  71.5 11.0 %collective-permute-start.18 = (bf16[1,96,768]{2,1,0:T(8,128)(2,1)S(1)}, bf16[1,96,768]{2,1,0:T(8,128)(2,1)S(1)}, u32[]{:S(2)}, u32[]{:S(2)}) collective-permute-start(bf16[1,96,768]{2,1,0:T(8,128)(2,1)S(1)} %get-tuple-element.481), channel_id=1, source_target_pairs={{0,24},{4,28},{8,16},{12,20},{16,8},{20,12},{24,0},{28,4},{1,25},{... | collective-permute-start | bytes 442376 | tf_op jit(solution)/shard_map/ppermute | solution.py:94
  82.5 17.7 %collective-permute-start.22 = (bf16[2,2,96,768]{3,2,1,0:T(8,128)(2,1)S(1)}, bf16[2,2,96,768]{3,2,1,0:T(8,128)(2,1)S(1)}, u32[]{:S(2)}, u32[]{:S(2)}) collective-permute-start(bf16[2,2,96,768]{3,2,1,0:T(8,128)(2,1)S(1)} %line_up.10.refs_0_), channel_id=1, source_target_pairs={{0,1},{1,0},{2,3},{3,2},{4,5},{5,4},{6,7},{7,6},{8,9},{9,8},{10,11... | collective-permute-start | bytes 1769480 | tf_op jit(solution)/shard_map/ppermute | solution.py:80
  82.5 17.7 %collective-permute-start.23 = (bf16[2,2,96,768]{3,2,1,0:T(8,128)(2,1)S(1)}, bf16[2,2,96,768]{3,2,1,0:T(8,128)(2,1)S(1)}, u32[]{:S(2)}, u32[]{:S(2)}) collective-permute-start(bf16[2,2,96,768]{3,2,1,0:T(8,128)(2,1)S(1)} %collective-permute-done.20.refs_2_), channel_id=1, source_target_pairs={{0,1},{1,0},{2,3},{3,2},{4,5},{5,4},{6,7},{7,6},{8,9},{9,8},{10,11... | collective-permute-start | bytes 1769480 | tf_op jit(solution)/shard_map/ppermute | solution.py:80
  83.2 17.1 %collective-permute-start.24 = (bf16[2,2,96,768]{3,2,1,0:T(8,128)(2,1)S(1)}, bf16[2,2,96,768]{3,2,1,0:T(8,128)(2,1)S(1)}, u32[]{:S(2)}, u32[]{:S(2)}) collective-permute-start(bf16[2,2,96,768]{3,2,1,0:T(8,128)(2,1)S(1)} %line_up.11.refs_1_), channel_id=1, source_target_pairs={{0,2},{1,3},{2,0},{3,1},{4,6},{5,7},{6,4},{7,5},{8,10},{9,11},{10,... | collective-permute-start | bytes 1769480 | tf_op jit(solution)/shard_map/ppermute | solution.py:84
  84.7 15.6 %collective-permute-start.25 = (bf16[2,2,96,768]{3,2,1,0:T(8,128)(2,1)S(1)}, bf16[2,2,96,768]{3,2,1,0:T(8,128)(2,1)S(1)}, u32[]{:S(2)}, u32[]{:S(2)}) collective-permute-start(bf16[2,2,96,768]{3,2,1,0:T(8,128)(2,1)S(1)} %line_up.11.refs_1_), channel_id=1, source_target_pairs={{0,4},{4,0},{8,12},{12,8},{16,20},{20,16},{24,28},{28,24},{1,5},{5... | collective-permute-start | bytes 1769480 | tf_op jit(solution)/shard_map/ppermute | solution.py:89
  90.2 19.4 %collective-permute-start.26 = (bf16[2,2,96,768]{3,2,1,0:T(8,128)(2,1)S(1)}, bf16[2,2,96,768]{3,2,1,0:T(8,128)(2,1)S(1)}, u32[]{:S(2)}, u32[]{:S(2)}) collective-permute-start(bf16[2,2,96,768]{3,2,1,0:T(8,128)(2,1)S(1)} %line_up.11.refs_1_), channel_id=1, source_target_pairs={{0,1},{1,0},{2,3},{3,2},{4,5},{5,4},{6,7},{7,6},{8,9},{9,8},{10,11... | collective-permute-start | bytes 1769480 | tf_op jit(solution)/shard_map/ppermute | solution.py:80
  100.3 9.3 %collective-permute-start.27 = (bf16[2,2,96,768]{3,2,1,0:T(8,128)(2,1)S(1)}, bf16[2,2,96,768]{3,2,1,0:T(8,128)(2,1)S(1)}, u32[]{:S(2)}, u32[]{:S(2)}) collective-permute-start(bf16[2,2,96,768]{3,2,1,0:T(8,128)(2,1)S(1)} %collective-permute-done.25.refs_3_), channel_id=1, source_target_pairs={{0,1},{1,0},{2,3},{3,2},{4,5},{5,4},{6,7},{7,6},{8,9},{9,8},{10,11... | collective-permute-start | bytes 1769480 | tf_op jit(solution)/shard_map/ppermute | solution.py:80
  100.8 15.3 %collective-permute-start.28 = (bf16[2,2,96,768]{3,2,1,0:T(8,128)(2,1)S(1)}, bf16[2,2,96,768]{3,2,1,0:T(8,128)(2,1)S(1)}, u32[]{:S(2)}, u32[]{:S(2)}) collective-permute-start(bf16[2,2,96,768]{3,2,1,0:T(8,128)(2,1)S(1)} %collective-permute-done.19.refs_2_), channel_id=1, source_target_pairs={{0,4},{4,0},{8,12},{12,8},{16,20},{20,16},{24,28},{28,24},{1,5},{5... | collective-permute-start | bytes 1769480 | tf_op jit(solution)/shard_map/ppermute | solution.py:89
  102.3 15.0 %collective-permute-start.29 = (bf16[2,2,96,768]{3,2,1,0:T(8,128)(2,1)S(1)}, bf16[2,2,96,768]{3,2,1,0:T(8,128)(2,1)S(1)}, u32[]{:S(2)}, u32[]{:S(2)}) collective-permute-start(bf16[2,2,96,768]{3,2,1,0:T(8,128)(2,1)S(1)} %collective-permute-done.25.refs_3_), channel_id=1, source_target_pairs={{0,2},{1,3},{2,0},{3,1},{4,6},{5,7},{6,4},{7,5},{8,10},{9,11},{10,... | collective-permute-start | bytes 1769480 | tf_op jit(solution)/shard_map/ppermute | solution.py:84
  123.2 8.3 %collective-permute-start.34 = (bf16[2,2,2,2,96,768]{5,4,3,2,1,0:T(8,128)(2,1)S(1)}, bf16[2,2,2,2,96,768]{5,4,3,2,1,0:T(8,128)(2,1)S(1)}, u32[]{:S(2)}, u32[]{:S(2)}) collective-permute-start(bf16[2,2,2,2,96,768]{5,4,3,2,1,0:T(8,128)(2,1)S(1)} %get-tuple-element.574), channel_id=1, source_target_pairs={{0,1},{1,0},{2,3},{3,2},{4,5},{5,4},{6,7},{7,6},{8,9},{9,8},{10,11... | collective-permute-start | bytes 7077896 | tf_op jit(solution)/shard_map/ppermute | solution.py:80
  133.8 31.8 %collective-permute-start.36 = (bf16[2,2,2,96,768]{4,3,2,1,0:T(8,128)(2,1)S(1)}, bf16[2,2,2,96,768]{4,3,2,1,0:T(8,128)(2,1)S(1)}, u32[]{:S(2)}, u32[]{:S(2)}) collective-permute-start(bf16[2,2,2,96,768]{4,3,2,1,0:T(8,128)(2,1)S(1)} %get-tuple-element.662), channel_id=1, source_target_pairs={{0,2},{1,3},{2,0},{3,1},{4,6},{5,7},{6,4},{7,5},{8,10},{9,11},{10,... | collective-permute-start | bytes 3538952 | tf_op jit(solution)/shard_map/ppermute | solution.py:84
  134.4 31.2 %collective-permute-start.37 = (bf16[2,2,2,96,768]{4,3,2,1,0:T(8,128)(2,1)S(1)}, bf16[2,2,2,96,768]{4,3,2,1,0:T(8,128)(2,1)S(1)}, u32[]{:S(2)}, u32[]{:S(2)}) collective-permute-start(bf16[2,2,2,96,768]{4,3,2,1,0:T(8,128)(2,1)S(1)} %get-tuple-element.663), channel_id=1, source_target_pairs={{0,4},{4,0},{8,12},{12,8},{16,20},{20,16},{24,28},{28,24},{1,5},{5... | collective-permute-start | bytes 3538952 | tf_op jit(solution)/shard_map/ppermute | solution.py:89
  148.7 15.0 %collective-permute-start.38 = (bf16[512,384]{1,0:T(8,128)(2,1)S(1)}, bf16[512,384]{1,0:T(8,128)(2,1)S(1)}, u32[]{:S(2)}, u32[]{:S(2)}) collective-permute-start(bf16[512,384]{1,0:T(8,128)(2,1)S(1)} %get-tuple-element.638), channel_id=1, source_target_pairs={{0,1},{1,0},{2,3},{3,2},{4,5},{5,4},{6,7},{7,6},{8,9},{9,8},{10,11... | collective-permute-start | bytes 1179656 | tf_op jit(solution)/shard_map/ppermute | solution.py:80
  149.3 15.7 %collective-permute-start.40 = (bf16[512,384]{1,0:T(8,128)(2,1)S(1)}, bf16[512,384]{1,0:T(8,128)(2,1)S(1)}, u32[]{:S(2)}, u32[]{:S(2)}) collective-permute-start(bf16[512,384]{1,0:T(8,128)(2,1)S(1)} %get-tuple-element.625), channel_id=1, source_target_pairs={{0,1},{1,0},{2,3},{3,2},{4,5},{5,4},{6,7},{7,6},{8,9},{9,8},{10,11... | collective-permute-start | bytes 1179656 | tf_op jit(solution)/shard_map/ppermute | solution.py:80
  171.3 17.4 %collective-permute-start.42 = (bf16[2,2,2,1,96,768]{5,4,3,2,1,0:T(8,128)(2,1)S(1)}, bf16[2,2,2,1,96,768]{5,4,3,2,1,0:T(8,128)(2,1)S(1)}, u32[]{:S(2)}, u32[]{:S(2)}) collective-permute-start(bf16[2,2,2,1,96,768]{5,4,3,2,1,0:T(8,128)(2,1)S(1)} %get-tuple-element.692), channel_id=1, source_target_pairs={{0,1},{1,0},{2,3},{3,2},{4,5},{5,4},{6,7},{7,6},{8,9},{9,8},{10,11... | collective-permute-start | bytes 3538952 | tf_op jit(solution)/shard_map/ppermute | solution.py:80
  171.7 16.9 %collective-permute-start.43 = (bf16[2,2,2,1,96,768]{5,4,3,2,1,0:T(8,128)(2,1)S(1)}, bf16[2,2,2,1,96,768]{5,4,3,2,1,0:T(8,128)(2,1)S(1)}, u32[]{:S(2)}, u32[]{:S(2)}) collective-permute-start(bf16[2,2,2,1,96,768]{5,4,3,2,1,0:T(8,128)(2,1)S(1)} %get-tuple-element.689), channel_id=1, source_target_pairs={{0,1},{1,0},{2,3},{3,2},{4,5},{5,4},{6,7},{7,6},{8,9},{9,8},{10,11... | collective-permute-start | bytes 3538952 | tf_op jit(solution)/shard_map/ppermute | solution.py:80
  171.9 15.6 %collective-permute-start.44 = (bf16[2,2,96,768]{3,2,1,0:T(8,128)(2,1)S(1)}, bf16[2,2,96,768]{3,2,1,0:T(8,128)(2,1)S(1)}, u32[]{:S(2)}, u32[]{:S(2)}) collective-permute-start(bf16[2,2,96,768]{3,2,1,0:T(8,128)(2,1)S(1)} %get-tuple-element.701), channel_id=1, source_target_pairs={{0,4},{4,0},{8,12},{12,8},{16,20},{20,16},{24,28},{28,24},{1,5},{5... | collective-permute-start | bytes 1769480 | tf_op jit(solution)/shard_map/ppermute | solution.py:89
  173.3 15.3 %collective-permute-start.45 = (bf16[2,2,96,768]{3,2,1,0:T(8,128)(2,1)S(1)}, bf16[2,2,96,768]{3,2,1,0:T(8,128)(2,1)S(1)}, u32[]{:S(2)}, u32[]{:S(2)}) collective-permute-start(bf16[2,2,96,768]{3,2,1,0:T(8,128)(2,1)S(1)} %get-tuple-element.702), channel_id=1, source_target_pairs={{0,2},{1,3},{2,0},{3,1},{4,6},{5,7},{6,4},{7,5},{8,10},{9,11},{10,... | collective-permute-start | bytes 1769480 | tf_op jit(solution)/shard_map/ppermute | solution.py:84
  191.8 29.2 %collective-permute-start.46 = (bf16[2,2,1,96,768]{4,3,2,1,0:T(8,128)(2,1)}, bf16[2,2,1,96,768]{4,3,2,1,0:T(8,128)(2,1)}, u32[]{:S(2)}, u32[]{:S(2)}) collective-permute-start(bf16[2,2,1,96,768]{4,3,2,1,0:T(8,128)(2,1)} %get-tuple-element.729), channel_id=1, source_target_pairs={{0,2},{1,3},{2,0},{3,1},{4,6},{5,7},{6,4},{7,5},{8,10},{9,11},{10,... | collective-permute-start | bytes 1769480 | tf_op jit(solution)/shard_map/ppermute | solution.py:84
  193.3 27.7 %collective-permute-start.47 = (bf16[2,2,1,96,768]{4,3,2,1,0:T(8,128)(2,1)}, bf16[2,2,1,96,768]{4,3,2,1,0:T(8,128)(2,1)}, u32[]{:S(2)}, u32[]{:S(2)}) collective-permute-start(bf16[2,2,1,96,768]{4,3,2,1,0:T(8,128)(2,1)} %get-tuple-element.730), channel_id=1, source_target_pairs={{0,4},{4,0},{8,12},{12,8},{16,20},{20,16},{24,28},{28,24},{1,5},{5... | collective-permute-start | bytes 1769480 | tf_op jit(solution)/shard_map/ppermute | solution.py:89
  202.1 10.7 %collective-permute-start.48 = (bf16[2,96,768]{2,1,0:T(8,128)(2,1)}, bf16[2,96,768]{2,1,0:T(8,128)(2,1)}, u32[]{:S(2)}, u32[]{:S(2)}) collective-permute-start(bf16[2,96,768]{2,1,0:T(8,128)(2,1)} %get-tuple-element.724), channel_id=1, source_target_pairs={{0,8},{4,12},{8,0},{12,4},{16,24},{20,28},{24,16},{28,20},{1,9},{5... | collective-permute-start | bytes 884744 | tf_op jit(solution)/shard_map/ppermute | solution.py:94
  205.0 16.1 %collective-permute-start.49 = (bf16[2,96,768]{2,1,0:T(8,128)(2,1)}, bf16[2,96,768]{2,1,0:T(8,128)(2,1)}, u32[]{:S(2)}, u32[]{:S(2)}) collective-permute-start(bf16[2,96,768]{2,1,0:T(8,128)(2,1)} %get-tuple-element.726), channel_id=1, source_target_pairs={{0,24},{4,28},{8,16},{12,20},{16,8},{20,12},{24,0},{28,4},{1,25},{... | collective-permute-start | bytes 884744 | tf_op jit(solution)/shard_map/ppermute | solution.py:94
  211.6 21.4 %collective-permute-start.52 = (bf16[2,96,768]{2,1,0:T(8,128)(2,1)}, bf16[2,96,768]{2,1,0:T(8,128)(2,1)S(1)}, u32[]{:S(2)}, u32[]{:S(2)}) collective-permute-start(bf16[2,96,768]{2,1,0:T(8,128)(2,1)} %copy-done.48), channel_id=1, source_target_pairs={{0,16},{4,20},{8,24},{12,28},{16,0},{20,4},{24,8},{28,12},{1,17},{... | collective-permute-start | bytes 884744 | tf_op jit(solution)/shard_map/ppermute | solution.py:94
  223.6 9.4 %collective-permute-start.50 = (bf16[2,1,96,768]{3,2,1,0:T(8,128)(2,1)S(1)}, bf16[2,1,96,768]{3,2,1,0:T(8,128)(2,1)S(1)}, u32[]{:S(2)}, u32[]{:S(2)}) collective-permute-start(bf16[2,1,96,768]{3,2,1,0:T(8,128)(2,1)S(1)} %get-tuple-element.740), channel_id=1, source_target_pairs={{0,4},{4,0},{8,12},{12,8},{16,20},{20,16},{24,28},{28,24},{1,5},{5... | collective-permute-start | bytes 884744 | tf_op jit(solution)/shard_map/ppermute | solution.py:89
  224.6 8.4 %collective-permute-start.51 = (bf16[2,1,96,768]{3,2,1,0:T(8,128)(2,1)S(1)}, bf16[2,1,96,768]{3,2,1,0:T(8,128)(2,1)S(1)}, u32[]{:S(2)}, u32[]{:S(2)}) collective-permute-start(bf16[2,1,96,768]{3,2,1,0:T(8,128)(2,1)S(1)} %get-tuple-element.741), channel_id=1, source_target_pairs={{0,2},{1,3},{2,0},{3,1},{4,6},{5,7},{6,4},{7,5},{8,10},{9,11},{10,... | collective-permute-start | bytes 884744 | tf_op jit(solution)/shard_map/ppermute | solution.py:84
  225.6 24.6 %all-to-all-start.1 = ((f32[32,15,128]{2,1,0:T(8,128)}), f32[32,15,128]{2,1,0:T(8,128)}, u32[]{:S(2)}, u32[]{:S(2)}) async-start(f32[32,15,128]{2,1,0:T(8,128)} %broadcast_in_dim.35), calls=%async_computation.1 | async-start | bytes 524288 | tf_op jit(solution)/shard_map/all_to_all | solution.py:103
  233.0 20.4 %collective-permute-start.56 = (bf16[256,768]{1,0:T(8,128)(2,1)}, bf16[256,768]{1,0:T(8,128)(2,1)}, u32[]{:S(2)}, u32[]{:S(2)}) collective-permute-start(bf16[256,768]{1,0:T(8,128)(2,1)} %get-tuple-element.758), channel_id=1, source_target_pairs={{0,2},{1,3},{2,0},{3,1},{4,6},{5,7},{6,4},{7,5},{8,10},{9,11},{10,... | collective-permute-start | bytes 1179656 | tf_op jit(solution)/shard_map/ppermute | solution.py:84
  234.8 20.7 %collective-permute-start.57 = (bf16[256,768]{1,0:T(8,128)(2,1)}, bf16[256,768]{1,0:T(8,128)(2,1)}, u32[]{:S(2)}, u32[]{:S(2)}) collective-permute-start(bf16[256,768]{1,0:T(8,128)(2,1)} %get-tuple-element.759), channel_id=1, source_target_pairs={{0,2},{1,3},{2,0},{3,1},{4,6},{5,7},{6,4},{7,5},{8,10},{9,11},{10,... | collective-permute-start | bytes 1179656 | tf_op jit(solution)/shard_map/ppermute | solution.py:84
  236.6 16.7 %collective-permute-start.53 = (bf16[1,96,768]{2,1,0:T(8,128)(2,1)}, bf16[1,96,768]{2,1,0:T(8,128)(2,1)}, u32[]{:S(2)}, u32[]{:S(2)}) collective-permute-start(bf16[1,96,768]{2,1,0:T(8,128)(2,1)} %get-tuple-element.755), channel_id=1, source_target_pairs={{0,8},{4,12},{8,0},{12,4},{16,24},{20,28},{24,16},{28,20},{1,9},{5... | collective-permute-start | bytes 442376 | tf_op jit(solution)/shard_map/ppermute | solution.py:94
  239.9 13.5 %collective-permute-start.54 = (bf16[1,96,768]{2,1,0:T(8,128)(2,1)}, bf16[1,96,768]{2,1,0:T(8,128)(2,1)}, u32[]{:S(2)}, u32[]{:S(2)}) collective-permute-start(bf16[1,96,768]{2,1,0:T(8,128)(2,1)} %get-tuple-element.756), channel_id=1, source_target_pairs={{0,16},{4,20},{8,24},{12,28},{16,0},{20,4},{24,8},{28,12},{1,17},{... | collective-permute-start | bytes 442376 | tf_op jit(solution)/shard_map/ppermute | solution.py:94
  240.7 12.7 %collective-permute-start.55 = (bf16[1,96,768]{2,1,0:T(8,128)(2,1)}, bf16[1,96,768]{2,1,0:T(8,128)(2,1)}, u32[]{:S(2)}, u32[]{:S(2)}) collective-permute-start(bf16[1,96,768]{2,1,0:T(8,128)(2,1)} %get-tuple-element.757), channel_id=1, source_target_pairs={{0,24},{4,28},{8,16},{12,20},{16,8},{20,12},{24,0},{28,4},{1,25},{... | collective-permute-start | bytes 442376 | tf_op jit(solution)/shard_map/ppermute | solution.py:94
  259.8 11.8 %all-to-all-start.2 = ((f32[32,1,128]{2,1,0:T(1,128)}), f32[32,1,128]{2,1,0:T(1,128)}, u32[]{:S(2)}, u32[]{:S(2)}) async-start(f32[32,1,128]{2,1,0:T(1,128)} %broadcast_in_dim.37), calls=%async_computation.2 | async-start | bytes 32768 | tf_op jit(solution)/shard_map/all_to_all | solution.py:103
  (65 other events, 375.2 us)

commit v4 on v3

--- a/solution.py
+++ b/solution.py
@@ -669,15 +669,12 @@
     )(weights)
 
 
-def sort_kernel(place_ref, in_ref, back_ref, in_keep, in_send, back_keep, back_send, sems):
-    here = place_ref[0]
-    pairs = [
-        (in_ref.at[1 - here], in_send),
-        (back_ref.at[1 - here], back_send),
-        (in_ref.at[here], in_keep),
-        (back_ref.at[here], back_keep),
+def sort_kernel(place_ref, in_ref, back_ref, send, sems):
+    there = 1 - place_ref[0]
+    copies = [
+        pltpu.make_async_copy(ref.at[there], send.at[i], sems.at[i])
+        for i, ref in enumerate((in_ref, back_ref))
     ]
-    copies = [pltpu.make_async_copy(a, b, sems.at[i]) for i, (a, b) in enumerate(pairs)]
     for c in copies:
         c.start()
     for c in copies:
@@ -685,17 +682,46 @@
 
 
 def sort_rows(place, inputs, cotangent):
-    part = shape_of(inputs.shape[1:], BF)
     return pl.pallas_call(
         sort_kernel,
         in_specs=[in_smem] + [in_hbm] * 2,
-        out_specs=[in_vmem] * 4,
-        out_shape=[part] * 4,
-        scratch_shapes=[pltpu.SemaphoreType.DMA((4,))],
+        out_specs=in_vmem,
+        out_shape=shape_of(inputs.shape, BF),
+        scratch_shapes=[pltpu.SemaphoreType.DMA((2,))],
         compiler_params=params(MERGE_MIB),
         cost_estimate=cost(1, 1),
         name="sort_rows",
     )(place, keep_hbm(inputs), keep_hbm(cotangent))
+
+
+def join_rows_kernel(place_ref, keep_in_ref, keep_back_ref, came_ref, in_ref, back_ref, sems):
+    here = place_ref[0]
+    half = came_ref.shape[1]
+    pairs = ((keep_in_ref, in_ref), (keep_back_ref, back_ref))
+    copies = [
+        pltpu.make_async_copy(keep_ref.at[here], ref.at[pl.ds(0, half), :], sems.at[i])
+        for i, (keep_ref, ref) in enumerate(pairs)
+    ]
+    for c in copies:
+        c.start()
+    for i, (_, ref) in enumerate(pairs):
+        ref[pl.ds(half, half), :] = came_ref[i]
+    for c in copies:
+        c.wait()
+
+
+def join_rows(place, inputs, cotangent, came):
+    rows = shape_of((2 * came.shape[1], came.shape[2]), BF)
+    return pl.pallas_call(
+        join_rows_kernel,
+        in_specs=[in_smem] + [in_hbm] * 2 + [in_vmem],
+        out_specs=[in_vmem] * 2,
+        out_shape=[rows] * 2,
+        scratch_shapes=[pltpu.SemaphoreType.DMA((2,))],
+        compiler_params=params(MERGE_MIB),
+        cost_estimate=cost(1, 1),
+        name="join_rows",
+    )(place, keep_hbm(inputs), keep_hbm(cotangent), came)
 
 
 def join_gains_kernel(g_ref, out_ref):
@@ -758,110 +784,147 @@
     )(*parts)
 
 
-def place_rows_kernel(place_ref, *refs):
+def place_rows_kernel(place_ref, a_ref, b_ref, came_ref, out_a_ref, out_b_ref):
     here = place_ref[0]
-    for keep_ref, came_ref, out_ref in zip(refs[0:2], refs[2:4], refs[4:6]):
+    for i, (keep_ref, out_ref) in enumerate(((a_ref, out_a_ref), (b_ref, out_b_ref))):
         out_ref[here] = keep_ref[...]
-        out_ref[1 - here] = came_ref[...]
+        out_ref[1 - here] = came_ref[i]
 
 
 def place_rows(place, keep, came):
-    part = shape_of((2,) + keep[0].shape, BF)
     return pl.pallas_call(
         place_rows_kernel,
-        in_specs=[in_smem] + [in_vmem] * 4,
+        in_specs=[in_smem] + [in_vmem] * 3,
         out_specs=[in_vmem] * 2,
-        out_shape=[part] * 2,
+        out_shape=[shape_of(came.shape, BF)] * 2,
         compiler_params=params(MERGE_MIB),
         cost_estimate=cost(1, 1),
         name="place_rows",
-    )(place, *keep, *came)
-
-
-def finish_kernel(x_ref, gain_ref, t_ref, mid_grad_ref, keep_ref, send_ref, gain_grad_ref):
+    )(place, *keep, came)
+
+
+def finish_kernel(x_ref, gain_ref, t_ref, mid_grad_ref, out_send_ref, keep_ref, send_ref, gain_grad_ref):
     grad, gain_grad = rms_back(x_ref[...].astype(F32), gain_ref[0:1].astype(F32), t_ref[...])
     out = (mid_grad_ref[...] + grad).astype(BF)
     half = keep_ref.shape[0]
-    keep_ref[...], send_ref[...] = out[:half], out[half:]
+    keep_ref[...] = out[:half]
+    send_ref[0], send_ref[1] = out_send_ref[...], out[half:]
     gain_grad_ref[...] = gain_grad
 
 
-def finish(rows_in, gain_low, t_acc, mid_grad):
-    rows = rows_in.shape[0]
+def finish(rows_in, gain_low, t_acc, mid_grad, out_send):
+    part = out_send.shape
     return pl.pallas_call(
         finish_kernel,
-        in_specs=[in_vmem] * 4,
+        in_specs=[in_vmem] * 5,
         out_specs=[in_vmem] * 3,
-        out_shape=[shape_of((rows // 2, D), BF)] * 2 + [shape_of((1, D), F32)],
-        compiler_params=params(8),
-        cost_estimate=cost(rows * D * 12, 6e6),
+        out_shape=[shape_of(part, BF), shape_of((2,) + part, BF), shape_of((1, D), F32)],
+        compiler_params=params(12),
+        cost_estimate=cost(1, 1),
         name="finish",
-    )(rows_in, gain_low, t_acc, mid_grad)
-
-
-def fetch_kernel(*refs):
-    n = (len(refs) - 1) // 2
-    sems = refs[-1]
-    copies = [pltpu.make_async_copy(refs[i], refs[n + i], sems.at[i]) for i in range(n)]
+    )(rows_in, gain_low, t_acc, mid_grad, out_send)
+
+
+def small_kernel(place_ref, one_ref, two_ref, *refs):
+    out_ref = refs[-1]
+    out_ref[...] = jnp.zeros_like(out_ref)
+    out_ref[0:1], out_ref[1:2] = one_ref[...], two_ref[...]
+    heads = []
+    for m in range(4):
+        for h in range(GROUP):
+            lines = jnp.zeros((NB, TILE), F32)
+            for r in range(4):
+                lines = jnp.where((place_ref[2] ^ r) == m, refs[r][h], lines)
+            heads.append(jnp.sum(lines.T, axis=0, keepdims=True))
+    out_ref[2:3, 0 : H * NB] = jnp.concatenate(heads, 1)
+
+
+def small_sums(place, gain_one, gain_two, lines):
+    return pl.pallas_call(
+        small_kernel,
+        in_specs=[in_smem] + [in_vmem] * 6,
+        out_specs=in_vmem,
+        out_shape=shape_of((4, D), F32),
+        compiler_params=params(MERGE_MIB),
+        cost_estimate=cost(1, 1),
+        name="small_sums",
+    )(place, gain_one, gain_two, *lines)
+
+
+def total_with_kernel(own_ref, *refs):
+    squares_ref, small_ref, out_ref, sums_ref = refs[-4:]
+    total = own_ref[...]
+    for ref in refs[:-4]:
+        total = total + ref[...].astype(F32)
+    out_ref[...] = total
+    sums_ref[0:3] = small_ref[0:3]
+    squares = squares_ref[0:1, 0:1] + jnp.sum(total * total)
+    sums_ref[3:4] = jnp.broadcast_to(squares, (1, D))
+
+
+def total_with(own, came, squares, small):
+    return pl.pallas_call(
+        total_with_kernel,
+        in_specs=[in_vmem] * (3 + len(came)),
+        out_specs=[in_vmem] * 2,
+        out_shape=[shape_of(own.shape, F32), shape_of(small.shape, F32)],
+        compiler_params=params(MERGE_MIB),
+        cost_estimate=cost(1, 1),
+        name="total_with",
+    )(own, *came, squares, small)
+
+
+def update_kernel(place_ref, small_ref, attn_ref, ffn_ref, *refs):
+    sources, outs, olds, sems = refs[:12], refs[12:28], refs[28:40], refs[40]
+    copies = [pltpu.make_async_copy(sources[i], olds[i], sems.at[i]) for i in range(12)]
     for c in copies:
         c.start()
-    for c in copies:
-        c.wait()
-
-
-def fetch(arrays):
-    n = len(arrays)
-    return pl.pallas_call(
-        fetch_kernel,
-        in_specs=[in_hbm] * n,
-        out_specs=[in_vmem] * n,
-        out_shape=[pltpu.VMEM(v.shape, v.dtype) for v in arrays],
-        scratch_shapes=[pltpu.SemaphoreType.DMA((n,))],
-        compiler_params=params(MERGE_MIB),
-        cost_estimate=cost(1, 1),
-        name="fetch",
-    )(*[keep_hbm(v) for v in arrays])
-
-
-def update_kernel(squares_ref, small_ref, *refs):
-    grads, olds, outs = refs[:4], refs[4:16], refs[16:]
-    squares = jnp.sum(squares_ref[...], axis=0, keepdims=True)[:, 0:1]
-    small = small_ref[...]
-    small = jnp.sum(jnp.sum(small * small, axis=0, keepdims=True), axis=1, keepdims=True)
-    norm = jnp.sqrt(squares + small)
+    small = jnp.sum(small_ref[...], axis=0)
+    sums = small[0:3]
+    squares = jnp.sum(jnp.sum(sums * sums, axis=0, keepdims=True), axis=1, keepdims=True)
+    norm = jnp.sqrt(small[3:4, 0:1] + squares)
     outs[0][...] = norm
     clip = jnp.minimum(1.0, clip_level / (norm + 1e-06))
+    count = outs[2].shape[1]
+    gains = jnp.zeros((2, count), F32)
+    for d in range(D // count):
+        gains = jnp.where(place_ref[0] == d, small[0:2, d * count : (d + 1) * count], gains)
+    table = jnp.concatenate([small[2:3, h * NB : (h + 1) * NB] for h in range(H)], 0)
+    outs[2][...], outs[3][...] = gains, table
+    grads = (None, ffn_ref[...], gains, table)
     settings = [(rate_matrix, matrix_decay)] * 2 + [(rate_small, 0.0)] * 2
-
-    def step(kind, weight, first, second, gradient):
-        return adam_step(weight, first, second, gradient * clip, *settings[kind])
-
-    def spots(kind):
-        return olds[3 * kind : 3 * kind + 3], outs[2 + 3 * kind : 5 + 3 * kind]
-
-    old, new = spots(0)
-    for i in range(4):
-        gradient = grads[0][0, :, i * WIDTH : (i + 1) * WIDTH]
-        outs[1][i] = gradient
-        new[0][i], new[1][i], new[2][i] = step(0, old[0][i], old[1][i], old[2][i], gradient)
-    for kind in range(1, 4):
-        old, new = spots(kind)
-        values = step(kind, old[0][...], old[1][...], old[2][...], grads[kind][...])
-        new[0][...], new[1][...], new[2][...] = values
-
-
-def update(squares, small, grads, olds):
-    shapes = [shape_of((1, 1), F32), shape_of(olds[0].shape, F32)]
-    shapes += [shape_of(v.shape, F32) for v in olds]
+    for kind in (2, 3, 1, 0):
+        old, new = olds[3 * kind : 3 * kind + 3], outs[4 + 3 * kind : 7 + 3 * kind]
+        for c in copies[3 * kind : 3 * kind + 3]:
+            c.wait()
+        if kind == 0:
+            for i in range(4):
+                gradient = attn_ref[0, :, i * WIDTH : (i + 1) * WIDTH]
+                outs[1][i] = gradient
+                values = adam_step(
+                    old[0][i], old[1][i], old[2][i], gradient * clip, *settings[kind]
+                )
+                new[0][i], new[1][i], new[2][i] = values
+        else:
+            values = adam_step(
+                old[0][...], old[1][...], old[2][...], grads[kind] * clip, *settings[kind]
+            )
+            new[0][...], new[1][...], new[2][...] = values
+
+
+def update(dp_index, small, attn_total, ffn_total, olds):
+    gradients = [shape_of(olds[i].shape, F32) for i in (0, 6, 9)]
+    shapes = [shape_of((1, 1), F32)] + gradients + [shape_of(v.shape, F32) for v in olds]
     return pl.pallas_call(
         update_kernel,
-        in_specs=[in_vmem] * 18,
-        out_specs=[in_vmem] * 14,
+        in_specs=[in_smem] + [in_vmem] * 3 + [in_hbm] * 12,
+        out_specs=[in_vmem] * 16,
         out_shape=shapes,
+        scratch_shapes=[pltpu.VMEM(v.shape, F32) for v in olds] + [pltpu.SemaphoreType.DMA((12,))],
         compiler_params=params(20),
         cost_estimate=cost(1, 1),
         name="update",
-    )(squares, small, *grads, *olds)
+    )(dp_index, small, attn_total, ffn_total, *[keep_hbm(v) for v in olds])
 
 
 def per_device(
@@ -899,10 +962,8 @@
 
     attn_low = cast_attn(attn_weights)
     attn_z = [swap_z(attn_low, k) for k in range(1, depth)]
-    rows_keep, rows_send, back_keep, back_send = sort_rows(place, inputs, cotangent)
-    rows_came, back_came = swap_x(rows_send), swap_x(back_send)
+    rows_came = swap_x(sort_rows(place, inputs, cotangent))
     ffn_low, wi_low, wf_low = cast_ffn(ffn_weights)
-    gain_parts = gather_gains(norm_gains)
     bias = make_bias(place, bias_table)
     attn_low, attn_z, ffn_low, wi_low, wf_low, place, bias = fence(
         attn_low, attn_z, ffn_low, wi_low, wf_low, place, bias
@@ -911,20 +972,20 @@
     lined = [attn_low] + attn_z
     near, far = line_up(lined[:cut], cut), line_up(lined[cut:], cut)
     near_x, far_y = swap_x(near), swap_y(far)
-    ffn_near_z = [swap_z(ffn_low, k) for k in range(1, cut)]
-    near, far, near_x, far_y, rows_came, wi_low, ffn_near_z = fence(
-        near, far, near_x, far_y, rows_came, wi_low, ffn_near_z
+    wi_far_z = [swap_z(wi_low, k) for k in range(cut, depth)]
+    near, far, near_x, far_y, rows_came, ffn_low, wf_low, wi_far_z = fence(
+        near, far, near_x, far_y, rows_came, ffn_low, wf_low, wi_far_z
     )
     near, far = line_up([near, near_x], 2), line_up([far, far_y], 2)
     near_y, far_x = swap_y(near), swap_x(far)
-    wi_far_z = [swap_z(wi_low, k) for k in range(cut, depth)]
-    rows_in = jnp.concatenate([rows_keep, rows_came], 0)
-    ffn_near = line_up([ffn_low] + ffn_near_z, cut)
-    gains = join_gains(gain_parts)
-    near_y, far_x, near, far, ffn_near, rows_in, gains, wf_low, back_came = fence(
-        near_y, far_x, near, far, ffn_near, rows_in, gains, wf_low, back_came
-    )
-    back = jnp.concatenate([back_keep, back_came], 0)
+    ffn_near_z = [swap_z(ffn_low, k) for k in range(1, cut)]
+    wf_far_z = [swap_z(wf_low, k) for k in range(cut, depth)]
+    rows_in, back = join_rows(place, inputs, cotangent, rows_came)
+    rows_in, back, gain_low = fence(rows_in, back, norm_gains)
+    gains = join_gains(gather_gains(gain_low))
+    near_y, far_x, near, far, rows_in, back, gains, ffn_near_z, wf_far_z = fence(
+        near_y, far_x, near, far, rows_in, back, gains, ffn_near_z, wf_far_z
+    )
 
     def attn_block(near, far, near_y, far_x, i):
         here = far if i == 0 else far_x
@@ -936,11 +997,13 @@
     q[0], kv[0], normed_t = project(place, rows_in, gains, [attn_blocks[0], attn_blocks[2]], True)
     q, kv, normed_t = fence(q, kv, normed_t)
     other[1] = swap_core(kv[0])
-    q, kv, near_c, far_c, near_yc, far_xc, wi_far_z, wf_low, ffn_near = fence(
-        q, kv, near_c, far_c, near_yc, far_xc, wi_far_z, wf_low, ffn_near
-    )
-    ffn_near_x, ffn_near_y = swap_x(ffn_near), swap_y(ffn_near)
-    wf_far_z = [swap_z(wf_low, k) for k in range(cut, depth)]
+    ffn_near = line_up([ffn_low] + ffn_near_z, cut)
+    ffn_far = line_up([v for pair in zip(wi_far_z, wf_far_z) for v in pair], cut)
+    ffn_here = line_up([ffn_near, ffn_far], 2)
+    ffn_x, ffn_y = swap_x(ffn_here), swap_y(ffn_here)
+    q, kv, near_c, far_c, near_yc, far_xc, ffn_here = fence(
+        q, kv, near_c, far_c, near_yc, far_xc, ffn_here
+    )
     for i in range(2):
         attn_blocks[2 * i + 1] = attn_block(near_c, far_c, near_yc, far_xc, i)
     q[1], kv[1] = project(place, rows_in, gains, [attn_blocks[1], attn_blocks[3]], False)
@@ -954,28 +1017,21 @@
 
     attend_at(1)
     ctx, prob, q = fence(ctx, prob, q)
-    ctx, prob, q, wf_far_z, ffn_near_x, ffn_near_y, back = fence(
-        ctx, prob, q, wf_far_z, ffn_near_x, ffn_near_y, back
-    )
-    ffn_far = line_up([v for pair in zip(wi_far_z, wf_far_z) for v in pair], cut)
-    ffn_far_x, ffn_far_y = swap_x(ffn_far), swap_y(ffn_far)
     attend_at(3)
-    ctx, prob, q, ffn_far = fence(ctx, prob, q, ffn_far)
-    ffn_near_c, ffn_near_yc = swap_core(ffn_near), swap_core(ffn_near_y)
-    q, other = fence(q, other)
+    ctx, prob, q = fence(ctx, prob, q)
+    q, other, ffn_here = fence(q, other, ffn_here)
+    ffn_c = swap_core(ffn_here)
     attend_at(0)
     ctx, prob, q = fence(ctx, prob, q)
     attend_at(2)
     ctx, prob = fence(ctx, prob)
-    ctx, ffn_near_c, ffn_near_yc, ffn_far_x, ffn_far_y = fence(
-        ctx, ffn_near_c, ffn_near_yc, ffn_far_x, ffn_far_y
-    )
-    ffn_near_xy, ffn_far_xy = swap_y(ffn_near_x), swap_x(ffn_far_y)
-    ffn_far_c, ffn_far_yc = swap_core(ffn_far), swap_core(ffn_far_y)
     mid, normed_two, normed_two_t, back_t = middle(
         place, rows_in, gains, back, [ctx[r] for r in range(4)], [attn_blocks[r] for r in range(4)]
     )
     mid, normed_two, normed_two_t, back_t = fence(mid, normed_two, normed_two_t, back_t)
+    mid, ffn_x, ffn_y = fence(mid, ffn_x, ffn_y)
+    ffn_near_xy, ffn_far_xy = swap_y(ffn_x[0]), swap_x(ffn_y[1])
+    ffn_yc, ffn_xc = swap_core(ffn_y), swap_core(ffn_x)
     grads = {}
 
     def feed_at(r, sums, by_y):
@@ -985,22 +1041,17 @@
         grads[r] = by_place(out, depth, shard_rows)
         return sums
 
-    sums = feed_at(0, None, [[ffn_near, ffn_far], [ffn_near_y, ffn_far_y]])
-    sums, grads, ffn_far_c, ffn_far_yc = fence(sums, grads, ffn_far_c, ffn_far_yc)
-    sums = feed_at(1, sums, [[ffn_near_c, ffn_far_c], [ffn_near_yc, ffn_far_yc]])
+    sums = feed_at(0, None, [[(ffn_here, 0), (ffn_here, 1)], [(ffn_y, 0), (ffn_y, 1)]])
+    sums, grads, ffn_yc, ffn_xc, ffn_c = fence(sums, grads, ffn_yc, ffn_xc, ffn_c)
+    sums = feed_at(1, sums, [[(ffn_c, 0), (ffn_c, 1)], [(ffn_yc, 0), (ffn_yc, 1)]])
     sums, grads = fence(sums, grads)
-    sums, ffn_near_xy, ffn_far_xy, ffn_near_x, ffn_far_x = fence(
-        sums, ffn_near_xy, ffn_far_xy, ffn_near_x, ffn_far_x
-    )
-    ffn_near_xc, ffn_far_xc = swap_core(ffn_near_x), swap_core(ffn_far_x)
+    sums, ffn_near_xy, ffn_far_xy = fence(sums, ffn_near_xy, ffn_far_xy)
     ffn_near_xyc, ffn_far_xyc = swap_core(ffn_near_xy), swap_core(ffn_far_xy)
-    sums = feed_at(2, sums, [[ffn_near_x, ffn_far_x], [ffn_near_xy, ffn_far_xy]])
+    sums = feed_at(2, sums, [[(ffn_x, 0), (ffn_x, 1)], [ffn_near_xy, ffn_far_xy]])
     sums, grads = fence(sums, grads)
-    sums, ffn_near_xc, ffn_far_xc, ffn_near_xyc, ffn_far_xyc, grads = fence(
-        sums, ffn_near_xc, ffn_far_xc, ffn_near_xyc, ffn_far_xyc, grads
-    )
+    sums, ffn_near_xyc, ffn_far_xyc, grads = fence(sums, ffn_near_xyc, ffn_far_xyc, grads)
     came = {0: swap_core(grads[1])}
-    sums = feed_at(3, sums, [[ffn_near_xc, ffn_far_xc], [ffn_near_xyc, ffn_far_xyc]])
+    sums = feed_at(3, sums, [[(ffn_xc, 0), (ffn_xc, 1)], [ffn_near_xyc, ffn_far_xyc]])
     sums, grads = fence(sums, grads)
     came[2] = swap_core(grads[3])
     out_keep, out_send, mid_grad, mid_low_t, gain_two_grad, *cg = turn(
@@ -1043,55 +1094,43 @@
         t_one, attn_grads = fence(t_one, attn_grads)
         if r % 2:
             came[r - 1] = swap_core(attn_grads[r])
-    t_one, attn_grads, came, ffn_y1, ffn_x1 = fence(t_one, attn_grads, came, ffn_y1, ffn_x1)
+    t_one, attn_grads, came = fence(t_one, attn_grads, came)
     near0, near1, far0, far1 = merge_core(attn_grads[0], came[0], attn_grads[2], came[2])
     near1_x, far1_y = swap_x(near1), swap_y(far1)
+    near0, far0, ffn_y1, ffn_x1 = fence(near0, far0, ffn_y1, ffn_x1)
     ffn_own, *ffn_far_own = merge_last(ffn_y0, ffn_y1, ffn_x0, ffn_x1)
     soon = [k for k in range(1, depth) if k != cut]
     ffn_back = [swap_z(ffn_far_own[k - 1], k) for k in soon]
-    in_keep, in_send, gain_one_grad = finish(rows_in, gains, t_one, mid_grad)
-    lines = jnp.sum(jnp.stack([tiles[r] for r in range(4)]), -1)
-    table_part = jnp.take(lines, jnp.arange(4) ^ mp, axis=0).reshape(H * NB)
-    small = jnp.concatenate([gain_one_grad[0], gain_two_grad[0], table_part])
-    in_keep, in_send, small, ffn_own, near0, far0, ffn_far_own = fence(
-        in_keep, in_send, small, ffn_own, near0, far0, ffn_far_own
+    in_keep, send_last, gain_one_grad = finish(rows_in, gains, t_one, mid_grad, out_send)
+    small = small_sums(place, gain_one_grad, gain_two_grad, [tiles[r] for r in range(4)])
+    in_keep, send_last, small, ffn_own, near0, far0, ffn_far_own = fence(
+        in_keep, send_last, small, ffn_own, near0, far0, ffn_far_own
     )
     near1_x, far1_y, small, ffn_back = fence(near1_x, far1_y, small, ffn_back)
     attn_y0, attn_y1, attn_x0, attn_x1 = merge_half(near0, near1_x, far0, far1_y)
-    attn_y1, attn_x1, ffn_back, small = fence(attn_y1, attn_x1, ffn_back, small)
+    attn_y1, attn_x1, ffn_back = fence(attn_y1, attn_x1, ffn_back)
     attn_y1, attn_x1 = swap_y(attn_y1), swap_x(attn_x1)
     ffn_back += [swap_z(ffn_far_own[cut - 1], cut)]
-    small = jnp.sum(from_all(small.reshape(-1, TILE)), 0)
-    gain_total = small.reshape(-1)[: 2 * D].reshape(2, D)
-    table_grads = small.reshape(-1)[2 * D :].reshape(H, NB)
-    gain_cols = norm_gains.shape[1]
-    gain_grads = lax.dynamic_slice_in_dim(gain_total, dp * gain_cols, gain_cols, 1)
-    attn_y1, attn_x1, attn_y0, attn_x0, out_send, in_send, ffn_back = fence(
-        attn_y1, attn_x1, attn_y0, attn_x0, out_send, in_send, ffn_back
+    attn_y1, attn_x1, attn_y0, attn_x0, send_last, ffn_back = fence(
+        attn_y1, attn_x1, attn_y0, attn_x0, send_last, ffn_back
     )
     attn_own, *attn_far_own = merge_last(attn_y0, attn_y1, attn_x0, attn_x1)
     attn_back = [swap_z(v, k) for k, v in enumerate(attn_far_own, 1)]
-    out_came, in_came = swap_x(out_send), swap_x(in_send)
+    came_last = swap_x(send_last)
     ffn_total, ffn_squares = total_of(ffn_own, ffn_back)
+    attn_own, ffn_total, ffn_squares, small = fence(attn_own, ffn_total, ffn_squares, small)
+    attn_own, attn_back, came_last = fence(attn_own, attn_back, came_last)
+    attn_total, small = total_with(attn_own, attn_back, ffn_squares, small)
+    every_small = from_all(small)
+    block_out, input_grad = place_rows(place, (out_keep, in_keep), came_last)
     olds = [
         *(attn_weights, attn_first, attn_second),
         *(ffn_weights, ffn_first, ffn_second),
         *(norm_gains, gain_first, gain_second),
         *(bias_table, table_first, table_second),
     ]
-    attn_own, olds = fence(attn_own, olds)
-    olds = fetch(olds)
-    ffn_total, ffn_squares, gain_grads, table_grads, olds = fence(
-        ffn_total, ffn_squares, gain_grads, table_grads, olds
-    )
-    attn_own, attn_back, out_came, in_came, olds = fence(
-        attn_own, attn_back, out_came, in_came, olds
-    )
-    attn_total, attn_squares = total_of(attn_own, attn_back)
-    squares = from_all(attn_squares + ffn_squares)
-    block_out, input_grad = place_rows(place, (out_keep, in_keep), (out_came, in_came))
-    grad_norm, attn_reduced, *news = update(
-        squares.reshape(-1, TILE), small, (attn_total, ffn_total, gain_grads, table_grads), olds
+    grad_norm, attn_reduced, gain_grads, table_grads, *news = update(
+        dp.astype(jnp.int32).reshape(1), every_small.reshape(-1, *small.shape), attn_total, ffn_total, olds
     )
     return (
         block_out,

time: 285 us -> 253 us (0.89)
  local copies, waits for them, and re-layouts: 32.5 us -> 3.3 us
  waiting for transfers between devices: 46.1 us -> 71.4 us
  starting transfers between devices: 68.8 us -> 52.8 us
  other arithmetic: 5.71 us -> 0.01 us
  Pallas kernels: 115 us -> 110 us
    unnamed x106 -> x22, local copies, waits for them, and re-layouts: 27.1 us -> 1.68 us
    ppermute x14, waiting for transfers between devices: 20.1 us -> 37.9 us  [swap_z(): return lax.ppermute(v, 'dp', [(i, i ^ 2 * k) for i in range(n)])]
    all_to_all x2 -> x1, waiting for transfers between devices: 2.71 us -> 11.4 us  [from_all(): lax.all_to_all(jnp.broadcast_to(v[None], (n,) + v.shape), ('dp', 'mp'), 0...]
    all_to_all x2 -> x1, starting transfers between devices: 12.1 us -> 4.17 us  [from_all(): lax.all_to_all(jnp.broadcast_to(v[None], (n,) + v.shape), ('dp', 'mp'), 0...]
    ppermute x13 -> x10, waiting for transfers between devices: 9.4 us -> 2.89 us  [swap_x(): return lax.ppermute(v, 'mp', [(i, i ^ 2) for i in range(4)])]
    ppermute x22 -> x19, waiting for transfers between devices: 3.13 us -> 9.43 us  [swap_core(): return lax.ppermute(v, 'mp', [(i, i ^ 1) for i in range(4)])]
    ppermute x13 -> x10, starting transfers between devices: 14.1 us -> 10.5 us  [swap_x(): return lax.ppermute(v, 'mp', [(i, i ^ 2) for i in range(4)])]
    ppermute x9 -> x8, starting transfers between devices: 9.87 us -> 7.74 us  [swap_y(): return lax.ppermute(v, 'dp', [(i, i ^ 1) for i in range(n)])]
  transfers between devices with their start and end apart: 60 -> 52, of which waited for: 19 -> 21; matrix products, arithmetic and copies ran while one was open for 3% -> 0% of each run, Pallas kernels for 36% -> 37%
where the time goes in v4:
time: 253 us; the launch traced here: 250 us
  Pallas kernels  110 us (43%)
  waiting for transfers between devices  71.4 us (28%)
  starting transfers between devices  52.8 us (21%)
  blocking collectives  10.8 us (4%)
  local copies, waits for them, and re-layouts  3.3 us (1%)
    ppermute x14, waiting for transfers between devices, swap_z(): return lax.ppermute(v, 'dp', [(i, i ^ 2 * k) for i in range(n)])  37.9 us
    pallas_call x4, Pallas kernels, attend_back(): pl.pallas_call(functools.partial(attend_back_kernel, b), in_specs=[in_sme...  26.5 us
    ppermute x14, starting transfers between devices, swap_z(): return lax.ppermute(v, 'dp', [(i, i ^ 2 * k) for i in range(n)])  25.6 us
    pallas_call x4, Pallas kernels, attend(): pl.pallas_call(functools.partial(attend_kernel, b, r_index), in_specs=[in...  20.1 us
    pallas_call x4, Pallas kernels, feed(): pl.pallas_call(functools.partial(feed_kernel, indices, first), in_specs=[...  19.1 us
    all_to_all x1, waiting for transfers between devices, from_all(): lax.all_to_all(jnp.broadcast_to(v[None], (n,) + v.shape), ('dp', 'mp'), 0...  11.4 us
    all_to_all x1, blocking collectives, gather_gains(): lax.all_to_all(jnp.broadcast_to(low[None], (n,) + low.shape), 'dp', 0, 0)  10.8 us
    ppermute x10, starting transfers between devices, swap_x(): return lax.ppermute(v, 'mp', [(i, i ^ 2) for i in range(4)])  10.5 us
  transfers between devices with their start and end apart: 52, of which 21 were waited for; matrix products, arithmetic and copies ran while one was open for 0% of the time, Pallas kernels for 37%

profile of v4, /device:TPU:0, one launch (start us, length us, event | category | flops | bytes accessed | tf_op | source)
XLA Modules:
  0.0 250.0 jit_solution(2700643309966362242)
XLA Ops:
  2.4 5.0 %collective-permute-start.2 = (bf16[1,96,768]{2,1,0:T(8,128)(2,1)}, bf16[1,96,768]{2,1,0:T(8,128)(2,1)}, u32[]{:S(2)}, u32[]{:S(2)}) collective-permute-start(bf16[1,96,768]{2,1,0:T(8,128)(2,1)} %cast_attn.1.refs_0_), channel_id=1, source_target_pairs={{0,24},{4,28},{8,16},{12,20},{16,8},{20,12},{24,0},{28,4},{1,25},{... | collective-permute-start | bytes 442376 | tf_op jit(solution)/shard_map/ppermute | solution.py:94
  8.8 2.6 %sort_rows.1 = bf16[2,256,768]{2,1,0:T(8,128)(2,1)} custom-call(s32[13]{0:T(128)S(1)} %stack.47.place_ref, bf16[2,256,768]{2,1,0:T(8,128)(2,1)} %keep_in_ref.1, bf16[2,256,768]{2,1,0:T(8,128)(2,1)} %keep_back_ref.1), custom_call_target="tpu_custom_call" | custom-call | flops 1000 | bytes 1000 | tf_op jit(solution)/shard_map/sort_rows/pallas_call | solution.py:685
  11.3 1.8 collective-permute-start.5
  13.8 5.2 %bias_tiles.1.bias_ref = f32[4,3,5,128,128]{4,3,2,1,0:T(8,128)S(1)} custom-call(s32[13]{0:T(128)S(1)} %stack.47.place_ref, f32[12,32]{1,0:T(8,128)S(1)} %copy-done.9), custom_call_target="tpu_custom_call" | custom-call | flops 1000 | bytes 1000 | tf_op jit(solution)/shard_map/bias_tiles/pallas_call | solution.py:186
  21.3 1.6 collective-permute-start.4
  23.9 1.6 collective-permute-start.3
  25.4 2.5 %collective-permute-start.7 = (bf16[1,96,768]{2,1,0:T(8,128)(2,1)S(1)}, bf16[1,96,768]{2,1,0:T(8,128)(2,1)S(1)}, u32[]{:S(2)}, u32[]{:S(2)}) collective-permute-start(bf16[1,96,768]{2,1,0:T(8,128)(2,1)S(1)} %get-tuple-element.377), channel_id=1, source_target_pairs={{0,24},{4,28},{8,16},{12,20},{16,8},{20,12},{24,0},{28,4},{1,25},{... | collective-permute-start | bytes 442376 | tf_op jit(solution)/shard_map/ppermute | solution.py:94
  27.9 5.3 %collective-permute-done.7.refs_2_ = bf16[1,96,768]{2,1,0:T(8,128)(2,1)S(1)} collective-permute-done((bf16[1,96,768]{2,1,0:T(8,128)(2,1)S(1)}, bf16[1,96,768]{2,1,0:T(8,128)(2,1)S(1)}, u32[]{:S(2)}, u32[]{:S(2)}) %collective-permute-start.7) | collective-permute-done | bytes 147488 | tf_op jit(solution)/shard_map/ppermute | solution.py:94
  33.2 5.9 %collective-permute-done.6.refs_0_ = bf16[1,96,768]{2,1,0:T(8,128)(2,1)S(1)} collective-permute-done((bf16[1,96,768]{2,1,0:T(8,128)(2,1)S(1)}, bf16[1,96,768]{2,1,0:T(8,128)(2,1)S(1)}, u32[]{:S(2)}, u32[]{:S(2)}) %collective-permute-start.6) | collective-permute-done | bytes 147488 | tf_op jit(solution)/shard_map/ppermute | solution.py:94
  41.4 2.4 collective-permute-start.12
  44.2 2.3 join_rows.1
  46.5 10.8 %all_to_all.10.g_ref = bf16[8,2,96]{2,1,0:T(2,128)(2,1)S(1)} all-to-all(bf16[8,2,96]{2,1,0:T(2,128)(2,1)S(1)} %broadcast_in_dim.4), channel_id=1, replica_groups=mesh['dp'=8,'mp'=4] {'dp'}, dimensions={0} | all-to-all | bytes 6144 | tf_op jit(solution)/shard_map/all_to_all | solution.py:109
  58.1 2.2 project.2
  64.4 2.2 project.3
  66.8 4.9 %attend.4 = (bf16[512,192]{1,0:T(8,128)(2,1)S(1)}, bf16[3,512,1024]{2,1,0:T(8,128)(2,1)}) custom-call(s32[13]{0:T(128)S(1)} %stack.47.place_ref, bf16[2,512,192]{2,1,0:T(8,128)(2,1)S(1)} %get-tuple-element.510.q_ref, bf16[2,512,384]{2,1,0:T(8,128)(2,1)S(1)} %get-tuple-element.413.kv_ref, bf16[2,512,384]{2,1,0:T(8,128)(2,1)S(1)} %collective-permute-done.17.other_ref, ...), custom_call_target="tpu_custom_call" | custom-call | flops 1000 | bytes 1000 | tf_op jit(solution)/shard_map/attend/pallas_call | solution.py:298
  71.7 4.9 %attend.5 = (bf16[512,192]{1,0:T(8,128)(2,1)S(1)}, bf16[3,512,1024]{2,1,0:T(8,128)(2,1)}) custom-call(s32[13]{0:T(128)S(1)} %stack.47.place_ref, bf16[2,512,192]{2,1,0:T(8,128)(2,1)S(1)} %get-tuple-element.510.q_ref, bf16[2,512,384]{2,1,0:T(8,128)(2,1)S(1)} %get-tuple-element.413.kv_ref, bf16[2,512,384]{2,1,0:T(8,128)(2,1)S(1)} %collective-permute-done.17.other_ref, ...), custom_call_target="tpu_custom_call" | custom-call | flops 1000 | bytes 1000 | tf_op jit(solution)/shard_map/attend/pallas_call | solution.py:298
  77.0 5.4 %attend.6 = (bf16[512,192]{1,0:T(8,128)(2,1)S(1)}, bf16[3,512,1024]{2,1,0:T(8,128)(2,1)}) custom-call(s32[13]{0:T(128)S(1)} %stack.47.place_ref, bf16[2,512,192]{2,1,0:T(8,128)(2,1)S(1)} %get-tuple-element.440.q_ref, bf16[2,512,384]{2,1,0:T(8,128)(2,1)S(1)} %get-tuple-element.429.kv_ref, bf16[2,512,384]{2,1,0:T(8,128)(2,1)S(1)} %collective-permute-done.18.other_ref, ...), custom_call_target="tpu_custom_call" | custom-call | flops 1000 | bytes 1000 | tf_op jit(solution)/shard_map/attend/pallas_call | solution.py:298
  82.5 4.9 %attend.7 = (bf16[512,192]{1,0:T(8,128)(2,1)S(1)}, bf16[3,512,1024]{2,1,0:T(8,128)(2,1)}) custom-call(s32[13]{0:T(128)S(1)} %stack.47.place_ref, bf16[2,512,192]{2,1,0:T(8,128)(2,1)S(1)} %get-tuple-element.440.q_ref, bf16[2,512,384]{2,1,0:T(8,128)(2,1)S(1)} %get-tuple-element.429.kv_ref, bf16[2,512,384]{2,1,0:T(8,128)(2,1)S(1)} %collective-permute-done.18.other_ref, ...), custom_call_target="tpu_custom_call" | custom-call | flops 1000 | bytes 1000 | tf_op jit(solution)/shard_map/attend/pallas_call | solution.py:298
  87.4 2.1 middle.1
  90.4 1.5 collective-permute-start.24
  92.6 4.7 %feed.4 = (f32[512,768]{1,0:T(8,128)S(1)}, f32[512,768]{1,0:T(8,128)S(1)}, bf16[2,2,2,2,96,768]{5,4,3,2,1,0:T(8,128)(2,1)S(1)}) custom-call(s32[13]{0:T(128)S(1)} %stack.47.place_ref, bf16[512,768]{1,0:T(8,128)(2,1)S(1)} %get-tuple-element.453.n_ref, bf16[768,512]{1,0:T(8,128)(2,1)S(1)} %get-tuple-element.454.nt_ref, ...), custom_call_target="tpu_custom_call" | custom-call | flops 1000 | bytes 1000 | tf_op jit(solution)/shard_map/feed/pallas_call | solution.py:383
  97.3 5.0 %feed.5 = (f32[512,768]{1,0:T(8,128)S(1)}, f32[512,768]{1,0:T(8,128)S(1)}, bf16[2,2,2,2,96,768]{5,4,3,2,1,0:T(8,128)(2,1)S(1)}) custom-call(s32[13]{0:T(128)S(1)} %stack.47.place_ref, bf16[512,768]{1,0:T(8,128)(2,1)S(1)} %get-tuple-element.453.n_ref, bf16[768,512]{1,0:T(8,128)(2,1)S(1)} %get-tuple-element.454.nt_ref, ...), custom_call_target="tpu_custom_call", output_to_operand_aliasing={{0}: (5, {}), {1}: (6, {})} | custom-call | flops 1000 | bytes 1000 | tf_op jit(solution)/shard_map/feed/pallas_call | solution.py:383
  102.2 3.5 %collective-permute-done.24.refs_4_ = bf16[2,2,96,768]{3,2,1,0:T(8,128)(2,1)S(1)} collective-permute-done((bf16[2,2,96,768]{3,2,1,0:T(8,128)(2,1)S(1)}, bf16[2,2,96,768]{3,2,1,0:T(8,128)(2,1)S(1)}, u32[]{:S(2)}, u32[]{:S(2)}) %collective-permute-start.24) | collective-permute-done | bytes 589856 | tf_op jit(solution)/shard_map/ppermute | solution.py:89
  107.4 4.8 %feed.6 = (f32[512,768]{1,0:T(8,128)S(1)}, f32[512,768]{1,0:T(8,128)S(1)}, bf16[2,2,2,2,96,768]{5,4,3,2,1,0:T(8,128)(2,1)S(1)}) custom-call(s32[13]{0:T(128)S(1)} %stack.47.place_ref, bf16[512,768]{1,0:T(8,128)(2,1)S(1)} %get-tuple-element.453.n_ref, bf16[768,512]{1,0:T(8,128)(2,1)S(1)} %get-tuple-element.454.nt_ref, ...), custom_call_target="tpu_custom_call", output_to_operand_aliasing={{0}: (5, {}), {1}: (6, {})} | custom-call | flops 1000 | bytes 1000 | tf_op jit(solution)/shard_map/feed/pallas_call | solution.py:383
  112.2 4.8 %feed.7 = (f32[512,768]{1,0:T(8,128)S(1)}, f32[512,768]{1,0:T(8,128)S(1)}, bf16[2,2,2,2,96,768]{5,4,3,2,1,0:T(8,128)(2,1)S(1)}) custom-call(s32[13]{0:T(128)S(1)} %stack.47.place_ref, bf16[512,768]{1,0:T(8,128)(2,1)S(1)} %get-tuple-element.453.n_ref, bf16[768,512]{1,0:T(8,128)(2,1)S(1)} %get-tuple-element.454.nt_ref, ...), custom_call_target="tpu_custom_call", output_to_operand_aliasing={{0}: (5, {}), {1}: (6, {})} | custom-call | flops 1000 | bytes 1000 | tf_op jit(solution)/shard_map/feed/pallas_call | solution.py:383
  117.5 2.5 %turn.1 = (bf16[256,768]{1,0:T(8,128)(2,1)S(1)}, bf16[256,768]{1,0:T(8,128)(2,1)S(1)}, f32[512,768]{1,0:T(8,128)S(1)}, bf16[768,512]{1,0:T(8,128)(2,1)S(1)}, f32...) custom-call(s32[13]{0:T(128)S(1)} %stack.47.place_ref, ...), custom_call_target="tpu_custom_call" | custom-call | flops 1000 | bytes 1000 | tf_op jit(solution)/shard_map/turn/pallas_call | solution.py:422
  120.1 1.5 collective-permute-done.29.refs_3_
  121.6 3.4 %collective-permute-done.28.refs_1_ = bf16[2,2,2,2,96,768]{5,4,3,2,1,0:T(8,128)(2,1)S(1)} collective-permute-done((bf16[2,2,2,2,96,768]{5,4,3,2,1,0:T(8,128)(2,1)S(1)}, bf16[2,2,2,2,96,768]{5,4,3,2,1,0:T(8,128)(2,1)S(1)}, u32[]{:S(2)}, u32[]{:S(2)}) %collective-permute-start.28) | collective-permute-done | bytes 2359328 | tf_op jit(solution)/shard_map/ppermute | solution.py:80
  127.4 6.7 %attend_back.4 = (bf16[512,192]{1,0:T(8,128)(2,1)S(1)}, f32[512,384]{1,0:T(8,128)S(1)}, bf16[512,384]{1,0:T(8,128)(2,1)S(1)}, f32[3,32,128]{2,1,0:T(8,128)S(1)}) custom-call(s32[13]{0:T(128)S(1)} %stack.47.place_ref, bf16[2,512,192]{2,1,0:T(8,128)(2,1)S(1)} %get-tuple-element.510.q_ref, bf16[2,512,384]{2,1,0:T(8,128)(2,1)S(1)} %get-tuple-element.413.kv_ref, ...), custom_call_target="tpu_custom_call" | custom-call | flops 1000 | bytes 1000 | tf_op jit(solution)/shard_map/attend_back/pallas_call | solution.py:510
  134.1 6.5 %attend_back.5 = (bf16[512,192]{1,0:T(8,128)(2,1)S(1)}, f32[512,384]{1,0:T(8,128)S(1)}, bf16[512,384]{1,0:T(8,128)(2,1)S(1)}, f32[3,32,128]{2,1,0:T(8,128)S(1)}) custom-call(s32[13]{0:T(128)S(1)} %stack.47.place_ref, bf16[2,512,192]{2,1,0:T(8,128)(2,1)S(1)} %get-tuple-element.510.q_ref, bf16[2,512,384]{2,1,0:T(8,128)(2,1)S(1)} %get-tuple-element.413.kv_ref, ...), custom_call_target="tpu_custom_call" | custom-call | flops 1000 | bytes 1000 | tf_op jit(solution)/shard_map/attend_back/pallas_call | solution.py:510
  140.6 6.9 %attend_back.6 = (bf16[512,192]{1,0:T(8,128)(2,1)S(1)}, f32[512,384]{1,0:T(8,128)S(1)}, bf16[512,384]{1,0:T(8,128)(2,1)S(1)}, f32[3,32,128]{2,1,0:T(8,128)S(1)}) custom-call(s32[13]{0:T(128)S(1)} %stack.47.place_ref, bf16[2,512,192]{2,1,0:T(8,128)(2,1)S(1)} %get-tuple-element.440.q_ref, bf16[2,512,384]{2,1,0:T(8,128)(2,1)S(1)} %get-tuple-element.429.kv_ref, ...), custom_call_target="tpu_custom_call" | custom-call | flops 1000 | bytes 1000 | tf_op jit(solution)/shard_map/attend_back/pallas_call | solution.py:510
  147.6 6.4 %attend_back.7 = (bf16[512,192]{1,0:T(8,128)(2,1)S(1)}, f32[512,384]{1,0:T(8,128)S(1)}, bf16[512,384]{1,0:T(8,128)(2,1)S(1)}, f32[3,32,128]{2,1,0:T(8,128)S(1)}) custom-call(s32[13]{0:T(128)S(1)} %stack.47.place_ref, bf16[2,512,192]{2,1,0:T(8,128)(2,1)S(1)} %get-tuple-element.440.q_ref, bf16[2,512,384]{2,1,0:T(8,128)(2,1)S(1)} %get-tuple-element.429.kv_ref, ...), custom_call_target="tpu_custom_call" | custom-call | flops 1000 | bytes 1000 | tf_op jit(solution)/shard_map/attend_back/pallas_call | solution.py:510
  158.1 2.3 project_back.4
  160.4 2.5 project_back.5
  166.3 2.7 %project_back.6 = (f32[512,768]{1,0:T(8,128)S(1)}, bf16[2,2,2,1,96,768]{5,4,3,2,1,0:T(8,128)(2,1)S(1)}) custom-call(s32[13]{0:T(128)S(1)} %stack.47.place_ref, bf16[768,512]{1,0:T(8,128)(2,1)S(1)} %get-tuple-element.508.nt_ref, bf16[768,512]{1,0:T(8,128)(2,1)S(1)} %get-tuple-element.509.low_t_ref, ...), custom_call_target="tpu_custom_call", output_to_operand_aliasing={{0}: (7, {})} | custom-call | flops 1000 | bytes 1000 | tf_op jit(solution)/shard_map/project_back/pallas_call | solution.py:552
  169.0 2.5 %project_back.7 = (f32[512,768]{1,0:T(8,128)S(1)}, bf16[2,2,2,1,96,768]{5,4,3,2,1,0:T(8,128)(2,1)S(1)}) custom-call(s32[13]{0:T(128)S(1)} %stack.47.place_ref, bf16[768,512]{1,0:T(8,128)(2,1)S(1)} %get-tuple-element.508.nt_ref, bf16[768,512]{1,0:T(8,128)(2,1)S(1)} %get-tuple-element.509.low_t_ref, ...), custom_call_target="tpu_custom_call", output_to_operand_aliasing={{0}: (7, {})} | custom-call | flops 1000 | bytes 1000 | tf_op jit(solution)/shard_map/project_back/pallas_call | solution.py:552
  173.4 6.2 %collective-permute-done.38.near_came_ref = bf16[2,2,96,768]{3,2,1,0:T(8,128)(2,1)S(1)} collective-permute-done((bf16[2,2,96,768]{3,2,1,0:T(8,128)(2,1)S(1)}, bf16[2,2,96,768]{3,2,1,0:T(8,128)(2,1)S(1)}, u32[]{:S(2)}, u32[]{:S(2)}) %collective-permute-start.38) | collective-permute-done | bytes 589856 | tf_op jit(solution)/shard_map/ppermute | solution.py:89
  182.0 2.1 collective-permute-start.43
  186.9 6.4 %collective-permute-done.42.refs_0_ = bf16[2,96,768]{2,1,0:T(8,128)(2,1)S(1)} collective-permute-done((bf16[2,96,768]{2,1,0:T(8,128)(2,1)S(1)}, bf16[2,96,768]{2,1,0:T(8,128)(2,1)S(1)}, u32[]{:S(2)}, u32[]{:S(2)}) %collective-permute-start.42) | collective-permute-done | bytes 294944 | tf_op jit(solution)/shard_map/ppermute | solution.py:94
  193.2 5.1 %collective-permute-done.43.refs_1_ = bf16[2,96,768]{2,1,0:T(8,128)(2,1)S(1)} collective-permute-done((bf16[2,96,768]{2,1,0:T(8,128)(2,1)S(1)}, bf16[2,96,768]{2,1,0:T(8,128)(2,1)S(1)}, u32[]{:S(2)}, u32[]{:S(2)}) %collective-permute-start.43) | collective-permute-done | bytes 294944 | tf_op jit(solution)/shard_map/ppermute | solution.py:94
  200.1 8.2 %collective-permute-done.46.refs_2_ = bf16[2,96,768]{2,1,0:T(8,128)(2,1)S(1)} collective-permute-done((bf16[2,96,768]{2,1,0:T(8,128)(2,1)S(1)}, bf16[2,96,768]{2,1,0:T(8,128)(2,1)S(1)}, u32[]{:S(2)}, u32[]{:S(2)}) %collective-permute-start.46) | collective-permute-done | bytes 294944 | tf_op jit(solution)/shard_map/ppermute | solution.py:94
  209.9 7.9 %collective-permute-start.47 = (bf16[1,96,768]{2,1,0:T(8,128)(2,1)S(1)}, bf16[1,96,768]{2,1,0:T(8,128)(2,1)S(1)}, u32[]{:S(2)}, u32[]{:S(2)}) collective-permute-start(bf16[1,96,768]{2,1,0:T(8,128)(2,1)S(1)} %get-tuple-element.683), channel_id=1, source_target_pairs={{0,8},{4,12},{8,0},{12,4},{16,24},{20,28},{24,16},{28,20},{1,9},{5... | collective-permute-start | bytes 442376 | tf_op jit(solution)/shard_map/ppermute | solution.py:94
  217.8 2.4 collective-permute-start.49
  221.3 5.7 %collective-permute-done.48.refs_1_ = bf16[1,96,768]{2,1,0:T(8,128)(2,1)S(1)} collective-permute-done((bf16[1,96,768]{2,1,0:T(8,128)(2,1)S(1)}, bf16[1,96,768]{2,1,0:T(8,128)(2,1)S(1)}, u32[]{:S(2)}, u32[]{:S(2)}) %collective-permute-start.48) | collective-permute-done | bytes 147488 | tf_op jit(solution)/shard_map/ppermute | solution.py:94
  228.2 4.2 %all-to-all-start.1 = ((f32[32,4,768]{2,1,0:T(4,128)}), f32[32,4,768]{2,1,0:T(4,128)S(1)}, u32[]{:S(2)}, u32[]{:S(2)}) async-start(f32[32,4,768]{2,1,0:T(4,128)} %broadcast_in_dim.5), calls=%async_computation.1 | async-start | bytes 786432 | tf_op jit(solution)/shard_map/all_to_all | solution.py:103
  232.3 1.8 place_rows.1
  234.1 11.4 %all-to-all-done.1.small_ref = f32[32,4,768]{2,1,0:T(4,128)S(1)} async-done(((f32[32,4,768]{2,1,0:T(4,128)}), f32[32,4,768]{2,1,0:T(4,128)S(1)}, u32[]{:S(2)}, u32[]{:S(2)}) %all-to-all-start.1) | async-done | bytes 393248 | tf_op jit(solution)/shard_map/all_to_all | solution.py:103
  245.5 4.3 %update.1 = (f32[1,1]{1,0:T(1,128)}, f32[4,96,192]{2,1,0:T(8,128)}, f32[2,96]{1,0:T(2,128)}, f32[12,32]{1,0:T(8,128)}, f32[4,96,192]{2,1,0:T(8,128)}, /*index=5*...) custom-call(s32[1]{0:T(128)} %bitcast.13.place_ref, ...), custom_call_target="tpu_custom_call" | custom-call | flops 1000 | bytes 1000 | tf_op jit(solution)/shard_map/update/pallas_call | solution.py:918
  (130 shorter events, 41.2 us)
Async XLA Ops:
  2.4 16.6 %collective-permute-start.2 = (bf16[1,96,768]{2,1,0:T(8,128)(2,1)}, bf16[1,96,768]{2,1,0:T(8,128)(2,1)}, u32[]{:S(2)}, u32[]{:S(2)}) collective-permute-start(bf16[1,96,768]{2,1,0:T(8,128)(2,1)} %cast_attn.1.refs_0_), channel_id=1, source_target_pairs={{0,24},{4,28},{8,16},{12,20},{16,8},{20,12},{24,0},{28,4},{1,25},{... | collective-permute-start | bytes 442376 | tf_op jit(solution)/shard_map/ppermute | solution.py:94
  7.5 12.8 %collective-permute-start.1 = (bf16[1,96,768]{2,1,0:T(8,128)(2,1)}, bf16[1,96,768]{2,1,0:T(8,128)(2,1)}, u32[]{:S(2)}, u32[]{:S(2)}) collective-permute-start(bf16[1,96,768]{2,1,0:T(8,128)(2,1)} %cast_attn.1.refs_0_), channel_id=1, source_target_pairs={{0,16},{4,20},{8,24},{12,28},{16,0},{20,4},{24,8},{28,12},{1,17},{... | collective-permute-start | bytes 442376 | tf_op jit(solution)/shard_map/ppermute | solution.py:94
  7.5 12.8 %collective-permute-start = (bf16[1,96,768]{2,1,0:T(8,128)(2,1)}, bf16[1,96,768]{2,1,0:T(8,128)(2,1)}, u32[]{:S(2)}, u32[]{:S(2)}) collective-permute-start(bf16[1,96,768]{2,1,0:T(8,128)(2,1)} %cast_attn.1.refs_0_), channel_id=1, source_target_pairs={{0,8},{4,12},{8,0},{12,4},{16,24},{20,28},{24,16},{28,20},{1,9},{5... | collective-permute-start | bytes 442376 | tf_op jit(solution)/shard_map/ppermute | solution.py:94
  11.3 27.8 %collective-permute-start.5 = (bf16[2,256,768]{2,1,0:T(8,128)(2,1)}, bf16[2,256,768]{2,1,0:T(8,128)(2,1)}, u32[]{:S(2)}, u32[]{:S(2)}) collective-permute-start(bf16[2,256,768]{2,1,0:T(8,128)(2,1)} %sort_rows.1), channel_id=1, source_target_pairs={{0,2},{1,3},{2,0},{3,1},{4,6},{5,7},{6,4},{7,5},{8,10},{9,11},{10,... | collective-permute-start | bytes 2359304 | tf_op jit(solution)/shard_map/ppermute | solution.py:84
  21.3 17.9 %collective-permute-start.4 = (bf16[2,1,96,768]{3,2,1,0:T(8,128)(2,1)S(1)}, bf16[2,1,96,768]{3,2,1,0:T(8,128)(2,1)S(1)}, u32[]{:S(2)}, u32[]{:S(2)}) collective-permute-start(bf16[2,1,96,768]{3,2,1,0:T(8,128)(2,1)S(1)} %line_up.8.refs_0_), channel_id=1, source_target_pairs={{0,4},{4,0},{8,12},{12,8},{16,20},{20,16},{24,28},{28,24},{1,5},{5... | collective-permute-start | bytes 884744 | tf_op jit(solution)/shard_map/ppermute | solution.py:89
  23.9 15.3 %collective-permute-start.3 = (bf16[2,1,96,768]{3,2,1,0:T(8,128)(2,1)S(1)}, bf16[2,1,96,768]{3,2,1,0:T(8,128)(2,1)S(1)}, u32[]{:S(2)}, u32[]{:S(2)}) collective-permute-start(bf16[2,1,96,768]{3,2,1,0:T(8,128)(2,1)S(1)} %line_up.7.refs_0_), channel_id=1, source_target_pairs={{0,2},{1,3},{2,0},{3,1},{4,6},{5,7},{6,4},{7,5},{8,10},{9,11},{10,... | collective-permute-start | bytes 884744 | tf_op jit(solution)/shard_map/ppermute | solution.py:84
  25.4 7.8 %collective-permute-start.7 = (bf16[1,96,768]{2,1,0:T(8,128)(2,1)S(1)}, bf16[1,96,768]{2,1,0:T(8,128)(2,1)S(1)}, u32[]{:S(2)}, u32[]{:S(2)}) collective-permute-start(bf16[1,96,768]{2,1,0:T(8,128)(2,1)S(1)} %get-tuple-element.377), channel_id=1, source_target_pairs={{0,24},{4,28},{8,16},{12,20},{16,8},{20,12},{24,0},{28,4},{1,25},{... | collective-permute-start | bytes 442376 | tf_op jit(solution)/shard_map/ppermute | solution.py:94
  27.9 11.2 %collective-permute-start.6 = (bf16[1,96,768]{2,1,0:T(8,128)(2,1)S(1)}, bf16[1,96,768]{2,1,0:T(8,128)(2,1)S(1)}, u32[]{:S(2)}, u32[]{:S(2)}) collective-permute-start(bf16[1,96,768]{2,1,0:T(8,128)(2,1)S(1)} %get-tuple-element.377), channel_id=1, source_target_pairs={{0,16},{4,20},{8,24},{12,28},{16,0},{20,4},{24,8},{28,12},{1,17},{... | collective-permute-start | bytes 442376 | tf_op jit(solution)/shard_map/ppermute | solution.py:94
  39.2 18.2 %collective-permute-start.9 = (bf16[2,2,1,96,768]{4,3,2,1,0:T(8,128)(2,1)S(1)}, bf16[2,2,1,96,768]{4,3,2,1,0:T(8,128)(2,1)S(1)}, u32[]{:S(2)}, u32[]{:S(2)}) collective-permute-start(bf16[2,2,1,96,768]{4,3,2,1,0:T(8,128)(2,1)S(1)} %line_up.10.refs_1_.refs_3_.refs_5_.refs_7_.refs_2_.refs_4_), channel_id=1, source_target_pairs={{0,2},{1,3},{2,0},{3,1},{4,6},{5,7},{6,4},{7,5},{8,10},{9,11},{10,... | collective-permute-start | bytes 1769480 | tf_op jit(solution)/shard_map/ppermute | solution.py:84
  40.2 17.3 %collective-permute-start.8 = (bf16[2,2,1,96,768]{4,3,2,1,0:T(8,128)(2,1)S(1)}, bf16[2,2,1,96,768]{4,3,2,1,0:T(8,128)(2,1)S(1)}, u32[]{:S(2)}, u32[]{:S(2)}) collective-permute-start(bf16[2,2,1,96,768]{4,3,2,1,0:T(8,128)(2,1)S(1)} %line_up.9.refs_0_.refs_4_.refs_12_.refs_8_.refs_1_), channel_id=1, source_target_pairs={{0,4},{4,0},{8,12},{12,8},{16,20},{20,16},{24,28},{28,24},{1,5},{5... | collective-permute-start | bytes 1769480 | tf_op jit(solution)/shard_map/ppermute | solution.py:89
  40.7 16.7 %collective-permute-start.10 = (bf16[2,96,768]{2,1,0:T(8,128)(2,1)S(1)}, bf16[2,96,768]{2,1,0:T(8,128)(2,1)S(1)}, u32[]{:S(2)}, u32[]{:S(2)}) collective-permute-start(bf16[2,96,768]{2,1,0:T(8,128)(2,1)S(1)} %get-tuple-element.388.refs_0_), channel_id=1, source_target_pairs={{0,8},{4,12},{8,0},{12,4},{16,24},{20,28},{24,16},{28,20},{1,9},{5... | collective-permute-start | bytes 884744 | tf_op jit(solution)/shard_map/ppermute | solution.py:94
  41.4 16.1 %collective-permute-start.12 = (bf16[1,96,768]{2,1,0:T(8,128)(2,1)S(1)}, bf16[1,96,768]{2,1,0:T(8,128)(2,1)S(1)}, u32[]{:S(2)}, u32[]{:S(2)}) collective-permute-start(bf16[1,96,768]{2,1,0:T(8,128)(2,1)S(1)} %get-tuple-element.389), channel_id=1, source_target_pairs={{0,24},{4,28},{8,16},{12,20},{16,8},{20,12},{24,0},{28,4},{1,25},{... | collective-permute-start | bytes 442376 | tf_op jit(solution)/shard_map/ppermute | solution.py:94
  43.7 13.7 %collective-permute-start.11 = (bf16[1,96,768]{2,1,0:T(8,128)(2,1)S(1)}, bf16[1,96,768]{2,1,0:T(8,128)(2,1)S(1)}, u32[]{:S(2)}, u32[]{:S(2)}) collective-permute-start(bf16[1,96,768]{2,1,0:T(8,128)(2,1)S(1)} %get-tuple-element.389), channel_id=1, source_target_pairs={{0,16},{4,20},{8,24},{12,28},{16,0},{20,4},{24,8},{28,12},{1,17},{... | collective-permute-start | bytes 442376 | tf_op jit(solution)/shard_map/ppermute | solution.py:94
  57.5 3.7 %collective-permute-start.14 = (bf16[2,2,1,96,768]{4,3,2,1,0:T(8,128)(2,1)S(1)}, bf16[2,2,1,96,768]{4,3,2,1,0:T(8,128)(2,1)S(1)}, u32[]{:S(2)}, u32[]{:S(2)}) collective-permute-start(bf16[2,2,1,96,768]{4,3,2,1,0:T(8,128)(2,1)S(1)} %line_up.10.refs_1_.refs_3_.refs_5_.refs_7_.refs_2_.refs_4_), channel_id=1, source_target_pairs={{0,1},{1,0},{2,3},{3,2},{4,5},{5,4},{6,7},{7,6},{8,9},{9,8},{10,11... | collective-permute-start | bytes 1769480 | tf_op jit(solution)/shard_map/ppermute | solution.py:80
  57.6 4.2 %collective-permute-start.16 = (bf16[2,2,1,96,768]{4,3,2,1,0:T(8,128)(2,1)S(1)}, bf16[2,2,1,96,768]{4,3,2,1,0:T(8,128)(2,1)S(1)}, u32[]{:S(2)}, u32[]{:S(2)}) collective-permute-start(bf16[2,2,1,96,768]{4,3,2,1,0:T(8,128)(2,1)S(1)} %collective-permute-done.9.refs_5_.refs_7_.refs_13_.refs_15_.refs_9_.refs_11_., ...), channel_id=1, source_target_pairs={{0,1},{1,0},{2,3},{3,2},{4,5},{5,4},{6,7},{7,6},{8,9},{9,8},{10,11... | collective-permute-start | bytes 1769480 | tf_op jit(solution)/shard_map/ppermute | solution.py:80
  60.3 6.3 %collective-permute-start.17 = (bf16[2,512,384]{2,1,0:T(8,128)(2,1)S(1)}, bf16[2,512,384]{2,1,0:T(8,128)(2,1)S(1)}, u32[]{:S(2)}, u32[]{:S(2)}) collective-permute-start(bf16[2,512,384]{2,1,0:T(8,128)(2,1)S(1)} %get-tuple-element.429.kv_ref), channel_id=1, source_target_pairs={{0,1},{1,0},{2,3},{3,2},{4,5},{5,4},{6,7},{7,6},{8,9},{9,8},{10,11... | collective-permute-start | bytes 2359304 | tf_op jit(solution)/shard_map/ppermute | solution.py:80
  60.5 3.0 %collective-permute-start.13 = (bf16[2,2,1,96,768]{4,3,2,1,0:T(8,128)(2,1)S(1)}, bf16[2,2,1,96,768]{4,3,2,1,0:T(8,128)(2,1)S(1)}, u32[]{:S(2)}, u32[]{:S(2)}) collective-permute-start(bf16[2,2,1,96,768]{4,3,2,1,0:T(8,128)(2,1)S(1)} %line_up.9.refs_0_.refs_4_.refs_12_.refs_8_.refs_1_), channel_id=1, source_target_pairs={{0,1},{1,0},{2,3},{3,2},{4,5},{5,4},{6,7},{7,6},{8,9},{9,8},{10,11... | collective-permute-start | bytes 1769480 | tf_op jit(solution)/shard_map/ppermute | solution.py:80
  60.9 3.5 %collective-permute-start.15 = (bf16[2,2,1,96,768]{4,3,2,1,0:T(8,128)(2,1)S(1)}, bf16[2,2,1,96,768]{4,3,2,1,0:T(8,128)(2,1)S(1)}, u32[]{:S(2)}, u32[]{:S(2)}) collective-permute-start(bf16[2,2,1,96,768]{4,3,2,1,0:T(8,128)(2,1)S(1)} %collective-permute-done.8.refs_2_.refs_6_.refs_14_.refs_10_.refs_3_), channel_id=1, source_target_pairs={{0,1},{1,0},{2,3},{3,2},{4,5},{5,4},{6,7},{7,6},{8,9},{9,8},{10,11... | collective-permute-start | bytes 1769480 | tf_op jit(solution)/shard_map/ppermute | solution.py:80
  61.2 28.4 %collective-permute-start.20 = (bf16[2,2,2,96,768]{4,3,2,1,0:T(8,128)(2,1)S(1)}, bf16[2,2,2,96,768]{4,3,2,1,0:T(8,128)(2,1)S(1)}, u32[]{:S(2)}, u32[]{:S(2)}) collective-permute-start(bf16[2,2,2,96,768]{4,3,2,1,0:T(8,128)(2,1)S(1)} %line_up.13.refs_0_.refs_1_), channel_id=1, source_target_pairs={{0,4},{4,0},{8,12},{12,8},{16,20},{20,16},{24,28},{28,24},{1,5},{5... | collective-permute-start | bytes 3538952 | tf_op jit(solution)/shard_map/ppermute | solution.py:89
  61.8 28.0 %collective-permute-start.19 = (bf16[2,2,2,96,768]{4,3,2,1,0:T(8,128)(2,1)S(1)}, bf16[2,2,2,96,768]{4,3,2,1,0:T(8,128)(2,1)S(1)}, u32[]{:S(2)}, u32[]{:S(2)}) collective-permute-start(bf16[2,2,2,96,768]{4,3,2,1,0:T(8,128)(2,1)S(1)} %line_up.13.refs_0_.refs_1_), channel_id=1, source_target_pairs={{0,2},{1,3},{2,0},{3,1},{4,6},{5,7},{6,4},{7,5},{8,10},{9,11},{10,... | collective-permute-start | bytes 3538952 | tf_op jit(solution)/shard_map/ppermute | solution.py:84
  66.6 10.0 %collective-permute-start.18 = (bf16[2,512,384]{2,1,0:T(8,128)(2,1)S(1)}, bf16[2,512,384]{2,1,0:T(8,128)(2,1)S(1)}, u32[]{:S(2)}, u32[]{:S(2)}) collective-permute-start(bf16[2,512,384]{2,1,0:T(8,128)(2,1)S(1)} %get-tuple-element.413.kv_ref), channel_id=1, source_target_pairs={{0,1},{1,0},{2,3},{3,2},{4,5},{5,4},{6,7},{7,6},{8,9},{9,8},{10,11... | collective-permute-start | bytes 2359304 | tf_op jit(solution)/shard_map/ppermute | solution.py:80
  76.6 20.6 %collective-permute-start.23 = (bf16[2,2,2,96,768]{4,3,2,1,0:T(8,128)(2,1)S(1)}, bf16[2,2,2,96,768]{4,3,2,1,0:T(8,128)(2,1)S(1)}, u32[]{:S(2)}, u32[]{:S(2)}) collective-permute-start(bf16[2,2,2,96,768]{4,3,2,1,0:T(8,128)(2,1)S(1)} %line_up.13.refs_0_.refs_1_), channel_id=1, source_target_pairs={{0,1},{1,0},{2,3},{3,2},{4,5},{5,4},{6,7},{7,6},{8,9},{9,8},{10,11... | collective-permute-start | bytes 3538952 | tf_op jit(solution)/shard_map/ppermute | solution.py:80
  89.8 7.4 %collective-permute-start.21 = (bf16[2,2,2,96,768]{4,3,2,1,0:T(8,128)(2,1)S(1)}, bf16[2,2,2,96,768]{4,3,2,1,0:T(8,128)(2,1)S(1)}, u32[]{:S(2)}, u32[]{:S(2)}) collective-permute-start(bf16[2,2,2,96,768]{4,3,2,1,0:T(8,128)(2,1)S(1)} %collective-permute-done.20.refs_2_.refs_3_), channel_id=1, source_target_pairs={{0,1},{1,0},{2,3},{3,2},{4,5},{5,4},{6,7},{7,6},{8,9},{9,8},{10,11... | collective-permute-start | bytes 3538952 | tf_op jit(solution)/shard_map/ppermute | solution.py:80
  89.8 7.4 %collective-permute-start.22 = (bf16[2,2,2,96,768]{4,3,2,1,0:T(8,128)(2,1)S(1)}, bf16[2,2,2,96,768]{4,3,2,1,0:T(8,128)(2,1)S(1)}, u32[]{:S(2)}, u32[]{:S(2)}) collective-permute-start(bf16[2,2,2,96,768]{4,3,2,1,0:T(8,128)(2,1)S(1)} %collective-permute-done.19.refs_2_.refs_3_), channel_id=1, source_target_pairs={{0,1},{1,0},{2,3},{3,2},{4,5},{5,4},{6,7},{7,6},{8,9},{9,8},{10,11... | collective-permute-start | bytes 3538952 | tf_op jit(solution)/shard_map/ppermute | solution.py:80
  90.4 15.3 %collective-permute-start.24 = (bf16[2,2,96,768]{3,2,1,0:T(8,128)(2,1)S(1)}, bf16[2,2,96,768]{3,2,1,0:T(8,128)(2,1)S(1)}, u32[]{:S(2)}, u32[]{:S(2)}) collective-permute-start(bf16[2,2,96,768]{3,2,1,0:T(8,128)(2,1)S(1)} %slice_bitcast_fusion.1), channel_id=1, source_target_pairs={{0,4},{4,0},{8,12},{12,8},{16,20},{20,16},{24,28},{28,24},{1,5},{5... | collective-permute-start | bytes 1769480 | tf_op jit(solution)/shard_map/ppermute | solution.py:89
  92.0 15.0 %collective-permute-start.25 = (bf16[2,2,96,768]{3,2,1,0:T(8,128)(2,1)S(1)}, bf16[2,2,96,768]{3,2,1,0:T(8,128)(2,1)S(1)}, u32[]{:S(2)}, u32[]{:S(2)}) collective-permute-start(bf16[2,2,96,768]{3,2,1,0:T(8,128)(2,1)S(1)} %slice_bitcast_fusion), channel_id=1, source_target_pairs={{0,2},{1,3},{2,0},{3,1},{4,6},{5,7},{6,4},{7,5},{8,10},{9,11},{10,... | collective-permute-start | bytes 1769480 | tf_op jit(solution)/shard_map/ppermute | solution.py:84
  106.9 5.3 %collective-permute-start.26 = (bf16[2,2,96,768]{3,2,1,0:T(8,128)(2,1)S(1)}, bf16[2,2,96,768]{3,2,1,0:T(8,128)(2,1)S(1)}, u32[]{:S(2)}, u32[]{:S(2)}) collective-permute-start(bf16[2,2,96,768]{3,2,1,0:T(8,128)(2,1)S(1)} %collective-permute-done.24.refs_4_), channel_id=1, source_target_pairs={{0,1},{1,0},{2,3},{3,2},{4,5},{5,4},{6,7},{7,6},{8,9},{9,8},{10,11... | collective-permute-start | bytes 1769480 | tf_op jit(solution)/shard_map/ppermute | solution.py:80
  106.9 5.3 %collective-permute-start.27 = (bf16[2,2,96,768]{3,2,1,0:T(8,128)(2,1)S(1)}, bf16[2,2,96,768]{3,2,1,0:T(8,128)(2,1)S(1)}, u32[]{:S(2)}, u32[]{:S(2)}) collective-permute-start(bf16[2,2,96,768]{3,2,1,0:T(8,128)(2,1)S(1)} %collective-permute-done.25.refs_5_), channel_id=1, source_target_pairs={{0,1},{1,0},{2,3},{3,2},{4,5},{5,4},{6,7},{7,6},{8,9},{9,8},{10,11... | collective-permute-start | bytes 1769480 | tf_op jit(solution)/shard_map/ppermute | solution.py:80
  117.0 4.6 %collective-permute-start.29 = (bf16[2,2,2,2,96,768]{5,4,3,2,1,0:T(8,128)(2,1)S(1)}, bf16[2,2,2,2,96,768]{5,4,3,2,1,0:T(8,128)(2,1)S(1)}, u32[]{:S(2)}, u32[]{:S(2)}) collective-permute-start(bf16[2,2,2,2,96,768]{5,4,3,2,1,0:T(8,128)(2,1)S(1)} %get-tuple-element.516), channel_id=1, source_target_pairs={{0,1},{1,0},{2,3},{3,2},{4,5},{5,4},{6,7},{7,6},{8,9},{9,8},{10,11... | collective-permute-start | bytes 7077896 | tf_op jit(solution)/shard_map/ppermute | solution.py:80
  117.1 7.9 %collective-permute-start.28 = (bf16[2,2,2,2,96,768]{5,4,3,2,1,0:T(8,128)(2,1)S(1)}, bf16[2,2,2,2,96,768]{5,4,3,2,1,0:T(8,128)(2,1)S(1)}, u32[]{:S(2)}, u32[]{:S(2)}) collective-permute-start(bf16[2,2,2,2,96,768]{5,4,3,2,1,0:T(8,128)(2,1)S(1)} %get-tuple-element.494), channel_id=1, source_target_pairs={{0,1},{1,0},{2,3},{3,2},{4,5},{5,4},{6,7},{7,6},{8,9},{9,8},{10,11... | collective-permute-start | bytes 7077896 | tf_op jit(solution)/shard_map/ppermute | solution.py:80
  126.1 31.4 %collective-permute-start.30 = (bf16[2,2,2,96,768]{4,3,2,1,0:T(8,128)(2,1)S(1)}, bf16[2,2,2,96,768]{4,3,2,1,0:T(8,128)(2,1)S(1)}, u32[]{:S(2)}, u32[]{:S(2)}) collective-permute-start(bf16[2,2,2,96,768]{4,3,2,1,0:T(8,128)(2,1)S(1)} %get-tuple-element.582), channel_id=1, source_target_pairs={{0,2},{1,3},{2,0},{3,1},{4,6},{5,7},{6,4},{7,5},{8,10},{9,11},{10,... | collective-permute-start | bytes 3538952 | tf_op jit(solution)/shard_map/ppermute | solution.py:84
  126.8 30.8 %collective-permute-start.31 = (bf16[2,2,2,96,768]{4,3,2,1,0:T(8,128)(2,1)S(1)}, bf16[2,2,2,96,768]{4,3,2,1,0:T(8,128)(2,1)S(1)}, u32[]{:S(2)}, u32[]{:S(2)}) collective-permute-start(bf16[2,2,2,96,768]{4,3,2,1,0:T(8,128)(2,1)S(1)} %get-tuple-element.583), channel_id=1, source_target_pairs={{0,4},{4,0},{8,12},{12,8},{16,20},{20,16},{24,28},{28,24},{1,5},{5... | collective-permute-start | bytes 3538952 | tf_op jit(solution)/shard_map/ppermute | solution.py:89
  162.9 8.6 %collective-permute-start.36 = (bf16[2,2,2,1,96,768]{5,4,3,2,1,0:T(8,128)(2,1)S(1)}, bf16[2,2,2,1,96,768]{5,4,3,2,1,0:T(8,128)(2,1)S(1)}, u32[]{:S(2)}, u32[]{:S(2)}) collective-permute-start(bf16[2,2,2,1,96,768]{5,4,3,2,1,0:T(8,128)(2,1)S(1)} %get-tuple-element.612), channel_id=1, source_target_pairs={{0,1},{1,0},{2,3},{3,2},{4,5},{5,4},{6,7},{7,6},{8,9},{9,8},{10,11... | collective-permute-start | bytes 3538952 | tf_op jit(solution)/shard_map/ppermute | solution.py:80
  163.1 8.4 %collective-permute-start.37 = (bf16[2,2,2,1,96,768]{5,4,3,2,1,0:T(8,128)(2,1)S(1)}, bf16[2,2,2,1,96,768]{5,4,3,2,1,0:T(8,128)(2,1)S(1)}, u32[]{:S(2)}, u32[]{:S(2)}) collective-permute-start(bf16[2,2,2,1,96,768]{5,4,3,2,1,0:T(8,128)(2,1)S(1)} %get-tuple-element.609), channel_id=1, source_target_pairs={{0,1},{1,0},{2,3},{3,2},{4,5},{5,4},{6,7},{7,6},{8,9},{9,8},{10,11... | collective-permute-start | bytes 3538952 | tf_op jit(solution)/shard_map/ppermute | solution.py:80
  163.5 16.2 %collective-permute-start.38 = (bf16[2,2,96,768]{3,2,1,0:T(8,128)(2,1)S(1)}, bf16[2,2,96,768]{3,2,1,0:T(8,128)(2,1)S(1)}, u32[]{:S(2)}, u32[]{:S(2)}) collective-permute-start(bf16[2,2,96,768]{3,2,1,0:T(8,128)(2,1)S(1)} %get-tuple-element.639), channel_id=1, source_target_pairs={{0,4},{4,0},{8,12},{12,8},{16,20},{20,16},{24,28},{28,24},{1,5},{5... | collective-permute-start | bytes 1769480 | tf_op jit(solution)/shard_map/ppermute | solution.py:89
  164.9 16.2 %collective-permute-start.39 = (bf16[2,2,96,768]{3,2,1,0:T(8,128)(2,1)S(1)}, bf16[2,2,96,768]{3,2,1,0:T(8,128)(2,1)S(1)}, u32[]{:S(2)}, u32[]{:S(2)}) collective-permute-start(bf16[2,2,96,768]{3,2,1,0:T(8,128)(2,1)S(1)} %get-tuple-element.640), channel_id=1, source_target_pairs={{0,2},{1,3},{2,0},{3,1},{4,6},{5,7},{6,4},{7,5},{8,10},{9,11},{10,... | collective-permute-start | bytes 1769480 | tf_op jit(solution)/shard_map/ppermute | solution.py:84
  172.1 26.3 %collective-permute-start.40 = (bf16[2,2,1,96,768]{4,3,2,1,0:T(8,128)(2,1)S(1)}, bf16[2,2,1,96,768]{4,3,2,1,0:T(8,128)(2,1)S(1)}, u32[]{:S(2)}, u32[]{:S(2)}) collective-permute-start(bf16[2,2,1,96,768]{4,3,2,1,0:T(8,128)(2,1)S(1)} %get-tuple-element.652), channel_id=1, source_target_pairs={{0,2},{1,3},{2,0},{3,1},{4,6},{5,7},{6,4},{7,5},{8,10},{9,11},{10,... | collective-permute-start | bytes 1769480 | tf_op jit(solution)/shard_map/ppermute | solution.py:84
  172.8 25.6 %collective-permute-start.41 = (bf16[2,2,1,96,768]{4,3,2,1,0:T(8,128)(2,1)S(1)}, bf16[2,2,1,96,768]{4,3,2,1,0:T(8,128)(2,1)S(1)}, u32[]{:S(2)}, u32[]{:S(2)}) collective-permute-start(bf16[2,2,1,96,768]{4,3,2,1,0:T(8,128)(2,1)S(1)} %get-tuple-element.653), channel_id=1, source_target_pairs={{0,4},{4,0},{8,12},{12,8},{16,20},{20,16},{24,28},{28,24},{1,5},{5... | collective-permute-start | bytes 1769480 | tf_op jit(solution)/shard_map/ppermute | solution.py:89
  181.4 11.8 %collective-permute-start.42 = (bf16[2,96,768]{2,1,0:T(8,128)(2,1)S(1)}, bf16[2,96,768]{2,1,0:T(8,128)(2,1)S(1)}, u32[]{:S(2)}, u32[]{:S(2)}) collective-permute-start(bf16[2,96,768]{2,1,0:T(8,128)(2,1)S(1)} %get-tuple-element.647), channel_id=1, source_target_pairs={{0,8},{4,12},{8,0},{12,4},{16,24},{20,28},{24,16},{28,20},{1,9},{5... | collective-permute-start | bytes 884744 | tf_op jit(solution)/shard_map/ppermute | solution.py:94
  182.0 16.3 %collective-permute-start.43 = (bf16[2,96,768]{2,1,0:T(8,128)(2,1)S(1)}, bf16[2,96,768]{2,1,0:T(8,128)(2,1)S(1)}, u32[]{:S(2)}, u32[]{:S(2)}) collective-permute-start(bf16[2,96,768]{2,1,0:T(8,128)(2,1)S(1)} %get-tuple-element.649), channel_id=1, source_target_pairs={{0,24},{4,28},{8,16},{12,20},{16,8},{20,12},{24,0},{28,4},{1,25},{... | collective-permute-start | bytes 884744 | tf_op jit(solution)/shard_map/ppermute | solution.py:94
  186.0 22.3 %collective-permute-start.46 = (bf16[2,96,768]{2,1,0:T(8,128)(2,1)S(1)}, bf16[2,96,768]{2,1,0:T(8,128)(2,1)S(1)}, u32[]{:S(2)}, u32[]{:S(2)}) collective-permute-start(bf16[2,96,768]{2,1,0:T(8,128)(2,1)S(1)} %get-tuple-element.669), channel_id=1, source_target_pairs={{0,16},{4,20},{8,24},{12,28},{16,0},{20,4},{24,8},{28,12},{1,17},{... | collective-permute-start | bytes 884744 | tf_op jit(solution)/shard_map/ppermute | solution.py:94
  198.6 9.7 %collective-permute-start.44 = (bf16[2,1,96,768]{3,2,1,0:T(8,128)(2,1)S(1)}, bf16[2,1,96,768]{3,2,1,0:T(8,128)(2,1)S(1)}, u32[]{:S(2)}, u32[]{:S(2)}) collective-permute-start(bf16[2,1,96,768]{3,2,1,0:T(8,128)(2,1)S(1)} %get-tuple-element.662), channel_id=1, source_target_pairs={{0,4},{4,0},{8,12},{12,8},{16,20},{20,16},{24,28},{28,24},{1,5},{5... | collective-permute-start | bytes 884744 | tf_op jit(solution)/shard_map/ppermute | solution.py:89
  199.4 9.0 %collective-permute-start.45 = (bf16[2,1,96,768]{3,2,1,0:T(8,128)(2,1)S(1)}, bf16[2,1,96,768]{3,2,1,0:T(8,128)(2,1)S(1)}, u32[]{:S(2)}, u32[]{:S(2)}) collective-permute-start(bf16[2,1,96,768]{3,2,1,0:T(8,128)(2,1)S(1)} %get-tuple-element.663), channel_id=1, source_target_pairs={{0,2},{1,3},{2,0},{3,1},{4,6},{5,7},{6,4},{7,5},{8,10},{9,11},{10,... | collective-permute-start | bytes 884744 | tf_op jit(solution)/shard_map/ppermute | solution.py:84
  208.4 18.7 %collective-permute-start.50 = (bf16[2,256,768]{2,1,0:T(8,128)(2,1)S(1)}, bf16[2,256,768]{2,1,0:T(8,128)(2,1)S(1)}, u32[]{:S(2)}, u32[]{:S(2)}) collective-permute-start(bf16[2,256,768]{2,1,0:T(8,128)(2,1)S(1)} %get-tuple-element.686), channel_id=1, source_target_pairs={{0,2},{1,3},{2,0},{3,1},{4,6},{5,7},{6,4},{7,5},{8,10},{9,11},{10,... | collective-permute-start | bytes 2359304 | tf_op jit(solution)/shard_map/ppermute | solution.py:84
  209.9 11.4 %collective-permute-start.47 = (bf16[1,96,768]{2,1,0:T(8,128)(2,1)S(1)}, bf16[1,96,768]{2,1,0:T(8,128)(2,1)S(1)}, u32[]{:S(2)}, u32[]{:S(2)}) collective-permute-start(bf16[1,96,768]{2,1,0:T(8,128)(2,1)S(1)} %get-tuple-element.683), channel_id=1, source_target_pairs={{0,8},{4,12},{8,0},{12,4},{16,24},{20,28},{24,16},{28,20},{1,9},{5... | collective-permute-start | bytes 442376 | tf_op jit(solution)/shard_map/ppermute | solution.py:94
  217.8 9.2 %collective-permute-start.48 = (bf16[1,96,768]{2,1,0:T(8,128)(2,1)S(1)}, bf16[1,96,768]{2,1,0:T(8,128)(2,1)S(1)}, u32[]{:S(2)}, u32[]{:S(2)}) collective-permute-start(bf16[1,96,768]{2,1,0:T(8,128)(2,1)S(1)} %get-tuple-element.684), channel_id=1, source_target_pairs={{0,16},{4,20},{8,24},{12,28},{16,0},{20,4},{24,8},{28,12},{1,17},{... | collective-permute-start | bytes 442376 | tf_op jit(solution)/shard_map/ppermute | solution.py:94
  217.8 9.2 %collective-permute-start.49 = (bf16[1,96,768]{2,1,0:T(8,128)(2,1)S(1)}, bf16[1,96,768]{2,1,0:T(8,128)(2,1)S(1)}, u32[]{:S(2)}, u32[]{:S(2)}) collective-permute-start(bf16[1,96,768]{2,1,0:T(8,128)(2,1)S(1)} %get-tuple-element.685), channel_id=1, source_target_pairs={{0,24},{4,28},{8,16},{12,20},{16,8},{20,12},{24,0},{28,4},{1,25},{... | collective-permute-start | bytes 442376 | tf_op jit(solution)/shard_map/ppermute | solution.py:94
  228.2 17.4 %all-to-all-start.1 = ((f32[32,4,768]{2,1,0:T(4,128)}), f32[32,4,768]{2,1,0:T(4,128)S(1)}, u32[]{:S(2)}, u32[]{:S(2)}) async-start(f32[32,4,768]{2,1,0:T(4,128)} %broadcast_in_dim.5), calls=%async_computation.1 | async-start | bytes 786432 | tf_op jit(solution)/shard_map/all_to_all | solution.py:103
  (15 other events, 260.1 us)

commit v5 on v4

--- a/solution.py
+++ b/solution.py
@@ -94,6 +94,11 @@
     return lax.ppermute(v, "dp", [(i, i ^ (2 * k)) for i in range(n)])
 
 
+def shift_z(v):
+    n = lax.axis_size("dp")
+    return lax.ppermute(v, "dp", [(i, (i + 2) % n) for i in range(n)])
+
+
 def fence(*values):
     return lax.optimization_barrier(values)
 
@@ -109,7 +114,7 @@
     return lax.all_to_all(jnp.broadcast_to(low[None], (n,) + low.shape), "dp", 0, 0)
 
 
-def block_views(by_y):
+def block_views(by_y, ring=False):
     entries = [e if isinstance(e, tuple) else (e, None) for parts in by_y for e in parts]
     rows = entries[0][0].shape[-2]
     if rows % 16 == 0:
@@ -120,7 +125,9 @@
     both = jnp.stack([jnp.concatenate(plain[2 * y : 2 * y + 2], 0) for y in range(2)])
     depth = both.shape[1]
     sides = jnp.take(both, jnp.arange(2) ^ (dp % 2), axis=0)
-    lined = jnp.take(sides, jnp.arange(depth) ^ (dp // 2), axis=1)
+    steps = jnp.arange(depth)
+    order = (dp // 2 - steps) % depth if ring else steps ^ (dp // 2)
+    lined = jnp.take(sides, order, axis=1)
     return [jnp.transpose(lined, (2, 1, 0, 3, 4)).reshape(1, which, D, cols)], (None,)
 
 
@@ -145,8 +152,8 @@
     return turned.reshape(2, 2, depth // 2, which, rows, -1)
 
 
-def assemble(whole, refs, place_ref, which=0, cols=slice(None)):
-    count = 0
+def assemble(whole, refs, place_ref, which=0, cols=slice(None), ring=False):
+    count = sum(ref.shape[0] for ref in refs) if ring else 0
     for ref in refs:
         for j in range(ref.shape[0]):
             start = pl.multiple_of(place_ref[5 + count], 16)
@@ -244,27 +251,41 @@
 
 def tile_places(place_ref):
     x, core = place_ref[0], place_ref[1]
-    mine = [4 * (x if t < 2 else 1 - x) + 2 * core + t % 2 for t in range(4)]
-    theirs = [4 * (x if t < 2 else 1 - x) + 2 * (1 - core) + t % 2 for t in range(4)]
-    return mine, mine + theirs
+    return [
+        4 * (x if t < 2 else 1 - x) + 2 * side + t % 2 for side in (core, 1 - core) for t in range(4)
+    ]
 
 
 def attend_kernel(
-    b, r_index, place_ref, q_ref, kv_ref, other_ref, bias_ref, ctx_ref, p_out, p_ref, sems
+    b,
+    r_index,
+    place_ref,
+    q_own_ref,
+    q_other_ref,
+    kv_own_ref,
+    kv_other_ref,
+    bias_ref,
+    own_ref,
+    send_ref,
+    p_out,
+    p_ref,
+    sems,
 ):
-    rows = q_ref.shape[1]
+    half = q_own_ref.shape[1]
+    rows = 2 * half
     step = 256
     lane = lax.broadcasted_iota(jnp.int32, (1, 256), 1)
     key = lax.broadcasted_iota(jnp.int32, (1, TILE), 1)
     sub = lax.broadcasted_iota(jnp.int32, (64, 1), 0)
-    row_tiles, key_tiles = tile_places(place_ref)
+    tiles_at = tile_places(place_ref)
     length = place_ref[3 + place_ref[0]]
-    hide = jnp.concatenate([jnp.where(key + TILE * g < length, 0.0, -1e30) for g in key_tiles], 1)
+    hide = jnp.concatenate([jnp.where(key + TILE * g < length, 0.0, -1e30) for g in tiles_at], 1)
     extra = jnp.where(sub == 0, hide, 0.0).astype(BF)
-    both = jnp.concatenate([kv_ref[b], other_ref[b]], 0)
+    both = jnp.concatenate([kv_own_ref[b], kv_other_ref[b]], 0)
     keys_t = jnp.concatenate([both[:, :WIDTH].T, extra], 0)
     values = both[:, WIDTH:]
-    queries = jnp.concatenate([q_ref[b], jnp.ones((rows, 64), BF)], 1)
+    queries = jnp.concatenate([q_own_ref[b], q_other_ref[b]], 0)
+    queries = jnp.concatenate([queries, jnp.ones((rows, 64), BF)], 1)
     total = [jnp.zeros((step, WIDTH), F32) for _ in range(rows // step)]
     for h in range(GROUP):
         inside = (lane >= h * DH) & (lane < (h + 1) * DH)
@@ -276,7 +297,7 @@
             for c in range(8):
                 bias = []
                 for u in range(step // TILE):
-                    which = jnp.clip(key_tiles[c] - row_tiles[r * (step // TILE) + u] + 2, 0, 4)
+                    which = jnp.clip(tiles_at[c] - tiles_at[r * (step // TILE) + u] + 2, 0, 4)
                     bias.append(bias_ref[r_index, h, which])
                 tiles.append(scores[:, c * TILE : (c + 1) * TILE] + jnp.concatenate(bias, 0))
             top = jnp.max(functools.reduce(jnp.maximum, tiles), axis=-1, keepdims=True)
@@ -287,41 +308,46 @@
             p_ref[h, pl.ds(r * step, step), :] = prob
             total[r] = jnp.where(inside[:, :WIDTH], dot(prob, values, NN), total[r])
         pltpu.make_async_copy(p_ref.at[h], p_out.at[h], sems.at[h]).start()
+    blank = jnp.zeros((step, 64), BF)
     for r in range(rows // step):
-        ctx_ref[pl.ds(r * step, step), :] = total[r].astype(BF)
+        out = jnp.concatenate([blank, total[r].astype(BF)], 1)
+        at = r * step
+        if at < half:
+            own_ref[pl.ds(at, step), :] = out
+        else:
+            send_ref[pl.ds(at - half, step), :] = out
     for h in range(GROUP):
         pltpu.make_async_copy(p_ref.at[h], p_out.at[h], sems.at[h]).wait()
 
 
-def attend(place, q, kv, other, bias, b, r_index):
-    rows = q.shape[1]
-    return pl.pallas_call(
-        functools.partial(attend_kernel, b, r_index),
-        in_specs=[in_smem] + [in_vmem] * 4,
-        out_specs=[in_vmem, in_hbm],
-        out_shape=[shape_of((rows, WIDTH), BF), pltpu.HBM((GROUP, rows, 2 * rows), BF)],
+def attend(place, q, kv, bias, r):
+    half = q[0].shape[1]
+    rows = 2 * half
+    return pl.pallas_call(
+        functools.partial(attend_kernel, r // 2, r),
+        in_specs=[in_smem] + [in_vmem] * 5,
+        out_specs=[in_vmem, in_vmem, in_hbm],
+        out_shape=[shape_of((half, 256), BF)] * 2 + [pltpu.HBM((GROUP, rows, rows), BF)],
         scratch_shapes=[
-            pltpu.VMEM((GROUP, rows, 2 * rows), BF),
+            pltpu.VMEM((GROUP, rows, rows), BF),
             pltpu.SemaphoreType.DMA((GROUP,)),
         ],
-        compiler_params=params(12),
-        cost_estimate=cost(GROUP * rows * 2 * rows * 256 * 8, 6e6, GROUP * rows * 2 * rows),
+        compiler_params=params(18),
+        cost_estimate=cost(1, 1),
         name="attend",
-    )(place, q, kv, other, bias)
+    )(place, *q, *kv, bias)
 
 
 def middle_kernel(indices, place_ref, x_ref, gain_ref, back_ref, *refs):
     n_parts = len(indices[0])
     ctx_refs, w_refs = refs[:4], refs[4 : 4 + 4 * n_parts]
     mid_ref, normed_ref, normed_t_ref, back_t_ref, whole = refs[4 + 4 * n_parts :]
-    rows = x_ref.shape[0]
     total = x_ref[...].astype(F32)
     back_t_ref[...] = back_ref[...].T
-    blank = jnp.zeros((rows, 64), BF)
     for b in range(4):
         part = pick(w_refs[b * n_parts : (b + 1) * n_parts], indices[b])
         assemble(whole.at[b], part, place_ref, 0, slice(512, 768))
-        total = total + dot(jnp.concatenate([blank, ctx_refs[b][...]], 1), whole[b], NT)
+        total = total + dot(ctx_refs[b][...], whole[b], NT)
     mid_ref[...] = total
     normed = rms_of(total, gain_ref[1:2].astype(F32)).astype(BF)
     normed_ref[...] = normed
@@ -355,8 +381,8 @@
     n_parts = len(indices)
     w_refs, (acc_ref, t_ref, grads_ref, wi, wf, gi, gf) = refs[:n_parts], refs[n_parts:]
     w_refs = pick(w_refs, indices)
-    assemble(wi, w_refs, place_ref, 0)
-    assemble(wf, w_refs, place_ref, 1)
+    assemble(wi, w_refs, place_ref, 0, ring=True)
+    assemble(wf, w_refs, place_ref, 1, ring=True)
     pre = dot(n_ref[...], wi[...], NN)
     grad = dot(g_ref[...], wf[...], NN)
     cdf = 0.5 * (1.0 + lax.erf(pre * 0.7071067811865476))
@@ -394,12 +420,7 @@
     return (outs[0], outs[1]), outs[2]
 
 
-def turn_kernel(indices, place_ref, mid_ref, acc_ref, t_ref, back_ref, gain_ref, *refs):
-    n_parts = len(indices[0])
-    w_refs = refs[: 4 * n_parts]
-    rest = refs[4 * n_parts :]
-    keep_ref, send_ref, grad_ref, low_t_ref, gain_grad_ref = rest[:5]
-    cg_refs, whole = rest[5:9], rest[9]
+def turn_kernel(mid_ref, acc_ref, t_ref, back_ref, gain_ref, keep_ref, send_ref, grad_ref, low_ref, gain_grad_ref):
     mid = mid_ref[...]
     out = (mid + acc_ref[...]).astype(BF)
     half = keep_ref.shape[0]
@@ -408,62 +429,84 @@
     gain_grad_ref[...] = gain_grad
     grad = back_ref[...].astype(F32) + grad
     grad_ref[...] = grad
-    low = grad.astype(BF)
-    low_t_ref[...] = low.T
-    for b in range(4):
-        part = pick(w_refs[b * n_parts : (b + 1) * n_parts], indices[b])
-        assemble(whole.at[b], part, place_ref, 0, slice(512, 768))
-        cg_refs[b][...] = dot(low, whole[b], NN).astype(BF)[:, 64:]
-
-
-def turn(place, mid, acc, t_acc, back, gain_low, blocks):
+    low_ref[...] = grad.astype(BF)
+
+
+def turn(mid, acc, t_acc, back, gain_low):
     rows = mid.shape[0]
-    n_parts = len(blocks[0][0])
-    return pl.pallas_call(
-        functools.partial(turn_kernel, [i for _, i in blocks]),
-        in_specs=[in_smem] + [in_vmem] * (5 + 4 * n_parts),
-        out_specs=[in_vmem] * 9,
+    return pl.pallas_call(
+        turn_kernel,
+        in_specs=[in_vmem] * 5,
+        out_specs=[in_vmem] * 5,
         out_shape=[
             shape_of((rows // 2, D), BF),
             shape_of((rows // 2, D), BF),
             shape_of((rows, D), F32),
-            shape_of((D, rows), BF),
+            shape_of((rows, D), BF),
             shape_of((1, D), F32),
-        ]
-        + [shape_of((rows, WIDTH), BF)] * 4,
-        scratch_shapes=[pltpu.VMEM((4, D, 256), BF)],
+        ],
         compiler_params=params(12),
-        cost_estimate=cost(2 * rows * D * D, 10e6),
+        cost_estimate=cost(1, 1),
         name="turn",
-    )(place, mid, acc, t_acc, back, gain_low, *[p for b, _ in blocks for p in b])
+    )(mid, acc, t_acc, back, gain_low)
+
+
+def context_grad_kernel(indices, place_ref, own_ref, other_ref, *refs):
+    n_parts = len(indices[0])
+    w_refs, (g0_ref, g1_ref, low_t_ref, whole) = refs[: 2 * n_parts], refs[2 * n_parts :]
+    half = own_ref.shape[0]
+    for i, ref in enumerate((own_ref, other_ref)):
+        low_t_ref[:, pl.ds(i * half, half)] = ref[...].T
+    for b, g_ref in enumerate((g0_ref, g1_ref)):
+        part = pick(w_refs[b * n_parts : (b + 1) * n_parts], indices[b])
+        assemble(whole.at[b], part, place_ref, 0, slice(512, 768))
+        for i, ref in enumerate((own_ref, other_ref)):
+            g_ref[pl.ds(i * half, half), :] = dot(ref[...], whole[b], NN).astype(BF)[:, 64:]
+
+
+def context_grads(place, low_own, low_other, blocks):
+    half = low_own.shape[0]
+    n_parts = len(blocks[0][0])
+    return pl.pallas_call(
+        functools.partial(context_grad_kernel, [i for _, i in blocks]),
+        in_specs=[in_smem] + [in_vmem] * (2 + 2 * n_parts),
+        out_specs=[in_vmem] * 3,
+        out_shape=[shape_of((2 * half, WIDTH), BF)] * 2 + [shape_of((D, 2 * half), BF)],
+        scratch_shapes=[pltpu.VMEM((2, D, 256), BF)],
+        compiler_params=params(12),
+        cost_estimate=cost(1, 1),
+        name="context_grads",
+    )(place, low_own, low_other, *blocks[0][0], *blocks[1][0])
 
 
 def attend_back_kernel(
     b,
     place_ref,
-    q_ref,
-    kv_ref,
-    other_ref,
+    q_own_ref,
+    q_other_ref,
+    kv_own_ref,
+    kv_other_ref,
     g_ref,
-    ctx_ref,
+    ctx_own_ref,
+    ctx_other_ref,
     p_ref,
-    dq_ref,
-    own_ref,
-    send_ref,
+    heads_ref,
     bucket_ref,
     ds_ref,
     sums_ref,
 ):
-    rows = q_ref.shape[1]
+    rows = g_ref.shape[0]
     step = 128
     lane = lax.broadcasted_iota(jnp.int32, (1, WIDTH), 1)
-    row_tiles, key_tiles = tile_places(place_ref)
+    tiles_at = tile_places(place_ref)
     grads = g_ref[...]
-    both = jnp.concatenate([kv_ref[b], other_ref[b]], 0)
+    both = jnp.concatenate([kv_own_ref[b], kv_other_ref[b]], 0)
     keys = both[:, :WIDTH]
     values_t = both[:, WIDTH:].T
-    queries_t, grads_t = q_ref[b].T, grads.T
-    product = grads.astype(F32) * ctx_ref[...].astype(F32)
+    queries_t = jnp.concatenate([q_own_ref[b].T, q_other_ref[b].T], 1)
+    grads_t = grads.T
+    context = jnp.concatenate([ctx_own_ref[...], ctx_other_ref[...]], 0)[:, 64:]
+    product = grads.astype(F32) * context.astype(F32)
     sums_ref[...] = jnp.zeros_like(sums_ref)
     total = [jnp.zeros((step, WIDTH), F32) for _ in range(rows // step)]
     key_grads, value_grads = [], []
@@ -478,89 +521,105 @@
             for c in range(8):
                 prob = p_ref[h, pl.ds(r * step, step), pl.ds(c * TILE, TILE)].astype(F32)
                 dscore = prob * (prob_grad[:, c * TILE : (c + 1) * TILE] - row_dot)
-                which = jnp.clip(key_tiles[c] - row_tiles[r] + 2, 0, 4)
+                which = jnp.clip(tiles_at[c] - tiles_at[r] + 2, 0, 4)
                 sums_ref[h, which] += dscore
                 lows.append(dscore.astype(BF))
             low = jnp.concatenate(lows, 1)
-            ds_ref[pl.ds(r * step, step), :] = low
+            ds_ref[h, pl.ds(r * step, step), :] = low
             total[r] = jnp.where(inside, dot(low, keys, NN), total[r])
-        key_grads.append(dot(queries_t[h * DH : (h + 1) * DH], ds_ref[...], NN))
+        key_grads.append(dot(queries_t[h * DH : (h + 1) * DH], ds_ref[h], NN))
         value_grads.append(dot(grads_t[h * DH : (h + 1) * DH], p_ref[h], NN))
-    for r in range(rows // step):
-        dq_ref[pl.ds(r * step, step), :] = total[r].astype(BF)
-    grad = jnp.concatenate(key_grads + value_grads, 0).T
-    own_ref[...] = grad[:rows]
-    send_ref[...] = grad[rows:].astype(BF)
+    query_grad = jnp.concatenate([t.astype(BF) for t in total], 0)
+    others = jnp.concatenate(key_grads + value_grads, 0).T.astype(BF)
+    heads_ref[...] = jnp.concatenate([query_grad, others], 1)
     row = lax.broadcasted_iota(jnp.int32, (TILE, TILE), 0)
     col = lax.broadcasted_iota(jnp.int32, (TILE, TILE), 1)
     buckets = {t: bucket_of(col - row + (t - 2) * TILE) for t in range(1, 4)}
     for b in range(NB):
         masks = {t: buckets[t] == b for t in ((1, 2) if b < 16 else (2, 3))}
         for h in range(GROUP):
-            total = jnp.zeros((TILE, TILE), F32)
+            tile = jnp.zeros((TILE, TILE), F32)
             if b % 16 == 15:
-                total = sums_ref[h, 0 if b == 15 else 4]
+                tile = sums_ref[h, 0 if b == 15 else 4]
             for t, mask in masks.items():
-                total = total + jnp.where(mask, sums_ref[h, t], 0.0)
-            bucket_ref[h, pl.ds(b, 1), :] = jnp.sum(total, axis=0, keepdims=True)
-
-
-def attend_back(place, q, kv, other, grads, ctx, prob, b):
-    rows = q.shape[1]
-    return pl.pallas_call(
-        functools.partial(attend_back_kernel, b),
-        in_specs=[in_smem] + [in_vmem] * 6,
-        out_specs=[in_vmem] * 4,
-        out_shape=[
-            shape_of((rows, WIDTH), BF),
-            shape_of((rows, 2 * WIDTH), F32),
-            shape_of((rows, 2 * WIDTH), BF),
-            shape_of((GROUP, NB, TILE), F32),
-        ],
+                tile = tile + jnp.where(mask, sums_ref[h, t], 0.0)
+            bucket_ref[h, pl.ds(b, 1), :] = jnp.sum(tile, axis=0, keepdims=True)
+
+
+def attend_back(place, q, kv, grads, ctx, prob, r):
+    rows = grads.shape[0]
+    return pl.pallas_call(
+        functools.partial(attend_back_kernel, r // 2),
+        in_specs=[in_smem] + [in_vmem] * 8,
+        out_specs=[in_vmem] * 2,
+        out_shape=[shape_of((rows, 3 * WIDTH), BF), shape_of((GROUP, NB, TILE), F32)],
         scratch_shapes=[
-            pltpu.VMEM((rows, 2 * rows), BF),
+            pltpu.VMEM((GROUP, rows, rows), BF),
             pltpu.VMEM((GROUP, 5, TILE, TILE), F32),
         ],
-        compiler_params=params(8),
-        cost_estimate=cost(GROUP * rows * 2 * rows * 256 * 12, 8e6),
+        compiler_params=params(22),
+        cost_estimate=cost(1, 1),
         name="attend_back",
-    )(place, q, kv, other, grads, ctx, prob)
-
-
-def project_back_kernel(indices, first, place_ref, nt_ref, low_t_ref, ctx_ref, dq_ref, own_ref, came_ref, *refs):
-    if not first:
-        acc_in, refs = refs[0], refs[1:]
-    n_parts = len(indices)
-    w_refs, (acc_ref, grads_ref, whole, grad) = refs[:n_parts], refs[n_parts:]
-    w_refs = pick(w_refs, indices)
-    assemble(whole, w_refs, place_ref)
-    dkv = (own_ref[...] + came_ref[...].astype(F32)).astype(BF)
-    heads = jnp.concatenate([dq_ref[...], dkv], 1)
-    out = dot(nt_ref[...], heads, NN).astype(BF)
-    last = dot(low_t_ref[...], ctx_ref[...], NN).astype(BF)
-    grad[...] = jnp.concatenate([out, last], 1)
-    deal_out(grads_ref, grad, place_ref)
-    total = dot(heads, whole[:, 0:576], NT)
-    acc_ref[...] = total if first else acc_in[...] + total
-
-
-def project_back(place, normed_t, low_t, acc, ctx, dq, own, came, block, grads):
-    rows = normed_t.shape[1]
-    block, indices = block
-    n = len(block)
-    first = acc is None
+    )(place, *q, *kv, grads, *ctx, prob)
+
+
+def project_back_kernel(indices, split, place_ref, nt_own_ref, nt_other_ref, low_t_ref, *refs):
+    n_parts = len(indices[0])
+    heads_refs, ctx_refs, refs = refs[:2], refs[2:6], refs[6:]
+    w_refs, refs = refs[: 2 * n_parts], refs[2 * n_parts :]
+    own_ref, send_ref, out_refs, (whole, grad) = refs[0], refs[1], refs[2:-2], refs[-2:]
+    half = nt_own_ref.shape[1]
+    totals = [None, None]
+    for b in range(2):
+        part = pick(w_refs[b * n_parts : (b + 1) * n_parts], indices[b])
+        assemble(whole.at[b], part, place_ref)
+        ends = [heads_refs[b][pl.ds(i * half, half), :] for i in range(2)]
+        out = dot(nt_own_ref[...], ends[0], NN) + dot(nt_other_ref[...], ends[1], NN)
+        context = jnp.concatenate([ctx_refs[2 * b][...], ctx_refs[2 * b + 1][...]], 0)
+        last = dot(low_t_ref[...], context, NN)[:, 64:]
+        grad[b] = jnp.concatenate([out.astype(BF), last.astype(BF)], 1)
+        if split:
+            near_ref, far_refs = out_refs[b], out_refs[2:4]
+            cut = near_ref.shape[1]
+            for count in range(4 * cut):
+                y, z = count // (2 * cut), count % (2 * cut)
+                start = pl.multiple_of(place_ref[5 + count], 16)
+                piece = grad[b, pl.ds(start, near_ref.shape[3]), :]
+                if z < cut:
+                    near_ref[y, z, 0] = piece
+                else:
+                    far_refs[y][b, z - cut, 0] = piece
+        else:
+            out_refs[b][0, 0, 0, 0] = grad[b]
+        for i in range(2):
+            term = dot(ends[i], whole[b, :, 0:576], NT)
+            totals[i] = term if b == 0 else totals[i] + term
+    own_ref[...], send_ref[...] = totals
+
+
+def project_back(place, normed_t, low_t, heads, ctx, blocks, depth, shard_rows):
+    half = normed_t[0].shape[1]
+    n = len(blocks[0][0])
+    split = shard_rows % 16 == 0
+    if split:
+        shapes = [shape_of((2, depth // 2, 1, shard_rows, D), BF)] * 4
+    else:
+        shapes = [grads_shape(depth, 1, shard_rows, D)] * 2
     outs = pl.pallas_call(
-        functools.partial(project_back_kernel, indices, first),
-        in_specs=[in_smem] + [in_vmem] * (6 + n + (0 if first else 1)),
-        out_specs=[in_vmem] * 2,
-        out_shape=[shape_of((rows, D), F32), grads],
-        scratch_shapes=[pltpu.VMEM((D, D), BF)] * 2,
-        input_output_aliases={} if first else {7: 0},
-        compiler_params=params(8),
-        cost_estimate=cost(2 * 2 * rows * D * D, 8e6),
+        functools.partial(project_back_kernel, [i for _, i in blocks], split),
+        in_specs=[in_smem] + [in_vmem] * (9 + 2 * n),
+        out_specs=[in_vmem] * (2 + len(shapes)),
+        out_shape=[shape_of((half, D), F32)] * 2 + shapes,
+        scratch_shapes=[pltpu.VMEM((2, D, D), BF)] * 2,
+        compiler_params=params(16),
+        cost_estimate=cost(1, 1),
         name="project_back",
-    )(place, normed_t, low_t, ctx, dq, own, came, *([] if first else [acc]), *block)
-    return outs
+    )(place, *normed_t, low_t, *heads, *ctx, *blocks[0][0], *blocks[1][0])
+    if split:
+        return outs
+    both = [by_place(v, depth, shard_rows) for v in outs[2:]]
+    fars = [jnp.stack([v[y, 1] for v in both]) for y in range(2)]
+    return [outs[0], outs[1], both[0][:, 0], both[1][:, 0], *fars]
 
 
 def add(a, b):
@@ -740,21 +799,18 @@
     )(parts)
 
 
-def cast_ffn_kernel(w_ref, both_ref, wi_ref, wf_ref):
-    low = w_ref[...].astype(BF)
-    both_ref[...] = low
-    wi_ref[...], wf_ref[...] = low[0:1], low[1:2]
+def cast_ffn_kernel(w_ref, out_ref):
+    out_ref[...] = w_ref[...].astype(BF)
 
 
 def cast_ffn(weights):
-    one = shape_of((1,) + weights.shape[1:], BF)
     return pl.pallas_call(
         cast_ffn_kernel,
         in_specs=[in_vmem],
-        out_specs=[in_vmem] * 3,
-        out_shape=[shape_of(weights.shape, BF), one, one],
+        out_specs=in_vmem,
+        out_shape=shape_of(weights.shape, BF),
         compiler_params=params(MERGE_MIB),
-        cost_estimate=pl.CostEstimate(flops=10**12, bytes_accessed=10**9, transcendentals=0),
+        cost_estimate=cost(1, 1),
         name="cast_ffn",
     )(weights)
 
@@ -803,8 +859,9 @@
     )(place, *keep, came)
 
 
-def finish_kernel(x_ref, gain_ref, t_ref, mid_grad_ref, out_send_ref, keep_ref, send_ref, gain_grad_ref):
-    grad, gain_grad = rms_back(x_ref[...].astype(F32), gain_ref[0:1].astype(F32), t_ref[...])
+def finish_kernel(x_ref, gain_ref, t_ref, t_came_ref, mid_grad_ref, out_send_ref, keep_ref, send_ref, gain_grad_ref):
+    t = t_ref[...] + t_came_ref[...]
+    grad, gain_grad = rms_back(x_ref[...].astype(F32), gain_ref[0:1].astype(F32), t)
     out = (mid_grad_ref[...] + grad).astype(BF)
     half = keep_ref.shape[0]
     keep_ref[...] = out[:half]
@@ -812,39 +869,42 @@
     gain_grad_ref[...] = gain_grad
 
 
-def finish(rows_in, gain_low, t_acc, mid_grad, out_send):
+def finish(rows_in, gain_low, t_own, t_came, mid_grad, out_send):
     part = out_send.shape
     return pl.pallas_call(
         finish_kernel,
-        in_specs=[in_vmem] * 5,
+        in_specs=[in_vmem] * 6,
         out_specs=[in_vmem] * 3,
         out_shape=[shape_of(part, BF), shape_of((2,) + part, BF), shape_of((1, D), F32)],
         compiler_params=params(12),
         cost_estimate=cost(1, 1),
         name="finish",
-    )(rows_in, gain_low, t_acc, mid_grad, out_send)
+    )(rows_in, gain_low, t_own, t_came, mid_grad, out_send)
 
 
 def small_kernel(place_ref, one_ref, two_ref, *refs):
     out_ref = refs[-1]
-    out_ref[...] = jnp.zeros_like(out_ref)
-    out_ref[0:1], out_ref[1:2] = one_ref[...], two_ref[...]
+    out_ref[15:16] = jnp.zeros((1, TILE), F32)
+    for i in range(D // TILE):
+        out_ref[i : i + 1] = one_ref[:, i * TILE : (i + 1) * TILE]
+        out_ref[6 + i : 7 + i] = two_ref[:, i * TILE : (i + 1) * TILE]
     heads = []
     for m in range(4):
         for h in range(GROUP):
             lines = jnp.zeros((NB, TILE), F32)
-            for r in range(4):
-                lines = jnp.where((place_ref[2] ^ r) == m, refs[r][h], lines)
+            for r in (0, 2):
+                lines = jnp.where((place_ref[2] ^ r) == m, refs[r // 2][h], lines)
             heads.append(jnp.sum(lines.T, axis=0, keepdims=True))
-    out_ref[2:3, 0 : H * NB] = jnp.concatenate(heads, 1)
+    for i in range(3):
+        out_ref[12 + i : 13 + i] = jnp.concatenate(heads[4 * i : 4 * i + 4], 1)
 
 
 def small_sums(place, gain_one, gain_two, lines):
     return pl.pallas_call(
         small_kernel,
-        in_specs=[in_smem] + [in_vmem] * 6,
+        in_specs=[in_smem] + [in_vmem] * 4,
         out_specs=in_vmem,
-        out_shape=shape_of((4, D), F32),
+        out_shape=shape_of((16, TILE), F32),
         compiler_params=params(MERGE_MIB),
         cost_estimate=cost(1, 1),
         name="small_sums",
@@ -857,9 +917,8 @@
     for ref in refs[:-4]:
         total = total + ref[...].astype(F32)
     out_ref[...] = total
-    sums_ref[0:3] = small_ref[0:3]
-    squares = squares_ref[0:1, 0:1] + jnp.sum(total * total)
-    sums_ref[3:4] = jnp.broadcast_to(squares, (1, D))
+    sums_ref[0:15] = small_ref[0:15]
+    sums_ref[15:16] = squares_ref[...] + jnp.sum(total * total)
 
 
 def total_with(own, came, squares, small):
@@ -880,16 +939,20 @@
     for c in copies:
         c.start()
     small = jnp.sum(small_ref[...], axis=0)
-    sums = small[0:3]
+    sums = small[0:15]
     squares = jnp.sum(jnp.sum(sums * sums, axis=0, keepdims=True), axis=1, keepdims=True)
-    norm = jnp.sqrt(small[3:4, 0:1] + squares)
+    norm = jnp.sqrt(small[15:16, 0:1] + squares)
     outs[0][...] = norm
     clip = jnp.minimum(1.0, clip_level / (norm + 1e-06))
     count = outs[2].shape[1]
+    wide = jnp.concatenate(
+        [jnp.concatenate([small[g + i : g + i + 1] for i in range(6)], 1) for g in (0, 6)], 0
+    )
     gains = jnp.zeros((2, count), F32)
     for d in range(D // count):
-        gains = jnp.where(place_ref[0] == d, small[0:2, d * count : (d + 1) * count], gains)
-    table = jnp.concatenate([small[2:3, h * NB : (h + 1) * NB] for h in range(H)], 0)
+        gains = jnp.where(place_ref[0] == d, wide[:, d * count : (d + 1) * count], gains)
+    heads = [(12 + h // 4, h % 4 * NB) for h in range(H)]
+    table = jnp.concatenate([small[i : i + 1, j : j + NB] for i, j in heads], 0)
     outs[2][...], outs[3][...] = gains, table
     grads = (None, ffn_ref[...], gains, table)
     settings = [(rate_matrix, matrix_decay)] * 2 + [(rate_small, 0.0)] * 2
@@ -953,80 +1016,72 @@
     starts = [
         shard_rows * (((dp // 2) ^ s) * 2 + ((dp % 2) ^ y)) for y in range(2) for s in range(depth)
     ]
+    starts += [
+        shard_rows * (((dp // 2 - s) % depth) * 2 + ((dp % 2) ^ y))
+        for y in range(2)
+        for s in range(depth)
+    ]
     if shard_rows % 16:
-        starts = [jnp.zeros((), jnp.int32)]
+        starts = [jnp.zeros((), jnp.int32)] * 2
     place = jnp.stack([v.astype(jnp.int32) for v in [x, core, mp, lengths[0], lengths[1]] + starts])
     cut = depth // 2
     feed_shape = grads_shape(depth, 2, shard_rows, D)
-    attn_shape = grads_shape(depth, 1, shard_rows, D)
 
     attn_low = cast_attn(attn_weights)
     attn_z = [swap_z(attn_low, k) for k in range(1, depth)]
     rows_came = swap_x(sort_rows(place, inputs, cotangent))
-    ffn_low, wi_low, wf_low = cast_ffn(ffn_weights)
+    ffn_low = cast_ffn(ffn_weights)
     bias = make_bias(place, bias_table)
-    attn_low, attn_z, ffn_low, wi_low, wf_low, place, bias = fence(
-        attn_low, attn_z, ffn_low, wi_low, wf_low, place, bias
-    )
+    attn_low, attn_z, ffn_low, place, bias = fence(attn_low, attn_z, ffn_low, place, bias)
 
     lined = [attn_low] + attn_z
     near, far = line_up(lined[:cut], cut), line_up(lined[cut:], cut)
     near_x, far_y = swap_x(near), swap_y(far)
-    wi_far_z = [swap_z(wi_low, k) for k in range(cut, depth)]
-    near, far, near_x, far_y, rows_came, ffn_low, wf_low, wi_far_z = fence(
-        near, far, near_x, far_y, rows_came, ffn_low, wf_low, wi_far_z
-    )
+    ring = [ffn_low, shift_z(ffn_low)]
+    near, far, near_x, far_y, rows_came, ring = fence(near, far, near_x, far_y, rows_came, ring)
     near, far = line_up([near, near_x], 2), line_up([far, far_y], 2)
     near_y, far_x = swap_y(near), swap_x(far)
-    ffn_near_z = [swap_z(ffn_low, k) for k in range(1, cut)]
-    wf_far_z = [swap_z(wf_low, k) for k in range(cut, depth)]
+    ring.append(shift_z(ring[-1]))
     rows_in, back = join_rows(place, inputs, cotangent, rows_came)
-    rows_in, back, gain_low = fence(rows_in, back, norm_gains)
+    rows_in, back, gain_low, ring, near, far = fence(rows_in, back, norm_gains, ring, near, far)
+    while len(ring) < depth:
+        ring.append(shift_z(ring[-1]))
     gains = join_gains(gather_gains(gain_low))
-    near_y, far_x, near, far, rows_in, back, gains, ffn_near_z, wf_far_z = fence(
-        near_y, far_x, near, far, rows_in, back, gains, ffn_near_z, wf_far_z
+    near_y, far_x, near, far, rows_in, back, gains, ring = fence(
+        near_y, far_x, near, far, rows_in, back, gains, ring
     )
 
     def attn_block(near, far, near_y, far_x, i):
         here = far if i == 0 else far_x
         return block_views([[(near, i), (here, 0)], [(near_y, i), (here, 1)]])
 
-    attn_blocks = {2 * i: attn_block(near, far, near_y, far_x, i) for i in range(2)}
-    near_c, far_c, near_yc, far_xc = [swap_core(v) for v in (near, far, near_y, far_x)]
-    q, kv, other = {}, {}, {}
-    q[0], kv[0], normed_t = project(place, rows_in, gains, [attn_blocks[0], attn_blocks[2]], True)
-    q, kv, normed_t = fence(q, kv, normed_t)
-    other[1] = swap_core(kv[0])
-    ffn_near = line_up([ffn_low] + ffn_near_z, cut)
-    ffn_far = line_up([v for pair in zip(wi_far_z, wf_far_z) for v in pair], cut)
-    ffn_here = line_up([ffn_near, ffn_far], 2)
+    mine = [attn_block(near, far, near_y, far_x, i) for i in range(2)]
+    rows_other = swap_core(rows_in)
+    ffn_here = line_up([line_up(ring[:cut], cut), line_up(ring[cut:], cut)], 2)
     ffn_x, ffn_y = swap_x(ffn_here), swap_y(ffn_here)
-    q, kv, near_c, far_c, near_yc, far_xc, ffn_here = fence(
-        q, kv, near_c, far_c, near_yc, far_xc, ffn_here
+    q_own, kv_own, normed_t = project(place, rows_in, gains, mine, True)
+    q_own, kv_own, normed_t, ffn_here = fence(q_own, kv_own, normed_t, ffn_here)
+    q_own, rows_other = fence(q_own, rows_other)
+    q_other, kv_other, other_t = project(place, rows_other, gains, mine, True)
+    q, kv, normed_t, near, far, near_y, far_x = fence(
+        [q_own, q_other], [kv_own, kv_other], [normed_t, other_t], near, far, near_y, far_x
     )
-    for i in range(2):
-        attn_blocks[2 * i + 1] = attn_block(near_c, far_c, near_yc, far_xc, i)
-    q[1], kv[1] = project(place, rows_in, gains, [attn_blocks[1], attn_blocks[3]], False)
-    q, kv, other = fence(q, kv, other)
-    other[0] = swap_core(kv[1])
-
-    ctx, prob = {}, {}
-
-    def attend_at(r):
-        ctx[r], prob[r] = attend(place, q[r % 2], kv[r % 2], other[r % 2], bias, r // 2, r)
-
-    attend_at(1)
-    ctx, prob, q = fence(ctx, prob, q)
-    attend_at(3)
-    ctx, prob, q = fence(ctx, prob, q)
-    q, other, ffn_here = fence(q, other, ffn_here)
+    across = [swap_core(v) for v in (near, far, near_y, far_x)]
+    ctx, ctx_send, ctx_came, prob = {}, {}, {}, {}
+    for r in (0, 2):
+        ctx[r], ctx_send[r], prob[r] = attend(place, q, kv, bias, r)
+        ctx, ctx_send, prob, q, ffn_here = fence(ctx, ctx_send, prob, q, ffn_here)
+        ctx_came[r] = swap_core(ctx_send[r])
     ffn_c = swap_core(ffn_here)
-    attend_at(0)
-    ctx, prob, q = fence(ctx, prob, q)
-    attend_at(2)
-    ctx, prob = fence(ctx, prob)
+    ctx, ctx_came, across = fence(ctx, ctx_came, across)
+    theirs = [attn_block(*across, i) for i in range(2)]
     mid, normed_two, normed_two_t, back_t = middle(
-        place, rows_in, gains, back, [ctx[r] for r in range(4)], [attn_blocks[r] for r in range(4)]
+        place,
+        rows_in,
+        gains,
+        back,
+        [ctx[0], ctx_came[0], ctx[2], ctx_came[2]],
+        [mine[0], theirs[0], mine[1], theirs[1]],
     )
     mid, normed_two, normed_two_t, back_t = fence(mid, normed_two, normed_two_t, back_t)
     mid, ffn_x, ffn_y = fence(mid, ffn_x, ffn_y)
@@ -1036,7 +1091,7 @@
 
     def feed_at(r, sums, by_y):
         sums, out = feed(
-            place, normed_two, normed_two_t, back, back_t, sums, block_views(by_y), feed_shape
+            place, normed_two, normed_two_t, back, back_t, sums, block_views(by_y, True), feed_shape
         )
         grads[r] = by_place(out, depth, shard_rows)
         return sums
@@ -1054,55 +1109,46 @@
     sums = feed_at(3, sums, [[(ffn_xc, 0), (ffn_xc, 1)], [ffn_near_xyc, ffn_far_xyc]])
     sums, grads = fence(sums, grads)
     came[2] = swap_core(grads[3])
-    out_keep, out_send, mid_grad, mid_low_t, gain_two_grad, *cg = turn(
-        place, mid, sums[0], sums[1], back, gains, [attn_blocks[r] for r in range(4)]
-    )
-    cg, mid_grad, mid_low_t, out_keep, out_send = fence(cg, mid_grad, mid_low_t, out_keep, out_send)
-    cg, came, grads = fence(cg, came, grads)
+    out_keep, out_send, mid_grad, mid_low, gain_two_grad = turn(mid, sums[0], sums[1], back, gains)
+    mid_grad, mid_low, out_keep, out_send = fence(mid_grad, mid_low, out_keep, out_send)
+    low_other = swap_core(mid_low)
+    mid_low, low_other = fence(mid_low, low_other)
+    cg0, cg2, low_t = context_grads(place, mid_low, low_other, mine)
+    cg0, cg2, low_t = fence(cg0, cg2, low_t)
+    cg0, came, grads = fence(cg0, came, grads)
     near0, near1, far0, far1 = merge_core(grads[0], came[0], grads[2], came[2])
     near1_x, far1_y = swap_x(near1), swap_y(far1)
-    cg, near0, far0 = fence(cg, near0, far0)
-
-    dq, own, send, tiles, got = {}, {}, {}, {}, {}
-    attn_grads = {}
-
-    def attend_back_at(r):
-        c = r % 2
-        dq[r], own[r], send[r], tiles[r] = attend_back(
-            place, q[c], kv[c], other[c], cg[r], ctx[r], prob[r], r // 2
-        )
-
-    def project_back_at(r, total):
-        total, outs = project_back(
-            place, normed_t, mid_low_t, total, ctx[r], dq[r], own[r], got[r], attn_blocks[r], attn_shape
-        )
-        attn_grads[r] = by_place(outs, depth, shard_rows)
-        return total
-
-    for r in (3, 1, 2, 0):
-        attend_back_at(r)
-        dq, own, send, tiles, cg = fence(dq, own, send, tiles, cg)
-        got[r ^ 1] = swap_core(send[r])
-    cg, near1_x, far1_y, got, out_send = fence(cg, near1_x, far1_y, got, out_send)
+    cg0, near0, far0 = fence(cg0, near0, far0)
+
+    heads, lines = {}, {}
+    for r, cg in ((0, cg0), (2, cg2)):
+        cg, heads = fence(cg, heads)
+        heads[r], lines[r] = attend_back(place, q, kv, cg, (ctx[r], ctx_send[r]), prob[r], r)
+        heads, lines = fence(heads, lines)
+    heads, near1_x, far1_y, out_send = fence(heads, near1_x, far1_y, out_send)
     ffn_y0, ffn_y1, ffn_x0, ffn_x1 = merge_half(near0, near1_x, far0, far1_y)
     ffn_y1, ffn_x1 = swap_y(ffn_y1), swap_x(ffn_x1)
-    got, ffn_y0, ffn_x0 = fence(got, ffn_y0, ffn_x0)
-    t_one = None
-    came = {}
-    for r in (3, 1, 2, 0):
-        t_one = project_back_at(r, t_one)
-        t_one, attn_grads = fence(t_one, attn_grads)
-        if r % 2:
-            came[r - 1] = swap_core(attn_grads[r])
-    t_one, attn_grads, came = fence(t_one, attn_grads, came)
-    near0, near1, far0, far1 = merge_core(attn_grads[0], came[0], attn_grads[2], came[2])
+    heads, ffn_y0, ffn_x0 = fence(heads, ffn_y0, ffn_x0)
+    t_own, t_send, near0, near1, far0, far1 = project_back(
+        place,
+        normed_t,
+        low_t,
+        [heads[0], heads[2]],
+        [ctx[0], ctx_send[0], ctx[2], ctx_send[2]],
+        mine,
+        depth,
+        shard_rows,
+    )
+    t_own, t_send, near0, near1, far0, far1 = fence(t_own, t_send, near0, near1, far0, far1)
     near1_x, far1_y = swap_x(near1), swap_y(far1)
-    near0, far0, ffn_y1, ffn_x1 = fence(near0, far0, ffn_y1, ffn_x1)
+    t_own, t_send, ffn_y1, ffn_x1 = fence(t_own, t_send, ffn_y1, ffn_x1)
     ffn_own, *ffn_far_own = merge_last(ffn_y0, ffn_y1, ffn_x0, ffn_x1)
     soon = [k for k in range(1, depth) if k != cut]
     ffn_back = [swap_z(ffn_far_own[k - 1], k) for k in soon]
-    in_keep, send_last, gain_one_grad = finish(rows_in, gains, t_one, mid_grad, out_send)
-    small = small_sums(place, gain_one_grad, gain_two_grad, [tiles[r] for r in range(4)])
+    t_came = swap_core(t_send)
+    ffn_own, ffn_far_own, t_came = fence(ffn_own, ffn_far_own, t_came)
+    in_keep, send_last, gain_one_grad = finish(rows_in, gains, t_own, t_came, mid_grad, out_send)
+    small = small_sums(place, gain_one_grad, gain_two_grad, [lines[0], lines[2]])
     in_keep, send_last, small, ffn_own, near0, far0, ffn_far_own = fence(
         in_keep, send_last, small, ffn_own, near0, far0, ffn_far_own
     )

time: 253 us -> 247 us (0.976)
  waiting for transfers between devices: 71.4 us -> 95.5 us
  Pallas kernels: 110 us -> 94.9 us
  starting transfers between devices: 52.8 us -> 38.8 us
    ppermute x10, waiting for transfers between devices: 2.89 us -> 20.1 us  [swap_x(): return lax.ppermute(v, 'mp', [(i, i ^ 2) for i in range(4)])]
    ppermute x8, waiting for transfers between devices: 9.75 us -> 24.9 us  [swap_y(): return lax.ppermute(v, 'dp', [(i, i ^ 1) for i in range(n)])]
    ppermute x14 -> x9, starting transfers between devices: 25.6 us -> 11.6 us  [swap_z(): return lax.ppermute(v, 'dp', [(i, i ^ 2 * k) for i in range(n)])]
    ppermute x14 -> x9, waiting for transfers between devices: 37.9 us -> 24.4 us  [swap_z(): return lax.ppermute(v, 'dp', [(i, i ^ 2 * k) for i in range(n)])]
    pallas_call x16 -> x10, Pallas kernels: 61.1 us -> 50.5 us  [the longest x2 23.1 us: attend_back(): pl.pallas_call(functools.partial(attend_back_kernel, r // 2), in_specs=[i...]
    ppermute x0 -> x3, waiting for transfers between devices: none -> 6.66 us  [shift_z(): return lax.ppermute(v, 'dp', [(i, (i + 2) % n) for i in range(n)])]
    all_to_all x1, waiting for transfers between devices: 11.4 us -> 8.81 us  [from_all(): lax.all_to_all(jnp.broadcast_to(v[None], (n,) + v.shape), ('dp', 'mp'), 0...]
    ppermute x19 -> x16, waiting for transfers between devices: 9.43 us -> 10.5 us  [swap_core(): return lax.ppermute(v, 'mp', [(i, i ^ 1) for i in range(4)])]
  transfers between devices with their start and end apart: 52 -> 47, of which waited for: 21 -> 28; matrix products, arithmetic and copies ran while one was open for 0% -> 0% of each run, Pallas kernels for 37% -> 33%
where the time goes in v5:
time: 247 us; the launch traced here: 244 us
  waiting for transfers between devices  95.5 us (39%)
  Pallas kernels  94.9 us (38%)
  starting transfers between devices  38.8 us (16%)
  blocking collectives  11.4 us (5%)
    ppermute x8, waiting for transfers between devices, swap_y(): return lax.ppermute(v, 'dp', [(i, i ^ 1) for i in range(n)])  24.9 us
    ppermute x9, waiting for transfers between devices, swap_z(): return lax.ppermute(v, 'dp', [(i, i ^ 2 * k) for i in range(n)])  24.4 us
    pallas_call x2, Pallas kernels, attend_back(): pl.pallas_call(functools.partial(attend_back_kernel, r // 2), in_specs=[i...  23.1 us
    ppermute x10, waiting for transfers between devices, swap_x(): return lax.ppermute(v, 'mp', [(i, i ^ 2) for i in range(4)])  20.1 us
    pallas_call x4, Pallas kernels, feed(): pl.pallas_call(functools.partial(feed_kernel, indices, first), in_specs=[...  19.2 us
    pallas_call x2, Pallas kernels, attend(): pl.pallas_call(functools.partial(attend_kernel, r // 2, r), in_specs=[in_...  16.2 us
    ppermute x10, starting transfers between devices, swap_x(): return lax.ppermute(v, 'mp', [(i, i ^ 2) for i in range(4)])  12.9 us
    ppermute x9, starting transfers between devices, swap_z(): return lax.ppermute(v, 'dp', [(i, i ^ 2 * k) for i in range(n)])  11.6 us
  transfers between devices with their start and end apart: 47, of which 28 were waited for; matrix products, arithmetic and copies ran while one was open for 0% of the time, Pallas kernels for 33%

profile of v5, /device:TPU:0, one launch (start us, length us, event | category | flops | bytes accessed | tf_op | source)
XLA Modules:
  0.0 243.7 jit_solution(12468265364302067408)
XLA Ops:
  1.6 1.7 sort_rows.1
  3.3 3.0 %collective-permute-start.5 = (bf16[2,256,768]{2,1,0:T(8,128)(2,1)S(1)}, bf16[2,256,768]{2,1,0:T(8,128)(2,1)S(1)}, u32[]{:S(2)}, u32[]{:S(2)}) collective-permute-start(bf16[2,256,768]{2,1,0:T(8,128)(2,1)S(1)} %sort_rows.1), channel_id=1, source_target_pairs={{0,2},{1,3},{2,0},{3,1},{4,6},{5,7},{6,4},{7,5},{8,10},{9,11},{10,... | collective-permute-start | bytes 2359304 | tf_op jit(solution)/shard_map/ppermute | solution.py:84
  6.4 3.7 %collective-permute-start.2 = (bf16[1,96,768]{2,1,0:T(8,128)(2,1)S(1)}, bf16[1,96,768]{2,1,0:T(8,128)(2,1)S(1)}, u32[]{:S(2)}, u32[]{:S(2)}) collective-permute-start(bf16[1,96,768]{2,1,0:T(8,128)(2,1)S(1)} %cast_attn.1.refs_0_), channel_id=1, source_target_pairs={{0,24},{4,28},{8,16},{12,20},{16,8},{20,12},{24,0},{28,4},{1,25},{... | collective-permute-start | bytes 442376 | tf_op jit(solution)/shard_map/ppermute | solution.py:94
  10.9 5.2 %bias_tiles.1.bias_ref = f32[4,3,5,128,128]{4,3,2,1,0:T(8,128)S(1)} custom-call(s32[21]{0:T(128)S(1)} %stack.79.place_ref, f32[12,32]{1,0:T(8,128)S(1)} %copy-done.3), custom_call_target="tpu_custom_call" | custom-call | flops 1000 | bytes 1000 | tf_op jit(solution)/shard_map/bias_tiles/pallas_call | solution.py:193
  16.1 6.1 %collective-permute-done.1.refs_0_ = bf16[1,96,768]{2,1,0:T(8,128)(2,1)S(1)} collective-permute-done((bf16[1,96,768]{2,1,0:T(8,128)(2,1)S(1)}, bf16[1,96,768]{2,1,0:T(8,128)(2,1)S(1)}, u32[]{:S(2)}, u32[]{:S(2)}) %collective-permute-start.1) | collective-permute-done | bytes 147488 | tf_op jit(solution)/shard_map/ppermute | solution.py:94
  22.3 1.6 collective-permute-start.4
  24.5 5.9 %collective-permute-done.4.refs_1_ = bf16[2,1,96,768]{3,2,1,0:T(8,128)(2,1)S(1)} collective-permute-done((bf16[2,1,96,768]{3,2,1,0:T(8,128)(2,1)S(1)}, bf16[2,1,96,768]{3,2,1,0:T(8,128)(2,1)S(1)}, u32[]{:S(2)}, u32[]{:S(2)}) %collective-permute-start.4) | collective-permute-done | bytes 294944 | tf_op jit(solution)/shard_map/ppermute | solution.py:89
  31.7 2.1 collective-permute-done.6.refs_1_
  33.9 1.6 collective-permute-start.8
  36.0 1.7 join_rows.1
  37.7 4.6 %collective-permute-done.9.refs_0_ = bf16[2,96,768]{2,1,0:T(8,128)(2,1)S(1)} collective-permute-done((bf16[2,96,768]{2,1,0:T(8,128)(2,1)S(1)}, bf16[2,96,768]{2,1,0:T(8,128)(2,1)S(1)}, u32[]{:S(2)}, u32[]{:S(2)}) %collective-permute-start.9) | collective-permute-done | bytes 294944 | tf_op jit(solution)/shard_map/ppermute | solution.py:99
  42.3 11.4 %all_to_all.10.g_ref = bf16[8,2,96]{2,1,0:T(2,128)(2,1)S(1)} all-to-all(bf16[8,2,96]{2,1,0:T(2,128)(2,1)S(1)} %broadcast_in_dim.4), channel_id=1, replica_groups=mesh['dp'=8,'mp'=4] {'dp'}, dimensions={0} | all-to-all | bytes 6144 | tf_op jit(solution)/shard_map/all_to_all | solution.py:114
  54.1 2.2 project.2
  56.3 2.2 project.3
  59.7 1.5 collective-permute-start.18
  61.2 8.0 %attend.2 = (bf16[512,256]{1,0:T(8,128)(2,1)S(1)}, bf16[512,256]{1,0:T(8,128)(2,1)S(1)}, bf16[3,1024,1024]{2,1,0:T(8,128)(2,1)}) custom-call(s32[21]{0:T(128)S(1)} %stack.79.place_ref, bf16[2,512,192]{2,1,0:T(8,128)(2,1)S(1)} %get-tuple-element.425.q_own_ref, bf16[2,512,192]{2,1,0:T(8,128)(2,1)S(1)} %get-tuple-element.426.q_other_ref, ...), custom_call_target="tpu_custom_call" | custom-call | flops 1000 | bytes 1000 | tf_op jit(solution)/shard_map/attend/pallas_call | solution.py:326
  69.2 8.3 %attend.3 = (bf16[512,256]{1,0:T(8,128)(2,1)S(1)}, bf16[512,256]{1,0:T(8,128)(2,1)S(1)}, bf16[3,1024,1024]{2,1,0:T(8,128)(2,1)}) custom-call(s32[21]{0:T(128)S(1)} %stack.79.place_ref, bf16[2,512,192]{2,1,0:T(8,128)(2,1)S(1)} %get-tuple-element.425.q_own_ref, bf16[2,512,192]{2,1,0:T(8,128)(2,1)S(1)} %get-tuple-element.426.q_other_ref, ...), custom_call_target="tpu_custom_call" | custom-call | flops 1000 | bytes 1000 | tf_op jit(solution)/shard_map/attend/pallas_call | solution.py:326
  82.1 2.1 middle.1
  84.2 2.9 %collective-permute-done.19.refs_2_.refs_3_ = bf16[2,2,2,96,768]{4,3,2,1,0:T(8,128)(2,1)S(1)} collective-permute-done((bf16[2,2,2,96,768]{4,3,2,1,0:T(8,128)(2,1)S(1)}, bf16[2,2,2,96,768]{4,3,2,1,0:T(8,128)(2,1)S(1)}, u32[]{:S(2)}, u32[]{:S(2)}) %collective-permute-start.19) | collective-permute-done | bytes 1179680 | tf_op jit(solution)/shard_map/ppermute | solution.py:89
  88.0 1.5 collective-permute-start.23
  89.5 1.5 collective-permute-start.24
  91.0 4.6 %feed.4 = (f32[512,768]{1,0:T(8,128)S(1)}, f32[512,768]{1,0:T(8,128)S(1)}, bf16[2,2,2,2,96,768]{5,4,3,2,1,0:T(8,128)(2,1)S(1)}) custom-call(s32[21]{0:T(128)S(1)} %stack.79.place_ref, bf16[512,768]{1,0:T(8,128)(2,1)S(1)} %get-tuple-element.367.n_ref, bf16[768,512]{1,0:T(8,128)(2,1)S(1)} %get-tuple-element.368.nt_ref, ...), custom_call_target="tpu_custom_call" | custom-call | flops 1000 | bytes 1000 | tf_op jit(solution)/shard_map/feed/pallas_call | solution.py:409
  95.7 4.8 %feed.5 = (f32[512,768]{1,0:T(8,128)S(1)}, f32[512,768]{1,0:T(8,128)S(1)}, bf16[2,2,2,2,96,768]{5,4,3,2,1,0:T(8,128)(2,1)S(1)}) custom-call(s32[21]{0:T(128)S(1)} %stack.79.place_ref, bf16[512,768]{1,0:T(8,128)(2,1)S(1)} %get-tuple-element.367.n_ref, bf16[768,512]{1,0:T(8,128)(2,1)S(1)} %get-tuple-element.368.nt_ref, ...), custom_call_target="tpu_custom_call", output_to_operand_aliasing={{0}: (5, {}), {1}: (6, {})} | custom-call | flops 1000 | bytes 1000 | tf_op jit(solution)/shard_map/feed/pallas_call | solution.py:409
  100.4 2.8 %collective-permute-done.23.refs_4_ = bf16[2,2,96,768]{3,2,1,0:T(8,128)(2,1)S(1)} collective-permute-done((bf16[2,2,96,768]{3,2,1,0:T(8,128)(2,1)S(1)}, bf16[2,2,96,768]{3,2,1,0:T(8,128)(2,1)S(1)}, u32[]{:S(2)}, u32[]{:S(2)}) %collective-permute-start.23) | collective-permute-done | bytes 589856 | tf_op jit(solution)/shard_map/ppermute | solution.py:89
  105.0 5.0 %feed.6 = (f32[512,768]{1,0:T(8,128)S(1)}, f32[512,768]{1,0:T(8,128)S(1)}, bf16[2,2,2,2,96,768]{5,4,3,2,1,0:T(8,128)(2,1)S(1)}) custom-call(s32[21]{0:T(128)S(1)} %stack.79.place_ref, bf16[512,768]{1,0:T(8,128)(2,1)S(1)} %get-tuple-element.367.n_ref, bf16[768,512]{1,0:T(8,128)(2,1)S(1)} %get-tuple-element.368.nt_ref, ...), custom_call_target="tpu_custom_call", output_to_operand_aliasing={{0}: (5, {}), {1}: (6, {})} | custom-call | flops 1000 | bytes 1000 | tf_op jit(solution)/shard_map/feed/pallas_call | solution.py:409
  110.0 4.8 %feed.7 = (f32[512,768]{1,0:T(8,128)S(1)}, f32[512,768]{1,0:T(8,128)S(1)}, bf16[2,2,2,2,96,768]{5,4,3,2,1,0:T(8,128)(2,1)S(1)}) custom-call(s32[21]{0:T(128)S(1)} %stack.79.place_ref, bf16[512,768]{1,0:T(8,128)(2,1)S(1)} %get-tuple-element.367.n_ref, bf16[768,512]{1,0:T(8,128)(2,1)S(1)} %get-tuple-element.368.nt_ref, ...), custom_call_target="tpu_custom_call", output_to_operand_aliasing={{0}: (5, {}), {1}: (6, {})} | custom-call | flops 1000 | bytes 1000 | tf_op jit(solution)/shard_map/feed/pallas_call | solution.py:409
  116.4 7.4 %collective-permute-done.27.other_ref = bf16[512,768]{1,0:T(8,128)(2,1)S(1)} collective-permute-done((bf16[512,768]{1,0:T(8,128)(2,1)S(1)}, bf16[512,768]{1,0:T(8,128)(2,1)S(1)}, u32[]{:S(2)}, u32[]{:S(2)}) %collective-permute-start.27) | collective-permute-done | bytes 786464 | tf_op jit(solution)/shard_map/ppermute | solution.py:80
  123.9 1.7 context_grads.1
  126.7 1.6 collective-permute-start.30
  128.8 11.7 %attend_back.2 = (bf16[1024,576]{1,0:T(8,128)(2,1)S(1)}, f32[3,32,128]{2,1,0:T(8,128)S(1)}) custom-call(s32[21]{0:T(128)S(1)} %stack.79.place_ref, bf16[2,512,192]{2,1,0:T(8,128)(2,1)S(1)} %get-tuple-element.425.q_own_ref, bf16[2,512,192]{2,1,0:T(8,128)(2,1)S(1)} %get-tuple-element.426.q_other_ref, bf16[2,512,384]{2,1,0:T(8,128)(2,1)S(1)} %get-tuple-element.334.kv_own_ref, ...), custom_call_target="tpu_custom_call" | custom-call | flops 1000 | bytes 1000 | tf_op jit(solution)/shard_map/attend_back/pallas_call | solution.py:551
  140.5 11.4 %attend_back.3 = (bf16[1024,576]{1,0:T(8,128)(2,1)S(1)}, f32[3,32,128]{2,1,0:T(8,128)S(1)}) custom-call(s32[21]{0:T(128)S(1)} %stack.79.place_ref, bf16[2,512,192]{2,1,0:T(8,128)(2,1)S(1)} %get-tuple-element.425.q_own_ref, bf16[2,512,192]{2,1,0:T(8,128)(2,1)S(1)} %get-tuple-element.426.q_other_ref, bf16[2,512,384]{2,1,0:T(8,128)(2,1)S(1)} %get-tuple-element.334.kv_own_ref, ...), custom_call_target="tpu_custom_call" | custom-call | flops 1000 | bytes 1000 | tf_op jit(solution)/shard_map/attend_back/pallas_call | solution.py:551
  152.0 2.8 %collective-permute-done.30.near_came_ref = bf16[2,2,2,96,768]{4,3,2,1,0:T(8,128)(2,1)S(1)} collective-permute-done((bf16[2,2,2,96,768]{4,3,2,1,0:T(8,128)(2,1)S(1)}, bf16[2,2,2,96,768]{4,3,2,1,0:T(8,128)(2,1)S(1)}, u32[]{:S(2)}, u32[]{:S(2)}) %collective-permute-start.30) | collective-permute-done | bytes 1179680 | tf_op jit(solution)/shard_map/ppermute | solution.py:84
  157.6 6.6 %project_back.1 = (f32[512,768]{1,0:T(8,128)S(1)}, f32[512,768]{1,0:T(8,128)S(1)}, bf16[2,2,1,96,768]{4,3,2,1,0:T(8,128)(2,1)S(1)}, bf16[2,2,1,96,768]{4,3,2,1,0...) custom-call(s32[21]{0:T(128)S(1)} %stack.79.place_ref, ...), custom_call_target="tpu_custom_call" | custom-call | flops 1000 | bytes 1000 | tf_op jit(solution)/shard_map/project_back/pallas_call | solution.py:608
  164.2 6.5 %collective-permute-done.32.near_came_ref = bf16[2,2,96,768]{3,2,1,0:T(8,128)(2,1)S(1)} collective-permute-done((bf16[2,2,96,768]{3,2,1,0:T(8,128)(2,1)S(1)}, bf16[2,2,96,768]{3,2,1,0:T(8,128)(2,1)S(1)}, u32[]{:S(2)}, u32[]{:S(2)}) %collective-permute-start.32) | collective-permute-done | bytes 589856 | tf_op jit(solution)/shard_map/ppermute | solution.py:89
  174.0 1.5 collective-permute-start.38
  177.4 9.4 %collective-permute-done.35.near_came_ref = bf16[2,2,1,96,768]{4,3,2,1,0:T(8,128)(2,1)S(1)} collective-permute-done((bf16[2,2,1,96,768]{4,3,2,1,0:T(8,128)(2,1)S(1)}, bf16[2,2,1,96,768]{4,3,2,1,0:T(8,128)(2,1)S(1)}, u32[]{:S(2)}, u32[]{:S(2)}) %collective-permute-start.35) | collective-permute-done | bytes 589856 | tf_op jit(solution)/shard_map/ppermute | solution.py:84
  187.1 1.6 collective-permute-done.38.refs_1_
  191.7 5.4 %collective-permute-done.39.near_came_ref = bf16[2,1,96,768]{3,2,1,0:T(8,128)(2,1)S(1)} collective-permute-done((bf16[2,1,96,768]{3,2,1,0:T(8,128)(2,1)S(1)}, bf16[2,1,96,768]{3,2,1,0:T(8,128)(2,1)S(1)}, u32[]{:S(2)}, u32[]{:S(2)}) %collective-permute-start.39) | collective-permute-done | bytes 294944 | tf_op jit(solution)/shard_map/ppermute | solution.py:89
  197.3 8.1 %collective-permute-done.41.refs_2_ = bf16[2,96,768]{2,1,0:T(8,128)(2,1)S(1)} collective-permute-done((bf16[2,96,768]{2,1,0:T(8,128)(2,1)S(1)}, bf16[2,96,768]{2,1,0:T(8,128)(2,1)S(1)}, u32[]{:S(2)}, u32[]{:S(2)}) %collective-permute-start.41) | collective-permute-done | bytes 294944 | tf_op jit(solution)/shard_map/ppermute | solution.py:94
  206.2 2.0 collective-permute-start.43
  208.2 2.3 collective-permute-start.44
  211.5 2.1 collective-permute-done.42.refs_0_
  213.6 6.5 %collective-permute-done.43.refs_1_ = bf16[1,96,768]{2,1,0:T(8,128)(2,1)S(1)} collective-permute-done((bf16[1,96,768]{2,1,0:T(8,128)(2,1)S(1)}, bf16[1,96,768]{2,1,0:T(8,128)(2,1)S(1)}, u32[]{:S(2)}, u32[]{:S(2)}) %collective-permute-start.43) | collective-permute-done | bytes 147488 | tf_op jit(solution)/shard_map/ppermute | solution.py:94
  220.2 4.6 %collective-permute-done.45.came_ref = bf16[2,256,768]{2,1,0:T(8,128)(2,1)S(1)} collective-permute-done((bf16[2,256,768]{2,1,0:T(8,128)(2,1)S(1)}, bf16[2,256,768]{2,1,0:T(8,128)(2,1)S(1)}, u32[]{:S(2)}, u32[]{:S(2)}) %collective-permute-start.45) | collective-permute-done | bytes 786464 | tf_op jit(solution)/shard_map/ppermute | solution.py:84
  225.8 2.8 %all-to-all-start.1 = ((f32[32,16,128]{2,1,0:T(8,128)}), f32[32,16,128]{2,1,0:T(8,128)S(1)}, u32[]{:S(2)}, u32[]{:S(2)}) async-start(f32[32,16,128]{2,1,0:T(8,128)} %broadcast_in_dim.5), calls=%async_computation.1 | async-start | bytes 524288 | tf_op jit(solution)/shard_map/all_to_all | solution.py:108
  228.6 1.8 place_rows.1
  230.4 8.8 %all-to-all-done.1.small_ref = f32[32,16,128]{2,1,0:T(8,128)S(1)} async-done(((f32[32,16,128]{2,1,0:T(8,128)}), f32[32,16,128]{2,1,0:T(8,128)S(1)}, u32[]{:S(2)}, u32[]{:S(2)}) %all-to-all-start.1) | async-done | bytes 262176 | tf_op jit(solution)/shard_map/all_to_all | solution.py:108
  239.2 4.2 %update.1 = (f32[1,1]{1,0:T(1,128)}, f32[4,96,192]{2,1,0:T(8,128)}, f32[2,96]{1,0:T(2,128)}, f32[12,32]{1,0:T(8,128)}, f32[4,96,192]{2,1,0:T(8,128)}, /*index=5*...) custom-call(s32[1]{0:T(128)} %bitcast.21.place_ref, ...), custom_call_target="tpu_custom_call" | custom-call | flops 1000 | bytes 1000 | tf_op jit(solution)/shard_map/update/pallas_call | solution.py:981
  (111 shorter events, 30.7 us)
Async XLA Ops:
  3.3 30.5 %collective-permute-start.5 = (bf16[2,256,768]{2,1,0:T(8,128)(2,1)S(1)}, bf16[2,256,768]{2,1,0:T(8,128)(2,1)S(1)}, u32[]{:S(2)}, u32[]{:S(2)}) collective-permute-start(bf16[2,256,768]{2,1,0:T(8,128)(2,1)S(1)} %sort_rows.1), channel_id=1, source_target_pairs={{0,2},{1,3},{2,0},{3,1},{4,6},{5,7},{6,4},{7,5},{8,10},{9,11},{10,... | collective-permute-start | bytes 2359304 | tf_op jit(solution)/shard_map/ppermute | solution.py:84
  6.4 9.7 %collective-permute-start.2 = (bf16[1,96,768]{2,1,0:T(8,128)(2,1)S(1)}, bf16[1,96,768]{2,1,0:T(8,128)(2,1)S(1)}, u32[]{:S(2)}, u32[]{:S(2)}) collective-permute-start(bf16[1,96,768]{2,1,0:T(8,128)(2,1)S(1)} %cast_attn.1.refs_0_), channel_id=1, source_target_pairs={{0,24},{4,28},{8,16},{12,20},{16,8},{20,12},{24,0},{28,4},{1,25},{... | collective-permute-start | bytes 442376 | tf_op jit(solution)/shard_map/ppermute | solution.py:94
  10.1 12.2 %collective-permute-start.1 = (bf16[1,96,768]{2,1,0:T(8,128)(2,1)S(1)}, bf16[1,96,768]{2,1,0:T(8,128)(2,1)S(1)}, u32[]{:S(2)}, u32[]{:S(2)}) collective-permute-start(bf16[1,96,768]{2,1,0:T(8,128)(2,1)S(1)} %cast_attn.1.refs_0_), channel_id=1, source_target_pairs={{0,16},{4,20},{8,24},{12,28},{16,0},{20,4},{24,8},{28,12},{1,17},{... | collective-permute-start | bytes 442376 | tf_op jit(solution)/shard_map/ppermute | solution.py:94
  10.1 12.2 %collective-permute-start = (bf16[1,96,768]{2,1,0:T(8,128)(2,1)S(1)}, bf16[1,96,768]{2,1,0:T(8,128)(2,1)S(1)}, u32[]{:S(2)}, u32[]{:S(2)}) collective-permute-start(bf16[1,96,768]{2,1,0:T(8,128)(2,1)S(1)} %cast_attn.1.refs_0_), channel_id=1, source_target_pairs={{0,8},{4,12},{8,0},{12,4},{16,24},{20,28},{24,16},{28,20},{1,9},{5... | collective-permute-start | bytes 442376 | tf_op jit(solution)/shard_map/ppermute | solution.py:94
  22.3 8.1 %collective-permute-start.4 = (bf16[2,1,96,768]{3,2,1,0:T(8,128)(2,1)S(1)}, bf16[2,1,96,768]{3,2,1,0:T(8,128)(2,1)S(1)}, u32[]{:S(2)}, u32[]{:S(2)}) collective-permute-start(bf16[2,1,96,768]{3,2,1,0:T(8,128)(2,1)S(1)} %line_up.8.refs_0_), channel_id=1, source_target_pairs={{0,4},{4,0},{8,12},{12,8},{16,20},{20,16},{24,28},{28,24},{1,5},{5... | collective-permute-start | bytes 884744 | tf_op jit(solution)/shard_map/ppermute | solution.py:89
  23.9 7.8 %collective-permute-start.3 = (bf16[2,1,96,768]{3,2,1,0:T(8,128)(2,1)S(1)}, bf16[2,1,96,768]{3,2,1,0:T(8,128)(2,1)S(1)}, u32[]{:S(2)}, u32[]{:S(2)}) collective-permute-start(bf16[2,1,96,768]{3,2,1,0:T(8,128)(2,1)S(1)} %line_up.7.refs_0_), channel_id=1, source_target_pairs={{0,2},{1,3},{2,0},{3,1},{4,6},{5,7},{6,4},{7,5},{8,10},{9,11},{10,... | collective-permute-start | bytes 884744 | tf_op jit(solution)/shard_map/ppermute | solution.py:84
  24.5 9.3 %collective-permute-start.6 = (bf16[2,96,768]{2,1,0:T(8,128)(2,1)S(1)}, bf16[2,96,768]{2,1,0:T(8,128)(2,1)S(1)}, u32[]{:S(2)}, u32[]{:S(2)}) collective-permute-start(bf16[2,96,768]{2,1,0:T(8,128)(2,1)S(1)} %cast_ffn.1.refs_0_), channel_id=1, source_target_pairs={{0,8},{4,12},{8,16},{12,20},{16,24},{20,28},{24,0},{28,4},{1,9},{5... | collective-permute-start | bytes 884744 | tf_op jit(solution)/shard_map/ppermute | solution.py:99
  33.8 8.5 %collective-permute-start.9 = (bf16[2,96,768]{2,1,0:T(8,128)(2,1)S(1)}, bf16[2,96,768]{2,1,0:T(8,128)(2,1)S(1)}, u32[]{:S(2)}, u32[]{:S(2)}) collective-permute-start(bf16[2,96,768]{2,1,0:T(8,128)(2,1)S(1)} %collective-permute-done.6.refs_1_), channel_id=1, source_target_pairs={{0,8},{4,12},{8,16},{12,20},{16,24},{20,28},{24,0},{28,4},{1,9},{5... | collective-permute-start | bytes 884744 | tf_op jit(solution)/shard_map/ppermute | solution.py:99
  33.9 19.9 %collective-permute-start.8 = (bf16[2,2,1,96,768]{4,3,2,1,0:T(8,128)(2,1)S(1)}, bf16[2,2,1,96,768]{4,3,2,1,0:T(8,128)(2,1)S(1)}, u32[]{:S(2)}, u32[]{:S(2)}) collective-permute-start(bf16[2,2,1,96,768]{4,3,2,1,0:T(8,128)(2,1)S(1)} %line_up.10.refs_1_.refs_3_.refs_5_.refs_7_.refs_9_), channel_id=1, source_target_pairs={{0,2},{1,3},{2,0},{3,1},{4,6},{5,7},{6,4},{7,5},{8,10},{9,11},{10,... | collective-permute-start | bytes 1769480 | tf_op jit(solution)/shard_map/ppermute | solution.py:84
  35.5 18.3 %collective-permute-start.7 = (bf16[2,2,1,96,768]{4,3,2,1,0:T(8,128)(2,1)S(1)}, bf16[2,2,1,96,768]{4,3,2,1,0:T(8,128)(2,1)S(1)}, u32[]{:S(2)}, u32[]{:S(2)}) collective-permute-start(bf16[2,2,1,96,768]{4,3,2,1,0:T(8,128)(2,1)S(1)} %line_up.9.refs_0_.refs_4_.refs_12_.refs_6_.refs_10_), channel_id=1, source_target_pairs={{0,4},{4,0},{8,12},{12,8},{16,20},{20,16},{24,28},{28,24},{1,5},{5... | collective-permute-start | bytes 1769480 | tf_op jit(solution)/shard_map/ppermute | solution.py:89
  42.3 11.5 %collective-permute-start.10 = (bf16[2,96,768]{2,1,0:T(8,128)(2,1)S(1)}, bf16[2,96,768]{2,1,0:T(8,128)(2,1)S(1)}, u32[]{:S(2)}, u32[]{:S(2)}) collective-permute-start(bf16[2,96,768]{2,1,0:T(8,128)(2,1)S(1)} %collective-permute-done.9.refs_0_), channel_id=1, source_target_pairs={{0,8},{4,12},{8,16},{12,20},{16,24},{20,28},{24,0},{28,4},{1,9},{5... | collective-permute-start | bytes 884744 | tf_op jit(solution)/shard_map/ppermute | solution.py:99
  53.8 2.5 %collective-permute-start.11 = (bf16[512,768]{1,0:T(8,128)(2,1)S(1)}, bf16[512,768]{1,0:T(8,128)(2,1)S(1)}, u32[]{:S(2)}, u32[]{:S(2)}) collective-permute-start(bf16[512,768]{1,0:T(8,128)(2,1)S(1)} %get-tuple-element.310.x_ref), channel_id=1, source_target_pairs={{0,1},{1,0},{2,3},{3,2},{4,5},{5,4},{6,7},{7,6},{8,9},{9,8},{10,11... | collective-permute-start | bytes 2359304 | tf_op jit(solution)/shard_map/ppermute | solution.py:80
  58.6 21.0 %collective-permute-start.14 = (bf16[2,2,1,96,768]{4,3,2,1,0:T(8,128)(2,1)S(1)}, bf16[2,2,1,96,768]{4,3,2,1,0:T(8,128)(2,1)S(1)}, u32[]{:S(2)}, u32[]{:S(2)}) collective-permute-start(bf16[2,2,1,96,768]{4,3,2,1,0:T(8,128)(2,1)S(1)} %line_up.9.refs_0_.refs_4_.refs_12_.refs_6_.refs_10_), channel_id=1, source_target_pairs={{0,1},{1,0},{2,3},{3,2},{4,5},{5,4},{6,7},{7,6},{8,9},{9,8},{10,11... | collective-permute-start | bytes 1769480 | tf_op jit(solution)/shard_map/ppermute | solution.py:80
  59.1 28.0 %collective-permute-start.19 = (bf16[2,2,2,96,768]{4,3,2,1,0:T(8,128)(2,1)S(1)}, bf16[2,2,2,96,768]{4,3,2,1,0:T(8,128)(2,1)S(1)}, u32[]{:S(2)}, u32[]{:S(2)}) collective-permute-start(bf16[2,2,2,96,768]{4,3,2,1,0:T(8,128)(2,1)S(1)} %line_up.13.refs_0_.refs_1_), channel_id=1, source_target_pairs={{0,4},{4,0},{8,12},{12,8},{16,20},{20,16},{24,28},{28,24},{1,5},{5... | collective-permute-start | bytes 3538952 | tf_op jit(solution)/shard_map/ppermute | solution.py:89
  59.7 27.7 %collective-permute-start.18 = (bf16[2,2,2,96,768]{4,3,2,1,0:T(8,128)(2,1)S(1)}, bf16[2,2,2,96,768]{4,3,2,1,0:T(8,128)(2,1)S(1)}, u32[]{:S(2)}, u32[]{:S(2)}) collective-permute-start(bf16[2,2,2,96,768]{4,3,2,1,0:T(8,128)(2,1)S(1)} %line_up.13.refs_0_.refs_1_), channel_id=1, source_target_pairs={{0,2},{1,3},{2,0},{3,1},{4,6},{5,7},{6,4},{7,5},{8,10},{9,11},{10,... | collective-permute-start | bytes 3538952 | tf_op jit(solution)/shard_map/ppermute | solution.py:84
  69.2 8.9 %collective-permute-start.12 = (bf16[512,256]{1,0:T(8,128)(2,1)S(1)}, bf16[512,256]{1,0:T(8,128)(2,1)S(1)}, u32[]{:S(2)}, u32[]{:S(2)}) collective-permute-start(bf16[512,256]{1,0:T(8,128)(2,1)S(1)} %get-tuple-element.439.ctx_other_ref.refs_3_), channel_id=1, source_target_pairs={{0,1},{1,0},{2,3},{3,2},{4,5},{5,4},{6,7},{7,6},{8,9},{9,8},{10,11... | collective-permute-start | bytes 786440 | tf_op jit(solution)/shard_map/ppermute | solution.py:80
  77.5 1.7 collective-permute-start.13
  78.1 2.0 collective-permute-start.15
  79.2 2.0 collective-permute-start.16
  79.6 2.5 %collective-permute-start.17 = (bf16[2,2,1,96,768]{4,3,2,1,0:T(8,128)(2,1)S(1)}, bf16[2,2,1,96,768]{4,3,2,1,0:T(8,128)(2,1)S(1)}, u32[]{:S(2)}, u32[]{:S(2)}) collective-permute-start(bf16[2,2,1,96,768]{4,3,2,1,0:T(8,128)(2,1)S(1)} %collective-permute-done.8.refs_5_.refs_7_.refs_13_.refs_15_.refs_11_), channel_id=1, source_target_pairs={{0,1},{1,0},{2,3},{3,2},{4,5},{5,4},{6,7},{7,6},{8,9},{9,8},{10,11... | collective-permute-start | bytes 1769480 | tf_op jit(solution)/shard_map/ppermute | solution.py:80
  80.1 15.5 %collective-permute-start.22 = (bf16[2,2,2,96,768]{4,3,2,1,0:T(8,128)(2,1)S(1)}, bf16[2,2,2,96,768]{4,3,2,1,0:T(8,128)(2,1)S(1)}, u32[]{:S(2)}, u32[]{:S(2)}) collective-permute-start(bf16[2,2,2,96,768]{4,3,2,1,0:T(8,128)(2,1)S(1)} %line_up.13.refs_0_.refs_1_), channel_id=1, source_target_pairs={{0,1},{1,0},{2,3},{3,2},{4,5},{5,4},{6,7},{7,6},{8,9},{9,8},{10,11... | collective-permute-start | bytes 3538952 | tf_op jit(solution)/shard_map/ppermute | solution.py:80
  87.4 8.3 %collective-permute-start.20 = (bf16[2,2,2,96,768]{4,3,2,1,0:T(8,128)(2,1)S(1)}, bf16[2,2,2,96,768]{4,3,2,1,0:T(8,128)(2,1)S(1)}, u32[]{:S(2)}, u32[]{:S(2)}) collective-permute-start(bf16[2,2,2,96,768]{4,3,2,1,0:T(8,128)(2,1)S(1)} %collective-permute-done.19.refs_2_.refs_3_), channel_id=1, source_target_pairs={{0,1},{1,0},{2,3},{3,2},{4,5},{5,4},{6,7},{7,6},{8,9},{9,8},{10,11... | collective-permute-start | bytes 3538952 | tf_op jit(solution)/shard_map/ppermute | solution.py:80
  87.4 8.3 %collective-permute-start.21 = (bf16[2,2,2,96,768]{4,3,2,1,0:T(8,128)(2,1)S(1)}, bf16[2,2,2,96,768]{4,3,2,1,0:T(8,128)(2,1)S(1)}, u32[]{:S(2)}, u32[]{:S(2)}) collective-permute-start(bf16[2,2,2,96,768]{4,3,2,1,0:T(8,128)(2,1)S(1)} %collective-permute-done.18.refs_2_.refs_3_), channel_id=1, source_target_pairs={{0,1},{1,0},{2,3},{3,2},{4,5},{5,4},{6,7},{7,6},{8,9},{9,8},{10,11... | collective-permute-start | bytes 3538952 | tf_op jit(solution)/shard_map/ppermute | solution.py:80
  88.0 15.3 %collective-permute-start.23 = (bf16[2,2,96,768]{3,2,1,0:T(8,128)(2,1)S(1)}, bf16[2,2,96,768]{3,2,1,0:T(8,128)(2,1)S(1)}, u32[]{:S(2)}, u32[]{:S(2)}) collective-permute-start(bf16[2,2,96,768]{3,2,1,0:T(8,128)(2,1)S(1)} %slice_bitcast_fusion.1), channel_id=1, source_target_pairs={{0,4},{4,0},{8,12},{12,8},{16,20},{20,16},{24,28},{28,24},{1,5},{5... | collective-permute-start | bytes 1769480 | tf_op jit(solution)/shard_map/ppermute | solution.py:89
  89.5 15.0 %collective-permute-start.24 = (bf16[2,2,96,768]{3,2,1,0:T(8,128)(2,1)S(1)}, bf16[2,2,96,768]{3,2,1,0:T(8,128)(2,1)S(1)}, u32[]{:S(2)}, u32[]{:S(2)}) collective-permute-start(bf16[2,2,96,768]{3,2,1,0:T(8,128)(2,1)S(1)} %slice_bitcast_fusion), channel_id=1, source_target_pairs={{0,2},{1,3},{2,0},{3,1},{4,6},{5,7},{6,4},{7,5},{8,10},{9,11},{10,... | collective-permute-start | bytes 1769480 | tf_op jit(solution)/shard_map/ppermute | solution.py:84
  104.5 5.5 %collective-permute-start.25 = (bf16[2,2,96,768]{3,2,1,0:T(8,128)(2,1)S(1)}, bf16[2,2,96,768]{3,2,1,0:T(8,128)(2,1)S(1)}, u32[]{:S(2)}, u32[]{:S(2)}) collective-permute-start(bf16[2,2,96,768]{3,2,1,0:T(8,128)(2,1)S(1)} %collective-permute-done.23.refs_4_), channel_id=1, source_target_pairs={{0,1},{1,0},{2,3},{3,2},{4,5},{5,4},{6,7},{7,6},{8,9},{9,8},{10,11... | collective-permute-start | bytes 1769480 | tf_op jit(solution)/shard_map/ppermute | solution.py:80
  104.5 5.5 %collective-permute-start.26 = (bf16[2,2,96,768]{3,2,1,0:T(8,128)(2,1)S(1)}, bf16[2,2,96,768]{3,2,1,0:T(8,128)(2,1)S(1)}, u32[]{:S(2)}, u32[]{:S(2)}) collective-permute-start(bf16[2,2,96,768]{3,2,1,0:T(8,128)(2,1)S(1)} %collective-permute-done.24.refs_5_), channel_id=1, source_target_pairs={{0,1},{1,0},{2,3},{3,2},{4,5},{5,4},{6,7},{7,6},{8,9},{9,8},{10,11... | collective-permute-start | bytes 1769480 | tf_op jit(solution)/shard_map/ppermute | solution.py:80
  114.8 10.8 %collective-permute-start.29 = (bf16[2,2,2,2,96,768]{5,4,3,2,1,0:T(8,128)(2,1)S(1)}, bf16[2,2,2,2,96,768]{5,4,3,2,1,0:T(8,128)(2,1)S(1)}, u32[]{:S(2)}, u32[]{:S(2)}) collective-permute-start(bf16[2,2,2,2,96,768]{5,4,3,2,1,0:T(8,128)(2,1)S(1)} %get-tuple-element.428), channel_id=1, source_target_pairs={{0,1},{1,0},{2,3},{3,2},{4,5},{5,4},{6,7},{7,6},{8,9},{9,8},{10,11... | collective-permute-start | bytes 7077896 | tf_op jit(solution)/shard_map/ppermute | solution.py:80
  114.8 10.7 %collective-permute-start.28 = (bf16[2,2,2,2,96,768]{5,4,3,2,1,0:T(8,128)(2,1)S(1)}, bf16[2,2,2,2,96,768]{5,4,3,2,1,0:T(8,128)(2,1)S(1)}, u32[]{:S(2)}, u32[]{:S(2)}) collective-permute-start(bf16[2,2,2,2,96,768]{5,4,3,2,1,0:T(8,128)(2,1)S(1)} %get-tuple-element.408), channel_id=1, source_target_pairs={{0,1},{1,0},{2,3},{3,2},{4,5},{5,4},{6,7},{7,6},{8,9},{9,8},{10,11... | collective-permute-start | bytes 7077896 | tf_op jit(solution)/shard_map/ppermute | solution.py:80
  116.3 7.6 %collective-permute-start.27 = (bf16[512,768]{1,0:T(8,128)(2,1)S(1)}, bf16[512,768]{1,0:T(8,128)(2,1)S(1)}, u32[]{:S(2)}, u32[]{:S(2)}) collective-permute-start(bf16[512,768]{1,0:T(8,128)(2,1)S(1)} %get-tuple-element.421.own_ref), channel_id=1, source_target_pairs={{0,1},{1,0},{2,3},{3,2},{4,5},{5,4},{6,7},{7,6},{8,9},{9,8},{10,11... | collective-permute-start | bytes 2359304 | tf_op jit(solution)/shard_map/ppermute | solution.py:80
  126.7 28.1 %collective-permute-start.30 = (bf16[2,2,2,96,768]{4,3,2,1,0:T(8,128)(2,1)S(1)}, bf16[2,2,2,96,768]{4,3,2,1,0:T(8,128)(2,1)S(1)}, u32[]{:S(2)}, u32[]{:S(2)}) collective-permute-start(bf16[2,2,2,96,768]{4,3,2,1,0:T(8,128)(2,1)S(1)} %get-tuple-element.450), channel_id=1, source_target_pairs={{0,2},{1,3},{2,0},{3,1},{4,6},{5,7},{6,4},{7,5},{8,10},{9,11},{10,... | collective-permute-start | bytes 3538952 | tf_op jit(solution)/shard_map/ppermute | solution.py:84
  128.2 27.7 %collective-permute-start.31 = (bf16[2,2,2,96,768]{4,3,2,1,0:T(8,128)(2,1)S(1)}, bf16[2,2,2,96,768]{4,3,2,1,0:T(8,128)(2,1)S(1)}, u32[]{:S(2)}, u32[]{:S(2)}) collective-permute-start(bf16[2,2,2,96,768]{4,3,2,1,0:T(8,128)(2,1)S(1)} %get-tuple-element.451), channel_id=1, source_target_pairs={{0,4},{4,0},{8,12},{12,8},{16,20},{20,16},{24,28},{28,24},{1,5},{5... | collective-permute-start | bytes 3538952 | tf_op jit(solution)/shard_map/ppermute | solution.py:89
  156.5 14.3 %collective-permute-start.32 = (bf16[2,2,96,768]{3,2,1,0:T(8,128)(2,1)S(1)}, bf16[2,2,96,768]{3,2,1,0:T(8,128)(2,1)S(1)}, u32[]{:S(2)}, u32[]{:S(2)}) collective-permute-start(bf16[2,2,96,768]{3,2,1,0:T(8,128)(2,1)S(1)} %get-tuple-element.465), channel_id=1, source_target_pairs={{0,4},{4,0},{8,12},{12,8},{16,20},{20,16},{24,28},{28,24},{1,5},{5... | collective-permute-start | bytes 1769480 | tf_op jit(solution)/shard_map/ppermute | solution.py:89
  157.1 13.9 %collective-permute-start.33 = (bf16[2,2,96,768]{3,2,1,0:T(8,128)(2,1)S(1)}, bf16[2,2,96,768]{3,2,1,0:T(8,128)(2,1)S(1)}, u32[]{:S(2)}, u32[]{:S(2)}) collective-permute-start(bf16[2,2,96,768]{3,2,1,0:T(8,128)(2,1)S(1)} %get-tuple-element.466), channel_id=1, source_target_pairs={{0,2},{1,3},{2,0},{3,1},{4,6},{5,7},{6,4},{7,5},{8,10},{9,11},{10,... | collective-permute-start | bytes 1769480 | tf_op jit(solution)/shard_map/ppermute | solution.py:84
  171.0 4.4 %collective-permute-start.34 = (f32[512,768]{1,0:T(8,128)S(1)}, f32[512,768]{1,0:T(8,128)S(1)}, u32[]{:S(2)}, u32[]{:S(2)}) collective-permute-start(f32[512,768]{1,0:T(8,128)S(1)} %get-tuple-element.476), channel_id=1, source_target_pairs={{0,1},{1,0},{2,3},{3,2},{4,5},{5,4},{6,7},{7,6},{8,9},{9,8},{10,11... | collective-permute-start | bytes 4718600 | tf_op jit(solution)/shard_map/ppermute | solution.py:80
  171.0 15.7 %collective-permute-start.35 = (bf16[2,2,1,96,768]{4,3,2,1,0:T(8,128)(2,1)S(1)}, bf16[2,2,1,96,768]{4,3,2,1,0:T(8,128)(2,1)S(1)}, u32[]{:S(2)}, u32[]{:S(2)}) collective-permute-start(bf16[2,2,1,96,768]{4,3,2,1,0:T(8,128)(2,1)S(1)} %get-tuple-element.492), channel_id=1, source_target_pairs={{0,2},{1,3},{2,0},{3,1},{4,6},{5,7},{6,4},{7,5},{8,10},{9,11},{10,... | collective-permute-start | bytes 1769480 | tf_op jit(solution)/shard_map/ppermute | solution.py:84
  171.6 15.5 %collective-permute-start.36 = (bf16[2,2,1,96,768]{4,3,2,1,0:T(8,128)(2,1)S(1)}, bf16[2,2,1,96,768]{4,3,2,1,0:T(8,128)(2,1)S(1)}, u32[]{:S(2)}, u32[]{:S(2)}) collective-permute-start(bf16[2,2,1,96,768]{4,3,2,1,0:T(8,128)(2,1)S(1)} %get-tuple-element.493), channel_id=1, source_target_pairs={{0,4},{4,0},{8,12},{12,8},{16,20},{20,16},{24,28},{28,24},{1,5},{5... | collective-permute-start | bytes 1769480 | tf_op jit(solution)/shard_map/ppermute | solution.py:89
  173.4 13.7 %collective-permute-start.37 = (bf16[2,96,768]{2,1,0:T(8,128)(2,1)S(1)}, bf16[2,96,768]{2,1,0:T(8,128)(2,1)S(1)}, u32[]{:S(2)}, u32[]{:S(2)}) collective-permute-start(bf16[2,96,768]{2,1,0:T(8,128)(2,1)S(1)} %get-tuple-element.473), channel_id=1, source_target_pairs={{0,8},{4,12},{8,0},{12,4},{16,24},{20,28},{24,16},{28,20},{1,9},{5... | collective-permute-start | bytes 884744 | tf_op jit(solution)/shard_map/ppermute | solution.py:94
  174.0 14.8 %collective-permute-start.38 = (bf16[2,96,768]{2,1,0:T(8,128)(2,1)S(1)}, bf16[2,96,768]{2,1,0:T(8,128)(2,1)S(1)}, u32[]{:S(2)}, u32[]{:S(2)}) collective-permute-start(bf16[2,96,768]{2,1,0:T(8,128)(2,1)S(1)} %get-tuple-element.475), channel_id=1, source_target_pairs={{0,24},{4,28},{8,16},{12,20},{16,8},{20,12},{24,0},{28,4},{1,25},{... | collective-permute-start | bytes 884744 | tf_op jit(solution)/shard_map/ppermute | solution.py:94
  189.0 8.0 %collective-permute-start.39 = (bf16[2,1,96,768]{3,2,1,0:T(8,128)(2,1)S(1)}, bf16[2,1,96,768]{3,2,1,0:T(8,128)(2,1)S(1)}, u32[]{:S(2)}, u32[]{:S(2)}) collective-permute-start(bf16[2,1,96,768]{3,2,1,0:T(8,128)(2,1)S(1)} %get-tuple-element.502), channel_id=1, source_target_pairs={{0,4},{4,0},{8,12},{12,8},{16,20},{20,16},{24,28},{28,24},{1,5},{5... | collective-permute-start | bytes 884744 | tf_op jit(solution)/shard_map/ppermute | solution.py:89
  189.6 7.7 %collective-permute-start.40 = (bf16[2,1,96,768]{3,2,1,0:T(8,128)(2,1)S(1)}, bf16[2,1,96,768]{3,2,1,0:T(8,128)(2,1)S(1)}, u32[]{:S(2)}, u32[]{:S(2)}) collective-permute-start(bf16[2,1,96,768]{3,2,1,0:T(8,128)(2,1)S(1)} %get-tuple-element.503), channel_id=1, source_target_pairs={{0,2},{1,3},{2,0},{3,1},{4,6},{5,7},{6,4},{7,5},{8,10},{9,11},{10,... | collective-permute-start | bytes 884744 | tf_op jit(solution)/shard_map/ppermute | solution.py:84
  191.0 14.3 %collective-permute-start.41 = (bf16[2,96,768]{2,1,0:T(8,128)(2,1)S(1)}, bf16[2,96,768]{2,1,0:T(8,128)(2,1)S(1)}, u32[]{:S(2)}, u32[]{:S(2)}) collective-permute-start(bf16[2,96,768]{2,1,0:T(8,128)(2,1)S(1)} %get-tuple-element.509), channel_id=1, source_target_pairs={{0,16},{4,20},{8,24},{12,28},{16,0},{20,4},{24,8},{28,12},{1,17},{... | collective-permute-start | bytes 884744 | tf_op jit(solution)/shard_map/ppermute | solution.py:94
  205.3 19.5 %collective-permute-start.45 = (bf16[2,256,768]{2,1,0:T(8,128)(2,1)S(1)}, bf16[2,256,768]{2,1,0:T(8,128)(2,1)S(1)}, u32[]{:S(2)}, u32[]{:S(2)}) collective-permute-start(bf16[2,256,768]{2,1,0:T(8,128)(2,1)S(1)} %get-tuple-element.526), channel_id=1, source_target_pairs={{0,2},{1,3},{2,0},{3,1},{4,6},{5,7},{6,4},{7,5},{8,10},{9,11},{10,... | collective-permute-start | bytes 2359304 | tf_op jit(solution)/shard_map/ppermute | solution.py:84
  206.1 7.5 %collective-permute-start.42 = (bf16[1,96,768]{2,1,0:T(8,128)(2,1)S(1)}, bf16[1,96,768]{2,1,0:T(8,128)(2,1)S(1)}, u32[]{:S(2)}, u32[]{:S(2)}) collective-permute-start(bf16[1,96,768]{2,1,0:T(8,128)(2,1)S(1)} %get-tuple-element.523), channel_id=1, source_target_pairs={{0,8},{4,12},{8,0},{12,4},{16,24},{20,28},{24,16},{28,20},{1,9},{5... | collective-permute-start | bytes 442376 | tf_op jit(solution)/shard_map/ppermute | solution.py:94
  206.2 14.0 %collective-permute-start.43 = (bf16[1,96,768]{2,1,0:T(8,128)(2,1)S(1)}, bf16[1,96,768]{2,1,0:T(8,128)(2,1)S(1)}, u32[]{:S(2)}, u32[]{:S(2)}) collective-permute-start(bf16[1,96,768]{2,1,0:T(8,128)(2,1)S(1)} %get-tuple-element.524), channel_id=1, source_target_pairs={{0,16},{4,20},{8,24},{12,28},{16,0},{20,4},{24,8},{28,12},{1,17},{... | collective-permute-start | bytes 442376 | tf_op jit(solution)/shard_map/ppermute | solution.py:94
  208.2 12.0 %collective-permute-start.44 = (bf16[1,96,768]{2,1,0:T(8,128)(2,1)S(1)}, bf16[1,96,768]{2,1,0:T(8,128)(2,1)S(1)}, u32[]{:S(2)}, u32[]{:S(2)}) collective-permute-start(bf16[1,96,768]{2,1,0:T(8,128)(2,1)S(1)} %get-tuple-element.525), channel_id=1, source_target_pairs={{0,24},{4,28},{8,16},{12,20},{16,8},{20,12},{24,0},{28,4},{1,25},{... | collective-permute-start | bytes 442376 | tf_op jit(solution)/shard_map/ppermute | solution.py:94
  211.5 27.7 %copy-start.2 = (f32[2,96,768]{2,1,0:T(8,128)S(1)}, f32[2,96,768]{2,1,0:T(8,128)}, u32[]{:S(2)}) copy-start(f32[2,96,768]{2,1,0:T(8,128)} %get-tuple-element.271.ffn_ref) | copy-start | bytes 1769476
  225.8 13.4 %all-to-all-start.1 = ((f32[32,16,128]{2,1,0:T(8,128)}), f32[32,16,128]{2,1,0:T(8,128)S(1)}, u32[]{:S(2)}, u32[]{:S(2)}) async-start(f32[32,16,128]{2,1,0:T(8,128)} %broadcast_in_dim.5), calls=%async_computation.1 | async-start | bytes 524288 | tf_op jit(solution)/shard_map/all_to_all | solution.py:108
  (8 other events, 68.4 us)

commit v6 on v5

--- a/solution.py
+++ b/solution.py
@@ -22,7 +22,7 @@
 rate_small = 0.4
 clip_level = 1.0
 
-FEED_MIB = 18
+FEED_MIB = 20
 BACK_MIB = 12
 MERGE_MIB = 8
 
@@ -338,12 +338,11 @@
     )(place, *q, *kv, bias)
 
 
-def middle_kernel(indices, place_ref, x_ref, gain_ref, back_ref, *refs):
+def middle_kernel(indices, place_ref, x_ref, gain_ref, *refs):
     n_parts = len(indices[0])
     ctx_refs, w_refs = refs[:4], refs[4 : 4 + 4 * n_parts]
-    mid_ref, normed_ref, normed_t_ref, back_t_ref, whole = refs[4 + 4 * n_parts :]
+    mid_ref, normed_ref, normed_t_ref, whole = refs[4 + 4 * n_parts :]
     total = x_ref[...].astype(F32)
-    back_t_ref[...] = back_ref[...].T
     for b in range(4):
         part = pick(w_refs[b * n_parts : (b + 1) * n_parts], indices[b])
         assemble(whole.at[b], part, place_ref, 0, slice(512, 768))
@@ -354,101 +353,117 @@
     normed_t_ref[...] = normed.T
 
 
-def middle(place, rows_in, gain_low, back, ctx, blocks):
+def middle(place, rows_in, gain_low, ctx, blocks):
     rows = rows_in.shape[0]
     n_parts = len(blocks[0][0])
     return pl.pallas_call(
         functools.partial(middle_kernel, [i for _, i in blocks]),
-        in_specs=[in_smem] + [in_vmem] * (7 + 4 * n_parts),
-        out_specs=[in_vmem] * 4,
+        in_specs=[in_smem] + [in_vmem] * (6 + 4 * n_parts),
+        out_specs=[in_vmem] * 3,
         out_shape=[
             shape_of((rows, D), F32),
             shape_of((rows, D), BF),
-            shape_of((D, rows), BF),
             shape_of((D, rows), BF),
         ],
         scratch_shapes=[pltpu.VMEM((4, D, 256), BF)],
         compiler_params=params(10),
         cost_estimate=cost(2 * rows * D * D, 8e6),
         name="middle",
-    )(place, rows_in, gain_low, back, *ctx, *[p for b, _ in blocks for p in b])
-
-
-def feed_kernel(indices, first, place_ref, n_ref, nt_ref, g_ref, gt_ref, *refs):
+    )(place, rows_in, gain_low, *ctx, *[p for b, _ in blocks for p in b])
+
+
+def feed_kernel(indices, first, split, place_ref, *refs):
+    n_refs, nt_refs, g_refs, gt_refs = [refs[2 * i : 2 * i + 2] for i in range(4)]
+    refs = refs[8:]
     if not first:
-        acc_in, t_in = refs[:2]
-        refs = refs[2:]
+        acc_ins, t_ins, refs = refs[0:2], refs[2:4], refs[4:]
     n_parts = len(indices)
-    w_refs, (acc_ref, t_ref, grads_ref, wi, wf, gi, gf) = refs[:n_parts], refs[n_parts:]
-    w_refs = pick(w_refs, indices)
+    w_refs, refs = pick(refs[:n_parts], indices), refs[n_parts:]
+    acc_refs, t_refs, out_refs = refs[0:2], refs[2:4], refs[4:-6]
+    wi, wf, gi, gf, active, pre_grad = refs[-6:]
     assemble(wi, w_refs, place_ref, 0, ring=True)
     assemble(wf, w_refs, place_ref, 1, ring=True)
-    pre = dot(n_ref[...], wi[...], NN)
-    grad = dot(g_ref[...], wf[...], NN)
-    cdf = 0.5 * (1.0 + lax.erf(pre * 0.7071067811865476))
-    active = (pre * cdf).astype(BF)
-    density = jnp.exp(pre * pre * -0.5) * 0.3989422804014327
-    pre_grad = (grad * (cdf + pre * density)).astype(BF)
-    if first:
-        acc_ref[...] = dot(active, wf[...], NT)
-        t_ref[...] = dot(pre_grad, wi[...], NT)
-    else:
-        acc_ref[...] = acc_in[...] + dot(active, wf[...], NT)
-        t_ref[...] = t_in[...] + dot(pre_grad, wi[...], NT)
-    gi[...] = dot(nt_ref[...], pre_grad, NN).astype(BF)
-    deal_out(grads_ref, gi, place_ref, 0)
-    gf[...] = dot(gt_ref[...], active, NN).astype(BF)
-    deal_out(grads_ref, gf, place_ref, 1)
-
-
-def feed(place, normed, normed_t, back, back_t, sums, block, grads):
-    rows = normed.shape[0]
+    half = n_refs[0].shape[0]
+    for i in range(2):
+        rows = pl.ds(i * half, half)
+        pre = dot(n_refs[i][...], wi[...], NN)
+        grad = dot(g_refs[i][...], wf[...], NN)
+        cdf = 0.5 * (1.0 + lax.erf(pre * 0.7071067811865476))
+        density = jnp.exp(pre * pre * -0.5) * 0.3989422804014327
+        act_here = (pre * cdf).astype(BF)
+        grad_here = (grad * (cdf + pre * density)).astype(BF)
+        active[rows, :] = act_here
+        pre_grad[rows, :] = grad_here
+        acc, t = dot(act_here, wf[...], NT), dot(grad_here, wi[...], NT)
+        if not first:
+            acc, t = acc_ins[i][...] + acc, t_ins[i][...] + t
+        acc_refs[i][...] = acc.astype(acc_refs[i].dtype)
+        t_refs[i][...] = t.astype(t_refs[i].dtype)
+    for w, (out, turned, value) in enumerate(((gi, nt_refs, pre_grad), (gf, gt_refs, active))):
+        parts = [dot(turned[i][...], value[pl.ds(i * half, half), :], NN) for i in range(2)]
+        out[...] = (parts[0] + parts[1]).astype(BF)
+        if split:
+            near_ref, far_refs = out_refs[0], out_refs[1:3]
+            cut = near_ref.shape[1]
+            for count in range(4 * cut):
+                y, z = count // (2 * cut), count % (2 * cut)
+                start = pl.multiple_of(place_ref[5 + count], 16)
+                piece = out[pl.ds(start, near_ref.shape[3]), :]
+                if z < cut:
+                    near_ref[y, z, w] = piece
+                else:
+                    far_refs[y][z - cut, w] = piece
+        else:
+            out_refs[0][0, 0, 0, w] = out[...]
+
+
+def feed(place, normed, normed_t, back, back_t, sums, block, depth, shard_rows):
     block, indices = block
+    rows = normed[0].shape[0]
     n = len(block)
     first = sums is None
+    split = shard_rows % 16 == 0
+    if split:
+        part = (depth // 2, 2, shard_rows, D)
+        shapes = [shape_of((2,) + part, BF)] + [shape_of(part, BF)] * 2
+    else:
+        shapes = [grads_shape(depth, 2, shard_rows, D)]
+    sent = F32 if first else BF
     outs = pl.pallas_call(
-        functools.partial(feed_kernel, indices, first),
-        in_specs=[in_smem] + [in_vmem] * (4 + n + (0 if first else 2)),
-        out_specs=[in_vmem] * 3,
-        out_shape=[shape_of((rows, D), F32)] * 2 + [grads],
-        scratch_shapes=[pltpu.VMEM((D, D), BF)] * 4,
-        input_output_aliases={} if first else {5: 0, 6: 1},
-        compiler_params=params(14),
-        cost_estimate=cost(2 * 6 * rows * D * D, 15e6, 2 * rows * D),
+        functools.partial(feed_kernel, indices, first, split),
+        in_specs=[in_smem] + [in_vmem] * (8 + n + (0 if first else 4)),
+        out_specs=[in_vmem] * (4 + len(shapes)),
+        out_shape=[shape_of((rows, D), t) for t in (F32, sent, F32, sent)] + shapes,
+        scratch_shapes=[pltpu.VMEM((D, D), BF)] * 4 + [pltpu.VMEM((2 * rows, D), BF)] * 2,
+        compiler_params=params(FEED_MIB),
+        cost_estimate=cost(1, 1),
         name="feed",
-    )(place, normed, normed_t, back, back_t, *(sums or ()), *block)
-    return (outs[0], outs[1]), outs[2]
-
-
-def turn_kernel(mid_ref, acc_ref, t_ref, back_ref, gain_ref, keep_ref, send_ref, grad_ref, low_ref, gain_grad_ref):
-    mid = mid_ref[...]
-    out = (mid + acc_ref[...]).astype(BF)
-    half = keep_ref.shape[0]
-    keep_ref[...], send_ref[...] = out[:half], out[half:]
-    grad, gain_grad = rms_back(mid, gain_ref[1:2].astype(F32), t_ref[...])
+    )(place, *normed, *normed_t, *back, *back_t, *(sums or ()), *block)
+    if split:
+        return outs[:4], outs[4:]
+    whole = by_place(outs[4], depth, shard_rows)
+    return outs[:4], [whole[:, 0], whole[0, 1], whole[1, 1]]
+
+
+def turn_kernel(mid_ref, t_ref, t_came_ref, back_ref, gain_ref, grad_ref, low_ref, gain_grad_ref):
+    t = t_ref[...] + t_came_ref[...].astype(F32)
+    grad, gain_grad = rms_back(mid_ref[...], gain_ref[1:2].astype(F32), t)
     gain_grad_ref[...] = gain_grad
     grad = back_ref[...].astype(F32) + grad
     grad_ref[...] = grad
     low_ref[...] = grad.astype(BF)
 
 
-def turn(mid, acc, t_acc, back, gain_low):
-    rows = mid.shape[0]
+def turn(mid, t_own, t_came, back, gain_low):
     return pl.pallas_call(
         turn_kernel,
         in_specs=[in_vmem] * 5,
-        out_specs=[in_vmem] * 5,
-        out_shape=[
-            shape_of((rows // 2, D), BF),
-            shape_of((rows // 2, D), BF),
-            shape_of((rows, D), F32),
-            shape_of((rows, D), BF),
-            shape_of((1, D), F32),
-        ],
+        out_specs=[in_vmem] * 3,
+        out_shape=[shape_of(mid.shape, F32), shape_of(mid.shape, BF), shape_of((1, D), F32)],
         compiler_params=params(12),
         cost_estimate=cost(1, 1),
         name="turn",
-    )(mid, acc, t_acc, back, gain_low)
+    )(mid, t_own, t_came, back, gain_low)
 
 
 def context_grad_kernel(indices, place_ref, own_ref, other_ref, *refs):
@@ -489,12 +504,17 @@
     g_ref,
     ctx_own_ref,
     ctx_other_ref,
-    p_ref,
+    p_in,
     heads_ref,
     bucket_ref,
     ds_ref,
     sums_ref,
+    p_ref,
+    sems,
 ):
+    copies = [pltpu.make_async_copy(p_in.at[h], p_ref.at[h], sems.at[h]) for h in range(GROUP)]
+    for c in copies:
+        c.start()
     rows = g_ref.shape[0]
     step = 128
     lane = lax.broadcasted_iota(jnp.int32, (1, WIDTH), 1)
@@ -511,6 +531,7 @@
     total = [jnp.zeros((step, WIDTH), F32) for _ in range(rows // step)]
     key_grads, value_grads = [], []
     for h in range(GROUP):
+        copies[h].wait()
         inside = (lane >= h * DH) & (lane < (h + 1) * DH)
         for r in range(rows // step):
             span = slice(r * step, (r + 1) * step)
@@ -550,17 +571,19 @@
     rows = grads.shape[0]
     return pl.pallas_call(
         functools.partial(attend_back_kernel, r // 2),
-        in_specs=[in_smem] + [in_vmem] * 8,
+        in_specs=[in_smem] + [in_vmem] * 7 + [in_hbm],
         out_specs=[in_vmem] * 2,
         out_shape=[shape_of((rows, 3 * WIDTH), BF), shape_of((GROUP, NB, TILE), F32)],
         scratch_shapes=[
             pltpu.VMEM((GROUP, rows, rows), BF),
             pltpu.VMEM((GROUP, 5, TILE, TILE), F32),
+            pltpu.VMEM((GROUP, rows, rows), BF),
+            pltpu.SemaphoreType.DMA((GROUP,)),
         ],
-        compiler_params=params(22),
+        compiler_params=params(24),
         cost_estimate=cost(1, 1),
         name="attend_back",
-    )(place, *q, *kv, grads, *ctx, prob)
+    )(place, *q, *kv, grads, *ctx, keep_hbm(prob))
 
 
 def project_back_kernel(indices, split, place_ref, nt_own_ref, nt_other_ref, low_t_ref, *refs):
@@ -594,7 +617,7 @@
         for i in range(2):
             term = dot(ends[i], whole[b, :, 0:576], NT)
             totals[i] = term if b == 0 else totals[i] + term
-    own_ref[...], send_ref[...] = totals
+    own_ref[...], send_ref[...] = totals[0], totals[1].astype(BF)
 
 
 def project_back(place, normed_t, low_t, heads, ctx, blocks, depth, shard_rows):
@@ -609,7 +632,7 @@
         functools.partial(project_back_kernel, [i for _, i in blocks], split),
         in_specs=[in_smem] + [in_vmem] * (9 + 2 * n),
         out_specs=[in_vmem] * (2 + len(shapes)),
-        out_shape=[shape_of((half, D), F32)] * 2 + shapes,
+        out_shape=[shape_of((half, D), F32), shape_of((half, D), BF)] + shapes,
         scratch_shapes=[pltpu.VMEM((2, D, D), BF)] * 2,
         compiler_params=params(16),
         cost_estimate=cost(1, 1),
@@ -619,53 +642,36 @@
         return outs
     both = [by_place(v, depth, shard_rows) for v in outs[2:]]
     fars = [jnp.stack([v[y, 1] for v in both]) for y in range(2)]
-    return [outs[0], outs[1], both[0][:, 0], both[1][:, 0], *fars]
+    return [*outs[:2], both[0][:, 0], both[1][:, 0], *fars]
 
 
 def add(a, b):
     return (a.astype(F32) + b.astype(F32)).astype(BF)
 
 
-def merge_core_kernel(*refs):
-    near0_ref, near1_ref, far0_ref, far1_ref = refs[4:]
-    for i, near_ref in enumerate((near0_ref, near1_ref)):
-        a_ref, b_ref = refs[2 * i : 2 * i + 2]
-        for y, far_ref in enumerate((far0_ref, far1_ref)):
-            near_ref[y] = add(a_ref[y, 0], b_ref[y, 0])
-            far_ref[i] = add(a_ref[y, 1], b_ref[y, 1])
-
-
-def merge_core(grads0, came0, grads2, came2):
-    part = shape_of(grads0.shape[:1] + grads0.shape[2:], BF)
-    return pl.pallas_call(
-        merge_core_kernel,
-        in_specs=[in_vmem] * 4,
+def merge_half_kernel(n, near_ref, near_came_ref, *refs):
+    far_refs, far_came_refs, (y0_ref, y1_ref, x0_ref, x1_ref) = refs[:n], refs[n : 2 * n], refs[2 * n :]
+    y0_ref[...] = add(near_ref[0], near_came_ref[0])
+    y1_ref[...] = add(near_ref[1], near_came_ref[1])
+    for i, out_ref in enumerate((x0_ref, x1_ref)):
+        if n == 1:
+            out_ref[...] = add(far_refs[0][i], far_came_refs[0][i])
+        else:
+            out_ref[...] = add(far_refs[i][...], far_came_refs[i][...])
+
+
+def merge_half(near, near_came, far, far_came):
+    part = shape_of(near.shape[1:], BF)
+    n = len(far)
+    return pl.pallas_call(
+        functools.partial(merge_half_kernel, n),
+        in_specs=[in_vmem] * (2 + 2 * n),
         out_specs=[in_vmem] * 4,
         out_shape=[part] * 4,
         compiler_params=params(MERGE_MIB),
         cost_estimate=cost(1, 1),
-        name="merge_core",
-    )(grads0, came0, grads2, came2)
-
-
-def merge_half_kernel(near_ref, near_came_ref, far_ref, far_came_ref, y0_ref, y1_ref, x0_ref, x1_ref):
-    y0_ref[...] = add(near_ref[0], near_came_ref[0])
-    y1_ref[...] = add(near_ref[1], near_came_ref[1])
-    x0_ref[...] = add(far_ref[0], far_came_ref[0])
-    x1_ref[...] = add(far_ref[1], far_came_ref[1])
-
-
-def merge_half(near, near_came, far, far_came):
-    part = shape_of(near.shape[1:], BF)
-    return pl.pallas_call(
-        merge_half_kernel,
-        in_specs=[in_vmem] * 4,
-        out_specs=[in_vmem] * 4,
-        out_shape=[part] * 4,
-        compiler_params=params(MERGE_MIB),
-        cost_estimate=cost(1, 1),
         name="merge_half",
-    )(near, near_came, far, far_came)
+    )(near, near_came, *far, *far_came)
 
 
 def merge_last_kernel(near_ref, near_came_ref, far_ref, far_came_ref, own_ref, *outs):
@@ -753,7 +759,7 @@
     )(place, keep_hbm(inputs), keep_hbm(cotangent))
 
 
-def join_rows_kernel(place_ref, keep_in_ref, keep_back_ref, came_ref, in_ref, back_ref, sems):
+def join_rows_kernel(place_ref, keep_in_ref, keep_back_ref, came_ref, in_ref, back_ref, back_t_ref, sems):
     here = place_ref[0]
     half = came_ref.shape[1]
     pairs = ((keep_in_ref, in_ref), (keep_back_ref, back_ref))
@@ -767,6 +773,7 @@
         ref[pl.ds(half, half), :] = came_ref[i]
     for c in copies:
         c.wait()
+    back_t_ref[...] = back_ref[...].T
 
 
 def join_rows(place, inputs, cotangent, came):
@@ -774,8 +781,8 @@
     return pl.pallas_call(
         join_rows_kernel,
         in_specs=[in_smem] + [in_hbm] * 2 + [in_vmem],
-        out_specs=[in_vmem] * 2,
-        out_shape=[rows] * 2,
+        out_specs=[in_vmem] * 3,
+        out_shape=[rows] * 2 + [shape_of((rows.shape[1], rows.shape[0]), BF)],
         scratch_shapes=[pltpu.SemaphoreType.DMA((2,))],
         compiler_params=params(MERGE_MIB),
         cost_estimate=cost(1, 1),
@@ -859,27 +866,41 @@
     )(place, *keep, came)
 
 
-def finish_kernel(x_ref, gain_ref, t_ref, t_came_ref, mid_grad_ref, out_send_ref, keep_ref, send_ref, gain_grad_ref):
-    t = t_ref[...] + t_came_ref[...]
+def finish_kernel(
+    x_ref,
+    gain_ref,
+    t_ref,
+    t_came_ref,
+    mid_grad_ref,
+    mid_ref,
+    acc_ref,
+    acc_came_ref,
+    out_keep_ref,
+    in_keep_ref,
+    send_ref,
+    gain_grad_ref,
+):
+    t = t_ref[...] + t_came_ref[...].astype(F32)
     grad, gain_grad = rms_back(x_ref[...].astype(F32), gain_ref[0:1].astype(F32), t)
-    out = (mid_grad_ref[...] + grad).astype(BF)
-    half = keep_ref.shape[0]
-    keep_ref[...] = out[:half]
-    send_ref[0], send_ref[1] = out_send_ref[...], out[half:]
     gain_grad_ref[...] = gain_grad
-
-
-def finish(rows_in, gain_low, t_own, t_came, mid_grad, out_send):
-    part = out_send.shape
+    out = (mid_ref[...] + (acc_ref[...] + acc_came_ref[...].astype(F32))).astype(BF)
+    grad = (mid_grad_ref[...] + grad).astype(BF)
+    half = out_keep_ref.shape[0]
+    out_keep_ref[...], in_keep_ref[...] = out[:half], grad[:half]
+    send_ref[0], send_ref[1] = out[half:], grad[half:]
+
+
+def finish(rows_in, gain_low, t_own, t_came, mid_grad, mid, acc_own, acc_came):
+    part = (rows_in.shape[0] // 2, D)
     return pl.pallas_call(
         finish_kernel,
-        in_specs=[in_vmem] * 6,
-        out_specs=[in_vmem] * 3,
-        out_shape=[shape_of(part, BF), shape_of((2,) + part, BF), shape_of((1, D), F32)],
-        compiler_params=params(12),
+        in_specs=[in_vmem] * 8,
+        out_specs=[in_vmem] * 4,
+        out_shape=[shape_of(part, BF)] * 2 + [shape_of((2,) + part, BF), shape_of((1, D), F32)],
+        compiler_params=params(14),
         cost_estimate=cost(1, 1),
         name="finish",
-    )(rows_in, gain_low, t_own, t_came, mid_grad, out_send)
+    )(rows_in, gain_low, t_own, t_came, mid_grad, mid, acc_own, acc_came)
 
 
 def small_kernel(place_ref, one_ref, two_ref, *refs):
@@ -1025,7 +1046,6 @@
         starts = [jnp.zeros((), jnp.int32)] * 2
     place = jnp.stack([v.astype(jnp.int32) for v in [x, core, mp, lengths[0], lengths[1]] + starts])
     cut = depth // 2
-    feed_shape = grads_shape(depth, 2, shard_rows, D)
 
     attn_low = cast_attn(attn_weights)
     attn_z = [swap_z(attn_low, k) for k in range(1, depth)]
@@ -1042,13 +1062,15 @@
     near, far = line_up([near, near_x], 2), line_up([far, far_y], 2)
     near_y, far_x = swap_y(near), swap_x(far)
     ring.append(shift_z(ring[-1]))
-    rows_in, back = join_rows(place, inputs, cotangent, rows_came)
-    rows_in, back, gain_low, ring, near, far = fence(rows_in, back, norm_gains, ring, near, far)
+    rows_in, back, back_t = join_rows(place, inputs, cotangent, rows_came)
+    rows_in, back, back_t, gain_low, ring, near, far = fence(
+        rows_in, back, back_t, norm_gains, ring, near, far
+    )
     while len(ring) < depth:
         ring.append(shift_z(ring[-1]))
     gains = join_gains(gather_gains(gain_low))
-    near_y, far_x, near, far, rows_in, back, gains, ring = fence(
-        near_y, far_x, near, far, rows_in, back, gains, ring
+    near_y, far_x, near, far, rows_in, back, back_t, gains, ring = fence(
+        near_y, far_x, near, far, rows_in, back, back_t, gains, ring
     )
 
     def attn_block(near, far, near_y, far_x, i):
@@ -1063,8 +1085,16 @@
     q_own, kv_own, normed_t, ffn_here = fence(q_own, kv_own, normed_t, ffn_here)
     q_own, rows_other = fence(q_own, rows_other)
     q_other, kv_other, other_t = project(place, rows_other, gains, mine, True)
-    q, kv, normed_t, near, far, near_y, far_x = fence(
-        [q_own, q_other], [kv_own, kv_other], [normed_t, other_t], near, far, near_y, far_x
+    q, kv, normed_t, near, far, near_y, far_x, back, back_t = fence(
+        [q_own, q_other],
+        [kv_own, kv_other],
+        [normed_t, other_t],
+        near,
+        far,
+        near_y,
+        far_x,
+        back,
+        back_t,
     )
     across = [swap_core(v) for v in (near, far, near_y, far_x)]
     ctx, ctx_send, ctx_came, prob = {}, {}, {}, {}
@@ -1072,61 +1102,65 @@
         ctx[r], ctx_send[r], prob[r] = attend(place, q, kv, bias, r)
         ctx, ctx_send, prob, q, ffn_here = fence(ctx, ctx_send, prob, q, ffn_here)
         ctx_came[r] = swap_core(ctx_send[r])
-    ffn_c = swap_core(ffn_here)
+    back_other, back_other_t = swap_core(back), swap_core(back_t)
     ctx, ctx_came, across = fence(ctx, ctx_came, across)
     theirs = [attn_block(*across, i) for i in range(2)]
-    mid, normed_two, normed_two_t, back_t = middle(
+    mid, normed_two, normed_two_t = middle(
         place,
         rows_in,
         gains,
-        back,
         [ctx[0], ctx_came[0], ctx[2], ctx_came[2]],
         [mine[0], theirs[0], mine[1], theirs[1]],
     )
-    mid, normed_two, normed_two_t, back_t = fence(mid, normed_two, normed_two_t, back_t)
+    mid, normed_two, normed_two_t = fence(mid, normed_two, normed_two_t)
+    two_other, two_other_t = swap_core(normed_two), swap_core(normed_two_t)
     mid, ffn_x, ffn_y = fence(mid, ffn_x, ffn_y)
     ffn_near_xy, ffn_far_xy = swap_y(ffn_x[0]), swap_x(ffn_y[1])
-    ffn_yc, ffn_xc = swap_core(ffn_y), swap_core(ffn_x)
-    grads = {}
-
-    def feed_at(r, sums, by_y):
-        sums, out = feed(
-            place, normed_two, normed_two_t, back, back_t, sums, block_views(by_y, True), feed_shape
+    mid, two_other, two_other_t, back_other, back_other_t = fence(
+        mid, two_other, two_other_t, back_other, back_other_t
+    )
+
+    def feed_at(sums, by_y):
+        return feed(
+            place,
+            (normed_two, two_other),
+            (normed_two_t, two_other_t),
+            (back, back_other),
+            (back_t, back_other_t),
+            sums,
+            block_views(by_y, True),
+            depth,
+            shard_rows,
         )
-        grads[r] = by_place(out, depth, shard_rows)
-        return sums
-
-    sums = feed_at(0, None, [[(ffn_here, 0), (ffn_here, 1)], [(ffn_y, 0), (ffn_y, 1)]])
-    sums, grads, ffn_yc, ffn_xc, ffn_c = fence(sums, grads, ffn_yc, ffn_xc, ffn_c)
-    sums = feed_at(1, sums, [[(ffn_c, 0), (ffn_c, 1)], [(ffn_yc, 0), (ffn_yc, 1)]])
-    sums, grads = fence(sums, grads)
-    sums, ffn_near_xy, ffn_far_xy = fence(sums, ffn_near_xy, ffn_far_xy)
-    ffn_near_xyc, ffn_far_xyc = swap_core(ffn_near_xy), swap_core(ffn_far_xy)
-    sums = feed_at(2, sums, [[(ffn_x, 0), (ffn_x, 1)], [ffn_near_xy, ffn_far_xy]])
-    sums, grads = fence(sums, grads)
-    sums, ffn_near_xyc, ffn_far_xyc, grads = fence(sums, ffn_near_xyc, ffn_far_xyc, grads)
-    came = {0: swap_core(grads[1])}
-    sums = feed_at(3, sums, [[(ffn_xc, 0), (ffn_xc, 1)], [ffn_near_xyc, ffn_far_xyc]])
-    sums, grads = fence(sums, grads)
-    came[2] = swap_core(grads[3])
-    out_keep, out_send, mid_grad, mid_low, gain_two_grad = turn(mid, sums[0], sums[1], back, gains)
-    mid_grad, mid_low, out_keep, out_send = fence(mid_grad, mid_low, out_keep, out_send)
+
+    sums, outs = feed_at(None, [[(ffn_here, 0), (ffn_here, 1)], [(ffn_y, 0), (ffn_y, 1)]])
+    near0, far00, far01 = outs
+    sums, near0, far00, far01 = fence(sums, near0, far00, far01)
+    sums, ffn_near_xy, ffn_far_xy, far01 = fence(sums, ffn_near_xy, ffn_far_xy, far01)
+    far01_y = swap_y(far01)
+    sums, outs = feed_at(sums, [[(ffn_x, 0), (ffn_x, 1)], [ffn_near_xy, ffn_far_xy]])
+    near1, far10, far11 = outs
+    (acc_own, acc_send, t_own, t_send), near1, far10, far11 = fence(sums, near1, far10, far11)
+    near1_x, far11_y = swap_x(near1), swap_y(far11)
+    t_came = swap_core(t_send)
+    acc_came = swap_core(acc_send)
+    t_own, t_came = fence(t_own, t_came)
+    mid_grad, mid_low, gain_two_grad = turn(mid, t_own, t_came, back, gains)
+    mid_grad, mid_low = fence(mid_grad, mid_low)
     low_other = swap_core(mid_low)
-    mid_low, low_other = fence(mid_low, low_other)
+    mid_low, low_other, acc_came = fence(mid_low, low_other, acc_came)
     cg0, cg2, low_t = context_grads(place, mid_low, low_other, mine)
     cg0, cg2, low_t = fence(cg0, cg2, low_t)
-    cg0, came, grads = fence(cg0, came, grads)
-    near0, near1, far0, far1 = merge_core(grads[0], came[0], grads[2], came[2])
-    near1_x, far1_y = swap_x(near1), swap_y(far1)
-    cg0, near0, far0 = fence(cg0, near0, far0)
 
     heads, lines = {}, {}
     for r, cg in ((0, cg0), (2, cg2)):
         cg, heads = fence(cg, heads)
         heads[r], lines[r] = attend_back(place, q, kv, cg, (ctx[r], ctx_send[r]), prob[r], r)
         heads, lines = fence(heads, lines)
-    heads, near1_x, far1_y, out_send = fence(heads, near1_x, far1_y, out_send)
-    ffn_y0, ffn_y1, ffn_x0, ffn_x1 = merge_half(near0, near1_x, far0, far1_y)
+    heads, near1_x, far01_y, far11_y = fence(heads, near1_x, far01_y, far11_y)
+    ffn_y0, ffn_y1, ffn_x0, ffn_x1 = merge_half(
+        near0, near1_x, (far00, far10), (far01_y, far11_y)
+    )
     ffn_y1, ffn_x1 = swap_y(ffn_y1), swap_x(ffn_x1)
     heads, ffn_y0, ffn_x0 = fence(heads, ffn_y0, ffn_x0)
     t_own, t_send, near0, near1, far0, far1 = project_back(
@@ -1141,19 +1175,21 @@
     )
     t_own, t_send, near0, near1, far0, far1 = fence(t_own, t_send, near0, near1, far0, far1)
     near1_x, far1_y = swap_x(near1), swap_y(far1)
-    t_own, t_send, ffn_y1, ffn_x1 = fence(t_own, t_send, ffn_y1, ffn_x1)
+    t_came = swap_core(t_send)
+    t_own, ffn_y1, ffn_x1 = fence(t_own, ffn_y1, ffn_x1)
     ffn_own, *ffn_far_own = merge_last(ffn_y0, ffn_y1, ffn_x0, ffn_x1)
     soon = [k for k in range(1, depth) if k != cut]
     ffn_back = [swap_z(ffn_far_own[k - 1], k) for k in soon]
-    t_came = swap_core(t_send)
     ffn_own, ffn_far_own, t_came = fence(ffn_own, ffn_far_own, t_came)
-    in_keep, send_last, gain_one_grad = finish(rows_in, gains, t_own, t_came, mid_grad, out_send)
+    out_keep, in_keep, send_last, gain_one_grad = finish(
+        rows_in, gains, t_own, t_came, mid_grad, mid, acc_own, acc_came
+    )
     small = small_sums(place, gain_one_grad, gain_two_grad, [lines[0], lines[2]])
     in_keep, send_last, small, ffn_own, near0, far0, ffn_far_own = fence(
         in_keep, send_last, small, ffn_own, near0, far0, ffn_far_own
     )
     near1_x, far1_y, small, ffn_back = fence(near1_x, far1_y, small, ffn_back)
-    attn_y0, attn_y1, attn_x0, attn_x1 = merge_half(near0, near1_x, far0, far1_y)
+    attn_y0, attn_y1, attn_x0, attn_x1 = merge_half(near0, near1_x, (far0,), (far1_y,))
     attn_y1, attn_x1, ffn_back = fence(attn_y1, attn_x1, ffn_back)
     attn_y1, attn_x1 = swap_y(attn_y1), swap_x(attn_x1)
     ffn_back += [swap_z(ffn_far_own[cut - 1], cut)]

time: 247 us -> 233 us (0.943)
  waiting for transfers between devices: 95.5 us -> 69.8 us
  starting transfers between devices: 38.8 us -> 50 us
    ppermute x8 -> x9, waiting for transfers between devices: 24.9 us -> 14.6 us  [swap_y(): return lax.ppermute(v, 'dp', [(i, i ^ 1) for i in range(n)])]
    ppermute x10, waiting for transfers between devices: 20.1 us -> 10.6 us  [swap_x(): return lax.ppermute(v, 'mp', [(i, i ^ 2) for i in range(4)])]
    ppermute x9, starting transfers between devices: 11.6 us -> 19.2 us  [swap_z(): return lax.ppermute(v, 'dp', [(i, i ^ 2 * k) for i in range(n)])]
    ppermute x16 -> x15, waiting for transfers between devices: 10.5 us -> 5.48 us  [swap_core(): return lax.ppermute(v, 'mp', [(i, i ^ 1) for i in range(4)])]
    pallas_call x2, Pallas kernels: 23.1 us -> 26.1 us  [attend_back(): pl.pallas_call(functools.partial(attend_back_kernel, r // 2), in_specs=[i...]
    pallas_call x8 -> x5, Pallas kernels: 22.1 us -> 19.7 us  [the longest x2 17.3 us: feed(): pl.pallas_call(functools.partial(feed_kernel, indices, first, split), in_...]
    ppermute x8 -> x9, starting transfers between devices: 7.5 us -> 9.9 us  [swap_y(): return lax.ppermute(v, 'dp', [(i, i ^ 1) for i in range(n)])]
  transfers between devices with their start and end apart: 47 -> 47, of which waited for: 28 -> 24; matrix products, arithmetic and copies ran while one was open for 0% -> 0% of each run, Pallas kernels for 33% -> 34%
where the time goes in v6:
time: 233 us; the launch traced here: 230 us
  Pallas kernels  95.7 us (41%)
  waiting for transfers between devices  69.8 us (30%)
  starting transfers between devices  50 us (21%)
  blocking collectives  11.4 us (5%)
    pallas_call x2, Pallas kernels, attend_back(): pl.pallas_call(functools.partial(attend_back_kernel, r // 2), in_specs=[i...  26.1 us
    ppermute x9, waiting for transfers between devices, swap_z(): return lax.ppermute(v, 'dp', [(i, i ^ 2 * k) for i in range(n)])  23.9 us
    ppermute x9, starting transfers between devices, swap_z(): return lax.ppermute(v, 'dp', [(i, i ^ 2 * k) for i in range(n)])  19.2 us
    pallas_call x2, Pallas kernels, feed(): pl.pallas_call(functools.partial(feed_kernel, indices, first, split), in_...  17.3 us
    pallas_call x2, Pallas kernels, attend(): pl.pallas_call(functools.partial(attend_kernel, r // 2, r), in_specs=[in_...  16.2 us
    ppermute x10, starting transfers between devices, swap_x(): return lax.ppermute(v, 'mp', [(i, i ^ 2) for i in range(4)])  14.9 us
    ppermute x9, waiting for transfers between devices, swap_y(): return lax.ppermute(v, 'dp', [(i, i ^ 1) for i in range(n)])  14.6 us
    all_to_all x1, blocking collectives, gather_gains(): lax.all_to_all(jnp.broadcast_to(low[None], (n,) + low.shape), 'dp', 0, 0)  11.4 us
  transfers between devices with their start and end apart: 47, of which 24 were waited for; matrix products, arithmetic and copies ran while one was open for 0% of the time, Pallas kernels for 34%

profile of v6, /device:TPU:0, one launch (start us, length us, event | category | flops | bytes accessed | tf_op | source)
XLA Modules:
  0.0 230.0 jit_solution(16265264655906043734)
XLA Ops:
  1.6 1.7 sort_rows.1
  3.3 3.0 %collective-permute-start.5 = (bf16[2,256,768]{2,1,0:T(8,128)(2,1)S(1)}, bf16[2,256,768]{2,1,0:T(8,128)(2,1)S(1)}, u32[]{:S(2)}, u32[]{:S(2)}) collective-permute-start(bf16[2,256,768]{2,1,0:T(8,128)(2,1)S(1)} %sort_rows.1), channel_id=1, source_target_pairs={{0,2},{1,3},{2,0},{3,1},{4,6},{5,7},{6,4},{7,5},{8,10},{9,11},{10,... | collective-permute-start | bytes 2359304 | tf_op jit(solution)/shard_map/ppermute | solution.py:84
  6.4 3.7 %collective-permute-start.2 = (bf16[1,96,768]{2,1,0:T(8,128)(2,1)S(1)}, bf16[1,96,768]{2,1,0:T(8,128)(2,1)S(1)}, u32[]{:S(2)}, u32[]{:S(2)}) collective-permute-start(bf16[1,96,768]{2,1,0:T(8,128)(2,1)S(1)} %cast_attn.1.refs_0_), channel_id=1, source_target_pairs={{0,24},{4,28},{8,16},{12,20},{16,8},{20,12},{24,0},{28,4},{1,25},{... | collective-permute-start | bytes 442376 | tf_op jit(solution)/shard_map/ppermute | solution.py:94
  10.9 5.2 %bias_tiles.1.bias_ref = f32[4,3,5,128,128]{4,3,2,1,0:T(8,128)S(1)} custom-call(s32[21]{0:T(128)S(1)} %stack.79.place_ref, f32[12,32]{1,0:T(8,128)S(1)} %copy-done.3), custom_call_target="tpu_custom_call" | custom-call | flops 1000 | bytes 1000 | tf_op jit(solution)/shard_map/bias_tiles/pallas_call | solution.py:193
  16.1 6.1 %collective-permute-done.1.refs_0_ = bf16[1,96,768]{2,1,0:T(8,128)(2,1)S(1)} collective-permute-done((bf16[1,96,768]{2,1,0:T(8,128)(2,1)S(1)}, bf16[1,96,768]{2,1,0:T(8,128)(2,1)S(1)}, u32[]{:S(2)}, u32[]{:S(2)}) %collective-permute-start.1) | collective-permute-done | bytes 147488 | tf_op jit(solution)/shard_map/ppermute | solution.py:94
  22.3 1.6 collective-permute-start.4
  24.5 5.9 %collective-permute-done.4.refs_1_ = bf16[2,1,96,768]{3,2,1,0:T(8,128)(2,1)S(1)} collective-permute-done((bf16[2,1,96,768]{3,2,1,0:T(8,128)(2,1)S(1)}, bf16[2,1,96,768]{3,2,1,0:T(8,128)(2,1)S(1)}, u32[]{:S(2)}, u32[]{:S(2)}) %collective-permute-start.4) | collective-permute-done | bytes 294944 | tf_op jit(solution)/shard_map/ppermute | solution.py:89
  31.7 2.1 collective-permute-done.6.refs_1_
  33.9 1.6 collective-permute-start.8
  36.0 1.9 join_rows.1
  38.0 4.4 %collective-permute-done.9.refs_0_ = bf16[2,96,768]{2,1,0:T(8,128)(2,1)S(1)} collective-permute-done((bf16[2,96,768]{2,1,0:T(8,128)(2,1)S(1)}, bf16[2,96,768]{2,1,0:T(8,128)(2,1)S(1)}, u32[]{:S(2)}, u32[]{:S(2)}) %collective-permute-start.9) | collective-permute-done | bytes 294944 | tf_op jit(solution)/shard_map/ppermute | solution.py:99
  42.3 11.4 %all_to_all.10.g_ref = bf16[8,2,96]{2,1,0:T(2,128)(2,1)S(1)} all-to-all(bf16[8,2,96]{2,1,0:T(2,128)(2,1)S(1)} %broadcast_in_dim.4), channel_id=1, replica_groups=mesh['dp'=8,'mp'=4] {'dp'}, dimensions={0} | all-to-all | bytes 6144 | tf_op jit(solution)/shard_map/all_to_all | solution.py:114
  54.1 2.2 project.2
  56.3 2.2 project.3
  59.7 1.5 collective-permute-start.18
  61.2 8.0 %attend.2 = (bf16[512,256]{1,0:T(8,128)(2,1)S(1)}, bf16[512,256]{1,0:T(8,128)(2,1)S(1)}, bf16[3,1024,1024]{2,1,0:T(8,128)(2,1)}) custom-call(s32[21]{0:T(128)S(1)} %stack.79.place_ref, bf16[2,512,192]{2,1,0:T(8,128)(2,1)S(1)} %get-tuple-element.381.q_own_ref, bf16[2,512,192]{2,1,0:T(8,128)(2,1)S(1)} %get-tuple-element.382.q_other_ref, ...), custom_call_target="tpu_custom_call" | custom-call | flops 1000 | bytes 1000 | tf_op jit(solution)/shard_map/attend/pallas_call | solution.py:326
  69.7 8.2 %attend.3 = (bf16[512,256]{1,0:T(8,128)(2,1)S(1)}, bf16[512,256]{1,0:T(8,128)(2,1)S(1)}, bf16[3,1024,1024]{2,1,0:T(8,128)(2,1)}) custom-call(s32[21]{0:T(128)S(1)} %stack.79.place_ref, bf16[2,512,192]{2,1,0:T(8,128)(2,1)S(1)} %get-tuple-element.381.q_own_ref, bf16[2,512,192]{2,1,0:T(8,128)(2,1)S(1)} %get-tuple-element.382.q_other_ref, ...), custom_call_target="tpu_custom_call" | custom-call | flops 1000 | bytes 1000 | tf_op jit(solution)/shard_map/attend/pallas_call | solution.py:326
  82.4 2.1 middle.1
  84.5 2.6 %collective-permute-done.19.refs_10_.refs_11_ = bf16[2,2,2,96,768]{4,3,2,1,0:T(8,128)(2,1)S(1)} collective-permute-done((bf16[2,2,2,96,768]{4,3,2,1,0:T(8,128)(2,1)S(1)}, bf16[2,2,2,96,768]{4,3,2,1,0:T(8,128)(2,1)S(1)}, u32[]{:S(2)}, u32[]{:S(2)}) %collective-permute-start.19) | collective-permute-done | bytes 1179680 | tf_op jit(solution)/shard_map/ppermute | solution.py:89
  87.4 1.5 collective-permute-start.24
  89.5 1.6 collective-permute-start.25
  92.3 8.5 %feed.2 = (f32[512,768]{1,0:T(8,128)S(1)}, f32[512,768]{1,0:T(8,128)S(1)}, f32[512,768]{1,0:T(8,128)S(1)}, f32[512,768]{1,0:T(8,128)S(1)}, bf16[2,2,2,96,768]{4,...) custom-call(s32[21]{0:T(128)S(1)} %stack.79.place_ref, ...), custom_call_target="tpu_custom_call" | custom-call | flops 1000 | bytes 1000 | tf_op jit(solution)/shard_map/feed/pallas_call | solution.py:432
  101.7 3.1 %collective-permute-done.25.refs_15_ = bf16[2,2,96,768]{3,2,1,0:T(8,128)(2,1)S(1)} collective-permute-done((bf16[2,2,96,768]{3,2,1,0:T(8,128)(2,1)S(1)}, bf16[2,2,96,768]{3,2,1,0:T(8,128)(2,1)S(1)}, u32[]{:S(2)}, u32[]{:S(2)}) %collective-permute-start.25) | collective-permute-done | bytes 589856 | tf_op jit(solution)/shard_map/ppermute | solution.py:84
  104.8 8.8 %feed.3 = (f32[512,768]{1,0:T(8,128)S(1)}, bf16[512,768]{1,0:T(8,128)(2,1)S(1)}, f32[512,768]{1,0:T(8,128)S(1)}, bf16[512,768]{1,0:T(8,128)(2,1)S(1)}, bf16[2,2,...) custom-call(s32[21]{0:T(128)S(1)} %stack.79.place_ref, ...), custom_call_target="tpu_custom_call" | custom-call | flops 1000 | bytes 1000 | tf_op jit(solution)/shard_map/feed/pallas_call | solution.py:432
  113.7 1.5 collective-permute-start.29
  117.8 1.5 collective-permute-start.30
  119.4 1.7 context_grads.1
  121.1 13.2 %attend_back.2 = (bf16[1024,576]{1,0:T(8,128)(2,1)S(1)}, f32[3,32,128]{2,1,0:T(8,128)S(1)}) custom-call(s32[21]{0:T(128)S(1)} %stack.79.place_ref, bf16[2,512,192]{2,1,0:T(8,128)(2,1)S(1)} %get-tuple-element.381.q_own_ref, bf16[2,512,192]{2,1,0:T(8,128)(2,1)S(1)} %get-tuple-element.382.q_other_ref, bf16[2,512,384]{2,1,0:T(8,128)(2,1)S(1)} %get-tuple-element.313.kv_own_ref, ...), custom_call_target="tpu_custom_call" | custom-call | flops 1000 | bytes 1000 | tf_op jit(solution)/shard_map/attend_back/pallas_call | solution.py:572
  134.2 12.9 %attend_back.3 = (bf16[1024,576]{1,0:T(8,128)(2,1)S(1)}, f32[3,32,128]{2,1,0:T(8,128)S(1)}) custom-call(s32[21]{0:T(128)S(1)} %stack.79.place_ref, bf16[2,512,192]{2,1,0:T(8,128)(2,1)S(1)} %get-tuple-element.381.q_own_ref, bf16[2,512,192]{2,1,0:T(8,128)(2,1)S(1)} %get-tuple-element.382.q_other_ref, bf16[2,512,384]{2,1,0:T(8,128)(2,1)S(1)} %get-tuple-element.313.kv_own_ref, ...), custom_call_target="tpu_custom_call" | custom-call | flops 1000 | bytes 1000 | tf_op jit(solution)/shard_map/attend_back/pallas_call | solution.py:572
  148.3 1.5 collective-permute-start.33
  149.8 6.6 %project_back.1 = (f32[512,768]{1,0:T(8,128)S(1)}, bf16[512,768]{1,0:T(8,128)(2,1)S(1)}, bf16[2,2,1,96,768]{4,3,2,1,0:T(8,128)(2,1)S(1)}, bf16[2,2,1,96,768]{4,3...) custom-call(s32[21]{0:T(128)S(1)} %stack.79.place_ref, ...), custom_call_target="tpu_custom_call" | custom-call | flops 1000 | bytes 1000 | tf_op jit(solution)/shard_map/project_back/pallas_call | solution.py:631
  157.1 1.5 collective-permute-start.36
  158.6 5.4 %collective-permute-done.32.near_came_ref = bf16[2,2,96,768]{3,2,1,0:T(8,128)(2,1)S(1)} collective-permute-done((bf16[2,2,96,768]{3,2,1,0:T(8,128)(2,1)S(1)}, bf16[2,2,96,768]{3,2,1,0:T(8,128)(2,1)S(1)}, u32[]{:S(2)}, u32[]{:S(2)}) %collective-permute-start.32) | collective-permute-done | bytes 589856 | tf_op jit(solution)/shard_map/ppermute | solution.py:89
  166.9 1.5 finish.1
  169.3 1.5 collective-permute-start.41
  170.8 5.3 %collective-permute-done.35.near_came_ref = bf16[2,2,1,96,768]{4,3,2,1,0:T(8,128)(2,1)S(1)} collective-permute-done((bf16[2,2,1,96,768]{4,3,2,1,0:T(8,128)(2,1)S(1)}, bf16[2,2,1,96,768]{4,3,2,1,0:T(8,128)(2,1)S(1)}, u32[]{:S(2)}, u32[]{:S(2)}) %collective-permute-start.35) | collective-permute-done | bytes 589856 | tf_op jit(solution)/shard_map/ppermute | solution.py:84
  176.5 4.8 %collective-permute-done.38.refs_1_ = bf16[2,96,768]{2,1,0:T(8,128)(2,1)S(1)} collective-permute-done((bf16[2,96,768]{2,1,0:T(8,128)(2,1)S(1)}, bf16[2,96,768]{2,1,0:T(8,128)(2,1)S(1)}, u32[]{:S(2)}, u32[]{:S(2)}) %collective-permute-start.38) | collective-permute-done | bytes 294944 | tf_op jit(solution)/shard_map/ppermute | solution.py:94
  181.5 1.5 collective-permute-start.39
  183.1 1.5 collective-permute-start.40
  184.6 7.3 %collective-permute-done.41.refs_2_ = bf16[2,96,768]{2,1,0:T(8,128)(2,1)S(1)} collective-permute-done((bf16[2,96,768]{2,1,0:T(8,128)(2,1)S(1)}, bf16[2,96,768]{2,1,0:T(8,128)(2,1)S(1)}, u32[]{:S(2)}, u32[]{:S(2)}) %collective-permute-start.41) | collective-permute-done | bytes 294944 | tf_op jit(solution)/shard_map/ppermute | solution.py:94
  191.9 1.5 collective-permute-start.45
  193.5 8.7 %collective-permute-start.42 = (bf16[1,96,768]{2,1,0:T(8,128)(2,1)S(1)}, bf16[1,96,768]{2,1,0:T(8,128)(2,1)S(1)}, u32[]{:S(2)}, u32[]{:S(2)}) collective-permute-start(bf16[1,96,768]{2,1,0:T(8,128)(2,1)S(1)} %get-tuple-element.471), channel_id=1, source_target_pairs={{0,8},{4,12},{8,0},{12,4},{16,24},{20,28},{24,16},{28,20},{1,9},{5... | collective-permute-start | bytes 442376 | tf_op jit(solution)/shard_map/ppermute | solution.py:94
  202.2 2.4 %collective-permute-start.44 = (bf16[1,96,768]{2,1,0:T(8,128)(2,1)S(1)}, bf16[1,96,768]{2,1,0:T(8,128)(2,1)S(1)}, u32[]{:S(2)}, u32[]{:S(2)}) collective-permute-start(bf16[1,96,768]{2,1,0:T(8,128)(2,1)S(1)} %get-tuple-element.473), channel_id=1, source_target_pairs={{0,24},{4,28},{8,16},{12,20},{16,8},{20,12},{24,0},{28,4},{1,25},{... | collective-permute-start | bytes 442376 | tf_op jit(solution)/shard_map/ppermute | solution.py:94
  205.7 5.2 %collective-permute-done.43.refs_1_ = bf16[1,96,768]{2,1,0:T(8,128)(2,1)S(1)} collective-permute-done((bf16[1,96,768]{2,1,0:T(8,128)(2,1)S(1)}, bf16[1,96,768]{2,1,0:T(8,128)(2,1)S(1)}, u32[]{:S(2)}, u32[]{:S(2)}) %collective-permute-start.43) | collective-permute-done | bytes 147488 | tf_op jit(solution)/shard_map/ppermute | solution.py:94
  212.0 2.9 %all-to-all-start.1 = ((f32[32,16,128]{2,1,0:T(8,128)}), f32[32,16,128]{2,1,0:T(8,128)S(1)}, u32[]{:S(2)}, u32[]{:S(2)}) async-start(f32[32,16,128]{2,1,0:T(8,128)} %broadcast_in_dim.5), calls=%async_computation.1 | async-start | bytes 524288 | tf_op jit(solution)/shard_map/all_to_all | solution.py:108
  214.9 1.8 place_rows.1
  216.7 8.8 %all-to-all-done.1.small_ref = f32[32,16,128]{2,1,0:T(8,128)S(1)} async-done(((f32[32,16,128]{2,1,0:T(8,128)}), f32[32,16,128]{2,1,0:T(8,128)S(1)}, u32[]{:S(2)}, u32[]{:S(2)}) %all-to-all-start.1) | async-done | bytes 262176 | tf_op jit(solution)/shard_map/all_to_all | solution.py:108
  225.5 4.2 %update.1 = (f32[1,1]{1,0:T(1,128)}, f32[4,96,192]{2,1,0:T(8,128)}, f32[2,96]{1,0:T(2,128)}, f32[12,32]{1,0:T(8,128)}, f32[4,96,192]{2,1,0:T(8,128)}, /*index=5*...) custom-call(s32[1]{0:T(128)} %bitcast.21.place_ref, ...), custom_call_target="tpu_custom_call" | custom-call | flops 1000 | bytes 1000 | tf_op jit(solution)/shard_map/update/pallas_call | solution.py:1002
  (98 shorter events, 25.0 us)
Async XLA Ops:
  3.3 30.5 %collective-permute-start.5 = (bf16[2,256,768]{2,1,0:T(8,128)(2,1)S(1)}, bf16[2,256,768]{2,1,0:T(8,128)(2,1)S(1)}, u32[]{:S(2)}, u32[]{:S(2)}) collective-permute-start(bf16[2,256,768]{2,1,0:T(8,128)(2,1)S(1)} %sort_rows.1), channel_id=1, source_target_pairs={{0,2},{1,3},{2,0},{3,1},{4,6},{5,7},{6,4},{7,5},{8,10},{9,11},{10,... | collective-permute-start | bytes 2359304 | tf_op jit(solution)/shard_map/ppermute | solution.py:84
  6.4 9.7 %collective-permute-start.2 = (bf16[1,96,768]{2,1,0:T(8,128)(2,1)S(1)}, bf16[1,96,768]{2,1,0:T(8,128)(2,1)S(1)}, u32[]{:S(2)}, u32[]{:S(2)}) collective-permute-start(bf16[1,96,768]{2,1,0:T(8,128)(2,1)S(1)} %cast_attn.1.refs_0_), channel_id=1, source_target_pairs={{0,24},{4,28},{8,16},{12,20},{16,8},{20,12},{24,0},{28,4},{1,25},{... | collective-permute-start | bytes 442376 | tf_op jit(solution)/shard_map/ppermute | solution.py:94
  10.1 12.2 %collective-permute-start.1 = (bf16[1,96,768]{2,1,0:T(8,128)(2,1)S(1)}, bf16[1,96,768]{2,1,0:T(8,128)(2,1)S(1)}, u32[]{:S(2)}, u32[]{:S(2)}) collective-permute-start(bf16[1,96,768]{2,1,0:T(8,128)(2,1)S(1)} %cast_attn.1.refs_0_), channel_id=1, source_target_pairs={{0,16},{4,20},{8,24},{12,28},{16,0},{20,4},{24,8},{28,12},{1,17},{... | collective-permute-start | bytes 442376 | tf_op jit(solution)/shard_map/ppermute | solution.py:94
  10.1 12.2 %collective-permute-start = (bf16[1,96,768]{2,1,0:T(8,128)(2,1)S(1)}, bf16[1,96,768]{2,1,0:T(8,128)(2,1)S(1)}, u32[]{:S(2)}, u32[]{:S(2)}) collective-permute-start(bf16[1,96,768]{2,1,0:T(8,128)(2,1)S(1)} %cast_attn.1.refs_0_), channel_id=1, source_target_pairs={{0,8},{4,12},{8,0},{12,4},{16,24},{20,28},{24,16},{28,20},{1,9},{5... | collective-permute-start | bytes 442376 | tf_op jit(solution)/shard_map/ppermute | solution.py:94
  22.3 8.1 %collective-permute-start.4 = (bf16[2,1,96,768]{3,2,1,0:T(8,128)(2,1)S(1)}, bf16[2,1,96,768]{3,2,1,0:T(8,128)(2,1)S(1)}, u32[]{:S(2)}, u32[]{:S(2)}) collective-permute-start(bf16[2,1,96,768]{3,2,1,0:T(8,128)(2,1)S(1)} %line_up.8.refs_0_), channel_id=1, source_target_pairs={{0,4},{4,0},{8,12},{12,8},{16,20},{20,16},{24,28},{28,24},{1,5},{5... | collective-permute-start | bytes 884744 | tf_op jit(solution)/shard_map/ppermute | solution.py:89
  23.9 7.8 %collective-permute-start.3 = (bf16[2,1,96,768]{3,2,1,0:T(8,128)(2,1)S(1)}, bf16[2,1,96,768]{3,2,1,0:T(8,128)(2,1)S(1)}, u32[]{:S(2)}, u32[]{:S(2)}) collective-permute-start(bf16[2,1,96,768]{3,2,1,0:T(8,128)(2,1)S(1)} %line_up.7.refs_0_), channel_id=1, source_target_pairs={{0,2},{1,3},{2,0},{3,1},{4,6},{5,7},{6,4},{7,5},{8,10},{9,11},{10,... | collective-permute-start | bytes 884744 | tf_op jit(solution)/shard_map/ppermute | solution.py:84
  24.5 9.3 %collective-permute-start.6 = (bf16[2,96,768]{2,1,0:T(8,128)(2,1)S(1)}, bf16[2,96,768]{2,1,0:T(8,128)(2,1)S(1)}, u32[]{:S(2)}, u32[]{:S(2)}) collective-permute-start(bf16[2,96,768]{2,1,0:T(8,128)(2,1)S(1)} %cast_ffn.1.refs_0_), channel_id=1, source_target_pairs={{0,8},{4,12},{8,16},{12,20},{16,24},{20,28},{24,0},{28,4},{1,9},{5... | collective-permute-start | bytes 884744 | tf_op jit(solution)/shard_map/ppermute | solution.py:99
  33.8 8.5 %collective-permute-start.9 = (bf16[2,96,768]{2,1,0:T(8,128)(2,1)S(1)}, bf16[2,96,768]{2,1,0:T(8,128)(2,1)S(1)}, u32[]{:S(2)}, u32[]{:S(2)}) collective-permute-start(bf16[2,96,768]{2,1,0:T(8,128)(2,1)S(1)} %collective-permute-done.6.refs_1_), channel_id=1, source_target_pairs={{0,8},{4,12},{8,16},{12,20},{16,24},{20,28},{24,0},{28,4},{1,9},{5... | collective-permute-start | bytes 884744 | tf_op jit(solution)/shard_map/ppermute | solution.py:99
  33.9 19.9 %collective-permute-start.8 = (bf16[2,2,1,96,768]{4,3,2,1,0:T(8,128)(2,1)S(1)}, bf16[2,2,1,96,768]{4,3,2,1,0:T(8,128)(2,1)S(1)}, u32[]{:S(2)}, u32[]{:S(2)}) collective-permute-start(bf16[2,2,1,96,768]{4,3,2,1,0:T(8,128)(2,1)S(1)} %line_up.10.refs_1_.refs_3_.refs_5_.refs_7_.refs_9_), channel_id=1, source_target_pairs={{0,2},{1,3},{2,0},{3,1},{4,6},{5,7},{6,4},{7,5},{8,10},{9,11},{10,... | collective-permute-start | bytes 1769480 | tf_op jit(solution)/shard_map/ppermute | solution.py:84
  35.5 18.3 %collective-permute-start.7 = (bf16[2,2,1,96,768]{4,3,2,1,0:T(8,128)(2,1)S(1)}, bf16[2,2,1,96,768]{4,3,2,1,0:T(8,128)(2,1)S(1)}, u32[]{:S(2)}, u32[]{:S(2)}) collective-permute-start(bf16[2,2,1,96,768]{4,3,2,1,0:T(8,128)(2,1)S(1)} %line_up.9.refs_0_.refs_4_.refs_12_.refs_6_.refs_10_), channel_id=1, source_target_pairs={{0,4},{4,0},{8,12},{12,8},{16,20},{20,16},{24,28},{28,24},{1,5},{5... | collective-permute-start | bytes 1769480 | tf_op jit(solution)/shard_map/ppermute | solution.py:89
  42.3 11.5 %collective-permute-start.10 = (bf16[2,96,768]{2,1,0:T(8,128)(2,1)S(1)}, bf16[2,96,768]{2,1,0:T(8,128)(2,1)S(1)}, u32[]{:S(2)}, u32[]{:S(2)}) collective-permute-start(bf16[2,96,768]{2,1,0:T(8,128)(2,1)S(1)} %collective-permute-done.9.refs_0_), channel_id=1, source_target_pairs={{0,8},{4,12},{8,16},{12,20},{16,24},{20,28},{24,0},{28,4},{1,9},{5... | collective-permute-start | bytes 884744 | tf_op jit(solution)/shard_map/ppermute | solution.py:99
  53.8 2.5 %collective-permute-start.11 = (bf16[512,768]{1,0:T(8,128)(2,1)S(1)}, bf16[512,768]{1,0:T(8,128)(2,1)S(1)}, u32[]{:S(2)}, u32[]{:S(2)}) collective-permute-start(bf16[512,768]{1,0:T(8,128)(2,1)S(1)} %get-tuple-element.286.x_ref), channel_id=1, source_target_pairs={{0,1},{1,0},{2,3},{3,2},{4,5},{5,4},{6,7},{7,6},{8,9},{9,8},{10,11... | collective-permute-start | bytes 2359304 | tf_op jit(solution)/shard_map/ppermute | solution.py:80
  58.6 21.1 %collective-permute-start.14 = (bf16[2,2,1,96,768]{4,3,2,1,0:T(8,128)(2,1)S(1)}, bf16[2,2,1,96,768]{4,3,2,1,0:T(8,128)(2,1)S(1)}, u32[]{:S(2)}, u32[]{:S(2)}) collective-permute-start(bf16[2,2,1,96,768]{4,3,2,1,0:T(8,128)(2,1)S(1)} %line_up.9.refs_0_.refs_4_.refs_12_.refs_6_.refs_10_), channel_id=1, source_target_pairs={{0,1},{1,0},{2,3},{3,2},{4,5},{5,4},{6,7},{7,6},{8,9},{9,8},{10,11... | collective-permute-start | bytes 1769480 | tf_op jit(solution)/shard_map/ppermute | solution.py:80
  59.1 28.0 %collective-permute-start.19 = (bf16[2,2,2,96,768]{4,3,2,1,0:T(8,128)(2,1)S(1)}, bf16[2,2,2,96,768]{4,3,2,1,0:T(8,128)(2,1)S(1)}, u32[]{:S(2)}, u32[]{:S(2)}) collective-permute-start(bf16[2,2,2,96,768]{4,3,2,1,0:T(8,128)(2,1)S(1)} %line_up.13.refs_8_.refs_9_), channel_id=1, source_target_pairs={{0,4},{4,0},{8,12},{12,8},{16,20},{20,16},{24,28},{28,24},{1,5},{5... | collective-permute-start | bytes 3538952 | tf_op jit(solution)/shard_map/ppermute | solution.py:89
  59.7 27.7 %collective-permute-start.18 = (bf16[2,2,2,96,768]{4,3,2,1,0:T(8,128)(2,1)S(1)}, bf16[2,2,2,96,768]{4,3,2,1,0:T(8,128)(2,1)S(1)}, u32[]{:S(2)}, u32[]{:S(2)}) collective-permute-start(bf16[2,2,2,96,768]{4,3,2,1,0:T(8,128)(2,1)S(1)} %line_up.13.refs_8_.refs_9_), channel_id=1, source_target_pairs={{0,2},{1,3},{2,0},{3,1},{4,6},{5,7},{6,4},{7,5},{8,10},{9,11},{10,... | collective-permute-start | bytes 3538952 | tf_op jit(solution)/shard_map/ppermute | solution.py:84
  69.1 8.8 %collective-permute-start.12 = (bf16[512,256]{1,0:T(8,128)(2,1)S(1)}, bf16[512,256]{1,0:T(8,128)(2,1)S(1)}, u32[]{:S(2)}, u32[]{:S(2)}) collective-permute-start(bf16[512,256]{1,0:T(8,128)(2,1)S(1)} %get-tuple-element.384.ctx_other_ref.refs_3_), channel_id=1, source_target_pairs={{0,1},{1,0},{2,3},{3,2},{4,5},{5,4},{6,7},{7,6},{8,9},{9,8},{10,11... | collective-permute-start | bytes 786440 | tf_op jit(solution)/shard_map/ppermute | solution.py:80
  69.2 10.9 %collective-permute-start.15 = (bf16[2,2,1,96,768]{4,3,2,1,0:T(8,128)(2,1)S(1)}, bf16[2,2,1,96,768]{4,3,2,1,0:T(8,128)(2,1)S(1)}, u32[]{:S(2)}, u32[]{:S(2)}) collective-permute-start(bf16[2,2,1,96,768]{4,3,2,1,0:T(8,128)(2,1)S(1)} %line_up.10.refs_1_.refs_3_.refs_5_.refs_7_.refs_9_), channel_id=1, source_target_pairs={{0,1},{1,0},{2,3},{3,2},{4,5},{5,4},{6,7},{7,6},{8,9},{9,8},{10,11... | collective-permute-start | bytes 1769480 | tf_op jit(solution)/shard_map/ppermute | solution.py:80
  78.0 1.6 collective-permute-start.13
  79.6 2.0 collective-permute-start.16
  79.7 2.7 %collective-permute-start.17 = (bf16[2,2,1,96,768]{4,3,2,1,0:T(8,128)(2,1)S(1)}, bf16[2,2,1,96,768]{4,3,2,1,0:T(8,128)(2,1)S(1)}, u32[]{:S(2)}, u32[]{:S(2)}) collective-permute-start(bf16[2,2,1,96,768]{4,3,2,1,0:T(8,128)(2,1)S(1)} %collective-permute-done.8.refs_5_.refs_7_.refs_13_.refs_15_.refs_11_), channel_id=1, source_target_pairs={{0,1},{1,0},{2,3},{3,2},{4,5},{5,4},{6,7},{7,6},{8,9},{9,8},{10,11... | collective-permute-start | bytes 1769480 | tf_op jit(solution)/shard_map/ppermute | solution.py:80
  80.1 9.4 %collective-permute-start.23 = (bf16[768,512]{1,0:T(8,128)(2,1)S(1)}, bf16[768,512]{1,0:T(8,128)(2,1)S(1)}, u32[]{:S(2)}, u32[]{:S(2)}) collective-permute-start(bf16[768,512]{1,0:T(8,128)(2,1)S(1)} %get-tuple-element.349.refs_6_), channel_id=1, source_target_pairs={{0,1},{1,0},{2,3},{3,2},{4,5},{5,4},{6,7},{7,6},{8,9},{9,8},{10,11... | collective-permute-start | bytes 2359304 | tf_op jit(solution)/shard_map/ppermute | solution.py:80
  81.6 9.5 %collective-permute-start.22 = (bf16[512,768]{1,0:T(8,128)(2,1)S(1)}, bf16[512,768]{1,0:T(8,128)(2,1)S(1)}, u32[]{:S(2)}, u32[]{:S(2)}) collective-permute-start(bf16[512,768]{1,0:T(8,128)(2,1)S(1)} %get-tuple-element.348.refs_4_.back_ref), channel_id=1, source_target_pairs={{0,1},{1,0},{2,3},{3,2},{4,5},{5,4},{6,7},{7,6},{8,9},{9,8},{10,11... | collective-permute-start | bytes 2359304 | tf_op jit(solution)/shard_map/ppermute | solution.py:80
  87.4 14.3 %collective-permute-start.24 = (bf16[2,2,96,768]{3,2,1,0:T(8,128)(2,1)S(1)}, bf16[2,2,96,768]{3,2,1,0:T(8,128)(2,1)S(1)}, u32[]{:S(2)}, u32[]{:S(2)}) collective-permute-start(bf16[2,2,96,768]{3,2,1,0:T(8,128)(2,1)S(1)} %slice_bitcast_fusion.1), channel_id=1, source_target_pairs={{0,4},{4,0},{8,12},{12,8},{16,20},{20,16},{24,28},{28,24},{1,5},{5... | collective-permute-start | bytes 1769480 | tf_op jit(solution)/shard_map/ppermute | solution.py:89
  88.9 2.3 collective-permute-start.20
  88.9 3.4 %collective-permute-start.21 = (bf16[768,512]{1,0:T(8,128)(2,1)S(1)}, bf16[768,512]{1,0:T(8,128)(2,1)S(1)}, u32[]{:S(2)}, u32[]{:S(2)}) collective-permute-start(bf16[768,512]{1,0:T(8,128)(2,1)S(1)} %get-tuple-element.347.refs_2_), channel_id=1, source_target_pairs={{0,1},{1,0},{2,3},{3,2},{4,5},{5,4},{6,7},{7,6},{8,9},{9,8},{10,11... | collective-permute-start | bytes 2359304 | tf_op jit(solution)/shard_map/ppermute | solution.py:80
  89.5 15.3 %collective-permute-start.25 = (bf16[2,2,96,768]{3,2,1,0:T(8,128)(2,1)S(1)}, bf16[2,2,96,768]{3,2,1,0:T(8,128)(2,1)S(1)}, u32[]{:S(2)}, u32[]{:S(2)}) collective-permute-start(bf16[2,2,96,768]{3,2,1,0:T(8,128)(2,1)S(1)} %slice_bitcast_fusion), channel_id=1, source_target_pairs={{0,2},{1,3},{2,0},{3,1},{4,6},{5,7},{6,4},{7,5},{8,10},{9,11},{10,... | collective-permute-start | bytes 1769480 | tf_op jit(solution)/shard_map/ppermute | solution.py:84
  113.6 2.4 %collective-permute-start.26 = (bf16[512,768]{1,0:T(8,128)(2,1)S(1)}, bf16[512,768]{1,0:T(8,128)(2,1)S(1)}, u32[]{:S(2)}, u32[]{:S(2)}) collective-permute-start(bf16[512,768]{1,0:T(8,128)(2,1)S(1)} %get-tuple-element.370), channel_id=1, source_target_pairs={{0,1},{1,0},{2,3},{3,2},{4,5},{5,4},{6,7},{7,6},{8,9},{9,8},{10,11... | collective-permute-start | bytes 2359304 | tf_op jit(solution)/shard_map/ppermute | solution.py:80
  113.7 33.4 %collective-permute-start.29 = (bf16[2,2,2,96,768]{4,3,2,1,0:T(8,128)(2,1)S(1)}, bf16[2,2,2,96,768]{4,3,2,1,0:T(8,128)(2,1)S(1)}, u32[]{:S(2)}, u32[]{:S(2)}) collective-permute-start(bf16[2,2,2,96,768]{4,3,2,1,0:T(8,128)(2,1)S(1)} %get-tuple-element.395), channel_id=1, source_target_pairs={{0,2},{1,3},{2,0},{3,1},{4,6},{5,7},{6,4},{7,5},{8,10},{9,11},{10,... | collective-permute-start | bytes 3538952 | tf_op jit(solution)/shard_map/ppermute | solution.py:84
  115.3 4.0 %collective-permute-start.28 = (bf16[512,768]{1,0:T(8,128)(2,1)S(1)}, bf16[512,768]{1,0:T(8,128)(2,1)S(1)}, u32[]{:S(2)}, u32[]{:S(2)}) collective-permute-start(bf16[512,768]{1,0:T(8,128)(2,1)S(1)} %get-tuple-element.376), channel_id=1, source_target_pairs={{0,1},{1,0},{2,3},{3,2},{4,5},{5,4},{6,7},{7,6},{8,9},{9,8},{10,11... | collective-permute-start | bytes 2359304 | tf_op jit(solution)/shard_map/ppermute | solution.py:80
  117.0 2.4 %collective-permute-start.27 = (bf16[512,768]{1,0:T(8,128)(2,1)S(1)}, bf16[512,768]{1,0:T(8,128)(2,1)S(1)}, u32[]{:S(2)}, u32[]{:S(2)}) collective-permute-start(bf16[512,768]{1,0:T(8,128)(2,1)S(1)} %get-tuple-element.377.own_ref), channel_id=1, source_target_pairs={{0,1},{1,0},{2,3},{3,2},{4,5},{5,4},{6,7},{7,6},{8,9},{9,8},{10,11... | collective-permute-start | bytes 2359304 | tf_op jit(solution)/shard_map/ppermute | solution.py:80
  117.2 29.9 %collective-permute-start.31 = (bf16[2,2,96,768]{3,2,1,0:T(8,128)(2,1)S(1)}, bf16[2,2,96,768]{3,2,1,0:T(8,128)(2,1)S(1)}, u32[]{:S(2)}, u32[]{:S(2)}) collective-permute-start(bf16[2,2,96,768]{3,2,1,0:T(8,128)(2,1)S(1)} %get-tuple-element.397), channel_id=1, source_target_pairs={{0,4},{4,0},{8,12},{12,8},{16,20},{20,16},{24,28},{28,24},{1,5},{5... | collective-permute-start | bytes 1769480 | tf_op jit(solution)/shard_map/ppermute | solution.py:89
  117.8 29.4 %collective-permute-start.30 = (bf16[2,2,96,768]{3,2,1,0:T(8,128)(2,1)S(1)}, bf16[2,2,96,768]{3,2,1,0:T(8,128)(2,1)S(1)}, u32[]{:S(2)}, u32[]{:S(2)}) collective-permute-start(bf16[2,2,96,768]{3,2,1,0:T(8,128)(2,1)S(1)} %get-tuple-element.396), channel_id=1, source_target_pairs={{0,4},{4,0},{8,12},{12,8},{16,20},{20,16},{24,28},{28,24},{1,5},{5... | collective-permute-start | bytes 1769480 | tf_op jit(solution)/shard_map/ppermute | solution.py:89
  147.7 16.2 %collective-permute-start.32 = (bf16[2,2,96,768]{3,2,1,0:T(8,128)(2,1)S(1)}, bf16[2,2,96,768]{3,2,1,0:T(8,128)(2,1)S(1)}, u32[]{:S(2)}, u32[]{:S(2)}) collective-permute-start(bf16[2,2,96,768]{3,2,1,0:T(8,128)(2,1)S(1)} %get-tuple-element.411), channel_id=1, source_target_pairs={{0,4},{4,0},{8,12},{12,8},{16,20},{20,16},{24,28},{28,24},{1,5},{5... | collective-permute-start | bytes 1769480 | tf_op jit(solution)/shard_map/ppermute | solution.py:89
  148.3 16.2 %collective-permute-start.33 = (bf16[2,2,96,768]{3,2,1,0:T(8,128)(2,1)S(1)}, bf16[2,2,96,768]{3,2,1,0:T(8,128)(2,1)S(1)}, u32[]{:S(2)}, u32[]{:S(2)}) collective-permute-start(bf16[2,2,96,768]{3,2,1,0:T(8,128)(2,1)S(1)} %get-tuple-element.412), channel_id=1, source_target_pairs={{0,2},{1,3},{2,0},{3,1},{4,6},{5,7},{6,4},{7,5},{8,10},{9,11},{10,... | collective-permute-start | bytes 1769480 | tf_op jit(solution)/shard_map/ppermute | solution.py:84
  156.4 10.5 %collective-permute-start.34 = (bf16[512,768]{1,0:T(8,128)(2,1)S(1)}, bf16[512,768]{1,0:T(8,128)(2,1)S(1)}, u32[]{:S(2)}, u32[]{:S(2)}) collective-permute-start(bf16[512,768]{1,0:T(8,128)(2,1)S(1)} %get-tuple-element.422), channel_id=1, source_target_pairs={{0,1},{1,0},{2,3},{3,2},{4,5},{5,4},{6,7},{7,6},{8,9},{9,8},{10,11... | collective-permute-start | bytes 2359304 | tf_op jit(solution)/shard_map/ppermute | solution.py:80
  156.5 19.5 %collective-permute-start.35 = (bf16[2,2,1,96,768]{4,3,2,1,0:T(8,128)(2,1)S(1)}, bf16[2,2,1,96,768]{4,3,2,1,0:T(8,128)(2,1)S(1)}, u32[]{:S(2)}, u32[]{:S(2)}) collective-permute-start(bf16[2,2,1,96,768]{4,3,2,1,0:T(8,128)(2,1)S(1)} %get-tuple-element.440), channel_id=1, source_target_pairs={{0,2},{1,3},{2,0},{3,1},{4,6},{5,7},{6,4},{7,5},{8,10},{9,11},{10,... | collective-permute-start | bytes 1769480 | tf_op jit(solution)/shard_map/ppermute | solution.py:84
  157.1 19.0 %collective-permute-start.36 = (bf16[2,2,1,96,768]{4,3,2,1,0:T(8,128)(2,1)S(1)}, bf16[2,2,1,96,768]{4,3,2,1,0:T(8,128)(2,1)S(1)}, u32[]{:S(2)}, u32[]{:S(2)}) collective-permute-start(bf16[2,2,1,96,768]{4,3,2,1,0:T(8,128)(2,1)S(1)} %get-tuple-element.441), channel_id=1, source_target_pairs={{0,4},{4,0},{8,12},{12,8},{16,20},{20,16},{24,28},{28,24},{1,5},{5... | collective-permute-start | bytes 1769480 | tf_op jit(solution)/shard_map/ppermute | solution.py:89
  164.8 11.6 %collective-permute-start.37 = (bf16[2,96,768]{2,1,0:T(8,128)(2,1)S(1)}, bf16[2,96,768]{2,1,0:T(8,128)(2,1)S(1)}, u32[]{:S(2)}, u32[]{:S(2)}) collective-permute-start(bf16[2,96,768]{2,1,0:T(8,128)(2,1)S(1)} %get-tuple-element.419), channel_id=1, source_target_pairs={{0,8},{4,12},{8,0},{12,4},{16,24},{20,28},{24,16},{28,20},{1,9},{5... | collective-permute-start | bytes 884744 | tf_op jit(solution)/shard_map/ppermute | solution.py:94
  165.5 15.8 %collective-permute-start.38 = (bf16[2,96,768]{2,1,0:T(8,128)(2,1)S(1)}, bf16[2,96,768]{2,1,0:T(8,128)(2,1)S(1)}, u32[]{:S(2)}, u32[]{:S(2)}) collective-permute-start(bf16[2,96,768]{2,1,0:T(8,128)(2,1)S(1)} %get-tuple-element.421), channel_id=1, source_target_pairs={{0,24},{4,28},{8,16},{12,20},{16,8},{20,12},{24,0},{28,4},{1,25},{... | collective-permute-start | bytes 884744 | tf_op jit(solution)/shard_map/ppermute | solution.py:94
  169.3 22.5 %collective-permute-start.41 = (bf16[2,96,768]{2,1,0:T(8,128)(2,1)S(1)}, bf16[2,96,768]{2,1,0:T(8,128)(2,1)S(1)}, u32[]{:S(2)}, u32[]{:S(2)}) collective-permute-start(bf16[2,96,768]{2,1,0:T(8,128)(2,1)S(1)} %get-tuple-element.457), channel_id=1, source_target_pairs={{0,16},{4,20},{8,24},{12,28},{16,0},{20,4},{24,8},{28,12},{1,17},{... | collective-permute-start | bytes 884744 | tf_op jit(solution)/shard_map/ppermute | solution.py:94
  181.5 10.3 %collective-permute-start.39 = (bf16[2,1,96,768]{3,2,1,0:T(8,128)(2,1)S(1)}, bf16[2,1,96,768]{3,2,1,0:T(8,128)(2,1)S(1)}, u32[]{:S(2)}, u32[]{:S(2)}) collective-permute-start(bf16[2,1,96,768]{3,2,1,0:T(8,128)(2,1)S(1)} %get-tuple-element.450), channel_id=1, source_target_pairs={{0,4},{4,0},{8,12},{12,8},{16,20},{20,16},{24,28},{28,24},{1,5},{5... | collective-permute-start | bytes 884744 | tf_op jit(solution)/shard_map/ppermute | solution.py:89
  183.1 8.8 %collective-permute-start.40 = (bf16[2,1,96,768]{3,2,1,0:T(8,128)(2,1)S(1)}, bf16[2,1,96,768]{3,2,1,0:T(8,128)(2,1)S(1)}, u32[]{:S(2)}, u32[]{:S(2)}) collective-permute-start(bf16[2,1,96,768]{3,2,1,0:T(8,128)(2,1)S(1)} %get-tuple-element.451), channel_id=1, source_target_pairs={{0,2},{1,3},{2,0},{3,1},{4,6},{5,7},{6,4},{7,5},{8,10},{9,11},{10,... | collective-permute-start | bytes 884744 | tf_op jit(solution)/shard_map/ppermute | solution.py:84
  191.9 19.1 %collective-permute-start.45 = (bf16[2,256,768]{2,1,0:T(8,128)(2,1)S(1)}, bf16[2,256,768]{2,1,0:T(8,128)(2,1)S(1)}, u32[]{:S(2)}, u32[]{:S(2)}) collective-permute-start(bf16[2,256,768]{2,1,0:T(8,128)(2,1)S(1)} %get-tuple-element.474), channel_id=1, source_target_pairs={{0,2},{1,3},{2,0},{3,1},{4,6},{5,7},{6,4},{7,5},{8,10},{9,11},{10,... | collective-permute-start | bytes 2359304 | tf_op jit(solution)/shard_map/ppermute | solution.py:84
  193.5 12.2 %collective-permute-start.42 = (bf16[1,96,768]{2,1,0:T(8,128)(2,1)S(1)}, bf16[1,96,768]{2,1,0:T(8,128)(2,1)S(1)}, u32[]{:S(2)}, u32[]{:S(2)}) collective-permute-start(bf16[1,96,768]{2,1,0:T(8,128)(2,1)S(1)} %get-tuple-element.471), channel_id=1, source_target_pairs={{0,8},{4,12},{8,0},{12,4},{16,24},{20,28},{24,16},{28,20},{1,9},{5... | collective-permute-start | bytes 442376 | tf_op jit(solution)/shard_map/ppermute | solution.py:94
  202.2 8.7 %collective-permute-start.43 = (bf16[1,96,768]{2,1,0:T(8,128)(2,1)S(1)}, bf16[1,96,768]{2,1,0:T(8,128)(2,1)S(1)}, u32[]{:S(2)}, u32[]{:S(2)}) collective-permute-start(bf16[1,96,768]{2,1,0:T(8,128)(2,1)S(1)} %get-tuple-element.472), channel_id=1, source_target_pairs={{0,16},{4,20},{8,24},{12,28},{16,0},{20,4},{24,8},{28,12},{1,17},{... | collective-permute-start | bytes 442376 | tf_op jit(solution)/shard_map/ppermute | solution.py:94
  202.2 8.7 %collective-permute-start.44 = (bf16[1,96,768]{2,1,0:T(8,128)(2,1)S(1)}, bf16[1,96,768]{2,1,0:T(8,128)(2,1)S(1)}, u32[]{:S(2)}, u32[]{:S(2)}) collective-permute-start(bf16[1,96,768]{2,1,0:T(8,128)(2,1)S(1)} %get-tuple-element.473), channel_id=1, source_target_pairs={{0,24},{4,28},{8,16},{12,20},{16,8},{20,12},{24,0},{28,4},{1,25},{... | collective-permute-start | bytes 442376 | tf_op jit(solution)/shard_map/ppermute | solution.py:94
  205.7 19.8 %copy-start.2 = (f32[2,96,768]{2,1,0:T(8,128)S(1)}, f32[2,96,768]{2,1,0:T(8,128)}, u32[]{:S(2)}) copy-start(f32[2,96,768]{2,1,0:T(8,128)} %get-tuple-element.245.ffn_ref) | copy-start | bytes 1769476
  212.0 13.5 %all-to-all-start.1 = ((f32[32,16,128]{2,1,0:T(8,128)}), f32[32,16,128]{2,1,0:T(8,128)S(1)}, u32[]{:S(2)}, u32[]{:S(2)}) async-start(f32[32,16,128]{2,1,0:T(8,128)} %broadcast_in_dim.5), calls=%async_computation.1 | async-start | bytes 524288 | tf_op jit(solution)/shard_map/all_to_all | solution.py:108
  (4 other events, 33.6 us)

commit v7 on v6

--- a/solution.py
+++ b/solution.py
@@ -1178,21 +1178,18 @@
     t_came = swap_core(t_send)
     t_own, ffn_y1, ffn_x1 = fence(t_own, ffn_y1, ffn_x1)
     ffn_own, *ffn_far_own = merge_last(ffn_y0, ffn_y1, ffn_x0, ffn_x1)
-    soon = [k for k in range(1, depth) if k != cut]
-    ffn_back = [swap_z(ffn_far_own[k - 1], k) for k in soon]
+    ffn_back = [swap_z(v, k) for k, v in enumerate(ffn_far_own, 1)]
     ffn_own, ffn_far_own, t_came = fence(ffn_own, ffn_far_own, t_came)
     out_keep, in_keep, send_last, gain_one_grad = finish(
         rows_in, gains, t_own, t_came, mid_grad, mid, acc_own, acc_came
     )
     small = small_sums(place, gain_one_grad, gain_two_grad, [lines[0], lines[2]])
-    in_keep, send_last, small, ffn_own, near0, far0, ffn_far_own = fence(
-        in_keep, send_last, small, ffn_own, near0, far0, ffn_far_own
-    )
-    near1_x, far1_y, small, ffn_back = fence(near1_x, far1_y, small, ffn_back)
+    in_keep, send_last, small, ffn_own, near0, far0 = fence(
+        in_keep, send_last, small, ffn_own, near0, far0
+    )
+    near1_x, far1_y, small, ffn_back[0] = fence(near1_x, far1_y, small, ffn_back[0])
     attn_y0, attn_y1, attn_x0, attn_x1 = merge_half(near0, near1_x, (far0,), (far1_y,))
-    attn_y1, attn_x1, ffn_back = fence(attn_y1, attn_x1, ffn_back)
     attn_y1, attn_x1 = swap_y(attn_y1), swap_x(attn_x1)
-    ffn_back += [swap_z(ffn_far_own[cut - 1], cut)]
     attn_y1, attn_x1, attn_y0, attn_x0, send_last, ffn_back = fence(
         attn_y1, attn_x1, attn_y0, attn_x0, send_last, ffn_back
     )

time: 233 us -> 231 us (level)
    ppermute x9, starting transfers between devices: 19.2 us -> 15.5 us  [swap_z(): return lax.ppermute(v, 'dp', [(i, i ^ 2 * k) for i in range(n)])]
    all_to_all x1, starting transfers between devices: 2.92 us -> 6.46 us  [from_all(): lax.all_to_all(jnp.broadcast_to(v[None], (n,) + v.shape), ('dp', 'mp'), 0...]
where the time goes in v7:
time: 231 us; the launch traced here: 228 us
  Pallas kernels  95.7 us (41%)
  waiting for transfers between devices  67.5 us (29%)
  starting transfers between devices  50 us (22%)
  blocking collectives  11.4 us (5%)
    pallas_call x2, Pallas kernels, attend_back(): pl.pallas_call(functools.partial(attend_back_kernel, r // 2), in_specs=[i...  26.1 us
    ppermute x9, waiting for transfers between devices, swap_z(): return lax.ppermute(v, 'dp', [(i, i ^ 2 * k) for i in range(n)])  22.4 us
    pallas_call x2, Pallas kernels, feed(): pl.pallas_call(functools.partial(feed_kernel, indices, first, split), in_...  17.3 us
    pallas_call x2, Pallas kernels, attend(): pl.pallas_call(functools.partial(attend_kernel, r // 2, r), in_specs=[in_...  16.2 us
    ppermute x9, starting transfers between devices, swap_z(): return lax.ppermute(v, 'dp', [(i, i ^ 2 * k) for i in range(n)])  15.5 us
    ppermute x10, starting transfers between devices, swap_x(): return lax.ppermute(v, 'mp', [(i, i ^ 2) for i in range(4)])  14.9 us
    ppermute x9, waiting for transfers between devices, swap_y(): return lax.ppermute(v, 'dp', [(i, i ^ 1) for i in range(n)])  14.6 us
    all_to_all x1, blocking collectives, gather_gains(): lax.all_to_all(jnp.broadcast_to(low[None], (n,) + low.shape), 'dp', 0, 0)  11.4 us
  transfers between devices with their start and end apart: 47, of which 24 were waited for; matrix products, arithmetic and copies ran while one was open for 0% of the time, Pallas kernels for 34%

profile of v7, /device:TPU:0, one launch (start us, length us, event | category | flops | bytes accessed | tf_op | source)
XLA Modules:
  0.0 227.5 jit_solution(15525607452330488706)
XLA Ops:
  1.6 1.7 sort_rows.1
  3.3 3.0 %collective-permute-start.5 = (bf16[2,256,768]{2,1,0:T(8,128)(2,1)S(1)}, bf16[2,256,768]{2,1,0:T(8,128)(2,1)S(1)}, u32[]{:S(2)}, u32[]{:S(2)}) collective-permute-start(bf16[2,256,768]{2,1,0:T(8,128)(2,1)S(1)} %sort_rows.1), channel_id=1, source_target_pairs={{0,2},{1,3},{2,0},{3,1},{4,6},{5,7},{6,4},{7,5},{8,10},{9,11},{10,... | collective-permute-start | bytes 2359304 | tf_op jit(solution)/shard_map/ppermute | solution.py:84
  6.4 3.7 %collective-permute-start.2 = (bf16[1,96,768]{2,1,0:T(8,128)(2,1)S(1)}, bf16[1,96,768]{2,1,0:T(8,128)(2,1)S(1)}, u32[]{:S(2)}, u32[]{:S(2)}) collective-permute-start(bf16[1,96,768]{2,1,0:T(8,128)(2,1)S(1)} %cast_attn.1.refs_0_), channel_id=1, source_target_pairs={{0,24},{4,28},{8,16},{12,20},{16,8},{20,12},{24,0},{28,4},{1,25},{... | collective-permute-start | bytes 442376 | tf_op jit(solution)/shard_map/ppermute | solution.py:94
  10.9 5.2 %bias_tiles.1.bias_ref = f32[4,3,5,128,128]{4,3,2,1,0:T(8,128)S(1)} custom-call(s32[21]{0:T(128)S(1)} %stack.79.place_ref, f32[12,32]{1,0:T(8,128)S(1)} %copy-done.3), custom_call_target="tpu_custom_call" | custom-call | flops 1000 | bytes 1000 | tf_op jit(solution)/shard_map/bias_tiles/pallas_call | solution.py:193
  16.1 6.1 %collective-permute-done.1.refs_0_ = bf16[1,96,768]{2,1,0:T(8,128)(2,1)S(1)} collective-permute-done((bf16[1,96,768]{2,1,0:T(8,128)(2,1)S(1)}, bf16[1,96,768]{2,1,0:T(8,128)(2,1)S(1)}, u32[]{:S(2)}, u32[]{:S(2)}) %collective-permute-start.1) | collective-permute-done | bytes 147488 | tf_op jit(solution)/shard_map/ppermute | solution.py:94
  22.3 1.6 collective-permute-start.4
  24.5 5.9 %collective-permute-done.4.refs_1_ = bf16[2,1,96,768]{3,2,1,0:T(8,128)(2,1)S(1)} collective-permute-done((bf16[2,1,96,768]{3,2,1,0:T(8,128)(2,1)S(1)}, bf16[2,1,96,768]{3,2,1,0:T(8,128)(2,1)S(1)}, u32[]{:S(2)}, u32[]{:S(2)}) %collective-permute-start.4) | collective-permute-done | bytes 294944 | tf_op jit(solution)/shard_map/ppermute | solution.py:89
  31.7 2.1 collective-permute-done.6.refs_1_
  33.9 1.6 collective-permute-start.8
  36.0 1.9 join_rows.1
  38.0 4.4 %collective-permute-done.9.refs_0_ = bf16[2,96,768]{2,1,0:T(8,128)(2,1)S(1)} collective-permute-done((bf16[2,96,768]{2,1,0:T(8,128)(2,1)S(1)}, bf16[2,96,768]{2,1,0:T(8,128)(2,1)S(1)}, u32[]{:S(2)}, u32[]{:S(2)}) %collective-permute-start.9) | collective-permute-done | bytes 294944 | tf_op jit(solution)/shard_map/ppermute | solution.py:99
  42.3 11.4 %all_to_all.10.g_ref = bf16[8,2,96]{2,1,0:T(2,128)(2,1)S(1)} all-to-all(bf16[8,2,96]{2,1,0:T(2,128)(2,1)S(1)} %broadcast_in_dim.4), channel_id=1, replica_groups=mesh['dp'=8,'mp'=4] {'dp'}, dimensions={0} | all-to-all | bytes 6144 | tf_op jit(solution)/shard_map/all_to_all | solution.py:114
  54.1 2.2 project.2
  56.3 2.2 project.3
  59.7 1.5 collective-permute-start.18
  61.2 8.0 %attend.2 = (bf16[512,256]{1,0:T(8,128)(2,1)S(1)}, bf16[512,256]{1,0:T(8,128)(2,1)S(1)}, bf16[3,1024,1024]{2,1,0:T(8,128)(2,1)}) custom-call(s32[21]{0:T(128)S(1)} %stack.79.place_ref, bf16[2,512,192]{2,1,0:T(8,128)(2,1)S(1)} %get-tuple-element.374.q_own_ref, bf16[2,512,192]{2,1,0:T(8,128)(2,1)S(1)} %get-tuple-element.375.q_other_ref, ...), custom_call_target="tpu_custom_call" | custom-call | flops 1000 | bytes 1000 | tf_op jit(solution)/shard_map/attend/pallas_call | solution.py:326
  69.7 8.2 %attend.3 = (bf16[512,256]{1,0:T(8,128)(2,1)S(1)}, bf16[512,256]{1,0:T(8,128)(2,1)S(1)}, bf16[3,1024,1024]{2,1,0:T(8,128)(2,1)}) custom-call(s32[21]{0:T(128)S(1)} %stack.79.place_ref, bf16[2,512,192]{2,1,0:T(8,128)(2,1)S(1)} %get-tuple-element.374.q_own_ref, bf16[2,512,192]{2,1,0:T(8,128)(2,1)S(1)} %get-tuple-element.375.q_other_ref, ...), custom_call_target="tpu_custom_call" | custom-call | flops 1000 | bytes 1000 | tf_op jit(solution)/shard_map/attend/pallas_call | solution.py:326
  82.4 2.1 middle.1
  84.5 2.6 %collective-permute-done.19.refs_10_.refs_11_ = bf16[2,2,2,96,768]{4,3,2,1,0:T(8,128)(2,1)S(1)} collective-permute-done((bf16[2,2,2,96,768]{4,3,2,1,0:T(8,128)(2,1)S(1)}, bf16[2,2,2,96,768]{4,3,2,1,0:T(8,128)(2,1)S(1)}, u32[]{:S(2)}, u32[]{:S(2)}) %collective-permute-start.19) | collective-permute-done | bytes 1179680 | tf_op jit(solution)/shard_map/ppermute | solution.py:89
  87.4 1.5 collective-permute-start.24
  89.5 1.6 collective-permute-start.25
  92.3 8.5 %feed.2 = (f32[512,768]{1,0:T(8,128)S(1)}, f32[512,768]{1,0:T(8,128)S(1)}, f32[512,768]{1,0:T(8,128)S(1)}, f32[512,768]{1,0:T(8,128)S(1)}, bf16[2,2,2,96,768]{4,...) custom-call(s32[21]{0:T(128)S(1)} %stack.79.place_ref, ...), custom_call_target="tpu_custom_call" | custom-call | flops 1000 | bytes 1000 | tf_op jit(solution)/shard_map/feed/pallas_call | solution.py:432
  101.7 3.1 %collective-permute-done.25.refs_15_ = bf16[2,2,96,768]{3,2,1,0:T(8,128)(2,1)S(1)} collective-permute-done((bf16[2,2,96,768]{3,2,1,0:T(8,128)(2,1)S(1)}, bf16[2,2,96,768]{3,2,1,0:T(8,128)(2,1)S(1)}, u32[]{:S(2)}, u32[]{:S(2)}) %collective-permute-start.25) | collective-permute-done | bytes 589856 | tf_op jit(solution)/shard_map/ppermute | solution.py:84
  104.8 8.8 %feed.3 = (f32[512,768]{1,0:T(8,128)S(1)}, bf16[512,768]{1,0:T(8,128)(2,1)S(1)}, f32[512,768]{1,0:T(8,128)S(1)}, bf16[512,768]{1,0:T(8,128)(2,1)S(1)}, bf16[2,2,...) custom-call(s32[21]{0:T(128)S(1)} %stack.79.place_ref, ...), custom_call_target="tpu_custom_call" | custom-call | flops 1000 | bytes 1000 | tf_op jit(solution)/shard_map/feed/pallas_call | solution.py:432
  113.7 1.5 collective-permute-start.29
  117.8 1.5 collective-permute-start.30
  119.4 1.7 context_grads.1
  121.1 13.2 %attend_back.2 = (bf16[1024,576]{1,0:T(8,128)(2,1)S(1)}, f32[3,32,128]{2,1,0:T(8,128)S(1)}) custom-call(s32[21]{0:T(128)S(1)} %stack.79.place_ref, bf16[2,512,192]{2,1,0:T(8,128)(2,1)S(1)} %get-tuple-element.374.q_own_ref, bf16[2,512,192]{2,1,0:T(8,128)(2,1)S(1)} %get-tuple-element.375.q_other_ref, bf16[2,512,384]{2,1,0:T(8,128)(2,1)S(1)} %get-tuple-element.306.kv_own_ref, ...), custom_call_target="tpu_custom_call" | custom-call | flops 1000 | bytes 1000 | tf_op jit(solution)/shard_map/attend_back/pallas_call | solution.py:572
  134.2 12.9 %attend_back.3 = (bf16[1024,576]{1,0:T(8,128)(2,1)S(1)}, f32[3,32,128]{2,1,0:T(8,128)S(1)}) custom-call(s32[21]{0:T(128)S(1)} %stack.79.place_ref, bf16[2,512,192]{2,1,0:T(8,128)(2,1)S(1)} %get-tuple-element.374.q_own_ref, bf16[2,512,192]{2,1,0:T(8,128)(2,1)S(1)} %get-tuple-element.375.q_other_ref, bf16[2,512,384]{2,1,0:T(8,128)(2,1)S(1)} %get-tuple-element.306.kv_own_ref, ...), custom_call_target="tpu_custom_call" | custom-call | flops 1000 | bytes 1000 | tf_op jit(solution)/shard_map/attend_back/pallas_call | solution.py:572
  148.3 1.5 collective-permute-start.33
  149.8 6.6 %project_back.1 = (f32[512,768]{1,0:T(8,128)S(1)}, bf16[512,768]{1,0:T(8,128)(2,1)S(1)}, bf16[2,2,1,96,768]{4,3,2,1,0:T(8,128)(2,1)S(1)}, bf16[2,2,1,96,768]{4,3...) custom-call(s32[21]{0:T(128)S(1)} %stack.79.place_ref, ...), custom_call_target="tpu_custom_call" | custom-call | flops 1000 | bytes 1000 | tf_op jit(solution)/shard_map/project_back/pallas_call | solution.py:631
  157.1 1.5 collective-permute-start.36
  158.6 5.4 %collective-permute-done.32.near_came_ref = bf16[2,2,96,768]{3,2,1,0:T(8,128)(2,1)S(1)} collective-permute-done((bf16[2,2,96,768]{3,2,1,0:T(8,128)(2,1)S(1)}, bf16[2,2,96,768]{3,2,1,0:T(8,128)(2,1)S(1)}, u32[]{:S(2)}, u32[]{:S(2)}) %collective-permute-start.32) | collective-permute-done | bytes 589856 | tf_op jit(solution)/shard_map/ppermute | solution.py:89
  166.0 3.2 %collective-permute-start.41 = (bf16[2,96,768]{2,1,0:T(8,128)(2,1)S(1)}, bf16[2,96,768]{2,1,0:T(8,128)(2,1)S(1)}, u32[]{:S(2)}, u32[]{:S(2)}) collective-permute-start(bf16[2,96,768]{2,1,0:T(8,128)(2,1)S(1)} %get-tuple-element.414), channel_id=1, source_target_pairs={{0,24},{4,28},{8,16},{12,20},{16,8},{20,12},{24,0},{28,4},{1,25},{... | collective-permute-start | bytes 884744 | tf_op jit(solution)/shard_map/ppermute | solution.py:94
  169.3 1.5 finish.1
  171.7 4.4 %collective-permute-done.35.near_came_ref = bf16[2,2,1,96,768]{4,3,2,1,0:T(8,128)(2,1)S(1)} collective-permute-done((bf16[2,2,1,96,768]{4,3,2,1,0:T(8,128)(2,1)S(1)}, bf16[2,2,1,96,768]{4,3,2,1,0:T(8,128)(2,1)S(1)}, u32[]{:S(2)}, u32[]{:S(2)}) %collective-permute-start.35) | collective-permute-done | bytes 589856 | tf_op jit(solution)/shard_map/ppermute | solution.py:84
  177.5 1.5 collective-permute-start.38
  179.0 1.5 collective-permute-start.39
  180.6 7.7 %collective-permute-done.40.refs_1_ = bf16[2,96,768]{2,1,0:T(8,128)(2,1)S(1)} collective-permute-done((bf16[2,96,768]{2,1,0:T(8,128)(2,1)S(1)}, bf16[2,96,768]{2,1,0:T(8,128)(2,1)S(1)}, u32[]{:S(2)}, u32[]{:S(2)}) %collective-permute-start.40) | collective-permute-done | bytes 294944 | tf_op jit(solution)/shard_map/ppermute | solution.py:94
  188.3 1.6 collective-permute-start.45
  190.0 4.1 %collective-permute-start.42 = (bf16[1,96,768]{2,1,0:T(8,128)(2,1)S(1)}, bf16[1,96,768]{2,1,0:T(8,128)(2,1)S(1)}, u32[]{:S(2)}, u32[]{:S(2)}) collective-permute-start(bf16[1,96,768]{2,1,0:T(8,128)(2,1)S(1)} %get-tuple-element.457), channel_id=1, source_target_pairs={{0,8},{4,12},{8,0},{12,4},{16,24},{20,28},{24,16},{28,20},{1,9},{5... | collective-permute-start | bytes 442376 | tf_op jit(solution)/shard_map/ppermute | solution.py:94
  194.3 2.3 %collective-permute-start.44 = (bf16[1,96,768]{2,1,0:T(8,128)(2,1)S(1)}, bf16[1,96,768]{2,1,0:T(8,128)(2,1)S(1)}, u32[]{:S(2)}, u32[]{:S(2)}) collective-permute-start(bf16[1,96,768]{2,1,0:T(8,128)(2,1)S(1)} %get-tuple-element.459), channel_id=1, source_target_pairs={{0,24},{4,28},{8,16},{12,20},{16,8},{20,12},{24,0},{28,4},{1,25},{... | collective-permute-start | bytes 442376 | tf_op jit(solution)/shard_map/ppermute | solution.py:94
  197.6 2.8 %collective-permute-done.42.refs_0_ = bf16[1,96,768]{2,1,0:T(8,128)(2,1)S(1)} collective-permute-done((bf16[1,96,768]{2,1,0:T(8,128)(2,1)S(1)}, bf16[1,96,768]{2,1,0:T(8,128)(2,1)S(1)}, u32[]{:S(2)}, u32[]{:S(2)}) %collective-permute-start.42) | collective-permute-done | bytes 147488 | tf_op jit(solution)/shard_map/ppermute | solution.py:94
  200.4 4.6 %collective-permute-done.43.refs_1_ = bf16[1,96,768]{2,1,0:T(8,128)(2,1)S(1)} collective-permute-done((bf16[1,96,768]{2,1,0:T(8,128)(2,1)S(1)}, bf16[1,96,768]{2,1,0:T(8,128)(2,1)S(1)}, u32[]{:S(2)}, u32[]{:S(2)}) %collective-permute-start.43) | collective-permute-done | bytes 147488 | tf_op jit(solution)/shard_map/ppermute | solution.py:94
  206.0 6.5 %all-to-all-start.1 = ((f32[32,16,128]{2,1,0:T(8,128)}), f32[32,16,128]{2,1,0:T(8,128)S(1)}, u32[]{:S(2)}, u32[]{:S(2)}) async-start(f32[32,16,128]{2,1,0:T(8,128)} %broadcast_in_dim.5), calls=%async_computation.1 | async-start | bytes 524288 | tf_op jit(solution)/shard_map/all_to_all | solution.py:108
  212.5 1.8 place_rows.1
  214.3 8.8 %all-to-all-done.1.small_ref = f32[32,16,128]{2,1,0:T(8,128)S(1)} async-done(((f32[32,16,128]{2,1,0:T(8,128)}), f32[32,16,128]{2,1,0:T(8,128)S(1)}, u32[]{:S(2)}, u32[]{:S(2)}) %all-to-all-start.1) | async-done | bytes 262176 | tf_op jit(solution)/shard_map/all_to_all | solution.py:108
  223.1 4.2 %update.1 = (f32[1,1]{1,0:T(1,128)}, f32[4,96,192]{2,1,0:T(8,128)}, f32[2,96]{1,0:T(2,128)}, f32[12,32]{1,0:T(8,128)}, f32[4,96,192]{2,1,0:T(8,128)}, /*index=5*...) custom-call(s32[1]{0:T(128)} %bitcast.21.place_ref, ...), custom_call_target="tpu_custom_call" | custom-call | flops 1000 | bytes 1000 | tf_op jit(solution)/shard_map/update/pallas_call | solution.py:1002
  (98 shorter events, 25.0 us)
Async XLA Ops:
  3.3 30.5 %collective-permute-start.5 = (bf16[2,256,768]{2,1,0:T(8,128)(2,1)S(1)}, bf16[2,256,768]{2,1,0:T(8,128)(2,1)S(1)}, u32[]{:S(2)}, u32[]{:S(2)}) collective-permute-start(bf16[2,256,768]{2,1,0:T(8,128)(2,1)S(1)} %sort_rows.1), channel_id=1, source_target_pairs={{0,2},{1,3},{2,0},{3,1},{4,6},{5,7},{6,4},{7,5},{8,10},{9,11},{10,... | collective-permute-start | bytes 2359304 | tf_op jit(solution)/shard_map/ppermute | solution.py:84
  6.4 9.7 %collective-permute-start.2 = (bf16[1,96,768]{2,1,0:T(8,128)(2,1)S(1)}, bf16[1,96,768]{2,1,0:T(8,128)(2,1)S(1)}, u32[]{:S(2)}, u32[]{:S(2)}) collective-permute-start(bf16[1,96,768]{2,1,0:T(8,128)(2,1)S(1)} %cast_attn.1.refs_0_), channel_id=1, source_target_pairs={{0,24},{4,28},{8,16},{12,20},{16,8},{20,12},{24,0},{28,4},{1,25},{... | collective-permute-start | bytes 442376 | tf_op jit(solution)/shard_map/ppermute | solution.py:94
  10.1 12.2 %collective-permute-start.1 = (bf16[1,96,768]{2,1,0:T(8,128)(2,1)S(1)}, bf16[1,96,768]{2,1,0:T(8,128)(2,1)S(1)}, u32[]{:S(2)}, u32[]{:S(2)}) collective-permute-start(bf16[1,96,768]{2,1,0:T(8,128)(2,1)S(1)} %cast_attn.1.refs_0_), channel_id=1, source_target_pairs={{0,16},{4,20},{8,24},{12,28},{16,0},{20,4},{24,8},{28,12},{1,17},{... | collective-permute-start | bytes 442376 | tf_op jit(solution)/shard_map/ppermute | solution.py:94
  10.1 12.2 %collective-permute-start = (bf16[1,96,768]{2,1,0:T(8,128)(2,1)S(1)}, bf16[1,96,768]{2,1,0:T(8,128)(2,1)S(1)}, u32[]{:S(2)}, u32[]{:S(2)}) collective-permute-start(bf16[1,96,768]{2,1,0:T(8,128)(2,1)S(1)} %cast_attn.1.refs_0_), channel_id=1, source_target_pairs={{0,8},{4,12},{8,0},{12,4},{16,24},{20,28},{24,16},{28,20},{1,9},{5... | collective-permute-start | bytes 442376 | tf_op jit(solution)/shard_map/ppermute | solution.py:94
  22.3 8.1 %collective-permute-start.4 = (bf16[2,1,96,768]{3,2,1,0:T(8,128)(2,1)S(1)}, bf16[2,1,96,768]{3,2,1,0:T(8,128)(2,1)S(1)}, u32[]{:S(2)}, u32[]{:S(2)}) collective-permute-start(bf16[2,1,96,768]{3,2,1,0:T(8,128)(2,1)S(1)} %line_up.8.refs_0_), channel_id=1, source_target_pairs={{0,4},{4,0},{8,12},{12,8},{16,20},{20,16},{24,28},{28,24},{1,5},{5... | collective-permute-start | bytes 884744 | tf_op jit(solution)/shard_map/ppermute | solution.py:89
  23.9 7.8 %collective-permute-start.3 = (bf16[2,1,96,768]{3,2,1,0:T(8,128)(2,1)S(1)}, bf16[2,1,96,768]{3,2,1,0:T(8,128)(2,1)S(1)}, u32[]{:S(2)}, u32[]{:S(2)}) collective-permute-start(bf16[2,1,96,768]{3,2,1,0:T(8,128)(2,1)S(1)} %line_up.7.refs_0_), channel_id=1, source_target_pairs={{0,2},{1,3},{2,0},{3,1},{4,6},{5,7},{6,4},{7,5},{8,10},{9,11},{10,... | collective-permute-start | bytes 884744 | tf_op jit(solution)/shard_map/ppermute | solution.py:84
  24.5 9.3 %collective-permute-start.6 = (bf16[2,96,768]{2,1,0:T(8,128)(2,1)S(1)}, bf16[2,96,768]{2,1,0:T(8,128)(2,1)S(1)}, u32[]{:S(2)}, u32[]{:S(2)}) collective-permute-start(bf16[2,96,768]{2,1,0:T(8,128)(2,1)S(1)} %cast_ffn.1.refs_0_), channel_id=1, source_target_pairs={{0,8},{4,12},{8,16},{12,20},{16,24},{20,28},{24,0},{28,4},{1,9},{5... | collective-permute-start | bytes 884744 | tf_op jit(solution)/shard_map/ppermute | solution.py:99
  33.8 8.5 %collective-permute-start.9 = (bf16[2,96,768]{2,1,0:T(8,128)(2,1)S(1)}, bf16[2,96,768]{2,1,0:T(8,128)(2,1)S(1)}, u32[]{:S(2)}, u32[]{:S(2)}) collective-permute-start(bf16[2,96,768]{2,1,0:T(8,128)(2,1)S(1)} %collective-permute-done.6.refs_1_), channel_id=1, source_target_pairs={{0,8},{4,12},{8,16},{12,20},{16,24},{20,28},{24,0},{28,4},{1,9},{5... | collective-permute-start | bytes 884744 | tf_op jit(solution)/shard_map/ppermute | solution.py:99
  33.9 19.9 %collective-permute-start.8 = (bf16[2,2,1,96,768]{4,3,2,1,0:T(8,128)(2,1)S(1)}, bf16[2,2,1,96,768]{4,3,2,1,0:T(8,128)(2,1)S(1)}, u32[]{:S(2)}, u32[]{:S(2)}) collective-permute-start(bf16[2,2,1,96,768]{4,3,2,1,0:T(8,128)(2,1)S(1)} %line_up.10.refs_1_.refs_3_.refs_5_.refs_7_.refs_9_), channel_id=1, source_target_pairs={{0,2},{1,3},{2,0},{3,1},{4,6},{5,7},{6,4},{7,5},{8,10},{9,11},{10,... | collective-permute-start | bytes 1769480 | tf_op jit(solution)/shard_map/ppermute | solution.py:84
  35.5 18.3 %collective-permute-start.7 = (bf16[2,2,1,96,768]{4,3,2,1,0:T(8,128)(2,1)S(1)}, bf16[2,2,1,96,768]{4,3,2,1,0:T(8,128)(2,1)S(1)}, u32[]{:S(2)}, u32[]{:S(2)}) collective-permute-start(bf16[2,2,1,96,768]{4,3,2,1,0:T(8,128)(2,1)S(1)} %line_up.9.refs_0_.refs_4_.refs_12_.refs_6_.refs_10_), channel_id=1, source_target_pairs={{0,4},{4,0},{8,12},{12,8},{16,20},{20,16},{24,28},{28,24},{1,5},{5... | collective-permute-start | bytes 1769480 | tf_op jit(solution)/shard_map/ppermute | solution.py:89
  42.3 11.5 %collective-permute-start.10 = (bf16[2,96,768]{2,1,0:T(8,128)(2,1)S(1)}, bf16[2,96,768]{2,1,0:T(8,128)(2,1)S(1)}, u32[]{:S(2)}, u32[]{:S(2)}) collective-permute-start(bf16[2,96,768]{2,1,0:T(8,128)(2,1)S(1)} %collective-permute-done.9.refs_0_), channel_id=1, source_target_pairs={{0,8},{4,12},{8,16},{12,20},{16,24},{20,28},{24,0},{28,4},{1,9},{5... | collective-permute-start | bytes 884744 | tf_op jit(solution)/shard_map/ppermute | solution.py:99
  53.8 2.5 %collective-permute-start.11 = (bf16[512,768]{1,0:T(8,128)(2,1)S(1)}, bf16[512,768]{1,0:T(8,128)(2,1)S(1)}, u32[]{:S(2)}, u32[]{:S(2)}) collective-permute-start(bf16[512,768]{1,0:T(8,128)(2,1)S(1)} %get-tuple-element.279.x_ref), channel_id=1, source_target_pairs={{0,1},{1,0},{2,3},{3,2},{4,5},{5,4},{6,7},{7,6},{8,9},{9,8},{10,11... | collective-permute-start | bytes 2359304 | tf_op jit(solution)/shard_map/ppermute | solution.py:80
  58.6 21.1 %collective-permute-start.14 = (bf16[2,2,1,96,768]{4,3,2,1,0:T(8,128)(2,1)S(1)}, bf16[2,2,1,96,768]{4,3,2,1,0:T(8,128)(2,1)S(1)}, u32[]{:S(2)}, u32[]{:S(2)}) collective-permute-start(bf16[2,2,1,96,768]{4,3,2,1,0:T(8,128)(2,1)S(1)} %line_up.9.refs_0_.refs_4_.refs_12_.refs_6_.refs_10_), channel_id=1, source_target_pairs={{0,1},{1,0},{2,3},{3,2},{4,5},{5,4},{6,7},{7,6},{8,9},{9,8},{10,11... | collective-permute-start | bytes 1769480 | tf_op jit(solution)/shard_map/ppermute | solution.py:80
  59.1 28.0 %collective-permute-start.19 = (bf16[2,2,2,96,768]{4,3,2,1,0:T(8,128)(2,1)S(1)}, bf16[2,2,2,96,768]{4,3,2,1,0:T(8,128)(2,1)S(1)}, u32[]{:S(2)}, u32[]{:S(2)}) collective-permute-start(bf16[2,2,2,96,768]{4,3,2,1,0:T(8,128)(2,1)S(1)} %line_up.13.refs_8_.refs_9_), channel_id=1, source_target_pairs={{0,4},{4,0},{8,12},{12,8},{16,20},{20,16},{24,28},{28,24},{1,5},{5... | collective-permute-start | bytes 3538952 | tf_op jit(solution)/shard_map/ppermute | solution.py:89
  59.7 27.7 %collective-permute-start.18 = (bf16[2,2,2,96,768]{4,3,2,1,0:T(8,128)(2,1)S(1)}, bf16[2,2,2,96,768]{4,3,2,1,0:T(8,128)(2,1)S(1)}, u32[]{:S(2)}, u32[]{:S(2)}) collective-permute-start(bf16[2,2,2,96,768]{4,3,2,1,0:T(8,128)(2,1)S(1)} %line_up.13.refs_8_.refs_9_), channel_id=1, source_target_pairs={{0,2},{1,3},{2,0},{3,1},{4,6},{5,7},{6,4},{7,5},{8,10},{9,11},{10,... | collective-permute-start | bytes 3538952 | tf_op jit(solution)/shard_map/ppermute | solution.py:84
  69.1 8.8 %collective-permute-start.12 = (bf16[512,256]{1,0:T(8,128)(2,1)S(1)}, bf16[512,256]{1,0:T(8,128)(2,1)S(1)}, u32[]{:S(2)}, u32[]{:S(2)}) collective-permute-start(bf16[512,256]{1,0:T(8,128)(2,1)S(1)} %get-tuple-element.377.ctx_other_ref.refs_3_), channel_id=1, source_target_pairs={{0,1},{1,0},{2,3},{3,2},{4,5},{5,4},{6,7},{7,6},{8,9},{9,8},{10,11... | collective-permute-start | bytes 786440 | tf_op jit(solution)/shard_map/ppermute | solution.py:80
  69.2 10.9 %collective-permute-start.15 = (bf16[2,2,1,96,768]{4,3,2,1,0:T(8,128)(2,1)S(1)}, bf16[2,2,1,96,768]{4,3,2,1,0:T(8,128)(2,1)S(1)}, u32[]{:S(2)}, u32[]{:S(2)}) collective-permute-start(bf16[2,2,1,96,768]{4,3,2,1,0:T(8,128)(2,1)S(1)} %line_up.10.refs_1_.refs_3_.refs_5_.refs_7_.refs_9_), channel_id=1, source_target_pairs={{0,1},{1,0},{2,3},{3,2},{4,5},{5,4},{6,7},{7,6},{8,9},{9,8},{10,11... | collective-permute-start | bytes 1769480 | tf_op jit(solution)/shard_map/ppermute | solution.py:80
  78.0 1.6 collective-permute-start.13
  79.6 2.0 collective-permute-start.16
  79.7 2.7 %collective-permute-start.17 = (bf16[2,2,1,96,768]{4,3,2,1,0:T(8,128)(2,1)S(1)}, bf16[2,2,1,96,768]{4,3,2,1,0:T(8,128)(2,1)S(1)}, u32[]{:S(2)}, u32[]{:S(2)}) collective-permute-start(bf16[2,2,1,96,768]{4,3,2,1,0:T(8,128)(2,1)S(1)} %collective-permute-done.8.refs_5_.refs_7_.refs_13_.refs_15_.refs_11_), channel_id=1, source_target_pairs={{0,1},{1,0},{2,3},{3,2},{4,5},{5,4},{6,7},{7,6},{8,9},{9,8},{10,11... | collective-permute-start | bytes 1769480 | tf_op jit(solution)/shard_map/ppermute | solution.py:80
  80.1 9.4 %collective-permute-start.23 = (bf16[768,512]{1,0:T(8,128)(2,1)S(1)}, bf16[768,512]{1,0:T(8,128)(2,1)S(1)}, u32[]{:S(2)}, u32[]{:S(2)}) collective-permute-start(bf16[768,512]{1,0:T(8,128)(2,1)S(1)} %get-tuple-element.342.refs_6_), channel_id=1, source_target_pairs={{0,1},{1,0},{2,3},{3,2},{4,5},{5,4},{6,7},{7,6},{8,9},{9,8},{10,11... | collective-permute-start | bytes 2359304 | tf_op jit(solution)/shard_map/ppermute | solution.py:80
  81.6 9.5 %collective-permute-start.22 = (bf16[512,768]{1,0:T(8,128)(2,1)S(1)}, bf16[512,768]{1,0:T(8,128)(2,1)S(1)}, u32[]{:S(2)}, u32[]{:S(2)}) collective-permute-start(bf16[512,768]{1,0:T(8,128)(2,1)S(1)} %get-tuple-element.341.refs_4_.back_ref), channel_id=1, source_target_pairs={{0,1},{1,0},{2,3},{3,2},{4,5},{5,4},{6,7},{7,6},{8,9},{9,8},{10,11... | collective-permute-start | bytes 2359304 | tf_op jit(solution)/shard_map/ppermute | solution.py:80
  87.4 14.3 %collective-permute-start.24 = (bf16[2,2,96,768]{3,2,1,0:T(8,128)(2,1)S(1)}, bf16[2,2,96,768]{3,2,1,0:T(8,128)(2,1)S(1)}, u32[]{:S(2)}, u32[]{:S(2)}) collective-permute-start(bf16[2,2,96,768]{3,2,1,0:T(8,128)(2,1)S(1)} %slice_bitcast_fusion.1), channel_id=1, source_target_pairs={{0,4},{4,0},{8,12},{12,8},{16,20},{20,16},{24,28},{28,24},{1,5},{5... | collective-permute-start | bytes 1769480 | tf_op jit(solution)/shard_map/ppermute | solution.py:89
  88.9 2.3 %collective-permute-start.20 = (bf16[512,768]{1,0:T(8,128)(2,1)S(1)}, bf16[512,768]{1,0:T(8,128)(2,1)S(1)}, u32[]{:S(2)}, u32[]{:S(2)}) collective-permute-start(bf16[512,768]{1,0:T(8,128)(2,1)S(1)} %get-tuple-element.339.refs_0_), channel_id=1, source_target_pairs={{0,1},{1,0},{2,3},{3,2},{4,5},{5,4},{6,7},{7,6},{8,9},{9,8},{10,11... | collective-permute-start | bytes 2359304 | tf_op jit(solution)/shard_map/ppermute | solution.py:80
  88.9 3.4 %collective-permute-start.21 = (bf16[768,512]{1,0:T(8,128)(2,1)S(1)}, bf16[768,512]{1,0:T(8,128)(2,1)S(1)}, u32[]{:S(2)}, u32[]{:S(2)}) collective-permute-start(bf16[768,512]{1,0:T(8,128)(2,1)S(1)} %get-tuple-element.340.refs_2_), channel_id=1, source_target_pairs={{0,1},{1,0},{2,3},{3,2},{4,5},{5,4},{6,7},{7,6},{8,9},{9,8},{10,11... | collective-permute-start | bytes 2359304 | tf_op jit(solution)/shard_map/ppermute | solution.py:80
  89.5 15.3 %collective-permute-start.25 = (bf16[2,2,96,768]{3,2,1,0:T(8,128)(2,1)S(1)}, bf16[2,2,96,768]{3,2,1,0:T(8,128)(2,1)S(1)}, u32[]{:S(2)}, u32[]{:S(2)}) collective-permute-start(bf16[2,2,96,768]{3,2,1,0:T(8,128)(2,1)S(1)} %slice_bitcast_fusion), channel_id=1, source_target_pairs={{0,2},{1,3},{2,0},{3,1},{4,6},{5,7},{6,4},{7,5},{8,10},{9,11},{10,... | collective-permute-start | bytes 1769480 | tf_op jit(solution)/shard_map/ppermute | solution.py:84
  113.6 2.4 %collective-permute-start.26 = (bf16[512,768]{1,0:T(8,128)(2,1)S(1)}, bf16[512,768]{1,0:T(8,128)(2,1)S(1)}, u32[]{:S(2)}, u32[]{:S(2)}) collective-permute-start(bf16[512,768]{1,0:T(8,128)(2,1)S(1)} %get-tuple-element.363), channel_id=1, source_target_pairs={{0,1},{1,0},{2,3},{3,2},{4,5},{5,4},{6,7},{7,6},{8,9},{9,8},{10,11... | collective-permute-start | bytes 2359304 | tf_op jit(solution)/shard_map/ppermute | solution.py:80
  113.7 33.4 %collective-permute-start.29 = (bf16[2,2,2,96,768]{4,3,2,1,0:T(8,128)(2,1)S(1)}, bf16[2,2,2,96,768]{4,3,2,1,0:T(8,128)(2,1)S(1)}, u32[]{:S(2)}, u32[]{:S(2)}) collective-permute-start(bf16[2,2,2,96,768]{4,3,2,1,0:T(8,128)(2,1)S(1)} %get-tuple-element.388), channel_id=1, source_target_pairs={{0,2},{1,3},{2,0},{3,1},{4,6},{5,7},{6,4},{7,5},{8,10},{9,11},{10,... | collective-permute-start | bytes 3538952 | tf_op jit(solution)/shard_map/ppermute | solution.py:84
  115.3 4.0 %collective-permute-start.28 = (bf16[512,768]{1,0:T(8,128)(2,1)S(1)}, bf16[512,768]{1,0:T(8,128)(2,1)S(1)}, u32[]{:S(2)}, u32[]{:S(2)}) collective-permute-start(bf16[512,768]{1,0:T(8,128)(2,1)S(1)} %get-tuple-element.369), channel_id=1, source_target_pairs={{0,1},{1,0},{2,3},{3,2},{4,5},{5,4},{6,7},{7,6},{8,9},{9,8},{10,11... | collective-permute-start | bytes 2359304 | tf_op jit(solution)/shard_map/ppermute | solution.py:80
  117.0 2.4 %collective-permute-start.27 = (bf16[512,768]{1,0:T(8,128)(2,1)S(1)}, bf16[512,768]{1,0:T(8,128)(2,1)S(1)}, u32[]{:S(2)}, u32[]{:S(2)}) collective-permute-start(bf16[512,768]{1,0:T(8,128)(2,1)S(1)} %get-tuple-element.370.own_ref), channel_id=1, source_target_pairs={{0,1},{1,0},{2,3},{3,2},{4,5},{5,4},{6,7},{7,6},{8,9},{9,8},{10,11... | collective-permute-start | bytes 2359304 | tf_op jit(solution)/shard_map/ppermute | solution.py:80
  117.2 29.9 %collective-permute-start.31 = (bf16[2,2,96,768]{3,2,1,0:T(8,128)(2,1)S(1)}, bf16[2,2,96,768]{3,2,1,0:T(8,128)(2,1)S(1)}, u32[]{:S(2)}, u32[]{:S(2)}) collective-permute-start(bf16[2,2,96,768]{3,2,1,0:T(8,128)(2,1)S(1)} %get-tuple-element.390), channel_id=1, source_target_pairs={{0,4},{4,0},{8,12},{12,8},{16,20},{20,16},{24,28},{28,24},{1,5},{5... | collective-permute-start | bytes 1769480 | tf_op jit(solution)/shard_map/ppermute | solution.py:89
  117.8 29.4 %collective-permute-start.30 = (bf16[2,2,96,768]{3,2,1,0:T(8,128)(2,1)S(1)}, bf16[2,2,96,768]{3,2,1,0:T(8,128)(2,1)S(1)}, u32[]{:S(2)}, u32[]{:S(2)}) collective-permute-start(bf16[2,2,96,768]{3,2,1,0:T(8,128)(2,1)S(1)} %get-tuple-element.389), channel_id=1, source_target_pairs={{0,4},{4,0},{8,12},{12,8},{16,20},{20,16},{24,28},{28,24},{1,5},{5... | collective-permute-start | bytes 1769480 | tf_op jit(solution)/shard_map/ppermute | solution.py:89
  147.7 16.2 %collective-permute-start.32 = (bf16[2,2,96,768]{3,2,1,0:T(8,128)(2,1)S(1)}, bf16[2,2,96,768]{3,2,1,0:T(8,128)(2,1)S(1)}, u32[]{:S(2)}, u32[]{:S(2)}) collective-permute-start(bf16[2,2,96,768]{3,2,1,0:T(8,128)(2,1)S(1)} %get-tuple-element.404), channel_id=1, source_target_pairs={{0,4},{4,0},{8,12},{12,8},{16,20},{20,16},{24,28},{28,24},{1,5},{5... | collective-permute-start | bytes 1769480 | tf_op jit(solution)/shard_map/ppermute | solution.py:89
  148.3 16.2 %collective-permute-start.33 = (bf16[2,2,96,768]{3,2,1,0:T(8,128)(2,1)S(1)}, bf16[2,2,96,768]{3,2,1,0:T(8,128)(2,1)S(1)}, u32[]{:S(2)}, u32[]{:S(2)}) collective-permute-start(bf16[2,2,96,768]{3,2,1,0:T(8,128)(2,1)S(1)} %get-tuple-element.405), channel_id=1, source_target_pairs={{0,2},{1,3},{2,0},{3,1},{4,6},{5,7},{6,4},{7,5},{8,10},{9,11},{10,... | collective-permute-start | bytes 1769480 | tf_op jit(solution)/shard_map/ppermute | solution.py:84
  156.4 9.6 %collective-permute-start.34 = (bf16[512,768]{1,0:T(8,128)(2,1)S(1)}, bf16[512,768]{1,0:T(8,128)(2,1)S(1)}, u32[]{:S(2)}, u32[]{:S(2)}) collective-permute-start(bf16[512,768]{1,0:T(8,128)(2,1)S(1)} %get-tuple-element.415), channel_id=1, source_target_pairs={{0,1},{1,0},{2,3},{3,2},{4,5},{5,4},{6,7},{7,6},{8,9},{9,8},{10,11... | collective-permute-start | bytes 2359304 | tf_op jit(solution)/shard_map/ppermute | solution.py:80
  156.5 19.5 %collective-permute-start.35 = (bf16[2,2,1,96,768]{4,3,2,1,0:T(8,128)(2,1)S(1)}, bf16[2,2,1,96,768]{4,3,2,1,0:T(8,128)(2,1)S(1)}, u32[]{:S(2)}, u32[]{:S(2)}) collective-permute-start(bf16[2,2,1,96,768]{4,3,2,1,0:T(8,128)(2,1)S(1)} %get-tuple-element.432), channel_id=1, source_target_pairs={{0,2},{1,3},{2,0},{3,1},{4,6},{5,7},{6,4},{7,5},{8,10},{9,11},{10,... | collective-permute-start | bytes 1769480 | tf_op jit(solution)/shard_map/ppermute | solution.py:84
  157.1 19.0 %collective-permute-start.36 = (bf16[2,2,1,96,768]{4,3,2,1,0:T(8,128)(2,1)S(1)}, bf16[2,2,1,96,768]{4,3,2,1,0:T(8,128)(2,1)S(1)}, u32[]{:S(2)}, u32[]{:S(2)}) collective-permute-start(bf16[2,2,1,96,768]{4,3,2,1,0:T(8,128)(2,1)S(1)} %get-tuple-element.433), channel_id=1, source_target_pairs={{0,4},{4,0},{8,12},{12,8},{16,20},{20,16},{24,28},{28,24},{1,5},{5... | collective-permute-start | bytes 1769480 | tf_op jit(solution)/shard_map/ppermute | solution.py:89
  164.8 12.4 %collective-permute-start.37 = (bf16[2,96,768]{2,1,0:T(8,128)(2,1)S(1)}, bf16[2,96,768]{2,1,0:T(8,128)(2,1)S(1)}, u32[]{:S(2)}, u32[]{:S(2)}) collective-permute-start(bf16[2,96,768]{2,1,0:T(8,128)(2,1)S(1)} %get-tuple-element.412), channel_id=1, source_target_pairs={{0,8},{4,12},{8,0},{12,4},{16,24},{20,28},{24,16},{28,20},{1,9},{5... | collective-permute-start | bytes 884744 | tf_op jit(solution)/shard_map/ppermute | solution.py:94
  165.5 22.8 %collective-permute-start.40 = (bf16[2,96,768]{2,1,0:T(8,128)(2,1)S(1)}, bf16[2,96,768]{2,1,0:T(8,128)(2,1)S(1)}, u32[]{:S(2)}, u32[]{:S(2)}) collective-permute-start(bf16[2,96,768]{2,1,0:T(8,128)(2,1)S(1)} %get-tuple-element.413), channel_id=1, source_target_pairs={{0,16},{4,20},{8,24},{12,28},{16,0},{20,4},{24,8},{28,12},{1,17},{... | collective-permute-start | bytes 884744 | tf_op jit(solution)/shard_map/ppermute | solution.py:94
  166.0 22.2 %collective-permute-start.41 = (bf16[2,96,768]{2,1,0:T(8,128)(2,1)S(1)}, bf16[2,96,768]{2,1,0:T(8,128)(2,1)S(1)}, u32[]{:S(2)}, u32[]{:S(2)}) collective-permute-start(bf16[2,96,768]{2,1,0:T(8,128)(2,1)S(1)} %get-tuple-element.414), channel_id=1, source_target_pairs={{0,24},{4,28},{8,16},{12,20},{16,8},{20,12},{24,0},{28,4},{1,25},{... | collective-permute-start | bytes 884744 | tf_op jit(solution)/shard_map/ppermute | solution.py:94
  177.5 10.8 %collective-permute-start.38 = (bf16[2,1,96,768]{3,2,1,0:T(8,128)(2,1)S(1)}, bf16[2,1,96,768]{3,2,1,0:T(8,128)(2,1)S(1)}, u32[]{:S(2)}, u32[]{:S(2)}) collective-permute-start(bf16[2,1,96,768]{3,2,1,0:T(8,128)(2,1)S(1)} %get-tuple-element.438), channel_id=1, source_target_pairs={{0,4},{4,0},{8,12},{12,8},{16,20},{20,16},{24,28},{28,24},{1,5},{5... | collective-permute-start | bytes 884744 | tf_op jit(solution)/shard_map/ppermute | solution.py:89
  179.0 9.3 %collective-permute-start.39 = (bf16[2,1,96,768]{3,2,1,0:T(8,128)(2,1)S(1)}, bf16[2,1,96,768]{3,2,1,0:T(8,128)(2,1)S(1)}, u32[]{:S(2)}, u32[]{:S(2)}) collective-permute-start(bf16[2,1,96,768]{3,2,1,0:T(8,128)(2,1)S(1)} %get-tuple-element.439), channel_id=1, source_target_pairs={{0,2},{1,3},{2,0},{3,1},{4,6},{5,7},{6,4},{7,5},{8,10},{9,11},{10,... | collective-permute-start | bytes 884744 | tf_op jit(solution)/shard_map/ppermute | solution.py:84
  188.3 16.7 %collective-permute-start.45 = (bf16[2,256,768]{2,1,0:T(8,128)(2,1)S(1)}, bf16[2,256,768]{2,1,0:T(8,128)(2,1)S(1)}, u32[]{:S(2)}, u32[]{:S(2)}) collective-permute-start(bf16[2,256,768]{2,1,0:T(8,128)(2,1)S(1)} %get-tuple-element.460), channel_id=1, source_target_pairs={{0,2},{1,3},{2,0},{3,1},{4,6},{5,7},{6,4},{7,5},{8,10},{9,11},{10,... | collective-permute-start | bytes 2359304 | tf_op jit(solution)/shard_map/ppermute | solution.py:84
  190.0 10.4 %collective-permute-start.42 = (bf16[1,96,768]{2,1,0:T(8,128)(2,1)S(1)}, bf16[1,96,768]{2,1,0:T(8,128)(2,1)S(1)}, u32[]{:S(2)}, u32[]{:S(2)}) collective-permute-start(bf16[1,96,768]{2,1,0:T(8,128)(2,1)S(1)} %get-tuple-element.457), channel_id=1, source_target_pairs={{0,8},{4,12},{8,0},{12,4},{16,24},{20,28},{24,16},{28,20},{1,9},{5... | collective-permute-start | bytes 442376 | tf_op jit(solution)/shard_map/ppermute | solution.py:94
  194.1 10.8 %collective-permute-start.43 = (bf16[1,96,768]{2,1,0:T(8,128)(2,1)S(1)}, bf16[1,96,768]{2,1,0:T(8,128)(2,1)S(1)}, u32[]{:S(2)}, u32[]{:S(2)}) collective-permute-start(bf16[1,96,768]{2,1,0:T(8,128)(2,1)S(1)} %get-tuple-element.458), channel_id=1, source_target_pairs={{0,16},{4,20},{8,24},{12,28},{16,0},{20,4},{24,8},{28,12},{1,17},{... | collective-permute-start | bytes 442376 | tf_op jit(solution)/shard_map/ppermute | solution.py:94
  194.3 10.7 %collective-permute-start.44 = (bf16[1,96,768]{2,1,0:T(8,128)(2,1)S(1)}, bf16[1,96,768]{2,1,0:T(8,128)(2,1)S(1)}, u32[]{:S(2)}, u32[]{:S(2)}) collective-permute-start(bf16[1,96,768]{2,1,0:T(8,128)(2,1)S(1)} %get-tuple-element.459), channel_id=1, source_target_pairs={{0,24},{4,28},{8,16},{12,20},{16,8},{20,12},{24,0},{28,4},{1,25},{... | collective-permute-start | bytes 442376 | tf_op jit(solution)/shard_map/ppermute | solution.py:94
  197.6 25.5 %copy-start.2 = (f32[2,96,768]{2,1,0:T(8,128)S(1)}, f32[2,96,768]{2,1,0:T(8,128)}, u32[]{:S(2)}) copy-start(f32[2,96,768]{2,1,0:T(8,128)} %get-tuple-element.238.ffn_ref) | copy-start | bytes 1769476
  206.0 17.1 %all-to-all-start.1 = ((f32[32,16,128]{2,1,0:T(8,128)}), f32[32,16,128]{2,1,0:T(8,128)S(1)}, u32[]{:S(2)}, u32[]{:S(2)}) async-start(f32[32,16,128]{2,1,0:T(8,128)} %broadcast_in_dim.5), calls=%async_computation.1 | async-start | bytes 524288 | tf_op jit(solution)/shard_map/all_to_all | solution.py:108
  (4 other events, 33.6 us)

commit v8 on v7

--- a/solution.py
+++ b/solution.py
@@ -101,11 +101,6 @@
 
 def fence(*values):
     return lax.optimization_barrier(values)
-
-
-def from_all(v):
-    n = lax.axis_size("dp") * lax.axis_size("mp")
-    return lax.all_to_all(jnp.broadcast_to(v[None], (n,) + v.shape), ("dp", "mp"), 0, 0)
 
 
 def gather_gains(gains):
@@ -938,16 +933,20 @@
     for ref in refs[:-4]:
         total = total + ref[...].astype(F32)
     out_ref[...] = total
-    sums_ref[0:15] = small_ref[0:15]
-    sums_ref[15:16] = squares_ref[...] + jnp.sum(total * total)
-
-
-def total_with(own, came, squares, small):
+    squares = squares_ref[...] + jnp.sum(total * total)
+    high = squares.astype(BF).astype(F32)
+    lane = lax.broadcasted_iota(jnp.int32, squares.shape, 1)
+    last = jnp.where(lane == 0, high, jnp.where(lane == 1, squares - high, 0.0))
+    sums = jnp.concatenate([small_ref[0:15], last], 0).astype(BF)
+    sums_ref[...] = jnp.broadcast_to(sums[None], sums_ref.shape)
+
+
+def total_with(own, came, squares, small, copies):
     return pl.pallas_call(
         total_with_kernel,
         in_specs=[in_vmem] * (3 + len(came)),
         out_specs=[in_vmem] * 2,
-        out_shape=[shape_of(own.shape, F32), shape_of(small.shape, F32)],
+        out_shape=[shape_of(own.shape, F32), shape_of((copies,) + small.shape, BF)],
         compiler_params=params(MERGE_MIB),
         cost_estimate=cost(1, 1),
         name="total_with",
@@ -959,10 +958,10 @@
     copies = [pltpu.make_async_copy(sources[i], olds[i], sems.at[i]) for i in range(12)]
     for c in copies:
         c.start()
-    small = jnp.sum(small_ref[...], axis=0)
+    small = jnp.sum(small_ref[...].astype(F32), axis=0)
     sums = small[0:15]
     squares = jnp.sum(jnp.sum(sums * sums, axis=0, keepdims=True), axis=1, keepdims=True)
-    norm = jnp.sqrt(small[15:16, 0:1] + squares)
+    norm = jnp.sqrt(small[15:16, 0:1] + small[15:16, 1:2] + squares)
     outs[0][...] = norm
     clip = jnp.minimum(1.0, clip_level / (norm + 1e-06))
     count = outs[2].shape[1]
@@ -1199,8 +1198,9 @@
     ffn_total, ffn_squares = total_of(ffn_own, ffn_back)
     attn_own, ffn_total, ffn_squares, small = fence(attn_own, ffn_total, ffn_squares, small)
     attn_own, attn_back, came_last = fence(attn_own, attn_back, came_last)
-    attn_total, small = total_with(attn_own, attn_back, ffn_squares, small)
-    every_small = from_all(small)
+    devices = 2 * depth * lax.axis_size("mp")
+    attn_total, small = total_with(attn_own, attn_back, ffn_squares, small, devices)
+    every_small = lax.all_to_all(small, ("dp", "mp"), 0, 0).reshape(small.shape)
     block_out, input_grad = place_rows(place, (out_keep, in_keep), came_last)
     olds = [
         *(attn_weights, attn_first, attn_second),
@@ -1209,7 +1209,7 @@
         *(bias_table, table_first, table_second),
     ]
     grad_norm, attn_reduced, gain_grads, table_grads, *news = update(
-        dp.astype(jnp.int32).reshape(1), every_small.reshape(-1, *small.shape), attn_total, ffn_total, olds
+        dp.astype(jnp.int32).reshape(1), every_small, attn_total, ffn_total, olds
     )
     return (
         block_out,

time: 231 us -> 228 us (0.987)
  waiting for transfers between devices: 67.5 us -> 65.1 us
    all_to_all x1, waiting for transfers between devices: 8.81 us -> 6.44 us  [per_device(): every_small = lax.all_to_all(small, ('dp', 'mp'), 0, 0).reshape(small.shape)]
  transfers between devices with their start and end apart: 47 -> 47, of which waited for: 24 -> 24; matrix products, arithmetic and copies ran while one was open for 0% -> 0% of each run, Pallas kernels for 34% -> 35%
where the time goes in v8:
time: 228 us; the launch traced here: 225 us
  Pallas kernels  96.4 us (42%)
  waiting for transfers between devices  65.1 us (29%)
  starting transfers between devices  50 us (22%)
  blocking collectives  11.4 us (5%)
    pallas_call x2, Pallas kernels, attend_back(): pl.pallas_call(functools.partial(attend_back_kernel, r // 2), in_specs=[i...  26.1 us
    ppermute x9, waiting for transfers between devices, swap_z(): return lax.ppermute(v, 'dp', [(i, i ^ 2 * k) for i in range(n)])  22.4 us
    pallas_call x2, Pallas kernels, feed(): pl.pallas_call(functools.partial(feed_kernel, indices, first, split), in_...  17.3 us
    pallas_call x2, Pallas kernels, attend(): pl.pallas_call(functools.partial(attend_kernel, r // 2, r), in_specs=[in_...  16.2 us
    ppermute x9, starting transfers between devices, swap_z(): return lax.ppermute(v, 'dp', [(i, i ^ 2 * k) for i in range(n)])  15.5 us
    ppermute x10, starting transfers between devices, swap_x(): return lax.ppermute(v, 'mp', [(i, i ^ 2) for i in range(4)])  14.9 us
    ppermute x9, waiting for transfers between devices, swap_y(): return lax.ppermute(v, 'dp', [(i, i ^ 1) for i in range(n)])  14.6 us
    all_to_all x1, blocking collectives, gather_gains(): lax.all_to_all(jnp.broadcast_to(low[None], (n,) + low.shape), 'dp', 0, 0)  11.4 us
  transfers between devices with their start and end apart: 47, of which 24 were waited for; matrix products, arithmetic and copies ran while one was open for 0% of the time, Pallas kernels for 35%

profile of v8, /device:TPU:0, one launch (start us, length us, event | category | flops | bytes accessed | tf_op | source)
XLA Modules:
  0.0 225.1 jit_solution(15205418109169298881)
XLA Ops:
  1.6 1.7 sort_rows.1
  3.3 3.0 %collective-permute-start.5 = (bf16[2,256,768]{2,1,0:T(8,128)(2,1)S(1)}, bf16[2,256,768]{2,1,0:T(8,128)(2,1)S(1)}, u32[]{:S(2)}, u32[]{:S(2)}) collective-permute-start(bf16[2,256,768]{2,1,0:T(8,128)(2,1)S(1)} %sort_rows.1), channel_id=1, source_target_pairs={{0,2},{1,3},{2,0},{3,1},{4,6},{5,7},{6,4},{7,5},{8,10},{9,11},{10,... | collective-permute-start | bytes 2359304 | tf_op jit(solution)/shard_map/ppermute | solution.py:84
  6.4 3.7 %collective-permute-start.2 = (bf16[1,96,768]{2,1,0:T(8,128)(2,1)S(1)}, bf16[1,96,768]{2,1,0:T(8,128)(2,1)S(1)}, u32[]{:S(2)}, u32[]{:S(2)}) collective-permute-start(bf16[1,96,768]{2,1,0:T(8,128)(2,1)S(1)} %cast_attn.1.refs_0_), channel_id=1, source_target_pairs={{0,24},{4,28},{8,16},{12,20},{16,8},{20,12},{24,0},{28,4},{1,25},{... | collective-permute-start | bytes 442376 | tf_op jit(solution)/shard_map/ppermute | solution.py:94
  10.9 5.2 %bias_tiles.1.bias_ref = f32[4,3,5,128,128]{4,3,2,1,0:T(8,128)S(1)} custom-call(s32[21]{0:T(128)S(1)} %stack.79.place_ref, f32[12,32]{1,0:T(8,128)S(1)} %copy-done.3), custom_call_target="tpu_custom_call" | custom-call | flops 1000 | bytes 1000 | tf_op jit(solution)/shard_map/bias_tiles/pallas_call | solution.py:188
  16.1 6.1 %collective-permute-done.1.refs_0_ = bf16[1,96,768]{2,1,0:T(8,128)(2,1)S(1)} collective-permute-done((bf16[1,96,768]{2,1,0:T(8,128)(2,1)S(1)}, bf16[1,96,768]{2,1,0:T(8,128)(2,1)S(1)}, u32[]{:S(2)}, u32[]{:S(2)}) %collective-permute-start.1) | collective-permute-done | bytes 147488 | tf_op jit(solution)/shard_map/ppermute | solution.py:94
  22.3 1.6 collective-permute-start.4
  24.5 5.9 %collective-permute-done.4.refs_1_ = bf16[2,1,96,768]{3,2,1,0:T(8,128)(2,1)S(1)} collective-permute-done((bf16[2,1,96,768]{3,2,1,0:T(8,128)(2,1)S(1)}, bf16[2,1,96,768]{3,2,1,0:T(8,128)(2,1)S(1)}, u32[]{:S(2)}, u32[]{:S(2)}) %collective-permute-start.4) | collective-permute-done | bytes 294944 | tf_op jit(solution)/shard_map/ppermute | solution.py:89
  31.7 2.1 collective-permute-done.6.refs_1_
  33.9 1.6 collective-permute-start.8
  36.0 1.9 join_rows.1
  38.0 4.4 %collective-permute-done.9.refs_0_ = bf16[2,96,768]{2,1,0:T(8,128)(2,1)S(1)} collective-permute-done((bf16[2,96,768]{2,1,0:T(8,128)(2,1)S(1)}, bf16[2,96,768]{2,1,0:T(8,128)(2,1)S(1)}, u32[]{:S(2)}, u32[]{:S(2)}) %collective-permute-start.9) | collective-permute-done | bytes 294944 | tf_op jit(solution)/shard_map/ppermute | solution.py:99
  42.3 11.4 %all_to_all.10.g_ref = bf16[8,2,96]{2,1,0:T(2,128)(2,1)S(1)} all-to-all(bf16[8,2,96]{2,1,0:T(2,128)(2,1)S(1)} %broadcast_in_dim.2), channel_id=1, replica_groups=mesh['dp'=8,'mp'=4] {'dp'}, dimensions={0} | all-to-all | bytes 6144 | tf_op jit(solution)/shard_map/all_to_all | solution.py:109
  54.1 2.2 project.2
  56.3 2.2 project.3
  59.7 1.5 collective-permute-start.18
  61.2 8.0 %attend.2 = (bf16[512,256]{1,0:T(8,128)(2,1)S(1)}, bf16[512,256]{1,0:T(8,128)(2,1)S(1)}, bf16[3,1024,1024]{2,1,0:T(8,128)(2,1)}) custom-call(s32[21]{0:T(128)S(1)} %stack.79.place_ref, bf16[2,512,192]{2,1,0:T(8,128)(2,1)S(1)} %get-tuple-element.374.q_own_ref, bf16[2,512,192]{2,1,0:T(8,128)(2,1)S(1)} %get-tuple-element.375.q_other_ref, ...), custom_call_target="tpu_custom_call" | custom-call | flops 1000 | bytes 1000 | tf_op jit(solution)/shard_map/attend/pallas_call | solution.py:321
  69.7 8.2 %attend.3 = (bf16[512,256]{1,0:T(8,128)(2,1)S(1)}, bf16[512,256]{1,0:T(8,128)(2,1)S(1)}, bf16[3,1024,1024]{2,1,0:T(8,128)(2,1)}) custom-call(s32[21]{0:T(128)S(1)} %stack.79.place_ref, bf16[2,512,192]{2,1,0:T(8,128)(2,1)S(1)} %get-tuple-element.374.q_own_ref, bf16[2,512,192]{2,1,0:T(8,128)(2,1)S(1)} %get-tuple-element.375.q_other_ref, ...), custom_call_target="tpu_custom_call" | custom-call | flops 1000 | bytes 1000 | tf_op jit(solution)/shard_map/attend/pallas_call | solution.py:321
  82.4 2.1 middle.1
  84.5 2.6 %collective-permute-done.19.refs_10_.refs_11_ = bf16[2,2,2,96,768]{4,3,2,1,0:T(8,128)(2,1)S(1)} collective-permute-done((bf16[2,2,2,96,768]{4,3,2,1,0:T(8,128)(2,1)S(1)}, bf16[2,2,2,96,768]{4,3,2,1,0:T(8,128)(2,1)S(1)}, u32[]{:S(2)}, u32[]{:S(2)}) %collective-permute-start.19) | collective-permute-done | bytes 1179680 | tf_op jit(solution)/shard_map/ppermute | solution.py:89
  87.4 1.5 collective-permute-start.24
  89.5 1.6 collective-permute-start.25
  92.3 8.5 %feed.2 = (f32[512,768]{1,0:T(8,128)S(1)}, f32[512,768]{1,0:T(8,128)S(1)}, f32[512,768]{1,0:T(8,128)S(1)}, f32[512,768]{1,0:T(8,128)S(1)}, bf16[2,2,2,96,768]{4,...) custom-call(s32[21]{0:T(128)S(1)} %stack.79.place_ref, ...), custom_call_target="tpu_custom_call" | custom-call | flops 1000 | bytes 1000 | tf_op jit(solution)/shard_map/feed/pallas_call | solution.py:427
  101.7 3.1 %collective-permute-done.25.refs_15_ = bf16[2,2,96,768]{3,2,1,0:T(8,128)(2,1)S(1)} collective-permute-done((bf16[2,2,96,768]{3,2,1,0:T(8,128)(2,1)S(1)}, bf16[2,2,96,768]{3,2,1,0:T(8,128)(2,1)S(1)}, u32[]{:S(2)}, u32[]{:S(2)}) %collective-permute-start.25) | collective-permute-done | bytes 589856 | tf_op jit(solution)/shard_map/ppermute | solution.py:84
  104.8 8.8 %feed.3 = (f32[512,768]{1,0:T(8,128)S(1)}, bf16[512,768]{1,0:T(8,128)(2,1)S(1)}, f32[512,768]{1,0:T(8,128)S(1)}, bf16[512,768]{1,0:T(8,128)(2,1)S(1)}, bf16[2,2,...) custom-call(s32[21]{0:T(128)S(1)} %stack.79.place_ref, ...), custom_call_target="tpu_custom_call" | custom-call | flops 1000 | bytes 1000 | tf_op jit(solution)/shard_map/feed/pallas_call | solution.py:427
  113.7 1.5 collective-permute-start.29
  117.8 1.5 collective-permute-start.30
  119.4 1.7 context_grads.1
  121.1 13.2 %attend_back.2 = (bf16[1024,576]{1,0:T(8,128)(2,1)S(1)}, f32[3,32,128]{2,1,0:T(8,128)S(1)}) custom-call(s32[21]{0:T(128)S(1)} %stack.79.place_ref, bf16[2,512,192]{2,1,0:T(8,128)(2,1)S(1)} %get-tuple-element.374.q_own_ref, bf16[2,512,192]{2,1,0:T(8,128)(2,1)S(1)} %get-tuple-element.375.q_other_ref, bf16[2,512,384]{2,1,0:T(8,128)(2,1)S(1)} %get-tuple-element.306.kv_own_ref, ...), custom_call_target="tpu_custom_call" | custom-call | flops 1000 | bytes 1000 | tf_op jit(solution)/shard_map/attend_back/pallas_call | solution.py:567
  134.2 12.9 %attend_back.3 = (bf16[1024,576]{1,0:T(8,128)(2,1)S(1)}, f32[3,32,128]{2,1,0:T(8,128)S(1)}) custom-call(s32[21]{0:T(128)S(1)} %stack.79.place_ref, bf16[2,512,192]{2,1,0:T(8,128)(2,1)S(1)} %get-tuple-element.374.q_own_ref, bf16[2,512,192]{2,1,0:T(8,128)(2,1)S(1)} %get-tuple-element.375.q_other_ref, bf16[2,512,384]{2,1,0:T(8,128)(2,1)S(1)} %get-tuple-element.306.kv_own_ref, ...), custom_call_target="tpu_custom_call" | custom-call | flops 1000 | bytes 1000 | tf_op jit(solution)/shard_map/attend_back/pallas_call | solution.py:567
  148.3 1.5 collective-permute-start.33
  149.8 6.6 %project_back.1 = (f32[512,768]{1,0:T(8,128)S(1)}, bf16[512,768]{1,0:T(8,128)(2,1)S(1)}, bf16[2,2,1,96,768]{4,3,2,1,0:T(8,128)(2,1)S(1)}, bf16[2,2,1,96,768]{4,3...) custom-call(s32[21]{0:T(128)S(1)} %stack.79.place_ref, ...), custom_call_target="tpu_custom_call" | custom-call | flops 1000 | bytes 1000 | tf_op jit(solution)/shard_map/project_back/pallas_call | solution.py:626
  157.1 1.5 collective-permute-start.36
  158.6 5.4 %collective-permute-done.32.near_came_ref = bf16[2,2,96,768]{3,2,1,0:T(8,128)(2,1)S(1)} collective-permute-done((bf16[2,2,96,768]{3,2,1,0:T(8,128)(2,1)S(1)}, bf16[2,2,96,768]{3,2,1,0:T(8,128)(2,1)S(1)}, u32[]{:S(2)}, u32[]{:S(2)}) %collective-permute-start.32) | collective-permute-done | bytes 589856 | tf_op jit(solution)/shard_map/ppermute | solution.py:89
  166.0 3.2 %collective-permute-start.41 = (bf16[2,96,768]{2,1,0:T(8,128)(2,1)S(1)}, bf16[2,96,768]{2,1,0:T(8,128)(2,1)S(1)}, u32[]{:S(2)}, u32[]{:S(2)}) collective-permute-start(bf16[2,96,768]{2,1,0:T(8,128)(2,1)S(1)} %get-tuple-element.414), channel_id=1, source_target_pairs={{0,24},{4,28},{8,16},{12,20},{16,8},{20,12},{24,0},{28,4},{1,25},{... | collective-permute-start | bytes 884744 | tf_op jit(solution)/shard_map/ppermute | solution.py:94
  169.3 1.5 finish.1
  171.7 4.4 %collective-permute-done.35.near_came_ref = bf16[2,2,1,96,768]{4,3,2,1,0:T(8,128)(2,1)S(1)} collective-permute-done((bf16[2,2,1,96,768]{4,3,2,1,0:T(8,128)(2,1)S(1)}, bf16[2,2,1,96,768]{4,3,2,1,0:T(8,128)(2,1)S(1)}, u32[]{:S(2)}, u32[]{:S(2)}) %collective-permute-start.35) | collective-permute-done | bytes 589856 | tf_op jit(solution)/shard_map/ppermute | solution.py:84
  177.5 1.5 collective-permute-start.38
  179.0 1.5 collective-permute-start.39
  180.6 7.7 %collective-permute-done.40.refs_1_ = bf16[2,96,768]{2,1,0:T(8,128)(2,1)S(1)} collective-permute-done((bf16[2,96,768]{2,1,0:T(8,128)(2,1)S(1)}, bf16[2,96,768]{2,1,0:T(8,128)(2,1)S(1)}, u32[]{:S(2)}, u32[]{:S(2)}) %collective-permute-start.40) | collective-permute-done | bytes 294944 | tf_op jit(solution)/shard_map/ppermute | solution.py:94
  188.3 1.6 collective-permute-start.45
  190.0 4.1 %collective-permute-start.42 = (bf16[1,96,768]{2,1,0:T(8,128)(2,1)S(1)}, bf16[1,96,768]{2,1,0:T(8,128)(2,1)S(1)}, u32[]{:S(2)}, u32[]{:S(2)}) collective-permute-start(bf16[1,96,768]{2,1,0:T(8,128)(2,1)S(1)} %get-tuple-element.457), channel_id=1, source_target_pairs={{0,8},{4,12},{8,0},{12,4},{16,24},{20,28},{24,16},{28,20},{1,9},{5... | collective-permute-start | bytes 442376 | tf_op jit(solution)/shard_map/ppermute | solution.py:94
  194.3 2.3 %collective-permute-start.44 = (bf16[1,96,768]{2,1,0:T(8,128)(2,1)S(1)}, bf16[1,96,768]{2,1,0:T(8,128)(2,1)S(1)}, u32[]{:S(2)}, u32[]{:S(2)}) collective-permute-start(bf16[1,96,768]{2,1,0:T(8,128)(2,1)S(1)} %get-tuple-element.459), channel_id=1, source_target_pairs={{0,24},{4,28},{8,16},{12,20},{16,8},{20,12},{24,0},{28,4},{1,25},{... | collective-permute-start | bytes 442376 | tf_op jit(solution)/shard_map/ppermute | solution.py:94
  197.6 2.8 %collective-permute-done.42.refs_0_ = bf16[1,96,768]{2,1,0:T(8,128)(2,1)S(1)} collective-permute-done((bf16[1,96,768]{2,1,0:T(8,128)(2,1)S(1)}, bf16[1,96,768]{2,1,0:T(8,128)(2,1)S(1)}, u32[]{:S(2)}, u32[]{:S(2)}) %collective-permute-start.42) | collective-permute-done | bytes 147488 | tf_op jit(solution)/shard_map/ppermute | solution.py:94
  200.4 4.6 %collective-permute-done.43.refs_1_ = bf16[1,96,768]{2,1,0:T(8,128)(2,1)S(1)} collective-permute-done((bf16[1,96,768]{2,1,0:T(8,128)(2,1)S(1)}, bf16[1,96,768]{2,1,0:T(8,128)(2,1)S(1)}, u32[]{:S(2)}, u32[]{:S(2)}) %collective-permute-start.43) | collective-permute-done | bytes 147488 | tf_op jit(solution)/shard_map/ppermute | solution.py:94
  205.9 6.5 %all-to-all-start.1 = ((bf16[32,16,128]{2,1,0:T(8,128)(2,1)}), bf16[32,16,128]{2,1,0:T(8,128)(2,1)S(1)}, u32[]{:S(2)}, u32[]{:S(2)}) async-start(bf16[32,16,128]{2,1,0:T(8,128)(2,1)} %get-tuple-element.470), calls=%async_computation.1 | async-start | bytes 262144 | tf_op jit(solution)/shard_map/all_to_all | solution.py:1203
  212.4 1.8 place_rows.1
  214.2 6.4 %all-to-all-done.1.small_ref = bf16[32,16,128]{2,1,0:T(8,128)(2,1)S(1)} async-done(((bf16[32,16,128]{2,1,0:T(8,128)(2,1)}), bf16[32,16,128]{2,1,0:T(8,128)(2,1)S(1)}, u32[]{:S(2)}, u32[]{:S(2)}) %all-to-all-start.1) | async-done | bytes 131104 | tf_op jit(solution)/shard_map/all_to_all | solution.py:1203
  220.6 4.3 %update.1 = (f32[1,1]{1,0:T(1,128)}, f32[4,96,192]{2,1,0:T(8,128)}, f32[2,96]{1,0:T(2,128)}, f32[12,32]{1,0:T(8,128)}, f32[4,96,192]{2,1,0:T(8,128)}, /*index=5*...) custom-call(s32[1]{0:T(128)} %bitcast.21.place_ref, ...), custom_call_target="tpu_custom_call" | custom-call | flops 1000 | bytes 1000 | tf_op jit(solution)/shard_map/update/pallas_call | solution.py:1001
  (97 shorter events, 24.9 us)
Async XLA Ops:
  3.3 30.5 %collective-permute-start.5 = (bf16[2,256,768]{2,1,0:T(8,128)(2,1)S(1)}, bf16[2,256,768]{2,1,0:T(8,128)(2,1)S(1)}, u32[]{:S(2)}, u32[]{:S(2)}) collective-permute-start(bf16[2,256,768]{2,1,0:T(8,128)(2,1)S(1)} %sort_rows.1), channel_id=1, source_target_pairs={{0,2},{1,3},{2,0},{3,1},{4,6},{5,7},{6,4},{7,5},{8,10},{9,11},{10,... | collective-permute-start | bytes 2359304 | tf_op jit(solution)/shard_map/ppermute | solution.py:84
  6.4 9.7 %collective-permute-start.2 = (bf16[1,96,768]{2,1,0:T(8,128)(2,1)S(1)}, bf16[1,96,768]{2,1,0:T(8,128)(2,1)S(1)}, u32[]{:S(2)}, u32[]{:S(2)}) collective-permute-start(bf16[1,96,768]{2,1,0:T(8,128)(2,1)S(1)} %cast_attn.1.refs_0_), channel_id=1, source_target_pairs={{0,24},{4,28},{8,16},{12,20},{16,8},{20,12},{24,0},{28,4},{1,25},{... | collective-permute-start | bytes 442376 | tf_op jit(solution)/shard_map/ppermute | solution.py:94
  10.1 12.2 %collective-permute-start.1 = (bf16[1,96,768]{2,1,0:T(8,128)(2,1)S(1)}, bf16[1,96,768]{2,1,0:T(8,128)(2,1)S(1)}, u32[]{:S(2)}, u32[]{:S(2)}) collective-permute-start(bf16[1,96,768]{2,1,0:T(8,128)(2,1)S(1)} %cast_attn.1.refs_0_), channel_id=1, source_target_pairs={{0,16},{4,20},{8,24},{12,28},{16,0},{20,4},{24,8},{28,12},{1,17},{... | collective-permute-start | bytes 442376 | tf_op jit(solution)/shard_map/ppermute | solution.py:94
  10.1 12.2 %collective-permute-start = (bf16[1,96,768]{2,1,0:T(8,128)(2,1)S(1)}, bf16[1,96,768]{2,1,0:T(8,128)(2,1)S(1)}, u32[]{:S(2)}, u32[]{:S(2)}) collective-permute-start(bf16[1,96,768]{2,1,0:T(8,128)(2,1)S(1)} %cast_attn.1.refs_0_), channel_id=1, source_target_pairs={{0,8},{4,12},{8,0},{12,4},{16,24},{20,28},{24,16},{28,20},{1,9},{5... | collective-permute-start | bytes 442376 | tf_op jit(solution)/shard_map/ppermute | solution.py:94
  22.3 8.1 %collective-permute-start.4 = (bf16[2,1,96,768]{3,2,1,0:T(8,128)(2,1)S(1)}, bf16[2,1,96,768]{3,2,1,0:T(8,128)(2,1)S(1)}, u32[]{:S(2)}, u32[]{:S(2)}) collective-permute-start(bf16[2,1,96,768]{3,2,1,0:T(8,128)(2,1)S(1)} %line_up.8.refs_0_), channel_id=1, source_target_pairs={{0,4},{4,0},{8,12},{12,8},{16,20},{20,16},{24,28},{28,24},{1,5},{5... | collective-permute-start | bytes 884744 | tf_op jit(solution)/shard_map/ppermute | solution.py:89
  23.9 7.8 %collective-permute-start.3 = (bf16[2,1,96,768]{3,2,1,0:T(8,128)(2,1)S(1)}, bf16[2,1,96,768]{3,2,1,0:T(8,128)(2,1)S(1)}, u32[]{:S(2)}, u32[]{:S(2)}) collective-permute-start(bf16[2,1,96,768]{3,2,1,0:T(8,128)(2,1)S(1)} %line_up.7.refs_0_), channel_id=1, source_target_pairs={{0,2},{1,3},{2,0},{3,1},{4,6},{5,7},{6,4},{7,5},{8,10},{9,11},{10,... | collective-permute-start | bytes 884744 | tf_op jit(solution)/shard_map/ppermute | solution.py:84
  24.5 9.3 %collective-permute-start.6 = (bf16[2,96,768]{2,1,0:T(8,128)(2,1)S(1)}, bf16[2,96,768]{2,1,0:T(8,128)(2,1)S(1)}, u32[]{:S(2)}, u32[]{:S(2)}) collective-permute-start(bf16[2,96,768]{2,1,0:T(8,128)(2,1)S(1)} %cast_ffn.1.refs_0_), channel_id=1, source_target_pairs={{0,8},{4,12},{8,16},{12,20},{16,24},{20,28},{24,0},{28,4},{1,9},{5... | collective-permute-start | bytes 884744 | tf_op jit(solution)/shard_map/ppermute | solution.py:99
  33.8 8.5 %collective-permute-start.9 = (bf16[2,96,768]{2,1,0:T(8,128)(2,1)S(1)}, bf16[2,96,768]{2,1,0:T(8,128)(2,1)S(1)}, u32[]{:S(2)}, u32[]{:S(2)}) collective-permute-start(bf16[2,96,768]{2,1,0:T(8,128)(2,1)S(1)} %collective-permute-done.6.refs_1_), channel_id=1, source_target_pairs={{0,8},{4,12},{8,16},{12,20},{16,24},{20,28},{24,0},{28,4},{1,9},{5... | collective-permute-start | bytes 884744 | tf_op jit(solution)/shard_map/ppermute | solution.py:99
  33.9 19.9 %collective-permute-start.8 = (bf16[2,2,1,96,768]{4,3,2,1,0:T(8,128)(2,1)S(1)}, bf16[2,2,1,96,768]{4,3,2,1,0:T(8,128)(2,1)S(1)}, u32[]{:S(2)}, u32[]{:S(2)}) collective-permute-start(bf16[2,2,1,96,768]{4,3,2,1,0:T(8,128)(2,1)S(1)} %line_up.10.refs_1_.refs_3_.refs_5_.refs_7_.refs_9_), channel_id=1, source_target_pairs={{0,2},{1,3},{2,0},{3,1},{4,6},{5,7},{6,4},{7,5},{8,10},{9,11},{10,... | collective-permute-start | bytes 1769480 | tf_op jit(solution)/shard_map/ppermute | solution.py:84
  35.5 18.3 %collective-permute-start.7 = (bf16[2,2,1,96,768]{4,3,2,1,0:T(8,128)(2,1)S(1)}, bf16[2,2,1,96,768]{4,3,2,1,0:T(8,128)(2,1)S(1)}, u32[]{:S(2)}, u32[]{:S(2)}) collective-permute-start(bf16[2,2,1,96,768]{4,3,2,1,0:T(8,128)(2,1)S(1)} %line_up.9.refs_0_.refs_4_.refs_12_.refs_6_.refs_10_), channel_id=1, source_target_pairs={{0,4},{4,0},{8,12},{12,8},{16,20},{20,16},{24,28},{28,24},{1,5},{5... | collective-permute-start | bytes 1769480 | tf_op jit(solution)/shard_map/ppermute | solution.py:89
  42.3 11.5 %collective-permute-start.10 = (bf16[2,96,768]{2,1,0:T(8,128)(2,1)S(1)}, bf16[2,96,768]{2,1,0:T(8,128)(2,1)S(1)}, u32[]{:S(2)}, u32[]{:S(2)}) collective-permute-start(bf16[2,96,768]{2,1,0:T(8,128)(2,1)S(1)} %collective-permute-done.9.refs_0_), channel_id=1, source_target_pairs={{0,8},{4,12},{8,16},{12,20},{16,24},{20,28},{24,0},{28,4},{1,9},{5... | collective-permute-start | bytes 884744 | tf_op jit(solution)/shard_map/ppermute | solution.py:99
  53.8 2.5 %collective-permute-start.11 = (bf16[512,768]{1,0:T(8,128)(2,1)S(1)}, bf16[512,768]{1,0:T(8,128)(2,1)S(1)}, u32[]{:S(2)}, u32[]{:S(2)}) collective-permute-start(bf16[512,768]{1,0:T(8,128)(2,1)S(1)} %get-tuple-element.279.x_ref), channel_id=1, source_target_pairs={{0,1},{1,0},{2,3},{3,2},{4,5},{5,4},{6,7},{7,6},{8,9},{9,8},{10,11... | collective-permute-start | bytes 2359304 | tf_op jit(solution)/shard_map/ppermute | solution.py:80
  58.6 21.1 %collective-permute-start.14 = (bf16[2,2,1,96,768]{4,3,2,1,0:T(8,128)(2,1)S(1)}, bf16[2,2,1,96,768]{4,3,2,1,0:T(8,128)(2,1)S(1)}, u32[]{:S(2)}, u32[]{:S(2)}) collective-permute-start(bf16[2,2,1,96,768]{4,3,2,1,0:T(8,128)(2,1)S(1)} %line_up.9.refs_0_.refs_4_.refs_12_.refs_6_.refs_10_), channel_id=1, source_target_pairs={{0,1},{1,0},{2,3},{3,2},{4,5},{5,4},{6,7},{7,6},{8,9},{9,8},{10,11... | collective-permute-start | bytes 1769480 | tf_op jit(solution)/shard_map/ppermute | solution.py:80
  59.1 28.0 %collective-permute-start.19 = (bf16[2,2,2,96,768]{4,3,2,1,0:T(8,128)(2,1)S(1)}, bf16[2,2,2,96,768]{4,3,2,1,0:T(8,128)(2,1)S(1)}, u32[]{:S(2)}, u32[]{:S(2)}) collective-permute-start(bf16[2,2,2,96,768]{4,3,2,1,0:T(8,128)(2,1)S(1)} %line_up.13.refs_8_.refs_9_), channel_id=1, source_target_pairs={{0,4},{4,0},{8,12},{12,8},{16,20},{20,16},{24,28},{28,24},{1,5},{5... | collective-permute-start | bytes 3538952 | tf_op jit(solution)/shard_map/ppermute | solution.py:89
  59.7 27.7 %collective-permute-start.18 = (bf16[2,2,2,96,768]{4,3,2,1,0:T(8,128)(2,1)S(1)}, bf16[2,2,2,96,768]{4,3,2,1,0:T(8,128)(2,1)S(1)}, u32[]{:S(2)}, u32[]{:S(2)}) collective-permute-start(bf16[2,2,2,96,768]{4,3,2,1,0:T(8,128)(2,1)S(1)} %line_up.13.refs_8_.refs_9_), channel_id=1, source_target_pairs={{0,2},{1,3},{2,0},{3,1},{4,6},{5,7},{6,4},{7,5},{8,10},{9,11},{10,... | collective-permute-start | bytes 3538952 | tf_op jit(solution)/shard_map/ppermute | solution.py:84
  69.1 8.8 %collective-permute-start.12 = (bf16[512,256]{1,0:T(8,128)(2,1)S(1)}, bf16[512,256]{1,0:T(8,128)(2,1)S(1)}, u32[]{:S(2)}, u32[]{:S(2)}) collective-permute-start(bf16[512,256]{1,0:T(8,128)(2,1)S(1)} %get-tuple-element.377.ctx_other_ref.refs_3_), channel_id=1, source_target_pairs={{0,1},{1,0},{2,3},{3,2},{4,5},{5,4},{6,7},{7,6},{8,9},{9,8},{10,11... | collective-permute-start | bytes 786440 | tf_op jit(solution)/shard_map/ppermute | solution.py:80
  69.2 10.9 %collective-permute-start.15 = (bf16[2,2,1,96,768]{4,3,2,1,0:T(8,128)(2,1)S(1)}, bf16[2,2,1,96,768]{4,3,2,1,0:T(8,128)(2,1)S(1)}, u32[]{:S(2)}, u32[]{:S(2)}) collective-permute-start(bf16[2,2,1,96,768]{4,3,2,1,0:T(8,128)(2,1)S(1)} %line_up.10.refs_1_.refs_3_.refs_5_.refs_7_.refs_9_), channel_id=1, source_target_pairs={{0,1},{1,0},{2,3},{3,2},{4,5},{5,4},{6,7},{7,6},{8,9},{9,8},{10,11... | collective-permute-start | bytes 1769480 | tf_op jit(solution)/shard_map/ppermute | solution.py:80
  78.0 1.6 collective-permute-start.13
  79.6 2.0 collective-permute-start.16
  79.7 2.7 %collective-permute-start.17 = (bf16[2,2,1,96,768]{4,3,2,1,0:T(8,128)(2,1)S(1)}, bf16[2,2,1,96,768]{4,3,2,1,0:T(8,128)(2,1)S(1)}, u32[]{:S(2)}, u32[]{:S(2)}) collective-permute-start(bf16[2,2,1,96,768]{4,3,2,1,0:T(8,128)(2,1)S(1)} %collective-permute-done.8.refs_5_.refs_7_.refs_13_.refs_15_.refs_11_), channel_id=1, source_target_pairs={{0,1},{1,0},{2,3},{3,2},{4,5},{5,4},{6,7},{7,6},{8,9},{9,8},{10,11... | collective-permute-start | bytes 1769480 | tf_op jit(solution)/shard_map/ppermute | solution.py:80
  80.1 9.4 %collective-permute-start.23 = (bf16[768,512]{1,0:T(8,128)(2,1)S(1)}, bf16[768,512]{1,0:T(8,128)(2,1)S(1)}, u32[]{:S(2)}, u32[]{:S(2)}) collective-permute-start(bf16[768,512]{1,0:T(8,128)(2,1)S(1)} %get-tuple-element.342.refs_6_), channel_id=1, source_target_pairs={{0,1},{1,0},{2,3},{3,2},{4,5},{5,4},{6,7},{7,6},{8,9},{9,8},{10,11... | collective-permute-start | bytes 2359304 | tf_op jit(solution)/shard_map/ppermute | solution.py:80
  81.6 9.5 %collective-permute-start.22 = (bf16[512,768]{1,0:T(8,128)(2,1)S(1)}, bf16[512,768]{1,0:T(8,128)(2,1)S(1)}, u32[]{:S(2)}, u32[]{:S(2)}) collective-permute-start(bf16[512,768]{1,0:T(8,128)(2,1)S(1)} %get-tuple-element.341.refs_4_.back_ref), channel_id=1, source_target_pairs={{0,1},{1,0},{2,3},{3,2},{4,5},{5,4},{6,7},{7,6},{8,9},{9,8},{10,11... | collective-permute-start | bytes 2359304 | tf_op jit(solution)/shard_map/ppermute | solution.py:80
  87.4 14.3 %collective-permute-start.24 = (bf16[2,2,96,768]{3,2,1,0:T(8,128)(2,1)S(1)}, bf16[2,2,96,768]{3,2,1,0:T(8,128)(2,1)S(1)}, u32[]{:S(2)}, u32[]{:S(2)}) collective-permute-start(bf16[2,2,96,768]{3,2,1,0:T(8,128)(2,1)S(1)} %slice_bitcast_fusion.1), channel_id=1, source_target_pairs={{0,4},{4,0},{8,12},{12,8},{16,20},{20,16},{24,28},{28,24},{1,5},{5... | collective-permute-start | bytes 1769480 | tf_op jit(solution)/shard_map/ppermute | solution.py:89
  88.9 2.3 %collective-permute-start.20 = (bf16[512,768]{1,0:T(8,128)(2,1)S(1)}, bf16[512,768]{1,0:T(8,128)(2,1)S(1)}, u32[]{:S(2)}, u32[]{:S(2)}) collective-permute-start(bf16[512,768]{1,0:T(8,128)(2,1)S(1)} %get-tuple-element.339.refs_0_), channel_id=1, source_target_pairs={{0,1},{1,0},{2,3},{3,2},{4,5},{5,4},{6,7},{7,6},{8,9},{9,8},{10,11... | collective-permute-start | bytes 2359304 | tf_op jit(solution)/shard_map/ppermute | solution.py:80
  88.9 3.4 %collective-permute-start.21 = (bf16[768,512]{1,0:T(8,128)(2,1)S(1)}, bf16[768,512]{1,0:T(8,128)(2,1)S(1)}, u32[]{:S(2)}, u32[]{:S(2)}) collective-permute-start(bf16[768,512]{1,0:T(8,128)(2,1)S(1)} %get-tuple-element.340.refs_2_), channel_id=1, source_target_pairs={{0,1},{1,0},{2,3},{3,2},{4,5},{5,4},{6,7},{7,6},{8,9},{9,8},{10,11... | collective-permute-start | bytes 2359304 | tf_op jit(solution)/shard_map/ppermute | solution.py:80
  89.5 15.3 %collective-permute-start.25 = (bf16[2,2,96,768]{3,2,1,0:T(8,128)(2,1)S(1)}, bf16[2,2,96,768]{3,2,1,0:T(8,128)(2,1)S(1)}, u32[]{:S(2)}, u32[]{:S(2)}) collective-permute-start(bf16[2,2,96,768]{3,2,1,0:T(8,128)(2,1)S(1)} %slice_bitcast_fusion), channel_id=1, source_target_pairs={{0,2},{1,3},{2,0},{3,1},{4,6},{5,7},{6,4},{7,5},{8,10},{9,11},{10,... | collective-permute-start | bytes 1769480 | tf_op jit(solution)/shard_map/ppermute | solution.py:84
  113.6 2.4 %collective-permute-start.26 = (bf16[512,768]{1,0:T(8,128)(2,1)S(1)}, bf16[512,768]{1,0:T(8,128)(2,1)S(1)}, u32[]{:S(2)}, u32[]{:S(2)}) collective-permute-start(bf16[512,768]{1,0:T(8,128)(2,1)S(1)} %get-tuple-element.363), channel_id=1, source_target_pairs={{0,1},{1,0},{2,3},{3,2},{4,5},{5,4},{6,7},{7,6},{8,9},{9,8},{10,11... | collective-permute-start | bytes 2359304 | tf_op jit(solution)/shard_map/ppermute | solution.py:80
  113.7 33.4 %collective-permute-start.29 = (bf16[2,2,2,96,768]{4,3,2,1,0:T(8,128)(2,1)S(1)}, bf16[2,2,2,96,768]{4,3,2,1,0:T(8,128)(2,1)S(1)}, u32[]{:S(2)}, u32[]{:S(2)}) collective-permute-start(bf16[2,2,2,96,768]{4,3,2,1,0:T(8,128)(2,1)S(1)} %get-tuple-element.388), channel_id=1, source_target_pairs={{0,2},{1,3},{2,0},{3,1},{4,6},{5,7},{6,4},{7,5},{8,10},{9,11},{10,... | collective-permute-start | bytes 3538952 | tf_op jit(solution)/shard_map/ppermute | solution.py:84
  115.3 4.0 %collective-permute-start.28 = (bf16[512,768]{1,0:T(8,128)(2,1)S(1)}, bf16[512,768]{1,0:T(8,128)(2,1)S(1)}, u32[]{:S(2)}, u32[]{:S(2)}) collective-permute-start(bf16[512,768]{1,0:T(8,128)(2,1)S(1)} %get-tuple-element.369), channel_id=1, source_target_pairs={{0,1},{1,0},{2,3},{3,2},{4,5},{5,4},{6,7},{7,6},{8,9},{9,8},{10,11... | collective-permute-start | bytes 2359304 | tf_op jit(solution)/shard_map/ppermute | solution.py:80
  117.0 2.4 %collective-permute-start.27 = (bf16[512,768]{1,0:T(8,128)(2,1)S(1)}, bf16[512,768]{1,0:T(8,128)(2,1)S(1)}, u32[]{:S(2)}, u32[]{:S(2)}) collective-permute-start(bf16[512,768]{1,0:T(8,128)(2,1)S(1)} %get-tuple-element.370.own_ref), channel_id=1, source_target_pairs={{0,1},{1,0},{2,3},{3,2},{4,5},{5,4},{6,7},{7,6},{8,9},{9,8},{10,11... | collective-permute-start | bytes 2359304 | tf_op jit(solution)/shard_map/ppermute | solution.py:80
  117.2 29.9 %collective-permute-start.31 = (bf16[2,2,96,768]{3,2,1,0:T(8,128)(2,1)S(1)}, bf16[2,2,96,768]{3,2,1,0:T(8,128)(2,1)S(1)}, u32[]{:S(2)}, u32[]{:S(2)}) collective-permute-start(bf16[2,2,96,768]{3,2,1,0:T(8,128)(2,1)S(1)} %get-tuple-element.390), channel_id=1, source_target_pairs={{0,4},{4,0},{8,12},{12,8},{16,20},{20,16},{24,28},{28,24},{1,5},{5... | collective-permute-start | bytes 1769480 | tf_op jit(solution)/shard_map/ppermute | solution.py:89
  117.8 29.4 %collective-permute-start.30 = (bf16[2,2,96,768]{3,2,1,0:T(8,128)(2,1)S(1)}, bf16[2,2,96,768]{3,2,1,0:T(8,128)(2,1)S(1)}, u32[]{:S(2)}, u32[]{:S(2)}) collective-permute-start(bf16[2,2,96,768]{3,2,1,0:T(8,128)(2,1)S(1)} %get-tuple-element.389), channel_id=1, source_target_pairs={{0,4},{4,0},{8,12},{12,8},{16,20},{20,16},{24,28},{28,24},{1,5},{5... | collective-permute-start | bytes 1769480 | tf_op jit(solution)/shard_map/ppermute | solution.py:89
  147.7 16.2 %collective-permute-start.32 = (bf16[2,2,96,768]{3,2,1,0:T(8,128)(2,1)S(1)}, bf16[2,2,96,768]{3,2,1,0:T(8,128)(2,1)S(1)}, u32[]{:S(2)}, u32[]{:S(2)}) collective-permute-start(bf16[2,2,96,768]{3,2,1,0:T(8,128)(2,1)S(1)} %get-tuple-element.404), channel_id=1, source_target_pairs={{0,4},{4,0},{8,12},{12,8},{16,20},{20,16},{24,28},{28,24},{1,5},{5... | collective-permute-start | bytes 1769480 | tf_op jit(solution)/shard_map/ppermute | solution.py:89
  148.3 16.2 %collective-permute-start.33 = (bf16[2,2,96,768]{3,2,1,0:T(8,128)(2,1)S(1)}, bf16[2,2,96,768]{3,2,1,0:T(8,128)(2,1)S(1)}, u32[]{:S(2)}, u32[]{:S(2)}) collective-permute-start(bf16[2,2,96,768]{3,2,1,0:T(8,128)(2,1)S(1)} %get-tuple-element.405), channel_id=1, source_target_pairs={{0,2},{1,3},{2,0},{3,1},{4,6},{5,7},{6,4},{7,5},{8,10},{9,11},{10,... | collective-permute-start | bytes 1769480 | tf_op jit(solution)/shard_map/ppermute | solution.py:84
  156.4 9.6 %collective-permute-start.34 = (bf16[512,768]{1,0:T(8,128)(2,1)S(1)}, bf16[512,768]{1,0:T(8,128)(2,1)S(1)}, u32[]{:S(2)}, u32[]{:S(2)}) collective-permute-start(bf16[512,768]{1,0:T(8,128)(2,1)S(1)} %get-tuple-element.415), channel_id=1, source_target_pairs={{0,1},{1,0},{2,3},{3,2},{4,5},{5,4},{6,7},{7,6},{8,9},{9,8},{10,11... | collective-permute-start | bytes 2359304 | tf_op jit(solution)/shard_map/ppermute | solution.py:80
  156.5 19.5 %collective-permute-start.35 = (bf16[2,2,1,96,768]{4,3,2,1,0:T(8,128)(2,1)S(1)}, bf16[2,2,1,96,768]{4,3,2,1,0:T(8,128)(2,1)S(1)}, u32[]{:S(2)}, u32[]{:S(2)}) collective-permute-start(bf16[2,2,1,96,768]{4,3,2,1,0:T(8,128)(2,1)S(1)} %get-tuple-element.432), channel_id=1, source_target_pairs={{0,2},{1,3},{2,0},{3,1},{4,6},{5,7},{6,4},{7,5},{8,10},{9,11},{10,... | collective-permute-start | bytes 1769480 | tf_op jit(solution)/shard_map/ppermute | solution.py:84
  157.1 19.0 %collective-permute-start.36 = (bf16[2,2,1,96,768]{4,3,2,1,0:T(8,128)(2,1)S(1)}, bf16[2,2,1,96,768]{4,3,2,1,0:T(8,128)(2,1)S(1)}, u32[]{:S(2)}, u32[]{:S(2)}) collective-permute-start(bf16[2,2,1,96,768]{4,3,2,1,0:T(8,128)(2,1)S(1)} %get-tuple-element.433), channel_id=1, source_target_pairs={{0,4},{4,0},{8,12},{12,8},{16,20},{20,16},{24,28},{28,24},{1,5},{5... | collective-permute-start | bytes 1769480 | tf_op jit(solution)/shard_map/ppermute | solution.py:89
  164.8 12.4 %collective-permute-start.37 = (bf16[2,96,768]{2,1,0:T(8,128)(2,1)S(1)}, bf16[2,96,768]{2,1,0:T(8,128)(2,1)S(1)}, u32[]{:S(2)}, u32[]{:S(2)}) collective-permute-start(bf16[2,96,768]{2,1,0:T(8,128)(2,1)S(1)} %get-tuple-element.412), channel_id=1, source_target_pairs={{0,8},{4,12},{8,0},{12,4},{16,24},{20,28},{24,16},{28,20},{1,9},{5... | collective-permute-start | bytes 884744 | tf_op jit(solution)/shard_map/ppermute | solution.py:94
  165.5 22.8 %collective-permute-start.40 = (bf16[2,96,768]{2,1,0:T(8,128)(2,1)S(1)}, bf16[2,96,768]{2,1,0:T(8,128)(2,1)S(1)}, u32[]{:S(2)}, u32[]{:S(2)}) collective-permute-start(bf16[2,96,768]{2,1,0:T(8,128)(2,1)S(1)} %get-tuple-element.413), channel_id=1, source_target_pairs={{0,16},{4,20},{8,24},{12,28},{16,0},{20,4},{24,8},{28,12},{1,17},{... | collective-permute-start | bytes 884744 | tf_op jit(solution)/shard_map/ppermute | solution.py:94
  166.0 22.2 %collective-permute-start.41 = (bf16[2,96,768]{2,1,0:T(8,128)(2,1)S(1)}, bf16[2,96,768]{2,1,0:T(8,128)(2,1)S(1)}, u32[]{:S(2)}, u32[]{:S(2)}) collective-permute-start(bf16[2,96,768]{2,1,0:T(8,128)(2,1)S(1)} %get-tuple-element.414), channel_id=1, source_target_pairs={{0,24},{4,28},{8,16},{12,20},{16,8},{20,12},{24,0},{28,4},{1,25},{... | collective-permute-start | bytes 884744 | tf_op jit(solution)/shard_map/ppermute | solution.py:94
  177.5 10.8 %collective-permute-start.38 = (bf16[2,1,96,768]{3,2,1,0:T(8,128)(2,1)S(1)}, bf16[2,1,96,768]{3,2,1,0:T(8,128)(2,1)S(1)}, u32[]{:S(2)}, u32[]{:S(2)}) collective-permute-start(bf16[2,1,96,768]{3,2,1,0:T(8,128)(2,1)S(1)} %get-tuple-element.438), channel_id=1, source_target_pairs={{0,4},{4,0},{8,12},{12,8},{16,20},{20,16},{24,28},{28,24},{1,5},{5... | collective-permute-start | bytes 884744 | tf_op jit(solution)/shard_map/ppermute | solution.py:89
  179.0 9.3 %collective-permute-start.39 = (bf16[2,1,96,768]{3,2,1,0:T(8,128)(2,1)S(1)}, bf16[2,1,96,768]{3,2,1,0:T(8,128)(2,1)S(1)}, u32[]{:S(2)}, u32[]{:S(2)}) collective-permute-start(bf16[2,1,96,768]{3,2,1,0:T(8,128)(2,1)S(1)} %get-tuple-element.439), channel_id=1, source_target_pairs={{0,2},{1,3},{2,0},{3,1},{4,6},{5,7},{6,4},{7,5},{8,10},{9,11},{10,... | collective-permute-start | bytes 884744 | tf_op jit(solution)/shard_map/ppermute | solution.py:84
  188.3 16.7 %collective-permute-start.45 = (bf16[2,256,768]{2,1,0:T(8,128)(2,1)S(1)}, bf16[2,256,768]{2,1,0:T(8,128)(2,1)S(1)}, u32[]{:S(2)}, u32[]{:S(2)}) collective-permute-start(bf16[2,256,768]{2,1,0:T(8,128)(2,1)S(1)} %get-tuple-element.460), channel_id=1, source_target_pairs={{0,2},{1,3},{2,0},{3,1},{4,6},{5,7},{6,4},{7,5},{8,10},{9,11},{10,... | collective-permute-start | bytes 2359304 | tf_op jit(solution)/shard_map/ppermute | solution.py:84
  190.0 10.4 %collective-permute-start.42 = (bf16[1,96,768]{2,1,0:T(8,128)(2,1)S(1)}, bf16[1,96,768]{2,1,0:T(8,128)(2,1)S(1)}, u32[]{:S(2)}, u32[]{:S(2)}) collective-permute-start(bf16[1,96,768]{2,1,0:T(8,128)(2,1)S(1)} %get-tuple-element.457), channel_id=1, source_target_pairs={{0,8},{4,12},{8,0},{12,4},{16,24},{20,28},{24,16},{28,20},{1,9},{5... | collective-permute-start | bytes 442376 | tf_op jit(solution)/shard_map/ppermute | solution.py:94
  194.1 10.8 %collective-permute-start.43 = (bf16[1,96,768]{2,1,0:T(8,128)(2,1)S(1)}, bf16[1,96,768]{2,1,0:T(8,128)(2,1)S(1)}, u32[]{:S(2)}, u32[]{:S(2)}) collective-permute-start(bf16[1,96,768]{2,1,0:T(8,128)(2,1)S(1)} %get-tuple-element.458), channel_id=1, source_target_pairs={{0,16},{4,20},{8,24},{12,28},{16,0},{20,4},{24,8},{28,12},{1,17},{... | collective-permute-start | bytes 442376 | tf_op jit(solution)/shard_map/ppermute | solution.py:94
  194.3 10.7 %collective-permute-start.44 = (bf16[1,96,768]{2,1,0:T(8,128)(2,1)S(1)}, bf16[1,96,768]{2,1,0:T(8,128)(2,1)S(1)}, u32[]{:S(2)}, u32[]{:S(2)}) collective-permute-start(bf16[1,96,768]{2,1,0:T(8,128)(2,1)S(1)} %get-tuple-element.459), channel_id=1, source_target_pairs={{0,24},{4,28},{8,16},{12,20},{16,8},{20,12},{24,0},{28,4},{1,25},{... | collective-permute-start | bytes 442376 | tf_op jit(solution)/shard_map/ppermute | solution.py:94
  197.6 23.0 %copy-start.2 = (f32[2,96,768]{2,1,0:T(8,128)S(1)}, f32[2,96,768]{2,1,0:T(8,128)}, u32[]{:S(2)}) copy-start(f32[2,96,768]{2,1,0:T(8,128)} %get-tuple-element.238.ffn_ref) | copy-start | bytes 1769476
  205.9 14.7 %all-to-all-start.1 = ((bf16[32,16,128]{2,1,0:T(8,128)(2,1)}), bf16[32,16,128]{2,1,0:T(8,128)(2,1)S(1)}, u32[]{:S(2)}, u32[]{:S(2)}) async-start(bf16[32,16,128]{2,1,0:T(8,128)(2,1)} %get-tuple-element.470), calls=%async_computation.1 | async-start | bytes 262144 | tf_op jit(solution)/shard_map/all_to_all | solution.py:1203
  (4 other events, 33.6 us)
